TPU v7x, 32 devices: a whole 2x2x4 slice. The times are simulated.
32 devices in a mesh: span: 16 (over z, x, core), elem: 2 (over y).
Axes of the slice: x: 2, y: 2, z: 4, core: 2. Of those that a mesh axis runs over, the one named last changes fastest.
Arguments:
- current_block: float32 [16, 64, 20480], P('span', None, 'elem'), may hold values from -6 to 6
- search_block: float32 [16, 64, 20480], P('span', None, 'elem'), may hold values from -6 to 6
- previous_block: float32 [16, 64, 20480], P('span', None, 'elem'), may hold values from -6 to 6
- ground_spring: float32 [20480], P('elem'), may hold values from 1 to 18
- wire_tension: float32 [20480], P('elem'), may hold values from 0.3 to 13.5
- dropper_stiff: float32 [20480], P('elem'), may hold values from 0.3 to 3
- dropper_offset: int32 [20480], P('elem'), may hold values from 1 to 8
- span_link: float32 [20480], P('elem'), may hold values from 0.1 to 0.4
- ritz_rotation: float32 [16, 192, 64], P('span'), may hold values from -0.4375 to 0.4375
Outputs:
- next_block: float32 [16, 64, 20480], P('span', None, 'elem')
- next_residual: float32 [16, 64, 20480], P('span', None, 'elem')
- ritz_values: float32 [16, 64], P('span')
Inputs may be any that keep to these rules, and one draw needn't show every extreme that they name: `dropper_offset`: 20480 * i is joined by a dropper to 20480 * i + dropper_offset_i; droppers that would reach past 20480 20480 - 1 are absent.
All inputs are finite; a program needn't handle non-finite values.
Results may differ from a plain program's by a relative error of at most 0.00016.
Values sent between devices are 32-bit elements; how exact they have to be, the bound alone decides.
No kernel may reach another device: no remote copies, remote signals or barrier semaphores. Data moves between devices by JAX's collectives and lax.ppermute only.
A program may use at most 192 MiB of HBM per device.

v0:
```python
import math

import jax
import jax.numpy as jnp
from jax import lax
from jax.sharding import PartitionSpec as P

REACH = 8


def shifted(value, axis, steps):
    count = lax.axis_size(axis)
    leading, last = (max(0, -steps), min(count, count - steps))
    return lax.ppermute(value, axis, [(source, source + steps) for source in range(leading, last)])


def with_halo(cells, sides, width):
    for axis, dim in sides:
        count = lax.axis_size(axis)
        ends = count - 1
        head = lax.slice_in_dim(cells, 0, width, axis=dim)
        tail = lax.slice_in_dim(cells, cells.shape[dim] - width, cells.shape[dim], axis=dim)
        cells = jnp.concatenate(
            [
                lax.ppermute(tail, axis, [(i, (i + 1) % count) for i in range(ends)]),
                cells,
                lax.ppermute(head, axis, [((i + 1) % count, i) for i in range(ends)]),
            ],
            axis=dim,
        )
    return cells


def fourier_rows(count):
    row = jnp.arange(count)[:, None]
    col = jnp.arange(count)[None, :]
    half = count // 2
    wave = jnp.where(row <= half, row, row - half)
    phase = (wave * col % count).astype(jnp.float32) * (2.0 * math.pi / count)
    scaled = jnp.where(row <= half, jnp.cos(phase), jnp.sin(phase)) * math.sqrt(2.0 / count)
    edge = (row == 0) | (row == half)
    matrix = jnp.where(edge, jnp.cos(phase) * math.sqrt(1.0 / count), scaled)
    slots = jnp.arange(count)
    slot_wave = jnp.where(slots <= half, slots, slots - half)
    cosines = jnp.cos(slot_wave.astype(jnp.float32) * (2.0 * math.pi / count))
    return (matrix, cosines)


def along_spans(matrix, block):
    shape = block.shape
    flat = block.reshape(shape[0], -1)
    return jnp.dot(matrix, flat, precision=lax.Precision.HIGHEST).reshape(shape)


def on_device(
    current_block,
    search_block,
    previous_block,
    ground_spring,
    wire_tension,
    dropper_stiff,
    dropper_offset,
    span_link,
    ritz_rotation,
):
    reach = REACH
    span_dev = current_block.shape[0]
    dof_dev = current_block.shape[2]
    total = span_dev * lax.axis_size("span")
    matrix, cosines = fourier_rows(total)
    my_cosines = lax.dynamic_slice_in_dim(cosines, lax.axis_index("span") * span_dev, span_dev)
    gathered = (
        lax.all_to_all(current_block, "span", split_axis=1, concat_axis=0, tiled=True),
        lax.all_to_all(search_block, "span", split_axis=1, concat_axis=0, tiled=True),
        lax.all_to_all(previous_block, "span", split_axis=1, concat_axis=0, tiled=True),
    )
    moved = [along_spans(matrix, piece) for piece in gathered]
    slot_x, slot_w, slot_p = (
        lax.all_to_all(moved[0], "span", split_axis=0, concat_axis=1, tiled=True),
        lax.all_to_all(moved[1], "span", split_axis=0, concat_axis=1, tiled=True),
        lax.all_to_all(moved[2], "span", split_axis=0, concat_axis=1, tiled=True),
    )
    stacked = jnp.concatenate([slot_x, slot_w, slot_p], 1)
    position = lax.axis_index("elem") * dof_dev + jnp.arange(dof_dev)
    dof_all = dof_dev * lax.axis_size("elem")
    tension_here = jnp.where(position < dof_all - 1, wire_tension, 0.0)
    dropper_rows = jnp.stack(
        [
            jnp.where(
                (dropper_offset == distance) & (position + distance < dof_all), dropper_stiff, 0.0
            )
            for distance in range(1, reach + 1)
        ]
    )
    left_tension, left_rows = shifted(
        (tension_here[dof_dev - 1 :], dropper_rows[:, dof_dev - reach :]), "elem", 1
    )
    extended = with_halo(stacked, (("elem", 2),), reach)
    center = extended[:, :, reach : reach + dof_dev]
    tensions = jnp.concatenate([left_tension, tension_here])
    flux = tensions * (
        extended[:, :, reach - 1 : reach + dof_dev] - extended[:, :, reach : reach + dof_dev + 1]
    )
    applied = ground_spring * center + flux[:, :, 1:] - flux[:, :, :-1]
    rows_all = jnp.concatenate([left_rows, dropper_rows], 1)
    near = extended[:, :, : reach + dof_dev]
    for distance in range(1, reach + 1):
        flux = rows_all[distance - 1] * (
            near - extended[:, :, distance : distance + reach + dof_dev]
        )
        applied = (
            applied + flux[:, :, reach:] - flux[:, :, reach - distance : reach - distance + dof_dev]
        )
    applied = applied + (2.0 * (1.0 - my_cosines))[:, None, None] * span_link * center
    projected = jnp.einsum("sjm,sjd->smd", ritz_rotation, stacked, precision=lax.Precision.HIGHEST)
    stiff_projected = jnp.einsum(
        "sjm,sjd->smd", ritz_rotation, applied, precision=lax.Precision.HIGHEST
    )
    gram_stiff = jnp.einsum("sjd,skd->sjk", stacked, applied, precision=lax.Precision.HIGHEST)
    gram_plain = jnp.einsum("sjd,skd->sjk", stacked, stacked, precision=lax.Precision.HIGHEST)
    gram_stiff, gram_plain = lax.psum((gram_stiff, gram_plain), "elem")
    energy = jnp.einsum(
        "sjm,sjk,skm->sm", ritz_rotation, gram_stiff, ritz_rotation, precision=lax.Precision.HIGHEST
    )
    weight_sum = jnp.einsum(
        "sjm,sjk,skm->sm", ritz_rotation, gram_plain, ritz_rotation, precision=lax.Precision.HIGHEST
    )
    ritz = energy / (weight_sum + 1e-06)
    residual = stiff_projected - ritz[:, :, None] * projected
    back_matrix = matrix.T
    gathered = (
        lax.all_to_all(projected, "span", split_axis=1, concat_axis=0, tiled=True),
        lax.all_to_all(residual, "span", split_axis=1, concat_axis=0, tiled=True),
    )
    moved = [along_spans(back_matrix, piece) for piece in gathered]
    next_block, next_residual = (
        lax.all_to_all(moved[0], "span", split_axis=0, concat_axis=1, tiled=True),
        lax.all_to_all(moved[1], "span", split_axis=0, concat_axis=1, tiled=True),
    )
    return (next_block, next_residual, ritz)


def solution(mesh):
    return jax.shard_map(
        on_device,
        mesh=mesh,
        in_specs=(
            P("span", None, "elem"),
            P("span", None, "elem"),
            P("span", None, "elem"),
            P("elem"),
            P("elem"),
            P("elem"),
            P("elem"),
            P("elem"),
            P("span", None, None),
        ),
        out_specs=(P("span", None, "elem"), P("span", None, "elem"), P("span", None)),
        check_vma=False,
    )
```

profile of v0, /device:TPU:15, one launch (start us, length us, event | category | flops | bytes accessed | tf_op | source)
XLA Modules:
  0.0 843.8 jit_solution(2322407860406375653)
XLA Ops:
  7.2 5.9 copy.46
  13.1 6.6 all-to-all-start
  19.6 5.9 copy.50
  25.6 52.7 %all-to-all-done = f32[1,64,10240]{2,0,1:T(1,128)S(1)} async-done(((f32[1,64,10240]{2,0,1:T(1,128)}), f32[1,64,10240]{2,0,1:T(1,128)S(1)}, u32[]{:S(2)}, u32[]{:S(2)}) %all-to-all-start) | async-done | bytes 2621472 | tf_op jit(solution)/shard_map/all_to_all | solution.py:73
  84.7 6.0 copy.54
  90.7 52.7 %all-to-all-done.2 = f32[1,64,10240]{2,0,1:T(1,128)S(1)} async-done(((f32[1,64,10240]{2,0,1:T(1,128)}), f32[1,64,10240]{2,0,1:T(1,128)S(1)}, u32[]{:S(2)}, u32[]{:S(2)}) %all-to-all-start.2) | async-done | bytes 2621472 | tf_op jit(solution)/shard_map/all_to_all | solution.py:74
  150.1 9.5 %reduce.2 = f32[64,10240]{1,0:T(8,128)} reduce(f32[1,64,10240]{2,0,1:T(1,128)} %copy-done.2, f32[]{:T(128)} %constant.73), dimensions={0}, to_apply=%all_to_all.30.reduce_sub_computation | reduce | bytes 5242884 | tf_op jit(solution)/shard_map/all_to_all | solution.py:73
  170.5 38.1 %all-to-all-done.4 = f32[1,64,10240]{2,0,1:T(1,128)S(1)} async-done(((f32[1,64,10240]{2,0,1:T(1,128)}), f32[1,64,10240]{2,0,1:T(1,128)S(1)}, u32[]{:S(2)}, u32[]{:S(2)}) %all-to-all-start.4) | async-done | bytes 2621472 | tf_op jit(solution)/shard_map/all_to_all | solution.py:75
  210.2 5.4 all-to-all-start.1
  215.6 9.5 %reduce.3 = f32[64,10240]{1,0:T(8,128)} reduce(f32[1,64,10240]{2,0,1:T(1,128)} %copy-done.1, f32[]{:T(128)} %constant.73), dimensions={0}, to_apply=%all_to_all.33.reduce_sub_computation | reduce | bytes 5242884 | tf_op jit(solution)/shard_map/all_to_all | solution.py:74
  236.0 38.1 %all-to-all-done.1 = f32[16,4,10240]{2,1,0:T(4,128)S(1)} async-done(((f32[16,4,10240]{2,1,0:T(4,128)}), f32[16,4,10240]{2,1,0:T(4,128)S(1)}, u32[]{:S(2)}, u32[]{:S(2)}) %all-to-all-start.1) | async-done | bytes 2621472 | tf_op jit(solution)/shard_map/all_to_all | solution.py:79
  279.3 9.5 %reduce.4 = f32[64,10240]{1,0:T(8,128)} reduce(f32[1,64,10240]{2,0,1:T(1,128)} %copy-done, f32[]{:T(128)} %constant.73), dimensions={0}, to_apply=%all_to_all.36.reduce_sub_computation | reduce | bytes 5242884 | tf_op jit(solution)/shard_map/all_to_all | solution.py:75
  299.8 38.1 %all-to-all-done.3 = f32[16,4,10240]{2,1,0:T(4,128)} async-done(((f32[16,4,10240]{2,1,0:T(4,128)}), f32[16,4,10240]{2,1,0:T(4,128)}, u32[]{:S(2)}, u32[]{:S(2)}) %all-to-all-start.3) | async-done | bytes 2621472 | tf_op jit(solution)/shard_map/all_to_all | solution.py:80
  338.0 5.2 all-to-all-start.5
  361.7 40.1 %all-to-all-done.5 = f32[16,4,10240]{2,1,0:T(4,128)} async-done(((f32[16,4,10240]{2,1,0:T(4,128)}), f32[16,4,10240]{2,1,0:T(4,128)}, u32[]{:S(2)}, u32[]{:S(2)}) %all-to-all-start.5) | async-done | bytes 2621472 | tf_op jit(solution)/shard_map/all_to_all | solution.py:81
  407.4 10.8 %fusion.17 = f32[192,192]{1,0:T(8,128)} fusion(f32[1,192,10240]{2,1,0:T(8,128)} %constant_dynamic-update-slice_fusion), kind=kOutput, calls=%fused_computation.47 | convolution fusion | flops 4529848320 | bytes 8011776 | tf_op jit(solution)/shard_map/sjd,skd->sjk/dot_general | solution.py:120
  423.5 7.5 fusion.21
  435.3 5.4 all-to-all-start.6
  441.2 9.7 %concatenate.53 = f32[1,192,10256]{2,1,0:T(8,128)} concatenate(f32[1,192,8]{2,1,0:T(8,128)S(1)} %collective-permute-done.1, f32[1,192,10240]{2,1,0:T(8,128)} %constant_dynamic-update-slice_fusion, f32[1,192,8]{2,1,0:T(8,128)S(1)} %collective-permute-done.2), dimensions={2} | concatenate | bytes 15753216 | tf_op jit(solution)/shard_map/concatenate | solution.py:23
  450.9 9.7 %fusion.6 = f32[1,192,10241]{2,1,0:T(8,128)} fusion(f32[1,192,8]{2,1,0:T(8,128)S(1)} %collective-permute-done.2, f32[1,192,8]{2,1,0:T(8,128)S(1)} %collective-permute-done.1, f32[1,192,10240]{2,1,0:T(8,128)} %constant_dynamic-update-slice_fusion, f32[10241]{0:T(1024)S(1)} %pad_maximum_fusion.2), kind=kLoop, calls=%fused_computation.11 | loop fusion | flops 7865088 | bytes 15782660 | tf_op jit(solution)/shard_map/mul | solution.py:101
  460.6 30.5 %fusion.14 = (f32[1,192,10248]{2,1,0:T(8,128)}, f32[1,192,10248]{2,1,0:T(8,128)}, f32[1,192,10248]{2,1,0:T(8,128)}, f32[1,192,10248]{2,1,0:T(8,128)}) fusion(f32[1,192,10256]{2,1,0:T(8,128)} %concatenate.53, f32[10248]{0:T(1024)S(1)} %get-tuple-element.3, f32[1,192,10240]{2,1,0:T(8,128)} %constant_dynamic-update-slice_fusion, ...), kind=kLoop, calls=%fused_computation.26 | loop fusion | flops 17708544 | bytes 70998144 | tf_op jit(solution)/shard_map/mul | solution.py:108
  491.1 30.1 %fusion.13 = (f32[1,192,10248]{2,1,0:T(8,128)}, f32[1,192,10248]{2,1,0:T(8,128)}, f32[1,192,10248]{2,1,0:T(8,128)}, f32[1,192,10248]{2,1,0:T(8,128)}) fusion(f32[1,192,10256]{2,1,0:T(8,128)} %concatenate.53, f32[10248]{0:T(1024)S(1)} %get-tuple-element.4, f32[1,192,10240]{2,1,0:T(8,128)} %constant_dynamic-update-slice_fusion, ...), kind=kLoop, calls=%fused_computation.24 | loop fusion | flops 19676160 | bytes 63133824 | tf_op jit(solution)/shard_map/mul | solution.py:108
  521.2 67.3 %fusion.16 = f32[192,10240]{1,0:T(8,128)} fusion(f32[1,192,10248]{2,1,0:T(8,128)} %get-tuple-element.20, f32[1,192,10248]{2,1,0:T(8,128)} %get-tuple-element.14, f32[1,192,10248]{2,1,0:T(8,128)} %get-tuple-element.15, f32[1,192,10248]{2,1,0:T(8,128)} %get-tuple-element.16, f32[1,192,10248]{2,1,0:T(8,128)} %get-tuple-element.18, ...), kind=kLoop, calls=%fused_computation.29 | loop fusion | flops 41287680 | bytes 157368320 | tf_op jit(solution)/shard_map/reshape.49
  588.5 10.6 %fusion.19 = f32[192,192]{1,0:T(8,128)} fusion(f32[192,10240]{1,0:T(8,128)} %fusion.16, f32[1,192,10240]{2,1,0:T(8,128)} %constant_dynamic-update-slice_fusion), kind=kOutput, calls=%fused_computation.49 | convolution fusion | flops 4529848320 | bytes 15876096 | tf_op jit(solution)/shard_map/sjd,skd->sjk/dot_general | solution.py:119
  599.1 25.7 %all-reduce.3.cloned.1.call-done = (f32[192,192]{1,0:T(8,128)}, f32[192,192]{1,0:T(8,128)}) async-done(((f32[192,192]{1,0:T(8,128)}, f32[192,192]{1,0:T(8,128)}), (f32[192,192]{1,0:T(8,128)}, f32[192,192]{1,0:T(8,128)})) %all-reduce.3.cloned.1.call-update) | async-done | bytes 294928 | tf_op jit(solution)/shard_map/psum | solution.py:121
  627.4 7.9 fusion.1
  639.6 6.4 all-to-all-start.8
  645.9 9.5 %reduce.5 = f32[64,10240]{1,0:T(8,128)} reduce(f32[1,64,10240]{2,0,1:T(1,128)} %all-to-all-done.6, f32[]{:T(128)} %constant.73), dimensions={0}, to_apply=%all_to_all.39.reduce_sub_computation | reduce | bytes 5242884 | tf_op jit(solution)/shard_map/all_to_all | solution.py:132
  666.3 38.3 %all-to-all-done.8 = f32[1,64,10240]{2,0,1:T(1,128)S(1)} async-done(((f32[1,64,10240]{2,0,1:T(1,128)}), f32[1,64,10240]{2,0,1:T(1,128)S(1)}, u32[]{:S(2)}, u32[]{:S(2)}) %all-to-all-start.8) | async-done | bytes 2621472 | tf_op jit(solution)/shard_map/all_to_all | solution.py:133
  711.3 9.5 %reduce.14 = f32[64,10240]{1,0:T(8,128)} reduce(f32[1,64,10240]{2,0,1:T(1,128)} %copy-done.3, f32[]{:T(128)} %constant.73), dimensions={0}, to_apply=%all_to_all.42.reduce_sub_computation | reduce | bytes 5242884 | tf_op jit(solution)/shard_map/all_to_all | solution.py:133
  731.7 38.1 %all-to-all-done.7 = f32[16,4,10240]{2,1,0:T(4,128)S(1)} async-done(((f32[16,4,10240]{2,1,0:T(4,128)}), f32[16,4,10240]{2,1,0:T(4,128)S(1)}, u32[]{:S(2)}, u32[]{:S(2)}) %all-to-all-start.7) | async-done | bytes 2621472 | tf_op jit(solution)/shard_map/all_to_all | solution.py:137
  776.7 56.8 %all-to-all-done.9 = f32[16,4,10240]{2,1,0:T(4,128)} async-done(((f32[16,4,10240]{2,1,0:T(4,128)}), f32[16,4,10240]{2,1,0:T(4,128)}, u32[]{:S(2)}, u32[]{:S(2)}) %all-to-all-start.9) | async-done | bytes 2621472 | tf_op jit(solution)/shard_map/all_to_all | solution.py:138
  (79 shorter events, 131.5 us)
Async XLA Ops:
  13.1 65.2 %all-to-all-start = ((f32[1,64,10240]{2,0,1:T(1,128)}), f32[1,64,10240]{2,0,1:T(1,128)S(1)}, u32[]{:S(2)}, u32[]{:S(2)}) async-start(f32[1,64,10240]{2,0,1:T(1,128)} %copy.46), calls=%async_computation | async-start | bytes 5242880 | tf_op jit(solution)/shard_map/all_to_all | solution.py:73
  78.3 1.5 copy-start.2
  79.8 63.6 %all-to-all-start.2 = ((f32[1,64,10240]{2,0,1:T(1,128)}), f32[1,64,10240]{2,0,1:T(1,128)S(1)}, u32[]{:S(2)}, u32[]{:S(2)}) async-start(f32[1,64,10240]{2,0,1:T(1,128)} %copy.50), calls=%async_computation.2 | async-start | bytes 5242880 | tf_op jit(solution)/shard_map/all_to_all | solution.py:74
  143.4 1.5 copy-start.1
  144.9 63.8 %all-to-all-start.4 = ((f32[1,64,10240]{2,0,1:T(1,128)}), f32[1,64,10240]{2,0,1:T(1,128)S(1)}, u32[]{:S(2)}, u32[]{:S(2)}) async-start(f32[1,64,10240]{2,0,1:T(1,128)} %copy.54), calls=%async_computation.4 | async-start | bytes 5242880 | tf_op jit(solution)/shard_map/all_to_all | solution.py:75
  208.6 1.5 copy-start
  210.2 64.0 %all-to-all-start.1 = ((f32[16,4,10240]{2,1,0:T(4,128)}), f32[16,4,10240]{2,1,0:T(4,128)S(1)}, u32[]{:S(2)}, u32[]{:S(2)}) async-start(f32[16,4,10240]{2,1,0:T(4,128)} %copy.49), calls=%async_computation.1 | async-start | bytes 5242880 | tf_op jit(solution)/shard_map/all_to_all | solution.py:79
  274.1 63.8 %all-to-all-start.3 = ((f32[16,4,10240]{2,1,0:T(4,128)}), f32[16,4,10240]{2,1,0:T(4,128)}, u32[]{:S(2)}, u32[]{:S(2)}) async-start(f32[16,4,10240]{2,1,0:T(4,128)} %copy.53), calls=%async_computation.3 | async-start | bytes 5242880 | tf_op jit(solution)/shard_map/all_to_all | solution.py:80
  292.4 50.8 %copy-start.6 = (f32[10240]{0:T(1024)S(1)}, f32[10240]{0:T(1024)}, u32[]{:S(2)}) copy-start(f32[10240]{0:T(1024)} %param.14) | copy-start | bytes 122884
  292.4 50.8 %copy-start.7 = (s32[10240]{0:T(1024)S(1)}, s32[10240]{0:T(1024)}, u32[]{:S(2)}) copy-start(s32[10240]{0:T(1024)} %param.15) | copy-start | bytes 122884
  292.4 52.8 %copy-start.8 = (f32[10240]{0:T(1024)S(1)}, f32[10240]{0:T(1024)}, u32[]{:S(2)}) copy-start(f32[10240]{0:T(1024)} %param.13) | copy-start | bytes 122884
  292.4 56.0 %copy-start.9 = (f32[10240]{0:T(1024)S(1)}, f32[10240]{0:T(1024)}, u32[]{:S(2)}) copy-start(f32[10240]{0:T(1024)} %param.16) | copy-start | bytes 122884
  338.0 63.9 %all-to-all-start.5 = ((f32[16,4,10240]{2,1,0:T(4,128)}), f32[16,4,10240]{2,1,0:T(4,128)}, u32[]{:S(2)}, u32[]{:S(2)}) async-start(f32[16,4,10240]{2,1,0:T(4,128)} %copy.57), calls=%async_computation.5 | async-start | bytes 5242880 | tf_op jit(solution)/shard_map/all_to_all | solution.py:81
  343.9 7.4 collective-permute-start.3
  345.8 4.8 collective-permute-start
  404.1 19.5 %copy-start.4 = (f32[1,192,64]{1,2,0:T(8,128)S(1)}, f32[1,192,64]{1,2,0:T(8,128)}, u32[]{:S(2)}) copy-start(f32[1,192,64]{1,2,0:T(8,128)} %param.17) | copy-start | bytes 147460
  418.2 22.9 %collective-permute-start.1 = (f32[1,192,8]{2,1,0:T(8,128)}, f32[1,192,8]{2,1,0:T(8,128)S(1)}, u32[]{:S(2)}, u32[]{:S(2)}) collective-permute-start(f32[1,192,8]{2,1,0:T(8,128)} %get-tuple-element.21), channel_id=1, source_target_pairs={{0,1},{2,3},{4,5},{6,7},{8,9},{10,11},{12,13},{14,15},{16,17},{18,... | collective-permute-start | bytes 18440 | tf_op jit(solution)/shard_map/ppermute | solution.py:25
  419.5 21.6 %collective-permute-start.2 = (f32[1,192,8]{2,1,0:T(8,128)S(1)}, f32[1,192,8]{2,1,0:T(8,128)S(1)}, u32[]{:S(2)}, u32[]{:S(2)}) collective-permute-start(f32[1,192,8]{2,1,0:T(8,128)S(1)} %get-tuple-element.22), channel_id=1, source_target_pairs={{1,0},{3,2},{5,4},{7,6},{9,8},{11,10},{13,12},{15,14},{17,16},{19,... | collective-permute-start | bytes 18440 | tf_op jit(solution)/shard_map/ppermute | solution.py:27
  435.3 204.3 %all-to-all-start.6 = ((f32[1,64,10240]{2,0,1:T(1,128)}), f32[1,64,10240]{2,0,1:T(1,128)}, u32[]{:S(2)}, u32[]{:S(2)}) async-start(f32[1,64,10240]{2,0,1:T(1,128)} %copy.58), calls=%async_computation.6 | async-start | bytes 5242880 | tf_op jit(solution)/shard_map/all_to_all | solution.py:132
  440.7 184.1 %all-reduce.3.cloned.1.call-start = ((), (), s32[]{:S(2)}) async-start(), calls=%async_computation.10 | async-start | bytes 786432 | tf_op jit(solution)/shard_map/psum | solution.py:121
  491.1 30.1 %copy-start.5 = (f32[10240]{0:T(1024)S(1)}, f32[10240]{0:T(1024)}, u32[]{:S(2)}) copy-start(f32[10240]{0:T(1024)} %param.12) | copy-start | bytes 122884
  627.4 12.2 %copy-start.10 = (f32[64]{0:T(128)}, f32[64]{0:T(128)S(1)}, u32[]{:S(2)}) copy-start(f32[64]{0:T(128)S(1)} %add_divide_fusion) | copy-start | bytes 772
  639.6 65.0 %all-to-all-start.8 = ((f32[1,64,10240]{2,0,1:T(1,128)}), f32[1,64,10240]{2,0,1:T(1,128)S(1)}, u32[]{:S(2)}, u32[]{:S(2)}) async-start(f32[1,64,10240]{2,0,1:T(1,128)} %copy.61), calls=%async_computation.8 | async-start | bytes 5242880 | tf_op jit(solution)/shard_map/all_to_all | solution.py:133
  704.6 1.5 copy-start.3
  706.1 63.7 %all-to-all-start.7 = ((f32[16,4,10240]{2,1,0:T(4,128)}), f32[16,4,10240]{2,1,0:T(4,128)S(1)}, u32[]{:S(2)}, u32[]{:S(2)}) async-start(f32[16,4,10240]{2,1,0:T(4,128)} %copy.60), calls=%async_computation.7 | async-start | bytes 5242880 | tf_op jit(solution)/shard_map/all_to_all | solution.py:137
  769.8 63.7 %all-to-all-start.9 = ((f32[16,4,10240]{2,1,0:T(4,128)}), f32[16,4,10240]{2,1,0:T(4,128)}, u32[]{:S(2)}, u32[]{:S(2)}) async-start(f32[16,4,10240]{2,1,0:T(4,128)} %copy.63), calls=%async_computation.9 | async-start | bytes 5242880 | tf_op jit(solution)/shard_map/all_to_all | solution.py:138
Sparse Core Ops, SparseCore 0:
  599.3 25.5 all-reduce.2
where the time goes:
time: 853 us; the launch traced here: 844 us
  waiting for transfers between devices  421 us (49%)
  other arithmetic  187 us (22%)
  local copies, waits for them, and re-layouts  97.8 us (11%)
  starting transfers between devices  62.7 us (7%)
  matrix products  60.4 us (7%)
  between operations  15.2 us (2%)
    all_to_all x2, waiting for transfers between devices, on_device(): lax.all_to_all(moved[1], 'span', split_axis=0, concat_axis=1, tiled=True)  94.9 us
    all_to_all x2, waiting for transfers between devices, on_device(): lax.all_to_all(moved[0], 'span', split_axis=0, concat_axis=1, tiled=True)  76.2 us
    another operation x1, other arithmetic  67.3 us
    mul x2, other arithmetic, on_device(): rows_all[distance - 1]  60.6 us
    all_to_all x1, waiting for transfers between devices, on_device(): lax.all_to_all(current_block, 'span', split_axis=1, concat_axis=0, tiled=...  52.7 us
    all_to_all x1, waiting for transfers between devices, on_device(): lax.all_to_all(search_block, 'span', split_axis=1, concat_axis=0, tiled=T...  52.7 us
    all_to_all x1, waiting for transfers between devices, on_device(): lax.all_to_all(moved[2], 'span', split_axis=0, concat_axis=1, tiled=True)  40.1 us
    all_to_all x1, waiting for transfers between devices, on_device(): lax.all_to_all(residual, 'span', split_axis=1, concat_axis=0, tiled=True)  38.3 us
  transfers between devices with their start and end apart: 15, of which 11 were waited for; matrix products, arithmetic and copies ran while one was open for 36% of the time, Pallas kernels for 0%

commit v1 on v0

v1 whole, which is shorter than its diff:
```python
import math

import jax
import jax.numpy as jnp
from jax import lax
from jax.sharding import PartitionSpec as P

REACH = 8
HIGHEST = lax.Precision.HIGHEST


def fourier_rows(count):
    row = jnp.arange(count)[:, None]
    col = jnp.arange(count)[None, :]
    half = count // 2
    wave = jnp.where(row <= half, row, row - half)
    phase = (wave * col % count).astype(jnp.float32) * (2.0 * math.pi / count)
    scaled = jnp.where(row <= half, jnp.cos(phase), jnp.sin(phase)) * math.sqrt(2.0 / count)
    edge = (row == 0) | (row == half)
    matrix = jnp.where(edge, jnp.cos(phase) * math.sqrt(1.0 / count), scaled)
    slots = jnp.arange(count)
    slot_wave = jnp.where(slots <= half, slots, slots - half)
    cosines = jnp.cos(slot_wave.astype(jnp.float32) * (2.0 * math.pi / count))
    return (matrix, cosines)


def along_spans(matrix, block):
    shape = block.shape
    flat = block.reshape(shape[0], -1)
    return jnp.dot(matrix, flat, precision=HIGHEST).reshape(shape)


def spread(block, count):
    rows, dofs = block.shape
    return block.reshape(rows, count, dofs // count).transpose(1, 0, 2)


def collect(pieces):
    count, rows, dofs = pieces.shape
    return pieces.transpose(1, 0, 2).reshape(1, rows, count * dofs)


def exchange(pieces):
    return lax.all_to_all(pieces, "span", split_axis=0, concat_axis=0, tiled=True)


def to_next(cells, step):
    count, parts = lax.axis_size("span"), lax.axis_size("elem")
    line = [s * parts + e for e in range(parts) for s in range(count)]
    pairs = list(zip(line, line[1:]))
    if step < 0:
        pairs = [(b, a) for a, b in pairs]
    return lax.ppermute(cells, ("span", "elem"), pairs)


def coefficients(ground, tension, stiff, offset, link, count, dofs):
    dof_dev = ground.shape[0]
    start = lax.axis_index("span") * dofs
    elem = lax.axis_index("elem")
    dof_all = dof_dev * lax.axis_size("elem")
    position = elem * dof_dev + jnp.arange(dof_dev)
    distance = jnp.arange(1, REACH + 1)[:, None]
    weights = jnp.where((offset == distance) & (position + distance < dof_all), stiff, 0.0)
    wire = jnp.where((distance == 1) & (position < dof_all - 1), tension, 0.0)
    weights = weights + wire
    pairs = [(i, i + 1) for i in range(lax.axis_size("elem") - 1)]
    left = lax.ppermute(weights[:, dof_dev - REACH :], "elem", pairs)
    weights = jnp.concatenate([left, weights], 1)
    weights = lax.dynamic_slice_in_dim(weights, start, dofs + REACH, 1)
    ground = lax.dynamic_slice_in_dim(ground, start, dofs, 0)
    link = lax.dynamic_slice_in_dim(link, start, dofs, 0)
    return weights, ground, link


def on_device(
    current_block,
    search_block,
    previous_block,
    ground_spring,
    wire_tension,
    dropper_stiff,
    dropper_offset,
    span_link,
    ritz_rotation,
):
    count = lax.axis_size("span")
    dof_dev = current_block.shape[2]
    dofs = dof_dev // count
    matrix, cosines = fourier_rows(count)
    blocks = (current_block, search_block, previous_block)
    stacked = exchange(jnp.concatenate([spread(b[0], count) for b in blocks], 1))
    rotation = lax.all_gather(ritz_rotation, "span", axis=0, tiled=True)
    weights, ground, link = coefficients(
        ground_spring, wire_tension, dropper_stiff, dropper_offset, span_link, count, dofs
    )
    slots = along_spans(matrix, stacked)
    projected = jnp.einsum("jvm,jvd->jmd", rotation, slots, precision=HIGHEST)
    back = matrix.T
    next_block = collect(exchange(along_spans(back, projected)))
    before = to_next(projected[:, :, dofs - REACH :], 1)
    after = to_next(projected[:, :, :REACH], -1)
    wide = jnp.concatenate([before, projected, after], 2)
    stiff = ground * projected
    near = wide[:, :, : REACH + dofs]
    for distance in range(1, REACH + 1):
        flux = weights[distance - 1] * (near - wide[:, :, distance : distance + REACH + dofs])
        stiff = stiff + flux[:, :, REACH:] - flux[:, :, REACH - distance : REACH - distance + dofs]
    stiff = stiff + (2.0 * (1.0 - cosines))[:, None, None] * link * projected
    sums = jnp.stack([jnp.sum(projected * stiff, 2), jnp.sum(projected * projected, 2)])
    sums = lax.psum(sums, ("elem", "span"))
    ritz = sums[0] / (sums[1] + 1e-06)
    residual = stiff - ritz[:, :, None] * projected
    next_residual = collect(exchange(along_spans(back, residual)))
    my_ritz = lax.dynamic_slice_in_dim(ritz, lax.axis_index("span"), 1, 0)
    return (next_block, next_residual, my_ritz)


def solution(mesh):
    return jax.shard_map(
        on_device,
        mesh=mesh,
        in_specs=(
            P("span", None, "elem"),
            P("span", None, "elem"),
            P("span", None, "elem"),
            P("elem"),
            P("elem"),
            P("elem"),
            P("elem"),
            P("elem"),
            P("span", None, None),
        ),
        out_specs=(P("span", None, "elem"), P("span", None, "elem"), P("span", None)),
        check_vma=False,
    )
```

time: 853 us -> 471 us (0.55)
  waiting for transfers between devices: 421 us -> 105 us
  blocking collectives: 0 us -> 222 us
  other arithmetic: 187 us -> 47.4 us
  local copies, waits for them, and re-layouts: 97.8 us -> 27.9 us
  starting transfers between devices: 62.7 us -> 28.3 us
  matrix products: 60.4 us -> 30.3 us
  between operations: 15.2 us -> 1.3 us
    all_to_all x10 -> x3, waiting for transfers between devices: 393 us -> 50.4 us  [exchange(): lax.all_to_all(pieces, 'span', split_axis=0, concat_axis=0, tiled=True)]
    all_gather x0 -> x1, blocking collectives: none -> 185 us  [on_device(): rotation = lax.all_gather(ritz_rotation, 'span', axis=0, tiled=True)]
    another operation x1, other arithmetic: 67.3 us -> 0.01 us  [on_device(): jnp.stack([jnp.sum(projected * stiff, 2), jnp.sum(projected * projected,...]
    mul x4, other arithmetic: 70.3 us -> 13.3 us  [the longest x2 13.2 us: on_device(): weights[distance - 1]]
    ppermute x4 -> x3, waiting for transfers between devices: 2.21 us -> 54.7 us  [the longest x2 52.9 us: to_next(): return lax.ppermute(cells, ('span', 'elem'), pairs)]
    all_to_all x5 -> x0, other arithmetic: 47.3 us -> none  [the longest x1 9.48 us: on_device(): lax.all_to_all(residual, 'span', split_axis=1, concat_axis=0, tiled=True)]
    psum x0 -> x1, blocking collectives: none -> 36.6 us  [on_device(): sums = lax.psum(sums, ('elem', 'span'))]
    all_to_all x10 -> x3, starting transfers between devices: 54.4 us -> 20.6 us  [exchange(): lax.all_to_all(pieces, 'span', split_axis=0, concat_axis=0, tiled=True)]
  transfers between devices with their start and end apart: 15 -> 6, of which waited for: 11 -> 4; matrix products, arithmetic and copies ran while one was open for 36% -> 13% of each run, Pallas kernels for 0% -> 0%
where the time goes in v1:
time: 471 us; the launch traced here: 462 us
  blocking collectives  222 us (47%)
  waiting for transfers between devices  105 us (22%)
  other arithmetic  47.4 us (10%)
  matrix products  30.3 us (6%)
  starting transfers between devices  28.3 us (6%)
  local copies, waits for them, and re-layouts  27.9 us (6%)
    all_gather x1, blocking collectives, on_device(): rotation = lax.all_gather(ritz_rotation, 'span', axis=0, tiled=True)  185 us
    ppermute x2, waiting for transfers between devices, to_next(): return lax.ppermute(cells, ('span', 'elem'), pairs)  52.9 us
    all_to_all x3, waiting for transfers between devices, exchange(): lax.all_to_all(pieces, 'span', split_axis=0, concat_axis=0, tiled=True)  50.4 us
    psum x1, blocking collectives, on_device(): sums = lax.psum(sums, ('elem', 'span'))  36.6 us
    reduce_sum x1, other arithmetic, on_device(): jnp.sum(projected * stiff, 2)  27.2 us
    dot_general x3, matrix products, along_spans(): return jnp.dot(matrix, flat, precision=HIGHEST).reshape(shape)  22.1 us
    all_to_all x3, starting transfers between devices, exchange(): lax.all_to_all(pieces, 'span', split_axis=0, concat_axis=0, tiled=True)  20.6 us
    mul x2, other arithmetic, on_device(): weights[distance - 1]  13.2 us
  transfers between devices with their start and end apart: 6, of which 4 were waited for; matrix products, arithmetic and copies ran while one was open for 13% of the time, Pallas kernels for 0%

profile of v1, /device:TPU:15, one launch (start us, length us, event | category | flops | bytes accessed | tf_op | source)
XLA Modules:
  0.0 462.2 jit_solution(7122211904246178162)
XLA Ops:
  0.6 2.4 copy.44
  3.6 1.3 copy-done.2
  5.4 0.8 copy.75
  6.2 1.6 copy_bitcast_fusion
  7.8 3.4 pad_maximum_fusion
  11.2 6.7 %all-to-all-start = ((f32[16,192,640]{2,1,0:T(8,128)}), f32[16,192,640]{2,1,0:T(8,128)}, u32[]{:S(2)}, u32[]{:S(2)}) async-start(f32[16,192,640]{2,1,0:T(8,128)} %pad_maximum_fusion), calls=%async_computation | async-start | bytes 15728640 | tf_op jit(solution)/shard_map/all_to_all | solution.py:44
  18.0 185.3 %all_gather.3 = f32[16,192,64]{1,2,0:T(8,128)} all-gather(f32[1,192,64]{1,2,0:T(8,128)S(1)} %copy-done.3), channel_id=1, replica_groups=mesh['span'=16,'elem'=2] {'span'}, dimensions={0}, use_global_device_ids=true | all-gather | bytes 835584 | tf_op jit(solution)/shard_map/all_gather | solution.py:92
  203.3 14.9 %fusion = f32[16,192,640]{2,0,1:T(8,128)S(1)} fusion(s32[16]{0:T(128)S(1)} %iota_select_fusion, pred[16]{0:T(512)(128)(4,1)S(1)} %get-tuple-element.27, pred[16]{0:T(512)(128)(4,1)S(1)} %get-tuple-element.26, f32[2,8,192,640]{3,2,1,0:T(8,128)} %bitcast.30), kind=kOutput, calls=%fused_computation | convolution fusion | flops 377491968 | bytes 15728736 | tf_op jit(solution)/shard_map/dot_general | solution.py:30
  218.2 8.2 %fusion.3 = f32[16,640,64]{1,2,0:T(8,128)S(1)} fusion(f32[16,192,64]{1,2,0:T(8,128)S(1)} %copy-done, f32[16,192,640]{2,0,1:T(8,128)S(1)} %fusion), kind=kOutput, calls=%fused_computation.4 | convolution fusion | flops 1509949440 | bytes 11272192 | tf_op jit(solution)/shard_map/jvm,jvd->jmd/dot_general | solution.py:97
  226.5 3.6 fusion.16
  230.1 2.3 copy.33
  232.4 5.2 %all-to-all-start.1 = ((f32[16,64,640]{2,1,0:T(8,128)}), f32[16,64,640]{2,1,0:T(8,128)}, u32[]{:S(2)}, u32[]{:S(2)}) async-start(f32[16,64,640]{2,1,0:T(8,128)} %copy.33), calls=%async_computation.1 | async-start | bytes 5242880 | tf_op jit(solution)/shard_map/all_to_all | solution.py:44
  237.9 1.3 collective-permute-start
  240.9 1.8 collective-permute-done
  242.9 4.4 collective-permute-start.1
  247.4 1.9 collective-permute-start.2
  249.4 50.8 %collective-permute-done.1 = f32[16,64,8]{2,1,0:T(8,128)S(1)} collective-permute-done((f32[16,64,8]{2,1,0:T(8,128)S(1)}, f32[16,64,8]{2,1,0:T(8,128)S(1)}, u32[]{:S(2)}, u32[]{:S(2)}) %collective-permute-start.1) | collective-permute-done | bytes 32800 | tf_op jit(solution)/shard_map/ppermute | solution.py:53
  300.2 2.1 collective-permute-done.2
  302.3 1.0 pad_maximum_fusion.2
  303.3 6.9 %fusion.11 = (f32[16,64,648]{2,1,0:T(8,128)}, f32[16,64,648]{2,1,0:T(8,128)}, f32[16,64,648]{2,1,0:T(8,128)}, f32[16,64,648]{2,1,0:T(8,128)}) fusion(f32[16,64,656]{2,1,0:T(8,128)S(1)} %pad_maximum_fusion.2, f32[648]{0:T(1024)S(1)} %get-tuple-element.5, f32[16,64,640]{2,1,0:T(8,128)S(1)} %bitcast.75, f32[16,64,8]{2,1,0:T(8,128)S(1)} %collective-permute-done.1, ...), kind=kLoop, calls=%fused_computation.19 | loop fusion | flops 5971968 | bytes 23898240 | tf_op jit(solution)/shard_map/mul | solution.py:106
  310.2 6.3 %fusion.10 = (f32[16,64,648]{2,1,0:T(8,128)}, f32[16,64,648]{2,1,0:T(8,128)}, f32[16,64,648]{2,1,0:T(8,128)}, f32[16,64,648]{2,1,0:T(8,128)}) fusion(f32[16,64,656]{2,1,0:T(8,128)S(1)} %pad_maximum_fusion.2, f32[648]{0:T(1024)S(1)} %get-tuple-element.11, f32[16,64,640]{2,1,0:T(8,128)S(1)} %bitcast.76, f32[16,64,8]{2,1,0:T(8,128)S(1)} %collective-permute-done.1, ...), kind=kLoop, calls=%fused_computation.17 | loop fusion | flops 6635520 | bytes 21276800 | tf_op jit(solution)/shard_map/mul | solution.py:106
  316.5 27.2 %multiply_reduce_fusion.1 = (f32[16,64]{1,0:T(8,128)S(1)}, f32[16,64]{1,0:T(8,128)S(1)}, f32[16,64,640]{2,1,0:T(8,128)}) fusion(f32[16,640,64]{1,2,0:T(8,128)S(1)} %fusion.3, f32[16,640]{1,0:T(8,128)S(1)} %broadcast_multiply_fusion, f32[16,64,648]{2,1,0:T(8,128)} %get-tuple-element.21, f32[16,64,648]{2,1,0:T(8,128)} %get-tuple-element.15, ...), kind=kLoop, calls=%fused_computation.52 | loop fusion | flops 15071232 | bytes 47237632 | tf_op jit(solution)/shard_map/reduce_sum | solution.py:109
  343.7 36.6 %psum.7 = f32[2,16,64]{2,1,0:T(8,128)S(1)} all-reduce(f32[2,16,64]{2,1,0:T(8,128)S(1)} %pad_maximum_fusion.3), channel_id=1, replica_groups=mesh['span'=16,'elem'=2] {'elem','span'}, use_global_device_ids=true, to_apply=%region_2.3 | all-reduce | flops 2048 | bytes 16384 | tf_op jit(solution)/shard_map/psum | solution.py:110
  380.4 2.1 multiply_subtract_fusion
  382.4 3.6 fusion.13
  386.0 2.3 copy.36
  388.4 8.7 %all-to-all-start.2 = ((f32[16,64,640]{2,1,0:T(8,128)}), f32[16,64,640]{2,1,0:T(8,128)S(1)}, u32[]{:S(2)}, u32[]{:S(2)}) async-start(f32[16,64,640]{2,1,0:T(8,128)} %copy.36), calls=%async_computation.2 | async-start | bytes 5242880 | tf_op jit(solution)/shard_map/all_to_all | solution.py:44
  397.6 4.8 %copy.34 = f32[64,16,640]{2,1,0:T(8,128)} copy(f32[64,16,640]{2,0,1:T(8,128)} %bitcast.8) | data formatting | bytes 5242880 | tf_op jit(solution)/shard_map/transpose | solution.py:40
  402.3 3.0 reshape.135
  405.3 50.4 %all-to-all-done.2 = f32[16,64,640]{2,1,0:T(8,128)S(1)} async-done(((f32[16,64,640]{2,1,0:T(8,128)}), f32[16,64,640]{2,1,0:T(8,128)S(1)}, u32[]{:S(2)}, u32[]{:S(2)}) %all-to-all-start.2) | async-done | bytes 2621472 | tf_op jit(solution)/shard_map/all_to_all | solution.py:44
  455.7 3.0 copy.37
  458.7 3.0 reshape.137
  (36 shorter events, 4.0 us)
Async XLA Ops:
  0.6 2.5 copy-start.1
  3.2 1.7 copy-start.2
  11.2 6.8 %copy-start.3 = (f32[1,192,64]{1,2,0:T(8,128)S(1)}, f32[1,192,64]{1,2,0:T(8,128)}, u32[]{:S(2)}) copy-start(f32[1,192,64]{1,2,0:T(8,128)} %param.17) | copy-start | bytes 147460
  11.2 192.1 %all-to-all-start = ((f32[16,192,640]{2,1,0:T(8,128)}), f32[16,192,640]{2,1,0:T(8,128)}, u32[]{:S(2)}, u32[]{:S(2)}) async-start(f32[16,192,640]{2,1,0:T(8,128)} %pad_maximum_fusion), calls=%async_computation | async-start | bytes 15728640 | tf_op jit(solution)/shard_map/all_to_all | solution.py:44
  203.3 14.9 %copy-start = (f32[16,192,64]{1,2,0:T(8,128)S(1)}, f32[16,192,64]{1,2,0:T(8,128)}, u32[]{:S(2)}) copy-start(f32[16,192,64]{1,2,0:T(8,128)} %all_gather.3) | copy-start | bytes 2359300
  232.4 5.3 %copy-start.4 = (f32[10240]{0:T(1024)S(1)}, f32[10240]{0:T(1024)}, u32[]{:S(2)}) copy-start(f32[10240]{0:T(1024)} %param.13) | copy-start | bytes 122884
  232.4 5.3 %copy-start.5 = (f32[10240]{0:T(1024)S(1)}, f32[10240]{0:T(1024)}, u32[]{:S(2)}) copy-start(f32[10240]{0:T(1024)} %param.14) | copy-start | bytes 122884
  232.4 5.3 %copy-start.6 = (s32[10240]{0:T(1024)S(1)}, s32[10240]{0:T(1024)}, u32[]{:S(2)}) copy-start(s32[10240]{0:T(1024)} %param.15) | copy-start | bytes 122884
  232.4 156.0 %all-to-all-start.1 = ((f32[16,64,640]{2,1,0:T(8,128)}), f32[16,64,640]{2,1,0:T(8,128)}, u32[]{:S(2)}, u32[]{:S(2)}) async-start(f32[16,64,640]{2,1,0:T(8,128)} %copy.33), calls=%async_computation.1 | async-start | bytes 5242880 | tf_op jit(solution)/shard_map/all_to_all | solution.py:44
  237.9 4.7 %collective-permute-start = (f32[8,8]{1,0:T(8,128)S(1)}, f32[8,8]{1,0:T(8,128)S(1)}, u32[]{:S(2)}, u32[]{:S(2)}) collective-permute-start(f32[8,8]{1,0:T(8,128)S(1)} %slice.148), channel_id=1, source_target_pairs={{0,1},{2,3},{4,5},{6,7},{8,9},{10,11},{12,13},{14,15},{16,17},{18,... | collective-permute-start | bytes 776 | tf_op jit(solution)/shard_map/ppermute | solution.py:67
  242.9 57.2 %collective-permute-start.1 = (f32[16,64,8]{2,1,0:T(8,128)S(1)}, f32[16,64,8]{2,1,0:T(8,128)S(1)}, u32[]{:S(2)}, u32[]{:S(2)}) collective-permute-start(f32[16,64,8]{2,1,0:T(8,128)S(1)} %get-tuple-element.22), channel_id=1, source_target_pairs={{0,2},{2,4},{4,6},{6,8},{8,10},{10,12},{12,14},{14,16},{16,18},{18... | collective-permute-start | bytes 98312 | tf_op jit(solution)/shard_map/ppermute | solution.py:53
  247.4 54.9 %collective-permute-start.2 = (f32[16,64,8]{2,1,0:T(8,128)S(1)}, f32[16,64,8]{2,1,0:T(8,128)S(1)}, u32[]{:S(2)}, u32[]{:S(2)}) collective-permute-start(f32[16,64,8]{2,1,0:T(8,128)S(1)} %get-tuple-element.23), channel_id=1, source_target_pairs={{2,0},{4,2},{6,4},{8,6},{10,8},{12,10},{14,12},{16,14},{18,16},{20... | collective-permute-start | bytes 98312 | tf_op jit(solution)/shard_map/ppermute | solution.py:53
  388.4 67.3 %all-to-all-start.2 = ((f32[16,64,640]{2,1,0:T(8,128)}), f32[16,64,640]{2,1,0:T(8,128)S(1)}, u32[]{:S(2)}, u32[]{:S(2)}) async-start(f32[16,64,640]{2,1,0:T(8,128)} %copy.36), calls=%async_computation.2 | async-start | bytes 5242880 | tf_op jit(solution)/shard_map/all_to_all | solution.py:44

commit v2 on v1

--- a/solution.py
+++ b/solution.py
@@ -3,9 +3,14 @@
 import jax
 import jax.numpy as jnp
 from jax import lax
+from jax.experimental import pallas as pl
+from jax.experimental.pallas import tpu as pltpu
 from jax.sharding import PartitionSpec as P
 
 REACH = 8
+LANES = 128
+ROWS = 8
+VMEM_LIMIT = 40 * 1024 * 1024
 HIGHEST = lax.Precision.HIGHEST
 
 
@@ -70,6 +75,342 @@
     ground = lax.dynamic_slice_in_dim(ground, start, dofs, 0)
     link = lax.dynamic_slice_in_dim(link, start, dofs, 0)
     return weights, ground, link
+
+
+def add_up(terms):
+    total = terms[0]
+    for term in terms[1:]:
+        total = total + term
+    return total
+
+
+def scaled(factor, value):
+    if abs(factor - 1.0) < 1e-12:
+        return value
+    return value * factor
+
+
+def cosine_sums(a):
+    n = len(a) - 1
+    if n == 1:
+        return [a[0] + a[1], a[0] - a[1]]
+    half = n // 2
+    even = cosine_sums([a[s] + a[n - s] for s in range(half)] + [a[half]])
+    diff = [a[s] - a[n - s] for s in range(half)]
+    out = [None] * (n + 1)
+    out[0::2] = even
+    for j in range(1, n, 2):
+        out[j] = add_up([scaled(math.cos(math.pi * j * s / n), diff[s]) for s in range(half)])
+    return out
+
+
+def sine_sums(b):
+    n = len(b) + 1
+    if n == 1:
+        return []
+    half = n // 2
+    at = [None] + list(b)
+    even = sine_sums([at[s] - at[n - s] for s in range(1, half)])
+    total = [None] + [at[s] + at[n - s] for s in range(1, half)] + [at[half]]
+    out = [None] * (n + 1)
+    for k, value in enumerate(even):
+        out[2 * k + 2] = value
+    for j in range(1, n, 2):
+        terms = [(math.sin(math.pi * j * s / n), total[s]) for s in range(1, half + 1)]
+        terms = [scaled(abs(f), t) if f > 0 else -scaled(abs(f), t) for f, t in terms]
+        out[j] = add_up(terms)
+    return out[1:n]
+
+
+def slot_scales(count):
+    edge, inner = math.sqrt(1.0 / count), math.sqrt(2.0 / count)
+    return [edge if j in (0, count // 2) else inner for j in range(count)]
+
+
+def to_slots(x):
+    n = len(x)
+    half = n // 2
+    plus = [x[0]] + [x[s] + x[n - s] for s in range(1, half)] + [x[half]]
+    minus = [x[s] - x[n - s] for s in range(1, half)]
+    return cosine_sums(plus) + sine_sums(minus)
+
+
+def to_spans(y):
+    n = len(y)
+    half = n // 2
+    even = cosine_sums(y[: half + 1])
+    odd = [None] + sine_sums(y[half + 1 :])
+    out = [None] * n
+    out[0], out[half] = even[0], even[half]
+    for s in range(1, half):
+        out[s] = even[s] + odd[s]
+        out[n - s] = even[s] - odd[s]
+    return out
+
+
+def params(**kw):
+    return pltpu.CompilerParams(vmem_limit_bytes=VMEM_LIMIT, **kw)
+
+
+def spread_blocks(blocks, count):
+    _, rows, dof_dev = blocks[0].shape
+    dofs = dof_dev // count
+    kinds = len(blocks)
+
+    def kernel(*refs):
+        out = refs[-1]
+        for k in range(kinds):
+            out[0, k * rows : (k + 1) * rows, :] = refs[k][0]
+
+    return pl.pallas_call(
+        kernel,
+        grid=(count,),
+        in_specs=[pl.BlockSpec((1, rows, dofs), lambda i: (0, 0, i))] * kinds,
+        out_specs=pl.BlockSpec((1, kinds * rows, dofs), lambda i: (i, 0, 0)),
+        out_shape=jax.ShapeDtypeStruct((count, kinds * rows, dofs), jnp.float32),
+        compiler_params=params(),
+        name="spread_blocks",
+    )(*blocks)
+
+
+def collect_block(pieces):
+    count, rows, dofs = pieces.shape
+
+    def kernel(piece, out):
+        out[...] = piece[...]
+
+    return pl.pallas_call(
+        kernel,
+        grid=(count,),
+        in_specs=[pl.BlockSpec((1, rows, dofs), lambda i: (i, 0, 0))],
+        out_specs=pl.BlockSpec((1, rows, dofs), lambda i: (0, 0, i)),
+        out_shape=jax.ShapeDtypeStruct((1, rows, count * dofs), jnp.float32),
+        compiler_params=params(),
+        name="collect_block",
+    )(pieces)
+
+
+def project(stacked, rotation):
+    count, wide, dofs = stacked.shape
+    rows = rotation.shape[1]
+    tiles = dofs // LANES
+    scales = slot_scales(count)
+    groups = -(-count * REACH // LANES)
+    per = LANES // REACH
+
+    def kernel(x, rot, proj, back, head, tail, slots):
+        tile = pl.program_id(0)
+
+        def transform(r, carry):
+            at = pl.ds(pl.multiple_of(r * ROWS, ROWS), ROWS)
+            out = to_slots([x[s, at, :] for s in range(count)])
+            for j in range(count):
+                slots[j, at, :] = out[j]
+            return carry
+
+        lax.fori_loop(0, wide // ROWS, transform, 0)
+        for j in range(count):
+            proj[j] = jnp.dot(
+                rot[j], slots[j], precision=HIGHEST, preferred_element_type=jnp.float32
+            )
+
+        def inverse(r, carry):
+            at = pl.ds(pl.multiple_of(r * ROWS, ROWS), ROWS)
+            out = to_spans([proj[j, at, :] * scales[j] for j in range(count)])
+            for s in range(count):
+                back[s, at, :] = out[s]
+            return carry
+
+        lax.fori_loop(0, rows // ROWS, inverse, 0)
+        lane = lax.broadcasted_iota(jnp.int32, (rows, LANES), 1)
+
+        def pack(ref, start):
+            for g in range(groups):
+                packed = jnp.zeros((rows, LANES), jnp.float32)
+                for k in range(min(per, count - g * per)):
+                    turn = (k * REACH - start) % LANES
+                    value = proj[g * per + k]
+                    value = pltpu.roll(value, turn, 1) if turn else value
+                    packed = jnp.where(lane // REACH == k, value, packed)
+                ref[g] = packed
+
+        @pl.when(tile == 0)
+        def _():
+            pack(head, 0)
+
+        @pl.when(tile == tiles - 1)
+        def _():
+            pack(tail, LANES - REACH)
+
+    cell = pl.BlockSpec((count, rows, LANES), lambda t: (0, 0, t))
+    edge = pl.BlockSpec((groups, rows, LANES), lambda t: (0, 0, 0))
+    field = jax.ShapeDtypeStruct((count, rows, dofs), jnp.float32)
+    edges = jax.ShapeDtypeStruct((groups, rows, LANES), jnp.float32)
+    return pl.pallas_call(
+        kernel,
+        grid=(tiles,),
+        in_specs=[
+            pl.BlockSpec((count, wide, LANES), lambda t: (0, 0, t)),
+            pl.BlockSpec((count, rows, wide), lambda t: (0, 0, 0)),
+        ],
+        out_specs=[cell, cell, edge, edge],
+        out_shape=[field, field, edges, edges],
+        scratch_shapes=[pltpu.VMEM((count, wide, LANES), jnp.float32)],
+        compiler_params=params(),
+        name="project",
+    )(stacked, rotation)
+
+
+def stiffness(projected, before, after, bands, links):
+    count, rows, dofs = projected.shape
+    per = LANES // REACH
+    strips = rows // ROWS
+
+    def kernel(x, left, right, band, lam, stiff, sums, energy, norm):
+        def strip(it, carry):
+            j, r = it // strips, it % strips
+            at = pl.ds(pl.multiple_of(r * ROWS, ROWS), ROWS)
+            to = pl.ds(pl.multiple_of(it * ROWS, ROWS), ROWS)
+            g, k = j // per, j % per
+            here = x[j, at, :]
+            low = pltpu.roll(left[g, at, :], (2 * LANES - REACH - REACH * k) % LANES, 1)
+            high = pltpu.roll(right[g, at, :], (LANES - REACH * k) % LANES, 1)
+            full = jnp.concatenate([low, here, high], 1)
+            size = dofs + 2 * LANES
+            total = (band[16:17, :] + lam[j] * band[17:18, :]) * here
+            for d in range(1, REACH + 1):
+                up = pltpu.roll(full, size - d, 1)[:, LANES : LANES + dofs]
+                down = pltpu.roll(full, d, 1)[:, LANES : LANES + dofs]
+                total = total - band[d - 1 : d, :] * up
+                total = total - band[REACH + d - 1 : REACH + d, :] * down
+            stiff[j, at, :] = total
+            both, own = total * here, here * here
+            tiles = [slice(t * LANES, (t + 1) * LANES) for t in range(dofs // LANES)]
+            energy[to, :] = add_up([both[:, t] for t in tiles])
+            norm[to, :] = add_up([own[:, t] for t in tiles])
+            return carry
+
+        lax.fori_loop(0, count * strips, strip, 0)
+        ones = jnp.ones((ROWS, LANES), jnp.float32)
+        for row, part in enumerate((energy, norm)):
+            line = lax.dot_general(
+                ones,
+                part[...],
+                (((1,), (1,)), ((), ())),
+                precision=HIGHEST,
+                preferred_element_type=jnp.float32,
+            )
+            sums[row : row + 1, :] = line[:1]
+
+    vmem = pl.BlockSpec(memory_space=pltpu.VMEM)
+    return pl.pallas_call(
+        kernel,
+        in_specs=[vmem, vmem, vmem, vmem, pl.BlockSpec(memory_space=pltpu.SMEM)],
+        out_specs=[vmem, vmem],
+        out_shape=[
+            jax.ShapeDtypeStruct((count, rows, dofs), jnp.float32),
+            jax.ShapeDtypeStruct((2, count * rows), jnp.float32),
+        ],
+        scratch_shapes=[pltpu.VMEM((count * rows, LANES), jnp.float32)] * 2,
+        compiler_params=params(),
+        name="stiffness",
+    )(projected, before, after, bands, links)
+
+
+def residual_back(projected, stiff, sums):
+    count, rows, dofs = projected.shape
+    scales = slot_scales(count)
+
+    def kernel(x, kx, total, back, ritz, wide):
+        @pl.when(pl.program_id(0) == 0)
+        def _():
+            value = total[0:1, :] / (total[1:2, :] + 1e-06)
+            ritz[...] = value
+            row = lax.broadcasted_iota(jnp.int32, (ROWS, count * rows), 0)
+            first = jnp.where(row == 0, value, 0.0)
+            ones = jnp.ones((ROWS, LANES), jnp.float32)
+            spread_out = lax.dot_general(
+                first,
+                ones,
+                (((0,), (0,)), ((), ())),
+                precision=HIGHEST,
+                preferred_element_type=jnp.float32,
+            )
+            wide[...] = spread_out
+
+        def strip(r, carry):
+            at = pl.ds(pl.multiple_of(r * ROWS, ROWS), ROWS)
+            terms = []
+            for j in range(count):
+                to = pl.ds(pl.multiple_of(j * rows + r * ROWS, ROWS), ROWS)
+                terms.append((kx[j, at, :] - wide[to, :] * x[j, at, :]) * scales[j])
+            out = to_spans(terms)
+            for s in range(count):
+                back[s, at, :] = out[s]
+            return carry
+
+        lax.fori_loop(0, rows // ROWS, strip, 0)
+
+    cell = pl.BlockSpec((count, rows, LANES), lambda t: (0, 0, t))
+    return pl.pallas_call(
+        kernel,
+        grid=(dofs // LANES,),
+        in_specs=[cell, cell, pl.BlockSpec((2, count * rows), lambda t: (0, 0))],
+        out_specs=[cell, pl.BlockSpec((1, count * rows), lambda t: (0, 0))],
+        out_shape=[
+            jax.ShapeDtypeStruct((count, rows, dofs), jnp.float32),
+            jax.ShapeDtypeStruct((1, count * rows), jnp.float32),
+        ],
+        scratch_shapes=[pltpu.VMEM((count * rows, LANES), jnp.float32)],
+        compiler_params=params(),
+        name="residual_back",
+    )(projected, stiff, sums)
+
+
+def sum_over_all(value):
+    for axis in ("elem", "span"):
+        size = lax.axis_size(axis)
+        step = 1
+        while step < size:
+            value = value + lax.ppermute(value, axis, [(i, i ^ step) for i in range(size)])
+            step *= 2
+    return value
+
+
+def tiled_device(
+    current_block,
+    search_block,
+    previous_block,
+    ground_spring,
+    wire_tension,
+    dropper_stiff,
+    dropper_offset,
+    span_link,
+    ritz_rotation,
+):
+    count = lax.axis_size("span")
+    dofs = current_block.shape[2] // count
+    rows = current_block.shape[1]
+    stacked = exchange(spread_blocks((current_block, search_block, previous_block), count))
+    scales = jnp.array(slot_scales(count), jnp.float32)[:, None, None]
+    rotation = lax.all_gather(ritz_rotation.transpose(0, 2, 1), "span", axis=0, tiled=True)
+    weights, ground, link = coefficients(
+        ground_spring, wire_tension, dropper_stiff, dropper_offset, span_link, count, dofs
+    )
+    up = weights[:, REACH:]
+    down = [weights[d - 1, REACH - d : REACH - d + dofs] for d in range(1, REACH + 1)]
+    down = jnp.stack(down)
+    diagonal = ground + jnp.sum(up, 0) + jnp.sum(down, 0)
+    bands = jnp.concatenate([up, down, diagonal[None], link[None]])
+    links = 2.0 * (1.0 - fourier_rows(count)[1])
+    projected, spans, head, tail = project(stacked, rotation * scales)
+    next_block = collect_block(exchange(spans))
+    before, after = to_next(tail, 1), to_next(head, -1)
+    stiff, sums = stiffness(projected, before, after, bands, links)
+    spans, ritz = residual_back(projected, stiff, sum_over_all(sums))
+    next_residual = collect_block(exchange(spans))
+    ritz = lax.dynamic_slice_in_dim(ritz, lax.axis_index("span") * rows, rows, 1)
+    return (next_block, next_residual, ritz)
 
 
 def on_device(
@@ -115,9 +456,17 @@
     return (next_block, next_residual, my_ritz)
 
 
+def by_shape(*args):
+    count, dof_dev = lax.axis_size("span"), args[0].shape[2]
+    halves = count & (count - 1) == 0 and lax.axis_size("elem") in (1, 2, 4, 8, 16)
+    if halves and count > 1 and dof_dev % (count * LANES) == 0:
+        return tiled_device(*args)
+    return on_device(*args)
+
+
 def solution(mesh):
     return jax.shard_map(
-        on_device,
+        by_shape,
         mesh=mesh,
         in_specs=(
             P("span", None, "elem"),

time: 471 us -> 409 us (0.87); the launches traced: 462 us -> 408 us
  Pallas kernels: 0 us -> 66 us
  other arithmetic: 47.4 us -> 1.48 us
  blocking collectives: 222 us -> 184 us
  matrix products: 30.3 us -> 0 us
  local copies, waits for them, and re-layouts: 27.9 us -> 13 us
  waiting for transfers between devices: 105 us -> 113 us
    pallas_call x0 -> x6, Pallas kernels: none -> 66 us  [the longest x1 26.3 us: stiffness(): pl.pallas_call(kernel, in_specs=[vmem, vmem, vmem, vmem, pl.BlockSpec(mem...]
    psum x1 -> x0, blocking collectives: 36.6 us -> none  [on_device(): sums = lax.psum(sums, ('elem', 'span'))]
    dot_general x4 -> x0, matrix products: 30.3 us -> none  [the longest x3 22.1 us: along_spans(): return jnp.dot(matrix, flat, precision=HIGHEST).reshape(shape)]
    reduce_sum x1 -> x2, other arithmetic: 27.2 us -> 0.2 us  [tiled_device(): diagonal = ground + jnp.sum(up, 0) + jnp.sum(down, 0)]
    mul x4 -> x2, other arithmetic: 13.3 us -> 0.18 us  [the longest x1 0.13 us: tiled_device(): projected, spans, head, tail = project(stacked, rotation * scales)]
    ppermute x0 -> x5, waiting for transfers between devices: none -> 10.8 us  [sum_over_all(): lax.ppermute(value, axis, [(i, i ^ step) for i in range(size)])]
    transpose x3 -> x0, local copies, waits for them, and re-layouts: 9.33 us -> none  [the longest x2 7.77 us: collect(): return pieces.transpose(1, 0, 2).reshape(1, rows, count * dofs)]
    unnamed x17 -> x24, local copies, waits for them, and re-layouts: 4.74 us -> 11.5 us
  transfers between devices with their start and end apart: 6 -> 11, of which waited for: 4 -> 9; matrix products, arithmetic and copies ran while one was open for 13% -> 1% of each run, Pallas kernels for 0% -> 8%
where the time goes in v2:
time: 409 us; the launch traced here: 408 us
  blocking collectives  184 us (45%)
  waiting for transfers between devices  113 us (28%)
  Pallas kernels  66 us (16%)
  starting transfers between devices  29.6 us (7%)
  local copies, waits for them, and re-layouts  13 us (3%)
    all_gather x1, blocking collectives, tiled_device(): lax.all_gather(ritz_rotation.transpose(0, 2, 1), 'span', axis=0, tiled=True)  184 us
    all_to_all x3, waiting for transfers between devices, exchange(): lax.all_to_all(pieces, 'span', split_axis=0, concat_axis=0, tiled=True)  52.7 us
    ppermute x2, waiting for transfers between devices, to_next(): return lax.ppermute(cells, ('span', 'elem'), pairs)  46.8 us
    pallas_call x1, Pallas kernels, stiffness(): pl.pallas_call(kernel, in_specs=[vmem, vmem, vmem, vmem, pl.BlockSpec(mem...  26.3 us
    all_to_all x3, starting transfers between devices, exchange(): lax.all_to_all(pieces, 'span', split_axis=0, concat_axis=0, tiled=True)  20.9 us
    pallas_call x2, Pallas kernels, collect_block(): pl.pallas_call(kernel, grid=(count,), in_specs=[pl.BlockSpec((1, rows, do...  15.1 us
    pallas_call x1, Pallas kernels, project(): pl.pallas_call(kernel, grid=(tiles,), in_specs=[pl.BlockSpec((count, wide...  14.6 us
    unnamed x24, local copies, waits for them, and re-layouts  11.5 us
  transfers between devices with their start and end apart: 11, of which 9 were waited for; matrix products, arithmetic and copies ran while one was open for 1% of the time, Pallas kernels for 8%

profile of v2, /device:TPU:15, one launch (start us, length us, event | category | flops | bytes accessed | tf_op | source)
XLA Modules:
  0.0 407.7 jit_solution(500222579472256607)
XLA Ops:
  0.6 1.7 copy-done.4
  2.4 1.7 copy-done.5
  4.1 1.7 copy-done.6
  5.9 7.2 %spread_blocks.1 = f32[16,192,640]{2,1,0:T(8,128)} custom-call(f32[1,64,10240]{2,1,0:T(8,128)S(1)} %copy-done.4, f32[1,64,10240]{2,1,0:T(8,128)S(1)} %copy-done.5, f32[1,64,10240]{2,1,0:T(8,128)S(1)} %copy-done.6), custom_call_target="tpu_custom_call" | custom-call | tf_op jit(solution)/shard_map/spread_blocks/pallas_call | solution.py:165
  13.0 6.7 %all-to-all-start = ((f32[16,192,640]{2,1,0:T(8,128)}), f32[16,192,640]{2,1,0:T(8,128)}, u32[]{:S(2)}, u32[]{:S(2)}) async-start(f32[16,192,640]{2,1,0:T(8,128)} %spread_blocks.1), calls=%async_computation | async-start | bytes 15728640 | tf_op jit(solution)/shard_map/all_to_all | solution.py:49
  19.7 184.0 %all_gather.3 = f32[16,64,192]{2,1,0:T(8,128)S(1)} all-gather(f32[1,64,192]{2,1,0:T(8,128)S(1)} %bitcast.1), channel_id=1, replica_groups=mesh['span'=16,'elem'=2] {'span'}, dimensions={0}, use_global_device_ids=true | all-gather | bytes 835584 | tf_op jit(solution)/shard_map/all_gather | solution.py:396
  203.9 14.6 %project.1 = (f32[16,64,640]{2,1,0:T(8,128)S(1)}, f32[16,64,640]{2,1,0:T(8,128)S(1)}, f32[1,64,128]{2,1,0:T(8,128)S(1)}, f32[1,64,128]{2,1,0:T(8,128)S(1)}) custom-call(f32[16,192,640]{2,1,0:T(8,128)} %all-to-all-done.x, f32[16,64,192]{2,1,0:T(8,128)S(1)} %broadcast_multiply_fusion.rot), custom_call_target="tpu_custom_call" | custom-call | tf_op jit(solution)/shard_map/project/pallas_call | solution.py:249
  218.5 1.5 copy-done
  220.0 1.5 copy-done.2
  221.5 5.3 %all-to-all-start.1 = ((f32[16,64,640]{2,1,0:T(8,128)}), f32[16,64,640]{2,1,0:T(8,128)S(1)}, u32[]{:S(2)}, u32[]{:S(2)}) async-start(f32[16,64,640]{2,1,0:T(8,128)} %copy-done.2), calls=%async_computation.1 | async-start | bytes 5242880 | tf_op jit(solution)/shard_map/all_to_all | solution.py:49
  227.1 1.3 collective-permute-start.2
  228.5 0.8 dynamic_slice.14
  229.2 2.5 collective-permute-done.2
  232.0 4.2 %collective-permute-start = (f32[1,64,128]{2,1,0:T(8,128)S(1)}, f32[1,64,128]{2,1,0:T(8,128)S(1)}, u32[]{:S(2)}, u32[]{:S(2)}) collective-permute-start(f32[1,64,128]{2,1,0:T(8,128)S(1)} %get-tuple-element.13), channel_id=1, source_target_pairs={{0,2},{2,4},{4,6},{6,8},{8,10},{10,12},{12,14},{14,16},{16,18},{18... | collective-permute-start | bytes 98312 | tf_op jit(solution)/shard_map/ppermute | solution.py:58
  236.2 1.9 collective-permute-start.1
  238.2 0.8 add_add_fusion
  239.0 44.9 %collective-permute-done.left = f32[1,64,128]{2,1,0:T(8,128)S(1)} collective-permute-done((f32[1,64,128]{2,1,0:T(8,128)S(1)}, f32[1,64,128]{2,1,0:T(8,128)S(1)}, u32[]{:S(2)}, u32[]{:S(2)}) %collective-permute-start) | collective-permute-done | bytes 32800 | tf_op jit(solution)/shard_map/ppermute | solution.py:58
  283.9 1.8 collective-permute-done.1.right
  285.8 1.7 copy-done.1
  287.5 26.3 %stiffness.1 = (f32[16,64,640]{2,1,0:T(8,128)S(1)}, f32[2,1024]{1,0:T(2,128)S(1)}) custom-call(f32[16,64,640]{2,1,0:T(8,128)S(1)} %copy-done.1, f32[1,64,128]{2,1,0:T(8,128)S(1)} %collective-permute-done.left, f32[1,64,128]{2,1,0:T(8,128)S(1)} %collective-permute-done.1.right, f32[18,640]{1,0:T(8,128)S(1)} %concatenate.8.band, f32[16]{0:T(128)S(1)} %fusion.6.lam), custom_call_target="tpu_custom_call" | custom-call | tf_op jit(solution)/shard_map/stiffness/pallas_call | solution.py:306
  314.1 2.3 collective-permute-done.3
  316.4 1.2 collective-permute-done.4
  317.6 2.5 collective-permute-done.5
  320.1 2.5 collective-permute-done.6
  322.6 1.0 collective-permute-start.7
  323.6 2.4 collective-permute-done.7
  326.0 2.8 residual_back.1
  328.8 1.6 copy-done.3
  330.3 8.9 %all-to-all-start.2 = ((f32[16,64,640]{2,1,0:T(8,128)}), f32[16,64,640]{2,1,0:T(8,128)}, u32[]{:S(2)}, u32[]{:S(2)}) async-start(f32[16,64,640]{2,1,0:T(8,128)} %copy-done.3), calls=%async_computation.2 | async-start | bytes 5242880 | tf_op jit(solution)/shard_map/all_to_all | solution.py:49
  339.9 5.5 %collect_block.2 = f32[1,64,10240]{2,1,0:T(8,128)} custom-call(f32[16,64,640]{2,1,0:T(8,128)S(1)} %all-to-all-done.1.piece), custom_call_target="tpu_custom_call" | custom-call | tf_op jit(solution)/shard_map/collect_block/pallas_call | solution.py:182
  345.3 52.7 %all-to-all-done.2.piece = f32[16,64,640]{2,1,0:T(8,128)} async-done(((f32[16,64,640]{2,1,0:T(8,128)}), f32[16,64,640]{2,1,0:T(8,128)}, u32[]{:S(2)}, u32[]{:S(2)}) %all-to-all-start.2) | async-done | bytes 2621472 | tf_op jit(solution)/shard_map/all_to_all | solution.py:49
  398.0 9.6 %collect_block.3 = f32[1,64,10240]{2,1,0:T(8,128)} custom-call(f32[16,64,640]{2,1,0:T(8,128)} %all-to-all-done.2.piece), custom_call_target="tpu_custom_call" | custom-call | tf_op jit(solution)/shard_map/collect_block/pallas_call | solution.py:182
  (43 shorter events, 1.7 us)
Async XLA Ops:
  0.6 1.7 copy-start.4
  2.4 1.7 copy-start.5
  4.1 1.7 copy-start.6
  13.0 6.7 %copy-start.7 = (f32[1,192,64]{1,2,0:T(8,128)S(1)}, f32[1,192,64]{1,2,0:T(8,128)}, u32[]{:S(2)}) copy-start(f32[1,192,64]{1,2,0:T(8,128)} %param.18) | copy-start | bytes 147460
  13.0 190.7 %copy-start.11 = (f32[16]{0:T(128)S(1)}, f32[16]{0:T(128)}, u32[]{:S(2)}) copy-start(f32[16]{0:T(128)} %constant.41.clone) | copy-start | bytes 196
  13.0 190.8 %all-to-all-start = ((f32[16,192,640]{2,1,0:T(8,128)}), f32[16,192,640]{2,1,0:T(8,128)}, u32[]{:S(2)}, u32[]{:S(2)}) async-start(f32[16,192,640]{2,1,0:T(8,128)} %spread_blocks.1), calls=%async_computation | async-start | bytes 15728640 | tf_op jit(solution)/shard_map/all_to_all | solution.py:49
  218.5 1.5 copy-start
  220.0 1.5 copy-start.2
  221.5 5.4 %copy-start.8 = (f32[10240]{0:T(1024)S(1)}, f32[10240]{0:T(1024)}, u32[]{:S(2)}) copy-start(f32[10240]{0:T(1024)} %param.14) | copy-start | bytes 122884
  221.5 5.4 %copy-start.9 = (f32[10240]{0:T(1024)S(1)}, f32[10240]{0:T(1024)}, u32[]{:S(2)}) copy-start(f32[10240]{0:T(1024)} %param.15) | copy-start | bytes 122884
  221.5 5.4 %copy-start.10 = (s32[10240]{0:T(1024)S(1)}, s32[10240]{0:T(1024)}, u32[]{:S(2)}) copy-start(s32[10240]{0:T(1024)} %param.16) | copy-start | bytes 122884
  221.5 108.9 %all-to-all-start.1 = ((f32[16,64,640]{2,1,0:T(8,128)}), f32[16,64,640]{2,1,0:T(8,128)S(1)}, u32[]{:S(2)}, u32[]{:S(2)}) async-start(f32[16,64,640]{2,1,0:T(8,128)} %copy-done.2), calls=%async_computation.1 | async-start | bytes 5242880 | tf_op jit(solution)/shard_map/all_to_all | solution.py:49
  227.1 4.6 %collective-permute-start.2 = (f32[8,8]{1,0:T(8,128)S(1)}, f32[8,8]{1,0:T(8,128)S(1)}, u32[]{:S(2)}, u32[]{:S(2)}) collective-permute-start(f32[8,8]{1,0:T(8,128)S(1)} %slice.40), channel_id=1, source_target_pairs={{0,1},{2,3},{4,5},{6,7},{8,9},{10,11},{12,13},{14,15},{16,17},{18,... | collective-permute-start | bytes 776 | tf_op jit(solution)/shard_map/ppermute | solution.py:72
  232.0 51.9 %collective-permute-start = (f32[1,64,128]{2,1,0:T(8,128)S(1)}, f32[1,64,128]{2,1,0:T(8,128)S(1)}, u32[]{:S(2)}, u32[]{:S(2)}) collective-permute-start(f32[1,64,128]{2,1,0:T(8,128)S(1)} %get-tuple-element.13), channel_id=1, source_target_pairs={{0,2},{2,4},{4,6},{6,8},{8,10},{10,12},{12,14},{14,16},{16,18},{18... | collective-permute-start | bytes 98312 | tf_op jit(solution)/shard_map/ppermute | solution.py:58
  236.2 49.5 %collective-permute-start.1 = (f32[1,64,128]{2,1,0:T(8,128)S(1)}, f32[1,64,128]{2,1,0:T(8,128)S(1)}, u32[]{:S(2)}, u32[]{:S(2)}) collective-permute-start(f32[1,64,128]{2,1,0:T(8,128)S(1)} %get-tuple-element.14), channel_id=1, source_target_pairs={{2,0},{4,2},{6,4},{8,6},{10,8},{12,10},{14,12},{16,14},{18,16},{20... | collective-permute-start | bytes 98312 | tf_op jit(solution)/shard_map/ppermute | solution.py:58
  285.8 1.7 copy-start.1
  313.8 2.5 collective-permute-start.3
  316.4 1.2 collective-permute-start.4
  317.5 2.5 collective-permute-start.5
  320.1 2.5 collective-permute-start.6
  322.6 3.4 collective-permute-start.7
  328.8 1.6 copy-start.3
  330.3 67.7 %all-to-all-start.2 = ((f32[16,64,640]{2,1,0:T(8,128)}), f32[16,64,640]{2,1,0:T(8,128)}, u32[]{:S(2)}, u32[]{:S(2)}) async-start(f32[16,64,640]{2,1,0:T(8,128)} %copy-done.3), calls=%async_computation.2 | async-start | bytes 5242880 | tf_op jit(solution)/shard_map/all_to_all | solution.py:49

commit v3 on v2

--- a/solution.py
+++ b/solution.py
@@ -156,35 +156,64 @@
     _, rows, dof_dev = blocks[0].shape
     dofs = dof_dev // count
     kinds = len(blocks)
+    cuts = 2 if rows % (2 * ROWS) == 0 else 1
+    strip = rows // cuts
 
     def kernel(*refs):
-        out = refs[-1]
-        for k in range(kinds):
-            out[0, k * rows : (k + 1) * rows, :] = refs[k][0]
-
+        out, held, come, go = refs[kinds:]
+        arrivals = []
+        for c in range(cuts):
+            for k in range(kinds):
+                at = slice(c * strip, (c + 1) * strip)
+                copy = pltpu.make_async_copy(
+                    refs[k].at[0, at, :], held.at[k, at, :], come.at[c * kinds + k]
+                )
+                copy.start()
+                arrivals.append((c, k, copy))
+        leaving = []
+        for c, k, copy in arrivals:
+            copy.wait()
+            for i in range(count):
+                piece = pltpu.make_async_copy(
+                    held.at[k, c * strip : (c + 1) * strip, i * dofs : (i + 1) * dofs],
+                    out.at[i, k * rows + c * strip : k * rows + (c + 1) * strip, :],
+                    go.at[(c * kinds + k) * count + i],
+                )
+                piece.start()
+                leaving.append(piece)
+        for piece in leaving:
+            piece.wait()
+
+    whole = pl.BlockSpec(memory_space=pltpu.HBM)
     return pl.pallas_call(
         kernel,
-        grid=(count,),
-        in_specs=[pl.BlockSpec((1, rows, dofs), lambda i: (0, 0, i))] * kinds,
-        out_specs=pl.BlockSpec((1, kinds * rows, dofs), lambda i: (i, 0, 0)),
-        out_shape=jax.ShapeDtypeStruct((count, kinds * rows, dofs), jnp.float32),
-        compiler_params=params(),
+        in_specs=[whole] * kinds,
+        out_specs=whole,
+        out_shape=pltpu.HBM((count, kinds * rows, dofs), jnp.float32),
+        scratch_shapes=[
+            pltpu.VMEM((kinds, rows, dof_dev), jnp.float32),
+            pltpu.SemaphoreType.DMA((cuts * kinds,)),
+            pltpu.SemaphoreType.DMA((cuts * kinds * count,)),
+        ],
+        compiler_params=pltpu.CompilerParams(vmem_limit_bytes=60 * 1024 * 1024),
         name="spread_blocks",
     )(*blocks)
 
 
 def collect_block(pieces):
     count, rows, dofs = pieces.shape
+    many = max(n for n in (1, 2, 4, 8) if count % n == 0)
 
     def kernel(piece, out):
-        out[...] = piece[...]
+        for i in range(many):
+            out[0, :, i * dofs : (i + 1) * dofs] = piece[i]
 
     return pl.pallas_call(
         kernel,
-        grid=(count,),
-        in_specs=[pl.BlockSpec((1, rows, dofs), lambda i: (i, 0, 0))],
-        out_specs=pl.BlockSpec((1, rows, dofs), lambda i: (0, 0, i)),
-        out_shape=jax.ShapeDtypeStruct((1, rows, count * dofs), jnp.float32),
+        grid=(count // many,),
+        in_specs=[pl.BlockSpec((many, rows, dofs), lambda i: (i, 0, 0))],
+        out_specs=pl.BlockSpec((1, rows, many * dofs), lambda i: (0, 0, i)),
+        out_shape=pltpu.HBM((1, rows, count * dofs), jnp.float32),
         compiler_params=params(),
         name="collect_block",
     )(pieces)
@@ -244,7 +273,7 @@
 
     cell = pl.BlockSpec((count, rows, LANES), lambda t: (0, 0, t))
     edge = pl.BlockSpec((groups, rows, LANES), lambda t: (0, 0, 0))
-    field = jax.ShapeDtypeStruct((count, rows, dofs), jnp.float32)
+    field = pltpu.HBM((count, rows, dofs), jnp.float32)
     edges = jax.ShapeDtypeStruct((groups, rows, LANES), jnp.float32)
     return pl.pallas_call(
         kernel,
@@ -264,35 +293,55 @@
 def stiffness(projected, before, after, bands, links):
     count, rows, dofs = projected.shape
     per = LANES // REACH
-    strips = rows // ROWS
-
-    def kernel(x, left, right, band, lam, stiff, sums, energy, norm):
-        def strip(it, carry):
-            j, r = it // strips, it % strips
-            at = pl.ds(pl.multiple_of(r * ROWS, ROWS), ROWS)
-            to = pl.ds(pl.multiple_of(it * ROWS, ROWS), ROWS)
+    tiles = dofs // LANES
+
+    def kernel(x, left, right, band, lam, stiff, sums, energy, norm, matrix):
+        row = lax.broadcasted_iota(jnp.int32, (LANES, LANES), 0)
+        gap = row - lax.broadcasted_iota(jnp.int32, (LANES, LANES), 1)
+        for t in range(tiles):
+            at = slice(t * LANES, (t + 1) * LANES)
+            here = jnp.where(gap == 0, band[16:17, at], 0.0)
+            halo = jnp.zeros((LANES, LANES), jnp.float32)
+            for d in range(1, REACH + 1):
+                up, down = band[d - 1 : d, at], band[REACH + d - 1 : REACH + d, at]
+                here = jnp.where(gap == d, -up, here)
+                here = jnp.where(gap == -d, -down, here)
+                halo = jnp.where(gap == d - LANES, -up, halo)
+                halo = jnp.where(gap == LANES - d, -down, halo)
+            matrix[t, :LANES, :] = here
+            matrix[t, LANES:, :] = halo
+        lane = lax.broadcasted_iota(jnp.int32, (rows, LANES), 1)
+
+        def slot(j, carry):
+            to = pl.ds(pl.multiple_of(j * rows, rows), rows)
             g, k = j // per, j % per
-            here = x[j, at, :]
-            low = pltpu.roll(left[g, at, :], (2 * LANES - REACH - REACH * k) % LANES, 1)
-            high = pltpu.roll(right[g, at, :], (LANES - REACH * k) % LANES, 1)
-            full = jnp.concatenate([low, here, high], 1)
-            size = dofs + 2 * LANES
-            total = (band[16:17, :] + lam[j] * band[17:18, :]) * here
-            for d in range(1, REACH + 1):
-                up = pltpu.roll(full, size - d, 1)[:, LANES : LANES + dofs]
-                down = pltpu.roll(full, d, 1)[:, LANES : LANES + dofs]
-                total = total - band[d - 1 : d, :] * up
-                total = total - band[REACH + d - 1 : REACH + d, :] * down
-            stiff[j, at, :] = total
-            both, own = total * here, here * here
-            tiles = [slice(t * LANES, (t + 1) * LANES) for t in range(dofs // LANES)]
-            energy[to, :] = add_up([both[:, t] for t in tiles])
-            norm[to, :] = add_up([own[:, t] for t in tiles])
+            low = pltpu.roll(left[g], (2 * LANES - REACH - REACH * k) % LANES, 1)
+            high = pltpu.roll(right[g], (LANES - REACH * k) % LANES, 1)
+            work = jnp.zeros((rows, LANES), jnp.float32)
+            size = jnp.zeros((rows, LANES), jnp.float32)
+            for t in range(tiles):
+                at = slice(t * LANES, (t + 1) * LANES)
+                here = x[j, :, at]
+                previous = low if t == 0 else x[j, :, (t - 1) * LANES : t * LANES]
+                following = high if t == tiles - 1 else x[j, :, (t + 1) * LANES : (t + 2) * LANES]
+                halo = jnp.where(lane < LANES // 2, following, previous)
+                total = jnp.dot(
+                    jnp.concatenate([here, halo], 1),
+                    matrix[t],
+                    precision=HIGHEST,
+                    preferred_element_type=jnp.float32,
+                )
+                total = total + (lam[j] * band[17:18, at]) * here
+                stiff[j, :, at] = total
+                work = work + total * here
+                size = size + here * here
+            energy[to, :] = work
+            norm[to, :] = size
             return carry
 
-        lax.fori_loop(0, count * strips, strip, 0)
+        lax.fori_loop(0, count, slot, 0)
         ones = jnp.ones((ROWS, LANES), jnp.float32)
-        for row, part in enumerate((energy, norm)):
+        for r, part in enumerate((energy, norm)):
             line = lax.dot_general(
                 ones,
                 part[...],
@@ -300,7 +349,7 @@
                 precision=HIGHEST,
                 preferred_element_type=jnp.float32,
             )
-            sums[row : row + 1, :] = line[:1]
+            sums[r : r + 1, :] = line[:1]
 
     vmem = pl.BlockSpec(memory_space=pltpu.VMEM)
     return pl.pallas_call(
@@ -311,7 +360,11 @@
             jax.ShapeDtypeStruct((count, rows, dofs), jnp.float32),
             jax.ShapeDtypeStruct((2, count * rows), jnp.float32),
         ],
-        scratch_shapes=[pltpu.VMEM((count * rows, LANES), jnp.float32)] * 2,
+        scratch_shapes=[
+            pltpu.VMEM((count * rows, LANES), jnp.float32),
+            pltpu.VMEM((count * rows, LANES), jnp.float32),
+            pltpu.VMEM((tiles, 2 * LANES, LANES), jnp.float32),
+        ],
         compiler_params=params(),
         name="stiffness",
     )(projected, before, after, bands, links)
@@ -358,7 +411,7 @@
         in_specs=[cell, cell, pl.BlockSpec((2, count * rows), lambda t: (0, 0))],
         out_specs=[cell, pl.BlockSpec((1, count * rows), lambda t: (0, 0))],
         out_shape=[
-            jax.ShapeDtypeStruct((count, rows, dofs), jnp.float32),
+            pltpu.HBM((count, rows, dofs), jnp.float32),
             jax.ShapeDtypeStruct((1, count * rows), jnp.float32),
         ],
         scratch_shapes=[pltpu.VMEM((count * rows, LANES), jnp.float32)],
@@ -367,14 +420,30 @@
     )(projected, stiff, sums)
 
 
+def halvings(axis):
+    step = lax.axis_size(axis) // 2
+    while step:
+        yield step, [(i, i ^ step) for i in range(lax.axis_size(axis))]
+        step //= 2
+
+
 def sum_over_all(value):
-    for axis in ("elem", "span"):
-        size = lax.axis_size(axis)
-        step = 1
-        while step < size:
-            value = value + lax.ppermute(value, axis, [(i, i ^ step) for i in range(size)])
-            step *= 2
+    for axis in ("span", "elem"):
+        for _, pairs in halvings(axis):
+            value = value + lax.ppermute(value, axis, pairs)
     return value
+
+
+def gather_spans(value):
+    tail = value.shape[1:]
+    held, bits = value.reshape(tail), 0
+    for step, pairs in halvings("span"):
+        other = lax.ppermute(held, "span", pairs)
+        upper = (lax.axis_index("span") & step) != 0
+        held = jnp.stack([jnp.where(upper, other, held), jnp.where(upper, held, other)])
+        bits += 1
+    order = tuple(range(bits))[::-1] + tuple(range(bits, bits + len(tail)))
+    return held.transpose(order).reshape((-1,) + tail)
 
 
 def tiled_device(
@@ -393,7 +462,7 @@
     rows = current_block.shape[1]
     stacked = exchange(spread_blocks((current_block, search_block, previous_block), count))
     scales = jnp.array(slot_scales(count), jnp.float32)[:, None, None]
-    rotation = lax.all_gather(ritz_rotation.transpose(0, 2, 1), "span", axis=0, tiled=True)
+    rotation = gather_spans(ritz_rotation.transpose(0, 2, 1))
     weights, ground, link = coefficients(
         ground_spring, wire_tension, dropper_stiff, dropper_offset, span_link, count, dofs
     )
@@ -404,8 +473,9 @@
     bands = jnp.concatenate([up, down, diagonal[None], link[None]])
     links = 2.0 * (1.0 - fourier_rows(count)[1])
     projected, spans, head, tail = project(stacked, rotation * scales)
+    before, after = to_next(tail, 1), to_next(head, -1)
+    spans, before, after = lax.optimization_barrier((spans, before, after))
     next_block = collect_block(exchange(spans))
-    before, after = to_next(tail, 1), to_next(head, -1)
     stiff, sums = stiffness(projected, before, after, bands, links)
     spans, ritz = residual_back(projected, stiff, sum_over_all(sums))
     next_residual = collect_block(exchange(spans))

time: 409 us -> 382 us (0.934)
  blocking collectives: 184 us -> 0 us
  waiting for transfers between devices: 113 us -> 285 us
  Pallas kernels: 66 us -> 41.6 us
  starting transfers between devices: 29.6 us -> 46.7 us
  local copies, waits for them, and re-layouts: 13 us -> 3.81 us
    ppermute x5 -> x9, waiting for transfers between devices: 10.8 us -> 220 us  [the longest x4 180 us: gather_spans(): other = lax.ppermute(held, 'span', pairs)]
    all_gather x1 -> x0, blocking collectives: 184 us -> none  [tiled_device(): lax.all_gather(ritz_rotation.transpose(0, 2, 1), 'span', axis=0, tiled=True)]
    ppermute x2, waiting for transfers between devices: 46.8 us -> 4.18 us  [to_next(): return lax.ppermute(cells, ('span', 'elem'), pairs)]
    ppermute x5 -> x9, starting transfers between devices: 1.25 us -> 20 us  [the longest x5 11.8 us: sum_over_all(): value = value + lax.ppermute(value, axis, pairs)]
    pallas_call x1, Pallas kernels: 26.3 us -> 10.5 us  [stiffness(): pl.pallas_call(kernel, in_specs=[vmem, vmem, vmem, vmem, pl.BlockSpec(mem...]
    pallas_call x3, Pallas kernels: 22.3 us -> 11.6 us  [the longest x1 7.13 us: spread_blocks(): pl.pallas_call(kernel, in_specs=[whole] * kinds, out_specs=whole, out_sha...]
    unnamed x24 -> x12, local copies, waits for them, and re-layouts: 11.5 us -> 2.21 us
  transfers between devices with their start and end apart: 11 -> 15, of which waited for: 9 -> 12; matrix products, arithmetic and copies ran while one was open for 1% -> 1% of each run, Pallas kernels for 8% -> 4%
where the time goes in v3:
time: 382 us; the launch traced here: 380 us
  waiting for transfers between devices  285 us (75%)
  starting transfers between devices  46.7 us (12%)
  Pallas kernels  41.6 us (11%)
    ppermute x4, waiting for transfers between devices, gather_spans(): other = lax.ppermute(held, 'span', pairs)  180 us
    all_to_all x3, waiting for transfers between devices, exchange(): lax.all_to_all(pieces, 'span', split_axis=0, concat_axis=0, tiled=True)  56.6 us
    ppermute x5, waiting for transfers between devices, sum_over_all(): value = value + lax.ppermute(value, axis, pairs)  40.2 us
    all_to_all x3, starting transfers between devices, exchange(): lax.all_to_all(pieces, 'span', split_axis=0, concat_axis=0, tiled=True)  21.1 us
    pallas_call x1, Pallas kernels, project(): pl.pallas_call(kernel, grid=(tiles,), in_specs=[pl.BlockSpec((count, wide...  15.3 us
    ppermute x5, starting transfers between devices, sum_over_all(): value = value + lax.ppermute(value, axis, pairs)  11.8 us
    pallas_call x1, Pallas kernels, stiffness(): pl.pallas_call(kernel, in_specs=[vmem, vmem, vmem, vmem, pl.BlockSpec(mem...  10.5 us
    ppermute x4, starting transfers between devices, gather_spans(): other = lax.ppermute(held, 'span', pairs)  8.2 us
  transfers between devices with their start and end apart: 15, of which 12 were waited for; matrix products, arithmetic and copies ran while one was open for 1% of the time, Pallas kernels for 4%

profile of v3, /device:TPU:15, one launch (start us, length us, event | category | flops | bytes accessed | tf_op | source)
XLA Modules:
  0.0 379.6 jit_solution(10176042846386302037)
XLA Ops:
  0.6 7.1 %spread_blocks.1 = f32[16,192,640]{2,1,0:T(8,128)} custom-call(f32[1,64,10240]{2,1,0:T(8,128)} %refs_0_.1, f32[1,64,10240]{2,1,0:T(8,128)} %refs_1_.1, f32[1,64,10240]{2,1,0:T(8,128)} %refs_2_.1), custom_call_target="tpu_custom_call" | custom-call | tf_op jit(solution)/shard_map/spread_blocks/pallas_call | solution.py:188
  7.8 6.7 %all-to-all-start = ((f32[16,192,640]{2,1,0:T(8,128)}), f32[16,192,640]{2,1,0:T(8,128)}, u32[]{:S(2)}, u32[]{:S(2)}) async-start(f32[16,192,640]{2,1,0:T(8,128)} %spread_blocks.1), calls=%async_computation | async-start | bytes 15728640 | tf_op jit(solution)/shard_map/all_to_all | solution.py:49
  14.5 2.2 collective-permute-start
  16.6 169.5 %collective-permute-done = f32[64,192]{1,0:T(8,128)S(1)} collective-permute-done((f32[64,192]{1,0:T(8,128)S(1)}, f32[64,192]{1,0:T(8,128)S(1)}, u32[]{:S(2)}, u32[]{:S(2)}) %collective-permute-start) | collective-permute-done | bytes 49184 | tf_op jit(solution)/shard_map/ppermute | solution.py:441
  186.1 3.3 collective-permute-start.1
  189.4 3.0 collective-permute-done.1
  192.8 6.1 %collective-permute-done.2 = f32[2,2,64,192]{3,2,1,0:T(8,128)S(1)} collective-permute-done((f32[2,2,64,192]{3,2,1,0:T(8,128)S(1)}, f32[2,2,64,192]{3,2,1,0:T(8,128)S(1)}, u32[]{:S(2)}, u32[]{:S(2)}) %collective-permute-start.2) | collective-permute-done | bytes 196640 | tf_op jit(solution)/shard_map/ppermute | solution.py:441
  199.0 2.4 collective-permute-start.3
  201.4 1.5 collective-permute-done.3
  203.9 15.3 %project.1 = (f32[16,64,640]{2,1,0:T(8,128)}, f32[16,64,640]{2,1,0:T(8,128)}, f32[1,64,128]{2,1,0:T(8,128)S(1)}, f32[1,64,128]{2,1,0:T(8,128)S(1)}) custom-call(f32[16,192,640]{2,1,0:T(8,128)} %all-to-all-done.x, f32[16,64,192]{2,1,0:T(8,128)S(1)} %bitcast_multiply_fusion.rot), custom_call_target="tpu_custom_call" | custom-call | tf_op jit(solution)/shard_map/project/pallas_call | solution.py:278
  219.1 2.4 collective-permute-start.4
  221.5 1.9 collective-permute-start.5
  223.5 4.2 %collective-permute-done.5.right = f32[1,64,128]{2,1,0:T(8,128)S(1)} collective-permute-done((f32[1,64,128]{2,1,0:T(8,128)S(1)}, f32[1,64,128]{2,1,0:T(8,128)S(1)}, u32[]{:S(2)}, u32[]{:S(2)}) %collective-permute-start.5) | collective-permute-done | bytes 32800 | tf_op jit(solution)/shard_map/ppermute | solution.py:58
  227.7 7.3 %all-to-all-start.1 = ((f32[16,64,640]{2,1,0:T(8,128)}), f32[16,64,640]{2,1,0:T(8,128)S(1)}, u32[]{:S(2)}, u32[]{:S(2)}) async-start(f32[16,64,640]{2,1,0:T(8,128)} %get-tuple-element.17), calls=%async_computation.1 | async-start | bytes 5242880 | tf_op jit(solution)/shard_map/all_to_all | solution.py:49
  235.3 1.3 collective-permute-start.6
  237.5 3.8 collective-permute-done.6
  242.4 1.7 copy-done
  244.1 10.5 %stiffness.1 = (f32[16,64,640]{2,1,0:T(8,128)S(1)}, f32[2,1024]{1,0:T(2,128)S(1)}) custom-call(f32[16,64,640]{2,1,0:T(8,128)S(1)} %copy-done, f32[1,64,128]{2,1,0:T(8,128)S(1)} %collective-permute-done.4.left, f32[1,64,128]{2,1,0:T(8,128)S(1)} %collective-permute-done.5.right, f32[18,640]{1,0:T(8,128)S(1)} %concatenate.8.band, f32[16]{0:T(128)S(1)} %fusion.6.lam), custom_call_target="tpu_custom_call" | custom-call | tf_op jit(solution)/shard_map/stiffness/pallas_call | solution.py:355
  254.7 2.1 collective-permute-start.7
  256.8 35.1 %collective-permute-done.7 = f32[2,1024]{1,0:T(2,128)S(1)} collective-permute-done((f32[2,1024]{1,0:T(2,128)S(1)}, f32[2,1024]{1,0:T(2,128)S(1)}, u32[]{:S(2)}, u32[]{:S(2)}) %collective-permute-start.7) | collective-permute-done | bytes 8224 | tf_op jit(solution)/shard_map/ppermute | solution.py:433
  291.8 2.9 collective-permute-start.8
  294.7 1.0 collective-permute-done.8
  296.1 2.2 collective-permute-done.9
  298.3 3.2 collective-permute-start.10
  301.5 0.8 collective-permute-done.10
  302.3 3.3 collective-permute-start.11
  305.7 1.0 collective-permute-done.11
  306.7 4.2 %residual_back.1 = (f32[16,64,640]{2,1,0:T(8,128)}, f32[1,1024]{1,0:T(1,128)S(1)}) custom-call(f32[16,64,640]{2,1,0:T(8,128)S(1)} %copy-done, f32[16,64,640]{2,1,0:T(8,128)S(1)} %get-tuple-element.21.kx, f32[2,1024]{1,0:T(2,128)S(1)} %add.87.total), custom_call_target="tpu_custom_call" | custom-call | tf_op jit(solution)/shard_map/residual_back/pallas_call | solution.py:408
  310.9 7.1 %all-to-all-start.2 = ((f32[16,64,640]{2,1,0:T(8,128)}), f32[16,64,640]{2,1,0:T(8,128)}, u32[]{:S(2)}, u32[]{:S(2)}) async-start(f32[16,64,640]{2,1,0:T(8,128)} %get-tuple-element.23), calls=%async_computation.2 | async-start | bytes 5242880 | tf_op jit(solution)/shard_map/all_to_all | solution.py:49
  318.6 1.6 collect_block.2
  320.1 56.6 %all-to-all-done.2.piece = f32[16,64,640]{2,1,0:T(8,128)} async-done(((f32[16,64,640]{2,1,0:T(8,128)}), f32[16,64,640]{2,1,0:T(8,128)}, u32[]{:S(2)}, u32[]{:S(2)}) %all-to-all-start.2) | async-done | bytes 2621472 | tf_op jit(solution)/shard_map/all_to_all | solution.py:49
  376.8 2.9 collect_block.3
  (47 shorter events, 4.5 us)
Async XLA Ops:
  7.8 6.7 %copy-start.1 = (f32[1,192,64]{1,2,0:T(8,128)S(1)}, f32[1,192,64]{1,2,0:T(8,128)}, u32[]{:S(2)}) copy-start(f32[1,192,64]{1,2,0:T(8,128)} %param.18) | copy-start | bytes 147460
  7.8 196.1 %all-to-all-start = ((f32[16,192,640]{2,1,0:T(8,128)}), f32[16,192,640]{2,1,0:T(8,128)}, u32[]{:S(2)}, u32[]{:S(2)}) async-start(f32[16,192,640]{2,1,0:T(8,128)} %spread_blocks.1), calls=%async_computation | async-start | bytes 15728640 | tf_op jit(solution)/shard_map/all_to_all | solution.py:49
  14.5 171.6 %collective-permute-start = (f32[64,192]{1,0:T(8,128)S(1)}, f32[64,192]{1,0:T(8,128)S(1)}, u32[]{:S(2)}, u32[]{:S(2)}) collective-permute-start(f32[64,192]{1,0:T(8,128)S(1)} %bitcast.25), channel_id=1, source_target_pairs={{0,16},{2,18},{4,20},{6,22},{8,24},{10,26},{12,28},{14,30},{16,0},... | collective-permute-start | bytes 147464 | tf_op jit(solution)/shard_map/ppermute | solution.py:441
  186.1 6.3 %collective-permute-start.1 = (f32[2,64,192]{2,1,0:T(8,128)S(1)}, f32[2,64,192]{2,1,0:T(8,128)S(1)}, u32[]{:S(2)}, u32[]{:S(2)}) collective-permute-start(f32[2,64,192]{2,1,0:T(8,128)S(1)} %pad_maximum_fusion.2), channel_id=1, source_target_pairs={{0,8},{2,10},{4,12},{6,14},{8,0},{10,2},{12,4},{14,6},{16,24},{18,... | collective-permute-start | bytes 294920 | tf_op jit(solution)/shard_map/ppermute | solution.py:441
  192.5 6.4 %collective-permute-start.2 = (f32[2,2,64,192]{3,2,1,0:T(8,128)S(1)}, f32[2,2,64,192]{3,2,1,0:T(8,128)S(1)}, u32[]{:S(2)}, u32[]{:S(2)}) collective-permute-start(f32[2,2,64,192]{3,2,1,0:T(8,128)S(1)} %pad_maximum_fusion.1), channel_id=1, source_target_pairs={{0,4},{2,6},{4,0},{6,2},{8,12},{10,14},{12,8},{14,10},{16,20},{18,... | collective-permute-start | bytes 589832 | tf_op jit(solution)/shard_map/ppermute | solution.py:441
  199.0 4.0 %collective-permute-start.3 = (f32[2,2,2,64,192]{4,3,2,1,0:T(8,128)S(1)}, f32[2,2,2,64,192]{4,3,2,1,0:T(8,128)S(1)}, u32[]{:S(2)}, u32[]{:S(2)}) collective-permute-start(f32[2,2,2,64,192]{4,3,2,1,0:T(8,128)S(1)} %pad_maximum_fusion), channel_id=1, source_target_pairs={{0,2},{2,0},{4,6},{6,4},{8,10},{10,8},{12,14},{14,12},{16,18},{18,... | collective-permute-start | bytes 1179656 | tf_op jit(solution)/shard_map/ppermute | solution.py:441
  203.1 0.7 copy-start.5
  219.1 4.3 %collective-permute-start.4 = (f32[1,64,128]{2,1,0:T(8,128)S(1)}, f32[1,64,128]{2,1,0:T(8,128)S(1)}, u32[]{:S(2)}, u32[]{:S(2)}) collective-permute-start(f32[1,64,128]{2,1,0:T(8,128)S(1)} %get-tuple-element.15), channel_id=1, source_target_pairs={{0,2},{2,4},{4,6},{6,8},{8,10},{10,12},{12,14},{14,16},{16,18},{18... | collective-permute-start | bytes 98312 | tf_op jit(solution)/shard_map/ppermute | solution.py:58
  221.5 6.1 %collective-permute-start.5 = (f32[1,64,128]{2,1,0:T(8,128)S(1)}, f32[1,64,128]{2,1,0:T(8,128)S(1)}, u32[]{:S(2)}, u32[]{:S(2)}) collective-permute-start(f32[1,64,128]{2,1,0:T(8,128)S(1)} %get-tuple-element.16), channel_id=1, source_target_pairs={{2,0},{4,2},{6,4},{8,6},{10,8},{12,10},{14,12},{16,14},{18,16},{20... | collective-permute-start | bytes 98312 | tf_op jit(solution)/shard_map/ppermute | solution.py:58
  227.7 7.4 %copy-start.2 = (f32[10240]{0:T(1024)S(1)}, f32[10240]{0:T(1024)}, u32[]{:S(2)}) copy-start(f32[10240]{0:T(1024)} %param.14) | copy-start | bytes 122884
  227.7 7.4 %copy-start.3 = (f32[10240]{0:T(1024)S(1)}, f32[10240]{0:T(1024)}, u32[]{:S(2)}) copy-start(f32[10240]{0:T(1024)} %param.15) | copy-start | bytes 122884
  227.7 7.4 %copy-start.4 = (s32[10240]{0:T(1024)S(1)}, s32[10240]{0:T(1024)}, u32[]{:S(2)}) copy-start(s32[10240]{0:T(1024)} %param.16) | copy-start | bytes 122884
  227.7 83.2 %all-to-all-start.1 = ((f32[16,64,640]{2,1,0:T(8,128)}), f32[16,64,640]{2,1,0:T(8,128)S(1)}, u32[]{:S(2)}, u32[]{:S(2)}) async-start(f32[16,64,640]{2,1,0:T(8,128)} %get-tuple-element.17), calls=%async_computation.1 | async-start | bytes 5242880 | tf_op jit(solution)/shard_map/all_to_all | solution.py:49
  235.3 5.9 %collective-permute-start.6 = (f32[8,8]{1,0:T(8,128)S(1)}, f32[8,8]{1,0:T(8,128)S(1)}, u32[]{:S(2)}, u32[]{:S(2)}) collective-permute-start(f32[8,8]{1,0:T(8,128)S(1)} %slice.40), channel_id=1, source_target_pairs={{0,1},{2,3},{4,5},{6,7},{8,9},{10,11},{12,13},{14,15},{16,17},{18,... | collective-permute-start | bytes 776 | tf_op jit(solution)/shard_map/ppermute | solution.py:72
  242.4 1.7 copy-start
  254.7 37.2 %collective-permute-start.7 = (f32[2,1024]{1,0:T(2,128)S(1)}, f32[2,1024]{1,0:T(2,128)S(1)}, u32[]{:S(2)}, u32[]{:S(2)}) collective-permute-start(f32[2,1024]{1,0:T(2,128)S(1)} %get-tuple-element.22), channel_id=1, source_target_pairs={{0,16},{2,18},{4,20},{6,22},{8,24},{10,26},{12,28},{14,30},{16,0},... | collective-permute-start | bytes 24584 | tf_op jit(solution)/shard_map/ppermute | solution.py:433
  291.8 4.0 %collective-permute-start.8 = (f32[2,1024]{1,0:T(2,128)S(1)}, f32[2,1024]{1,0:T(2,128)S(1)}, u32[]{:S(2)}, u32[]{:S(2)}) collective-permute-start(f32[2,1024]{1,0:T(2,128)S(1)} %add.83), channel_id=1, source_target_pairs={{0,8},{2,10},{4,12},{6,14},{8,0},{10,2},{12,4},{14,6},{16,24},{18,... | collective-permute-start | bytes 24584 | tf_op jit(solution)/shard_map/ppermute | solution.py:433
  295.8 2.5 collective-permute-start.9
  298.3 4.0 %collective-permute-start.10 = (f32[2,1024]{1,0:T(2,128)S(1)}, f32[2,1024]{1,0:T(2,128)S(1)}, u32[]{:S(2)}, u32[]{:S(2)}) collective-permute-start(f32[2,1024]{1,0:T(2,128)S(1)} %add.85), channel_id=1, source_target_pairs={{0,2},{2,0},{4,6},{6,4},{8,10},{10,8},{12,14},{14,12},{16,18},{18,... | collective-permute-start | bytes 24584 | tf_op jit(solution)/shard_map/ppermute | solution.py:433
  302.3 4.4 %collective-permute-start.11 = (f32[2,1024]{1,0:T(2,128)S(1)}, f32[2,1024]{1,0:T(2,128)S(1)}, u32[]{:S(2)}, u32[]{:S(2)}) collective-permute-start(f32[2,1024]{1,0:T(2,128)S(1)} %add.86), channel_id=1, source_target_pairs={{0,1},{1,0},{2,3},{3,2},{4,5},{5,4},{6,7},{7,6},{8,9},{9,8},{10,11... | collective-permute-start | bytes 24584 | tf_op jit(solution)/shard_map/ppermute | solution.py:433
  310.9 65.9 %all-to-all-start.2 = ((f32[16,64,640]{2,1,0:T(8,128)}), f32[16,64,640]{2,1,0:T(8,128)}, u32[]{:S(2)}, u32[]{:S(2)}) async-start(f32[16,64,640]{2,1,0:T(8,128)} %get-tuple-element.23), calls=%async_computation.2 | async-start | bytes 5242880 | tf_op jit(solution)/shard_map/all_to_all | solution.py:49

commit v4 on v3

--- a/solution.py
+++ b/solution.py
@@ -427,23 +427,16 @@
         step //= 2
 
 
-def sum_over_all(value):
-    for axis in ("span", "elem"):
-        for _, pairs in halvings(axis):
-            value = value + lax.ppermute(value, axis, pairs)
-    return value
-
-
-def gather_spans(value):
-    tail = value.shape[1:]
-    held, bits = value.reshape(tail), 0
-    for step, pairs in halvings("span"):
-        other = lax.ppermute(held, "span", pairs)
-        upper = (lax.axis_index("span") & step) != 0
-        held = jnp.stack([jnp.where(upper, other, held), jnp.where(upper, held, other)])
-        bits += 1
-    order = tuple(range(bits))[::-1] + tuple(range(bits, bits + len(tail)))
-    return held.transpose(order).reshape((-1,) + tail)
+def exchange_step(held, step, pairs):
+    other = lax.ppermute(held, "span", pairs)
+    upper = (lax.axis_index("span") & step) != 0
+    return jnp.stack([jnp.where(upper, other, held), jnp.where(upper, held, other)])
+
+
+def in_order(held, bits):
+    order = tuple(range(bits))[::-1] + tuple(range(bits, held.ndim))
+    held = held.transpose(order)
+    return held.reshape((-1,) + held.shape[bits:])
 
 
 def tiled_device(
@@ -460,9 +453,18 @@
     count = lax.axis_size("span")
     dofs = current_block.shape[2] // count
     rows = current_block.shape[1]
-    stacked = exchange(spread_blocks((current_block, search_block, previous_block), count))
+    steps = list(halvings("span"))
+    far, near = steps[: len(steps) // 2], steps[len(steps) // 2 :]
+    rotation = ritz_rotation[0].T
+    for step, pairs in far:
+        rotation = exchange_step(rotation, step, pairs)
+    pieces = spread_blocks((current_block, search_block, previous_block), count)
+    pieces, rotation = lax.optimization_barrier((pieces, rotation))
+    stacked = exchange(pieces)
+    for step, pairs in near:
+        rotation = exchange_step(rotation, step, pairs)
+    rotation = in_order(rotation, len(steps))
     scales = jnp.array(slot_scales(count), jnp.float32)[:, None, None]
-    rotation = gather_spans(ritz_rotation.transpose(0, 2, 1))
     weights, ground, link = coefficients(
         ground_spring, wire_tension, dropper_stiff, dropper_offset, span_link, count, dofs
     )
@@ -474,10 +476,16 @@
     links = 2.0 * (1.0 - fourier_rows(count)[1])
     projected, spans, head, tail = project(stacked, rotation * scales)
     before, after = to_next(tail, 1), to_next(head, -1)
-    spans, before, after = lax.optimization_barrier((spans, before, after))
+    stiff, sums = stiffness(projected, before, after, bands, links)
+    for _, pairs in far:
+        sums = sums + lax.ppermute(sums, "span", pairs)
+    spans, sums = lax.optimization_barrier((spans, sums))
     next_block = collect_block(exchange(spans))
-    stiff, sums = stiffness(projected, before, after, bands, links)
-    spans, ritz = residual_back(projected, stiff, sum_over_all(sums))
+    for _, pairs in near:
+        sums = sums + lax.ppermute(sums, "span", pairs)
+    for _, pairs in halvings("elem"):
+        sums = sums + lax.ppermute(sums, "elem", pairs)
+    spans, ritz = residual_back(projected, stiff, sums)
     next_residual = collect_block(exchange(spans))
     ritz = lax.dynamic_slice_in_dim(ritz, lax.axis_index("span") * rows, rows, 1)
     return (next_block, next_residual, ritz)

time: 382 us -> 369 us (0.966)
  starting transfers between devices: 46.7 us -> 31 us
    all_to_all x3, waiting for transfers between devices: 56.6 us -> 210 us  [exchange(): lax.all_to_all(pieces, 'span', split_axis=0, concat_axis=0, tiled=True)]
    ppermute x9, waiting for transfers between devices: 220 us -> 69.1 us  [the longest x4 48.1 us: exchange_step(): other = lax.ppermute(held, 'span', pairs)]
    ppermute x9, starting transfers between devices: 20 us -> 5.18 us  [the longest x4 3.73 us: exchange_step(): other = lax.ppermute(held, 'span', pairs)]
  transfers between devices with their start and end apart: 15 -> 15, of which waited for: 12 -> 13; matrix products, arithmetic and copies ran while one was open for 1% -> 1% of each run, Pallas kernels for 4% -> 4%
where the time goes in v4:
time: 369 us; the launch traced here: 368 us
  waiting for transfers between devices  285 us (77%)
  Pallas kernels  41.7 us (11%)
  starting transfers between devices  31 us (8%)
  local copies, waits for them, and re-layouts  7.11 us (2%)
    all_to_all x3, waiting for transfers between devices, exchange(): lax.all_to_all(pieces, 'span', split_axis=0, concat_axis=0, tiled=True)  210 us
    ppermute x4, waiting for transfers between devices, exchange_step(): other = lax.ppermute(held, 'span', pairs)  48.1 us
    all_to_all x3, starting transfers between devices, exchange(): lax.all_to_all(pieces, 'span', split_axis=0, concat_axis=0, tiled=True)  19.1 us
    ppermute x4, waiting for transfers between devices, tiled_device(): sums = sums + lax.ppermute(sums, 'span', pairs)  18.5 us
    pallas_call x1, Pallas kernels, project(): pl.pallas_call(kernel, grid=(tiles,), in_specs=[pl.BlockSpec((count, wide...  15.4 us
    pallas_call x1, Pallas kernels, stiffness(): pl.pallas_call(kernel, in_specs=[vmem, vmem, vmem, vmem, pl.BlockSpec(mem...  10.6 us
  transfers between devices with their start and end apart: 15, of which 13 were waited for; matrix products, arithmetic and copies ran while one was open for 1% of the time, Pallas kernels for 4%

profile of v4, /device:TPU:15, one launch (start us, length us, event | category | flops | bytes accessed | tf_op | source)
XLA Modules:
  0.0 368.3 jit_solution(15885337396587063317)
XLA Ops:
  0.6 2.4 collective-permute-start
  3.0 2.9 collective-permute-done
  5.9 0.8 select_bitcast_fusion.7
  6.9 7.1 %spread_blocks.1 = f32[16,192,640]{2,1,0:T(8,128)} custom-call(f32[1,64,10240]{2,1,0:T(8,128)} %refs_0_.1, f32[1,64,10240]{2,1,0:T(8,128)} %refs_1_.1, f32[1,64,10240]{2,1,0:T(8,128)} %refs_2_.1), custom_call_target="tpu_custom_call" | custom-call | tf_op jit(solution)/shard_map/spread_blocks/pallas_call | solution.py:188
  14.1 8.2 %all-to-all-start = ((f32[16,192,640]{2,1,0:T(8,128)}), f32[16,192,640]{2,1,0:T(8,128)}, u32[]{:S(2)}, u32[]{:S(2)}) async-start(f32[16,192,640]{2,1,0:T(8,128)} %spread_blocks.1), calls=%async_computation | async-start | bytes 15728640 | tf_op jit(solution)/shard_map/all_to_all | solution.py:49
  22.7 1.3 collective-permute-start.6
  25.2 2.3 collective-permute-done.6
  27.5 43.8 %collective-permute-done.2 = f32[2,2,64,192]{3,2,1,0:T(8,128)S(1)} collective-permute-done((f32[2,2,64,192]{3,2,1,0:T(8,128)S(1)}, f32[2,2,64,192]{3,2,1,0:T(8,128)S(1)}, u32[]{:S(2)}, u32[]{:S(2)}) %collective-permute-start.2) | collective-permute-done | bytes 196640 | tf_op jit(solution)/shard_map/ppermute | solution.py:431
  71.5 0.9 collective-permute-start.3
  72.6 1.3 collective-permute-done.3
  74.8 118.7 %all-to-all-done.x = f32[16,192,640]{2,1,0:T(8,128)} async-done(((f32[16,192,640]{2,1,0:T(8,128)}), f32[16,192,640]{2,1,0:T(8,128)}, u32[]{:S(2)}, u32[]{:S(2)}) %all-to-all-start) | async-done | bytes 7864352 | tf_op jit(solution)/shard_map/all_to_all | solution.py:49
  193.5 15.4 %project.1 = (f32[16,64,640]{2,1,0:T(8,128)}, f32[16,64,640]{2,1,0:T(8,128)}, f32[1,64,128]{2,1,0:T(8,128)S(1)}, f32[1,64,128]{2,1,0:T(8,128)S(1)}) custom-call(f32[16,192,640]{2,1,0:T(8,128)} %all-to-all-done.x, f32[16,64,192]{2,1,0:T(8,128)S(1)} %bitcast_multiply_fusion.rot), custom_call_target="tpu_custom_call" | custom-call | tf_op jit(solution)/shard_map/project/pallas_call | solution.py:278
  208.9 3.5 collective-permute-start.4
  212.4 1.9 collective-permute-start.5
  215.2 3.3 collective-permute-done.5.right
  218.5 1.7 copy-done
  220.3 10.6 %stiffness.1 = (f32[16,64,640]{2,1,0:T(8,128)S(1)}, f32[2,1024]{1,0:T(2,128)S(1)}) custom-call(f32[16,64,640]{2,1,0:T(8,128)S(1)} %copy-done, f32[1,64,128]{2,1,0:T(8,128)S(1)} %collective-permute-done.4.left, f32[1,64,128]{2,1,0:T(8,128)S(1)} %collective-permute-done.5.right, f32[18,640]{1,0:T(8,128)S(1)} %concatenate.8.band, f32[16]{0:T(128)S(1)} %fusion.6.lam), custom_call_target="tpu_custom_call" | custom-call | tf_op jit(solution)/shard_map/stiffness/pallas_call | solution.py:355
  230.9 1.6 copy-done.2
  232.5 3.4 collective-permute-done.7
  235.9 2.5 collective-permute-done.8
  238.4 6.0 %all-to-all-start.1 = ((f32[16,64,640]{2,1,0:T(8,128)}), f32[16,64,640]{2,1,0:T(8,128)}, u32[]{:S(2)}, u32[]{:S(2)}) async-start(f32[16,64,640]{2,1,0:T(8,128)} %get-tuple-element.22), calls=%async_computation.1 | async-start | bytes 5242880 | tf_op jit(solution)/shard_map/all_to_all | solution.py:49
  244.7 11.8 %collective-permute-done.9 = f32[2,1024]{1,0:T(2,128)S(1)} collective-permute-done((f32[2,1024]{1,0:T(2,128)S(1)}, f32[2,1024]{1,0:T(2,128)S(1)}, u32[]{:S(2)}, u32[]{:S(2)}) %collective-permute-start.9) | collective-permute-done | bytes 8224 | tf_op jit(solution)/shard_map/ppermute | solution.py:485
  256.5 0.8 collective-permute-start.10
  257.2 0.8 collective-permute-done.10
  258.5 2.5 collective-permute-done.11
  261.0 1.7 copy-done.3
  262.7 4.2 %residual_back.1 = (f32[16,64,640]{2,1,0:T(8,128)}, f32[1,1024]{1,0:T(1,128)S(1)}) custom-call(f32[16,64,640]{2,1,0:T(8,128)S(1)} %copy-done.1, f32[16,64,640]{2,1,0:T(8,128)S(1)} %copy-done.3, f32[2,1024]{1,0:T(2,128)S(1)} %add.87.total), custom_call_target="tpu_custom_call" | custom-call | tf_op jit(solution)/shard_map/residual_back/pallas_call | solution.py:408
  266.9 36.3 %all-to-all-done.1.piece = f32[16,64,640]{2,1,0:T(8,128)} async-done(((f32[16,64,640]{2,1,0:T(8,128)}), f32[16,64,640]{2,1,0:T(8,128)}, u32[]{:S(2)}, u32[]{:S(2)}) %all-to-all-start.1) | async-done | bytes 2621472 | tf_op jit(solution)/shard_map/all_to_all | solution.py:49
  303.2 4.9 %all-to-all-start.2 = ((f32[16,64,640]{2,1,0:T(8,128)}), f32[16,64,640]{2,1,0:T(8,128)S(1)}, u32[]{:S(2)}, u32[]{:S(2)}) async-start(f32[16,64,640]{2,1,0:T(8,128)} %get-tuple-element.25), calls=%async_computation.2 | async-start | bytes 5242880 | tf_op jit(solution)/shard_map/all_to_all | solution.py:49
  308.6 2.9 collect_block.2
  311.5 55.2 %all-to-all-done.2.piece = f32[16,64,640]{2,1,0:T(8,128)S(1)} async-done(((f32[16,64,640]{2,1,0:T(8,128)}), f32[16,64,640]{2,1,0:T(8,128)S(1)}, u32[]{:S(2)}, u32[]{:S(2)}) %all-to-all-start.2) | async-done | bytes 2621472 | tf_op jit(solution)/shard_map/all_to_all | solution.py:49
  366.7 1.6 collect_block.3
  (51 shorter events, 5.0 us)
Async XLA Ops:
  0.6 5.3 %collective-permute-start = (f32[64,192]{1,0:T(8,128)}, f32[64,192]{1,0:T(8,128)S(1)}, u32[]{:S(2)}, u32[]{:S(2)}) collective-permute-start(f32[64,192]{1,0:T(8,128)} %bitcast.25), channel_id=1, source_target_pairs={{0,16},{2,18},{4,20},{6,22},{8,24},{10,26},{12,28},{14,30},{16,0},... | collective-permute-start | bytes 147464 | tf_op jit(solution)/shard_map/ppermute | solution.py:431
  6.8 7.2 %collective-permute-start.1 = (f32[2,64,192]{2,1,0:T(8,128)S(1)}, f32[2,64,192]{2,1,0:T(8,128)S(1)}, u32[]{:S(2)}, u32[]{:S(2)}) collective-permute-start(f32[2,64,192]{2,1,0:T(8,128)S(1)} %pad_maximum_fusion.2), channel_id=1, source_target_pairs={{0,8},{2,10},{4,12},{6,14},{8,0},{10,2},{12,4},{14,6},{16,24},{18,... | collective-permute-start | bytes 294920 | tf_op jit(solution)/shard_map/ppermute | solution.py:431
  14.1 8.3 %copy-start.4 = (f32[10240]{0:T(1024)S(1)}, f32[10240]{0:T(1024)}, u32[]{:S(2)}) copy-start(f32[10240]{0:T(1024)} %param.14) | copy-start | bytes 122884
  14.1 8.3 %copy-start.5 = (f32[10240]{0:T(1024)S(1)}, f32[10240]{0:T(1024)}, u32[]{:S(2)}) copy-start(f32[10240]{0:T(1024)} %param.15) | copy-start | bytes 122884
  14.1 8.3 %copy-start.6 = (s32[10240]{0:T(1024)S(1)}, s32[10240]{0:T(1024)}, u32[]{:S(2)}) copy-start(s32[10240]{0:T(1024)} %param.16) | copy-start | bytes 122884
  14.1 179.4 %all-to-all-start = ((f32[16,192,640]{2,1,0:T(8,128)}), f32[16,192,640]{2,1,0:T(8,128)}, u32[]{:S(2)}, u32[]{:S(2)}) async-start(f32[16,192,640]{2,1,0:T(8,128)} %spread_blocks.1), calls=%async_computation | async-start | bytes 15728640 | tf_op jit(solution)/shard_map/all_to_all | solution.py:49
  22.7 4.7 %collective-permute-start.6 = (f32[8,8]{1,0:T(8,128)S(1)}, f32[8,8]{1,0:T(8,128)S(1)}, u32[]{:S(2)}, u32[]{:S(2)}) collective-permute-start(f32[8,8]{1,0:T(8,128)S(1)} %slice.40), channel_id=1, source_target_pairs={{0,1},{2,3},{4,5},{6,7},{8,9},{10,11},{12,13},{14,15},{16,17},{18,... | collective-permute-start | bytes 776 | tf_op jit(solution)/shard_map/ppermute | solution.py:72
  24.0 47.4 %collective-permute-start.2 = (f32[2,2,64,192]{3,2,1,0:T(8,128)S(1)}, f32[2,2,64,192]{3,2,1,0:T(8,128)S(1)}, u32[]{:S(2)}, u32[]{:S(2)}) collective-permute-start(f32[2,2,64,192]{3,2,1,0:T(8,128)S(1)} %pad_maximum_fusion.1), channel_id=1, source_target_pairs={{0,4},{2,6},{4,0},{6,2},{8,12},{10,14},{12,8},{14,10},{16,20},{18,... | collective-permute-start | bytes 589832 | tf_op jit(solution)/shard_map/ppermute | solution.py:431
  71.5 2.5 collective-permute-start.3
  74.0 0.7 copy-start.7
  208.9 6.3 %collective-permute-start.4 = (f32[1,64,128]{2,1,0:T(8,128)S(1)}, f32[1,64,128]{2,1,0:T(8,128)S(1)}, u32[]{:S(2)}, u32[]{:S(2)}) collective-permute-start(f32[1,64,128]{2,1,0:T(8,128)S(1)} %get-tuple-element.19), channel_id=1, source_target_pairs={{0,2},{2,4},{4,6},{6,8},{8,10},{10,12},{12,14},{14,16},{16,18},{18... | collective-permute-start | bytes 98312 | tf_op jit(solution)/shard_map/ppermute | solution.py:58
  212.4 6.1 %collective-permute-start.5 = (f32[1,64,128]{2,1,0:T(8,128)S(1)}, f32[1,64,128]{2,1,0:T(8,128)S(1)}, u32[]{:S(2)}, u32[]{:S(2)}) collective-permute-start(f32[1,64,128]{2,1,0:T(8,128)S(1)} %get-tuple-element.20), channel_id=1, source_target_pairs={{2,0},{4,2},{6,4},{8,6},{10,8},{12,10},{14,12},{16,14},{18,16},{20... | collective-permute-start | bytes 98312 | tf_op jit(solution)/shard_map/ppermute | solution.py:58
  218.5 1.7 copy-start
  230.9 1.6 copy-start.2
  232.4 3.4 collective-permute-start.7
  235.9 2.5 collective-permute-start.8
  238.4 22.6 %copy-start.1 = (f32[16,64,640]{2,1,0:T(8,128)S(1)}, f32[16,64,640]{2,1,0:T(8,128)}, u32[]{:S(2)}) copy-start(f32[16,64,640]{2,1,0:T(8,128)} %get-tuple-element.18.x) | copy-start | bytes 7864324
  238.4 64.8 %all-to-all-start.1 = ((f32[16,64,640]{2,1,0:T(8,128)}), f32[16,64,640]{2,1,0:T(8,128)}, u32[]{:S(2)}, u32[]{:S(2)}) async-start(f32[16,64,640]{2,1,0:T(8,128)} %get-tuple-element.22), calls=%async_computation.1 | async-start | bytes 5242880 | tf_op jit(solution)/shard_map/all_to_all | solution.py:49
  244.4 12.1 %collective-permute-start.9 = (f32[2,1024]{1,0:T(2,128)S(1)}, f32[2,1024]{1,0:T(2,128)S(1)}, u32[]{:S(2)}, u32[]{:S(2)}) collective-permute-start(f32[2,1024]{1,0:T(2,128)S(1)} %add.84), channel_id=1, source_target_pairs={{0,4},{2,6},{4,0},{6,2},{8,12},{10,14},{12,8},{14,10},{16,20},{18,... | collective-permute-start | bytes 24584 | tf_op jit(solution)/shard_map/ppermute | solution.py:485
  256.5 1.6 collective-permute-start.10
  258.1 2.9 collective-permute-start.11
  261.0 1.7 copy-start.3
  303.2 63.5 %all-to-all-start.2 = ((f32[16,64,640]{2,1,0:T(8,128)}), f32[16,64,640]{2,1,0:T(8,128)S(1)}, u32[]{:S(2)}, u32[]{:S(2)}) async-start(f32[16,64,640]{2,1,0:T(8,128)} %get-tuple-element.25), calls=%async_computation.2 | async-start | bytes 5242880 | tf_op jit(solution)/shard_map/all_to_all | solution.py:49

commit v5 on v4

--- a/solution.py
+++ b/solution.py
@@ -10,7 +10,7 @@
 REACH = 8
 LANES = 128
 ROWS = 8
-VMEM_LIMIT = 40 * 1024 * 1024
+VMEM_LIMIT = 20 * 1024 * 1024
 HIGHEST = lax.Precision.HIGHEST
 
 
@@ -200,23 +200,37 @@
     )(*blocks)
 
 
-def collect_block(pieces):
-    count, rows, dofs = pieces.shape
+def collect_blocks(pieces):
+    count, rows, dofs = pieces[0].shape
     many = max(n for n in (1, 2, 4, 8) if count % n == 0)
-
-    def kernel(piece, out):
-        for i in range(many):
-            out[0, :, i * dofs : (i + 1) * dofs] = piece[i]
+    kinds = len(pieces)
+
+    def kernel(*refs):
+        for piece, out in zip(refs[:kinds], refs[kinds:]):
+            for i in range(many):
+                out[0, :, i * dofs : (i + 1) * dofs] = piece[i]
 
     return pl.pallas_call(
         kernel,
         grid=(count // many,),
-        in_specs=[pl.BlockSpec((many, rows, dofs), lambda i: (i, 0, 0))],
-        out_specs=pl.BlockSpec((1, rows, many * dofs), lambda i: (0, 0, i)),
-        out_shape=pltpu.HBM((1, rows, count * dofs), jnp.float32),
+        in_specs=[pl.BlockSpec((many, rows, dofs), lambda i: (i, 0, 0))] * kinds,
+        out_specs=[pl.BlockSpec((1, rows, many * dofs), lambda i: (0, 0, i))] * kinds,
+        out_shape=[pltpu.HBM((1, rows, count * dofs), jnp.float32)] * kinds,
         compiler_params=params(),
-        name="collect_block",
-    )(pieces)
+        name="collect_blocks",
+    )(*pieces)
+
+
+PARTS = 3
+
+
+def bf16_parts(value):
+    parts = []
+    for i in range(PARTS):
+        parts.append(value.astype(jnp.bfloat16))
+        if i < PARTS - 1:
+            value = value - parts[i].astype(jnp.float32)
+    return parts
 
 
 def project(stacked, rotation):
@@ -227,21 +241,46 @@
     groups = -(-count * REACH // LANES)
     per = LANES // REACH
 
-    def kernel(x, rot, proj, back, head, tail, slots):
+    strip = 2 * ROWS
+
+    def kernel(x, rot, proj, back, head, tail, split_rot, *split_slots):
         tile = pl.program_id(0)
 
+        @pl.when(tile == 0)
+        def _():
+            def one(j, carry):
+                for i, part in enumerate(bf16_parts(rot[j])):
+                    split_rot[j, i * rows : (i + 1) * rows, :] = part
+                return carry
+
+            lax.fori_loop(0, count, one, 0)
+
         def transform(r, carry):
-            at = pl.ds(pl.multiple_of(r * ROWS, ROWS), ROWS)
-            out = to_slots([x[s, at, :] for s in range(count)])
+            at = pl.ds(pl.multiple_of(r * strip, strip), strip)
+            halves = []
+            for h in range(2):
+                own = pl.ds(pl.multiple_of(r * strip + h * ROWS, ROWS), ROWS)
+                halves.append(to_slots([x[s, own, :] for s in range(count)]))
             for j in range(count):
-                slots[j, at, :] = out[j]
+                value = jnp.concatenate([half[j] for half in halves], 0)
+                for part, ref in zip(bf16_parts(value), split_slots):
+                    ref[j, at, :] = part
             return carry
 
-        lax.fori_loop(0, wide // ROWS, transform, 0)
+        lax.fori_loop(0, wide // strip, transform, 0)
         for j in range(count):
-            proj[j] = jnp.dot(
-                rot[j], slots[j], precision=HIGHEST, preferred_element_type=jnp.float32
-            )
+            total = None
+            for i in range(PARTS - 1, -1, -1):
+                terms = PARTS - i
+                stacked_terms = jnp.dot(
+                    split_rot[j, : terms * rows, :],
+                    split_slots[i][j],
+                    preferred_element_type=jnp.float32,
+                )
+                for q in range(terms - 1, -1, -1):
+                    term = stacked_terms[q * rows : (q + 1) * rows]
+                    total = term if total is None else total + term
+            proj[j] = total
 
         def inverse(r, carry):
             at = pl.ds(pl.multiple_of(r * ROWS, ROWS), ROWS)
@@ -283,8 +322,9 @@
             pl.BlockSpec((count, rows, wide), lambda t: (0, 0, 0)),
         ],
         out_specs=[cell, cell, edge, edge],
-        out_shape=[field, field, edges, edges],
-        scratch_shapes=[pltpu.VMEM((count, wide, LANES), jnp.float32)],
+        out_shape=[jax.ShapeDtypeStruct(field.shape, jnp.float32), field, edges, edges],
+        scratch_shapes=[pltpu.VMEM((count, PARTS * rows, wide), jnp.bfloat16)]
+        + [pltpu.VMEM((count, wide, LANES), jnp.bfloat16)] * PARTS,
         compiler_params=params(),
         name="project",
     )(stacked, rotation)
@@ -480,13 +520,13 @@
     for _, pairs in far:
         sums = sums + lax.ppermute(sums, "span", pairs)
     spans, sums = lax.optimization_barrier((spans, sums))
-    next_block = collect_block(exchange(spans))
+    block_pieces = exchange(spans)
     for _, pairs in near:
         sums = sums + lax.ppermute(sums, "span", pairs)
     for _, pairs in halvings("elem"):
         sums = sums + lax.ppermute(sums, "elem", pairs)
     spans, ritz = residual_back(projected, stiff, sums)
-    next_residual = collect_block(exchange(spans))
+    next_block, next_residual = collect_blocks([block_pieces, exchange(spans)])
     ritz = lax.dynamic_slice_in_dim(ritz, lax.axis_index("span") * rows, rows, 1)
     return (next_block, next_residual, ritz)
 

time: 369 us -> 369 us (level)
  transfers between devices with their start and end apart: 15 -> 15, of which waited for: 13 -> 13; matrix products, arithmetic and copies ran while one was open for 1% -> 1% of each run, Pallas kernels for 4% -> 3%
where the time goes in v5:
time: 369 us; the launch traced here: 368 us
  waiting for transfers between devices  287 us (78%)
  Pallas kernels  39.4 us (11%)
  starting transfers between devices  30.8 us (8%)
  local copies, waits for them, and re-layouts  6.54 us (2%)
    all_to_all x3, waiting for transfers between devices, exchange(): lax.all_to_all(pieces, 'span', split_axis=0, concat_axis=0, tiled=True)  212 us
    ppermute x4, waiting for transfers between devices, exchange_step(): other = lax.ppermute(held, 'span', pairs)  48.1 us
    all_to_all x3, starting transfers between devices, exchange(): lax.all_to_all(pieces, 'span', split_axis=0, concat_axis=0, tiled=True)  18.8 us
    ppermute x4, waiting for transfers between devices, tiled_device(): sums = sums + lax.ppermute(sums, 'span', pairs)  18.5 us
    pallas_call x1, Pallas kernels, project(): pl.pallas_call(kernel, grid=(tiles,), in_specs=[pl.BlockSpec((count, wide...  13.3 us
    pallas_call x1, Pallas kernels, stiffness(): pl.pallas_call(kernel, in_specs=[vmem, vmem, vmem, vmem, pl.BlockSpec(mem...  10.9 us
  transfers between devices with their start and end apart: 15, of which 13 were waited for; matrix products, arithmetic and copies ran while one was open for 1% of the time, Pallas kernels for 3%

profile of v5, /device:TPU:15, one launch (start us, length us, event | category | flops | bytes accessed | tf_op | source)
XLA Modules:
  0.0 368.0 jit_solution(4195215188687415217)
XLA Ops:
  0.6 2.4 collective-permute-start
  3.0 2.9 collective-permute-done
  5.9 0.8 select_bitcast_fusion.7
  6.9 7.1 %spread_blocks.1 = f32[16,192,640]{2,1,0:T(8,128)} custom-call(f32[1,64,10240]{2,1,0:T(8,128)} %refs_0_.1, f32[1,64,10240]{2,1,0:T(8,128)} %refs_1_.1, f32[1,64,10240]{2,1,0:T(8,128)} %refs_2_.1), custom_call_target="tpu_custom_call" | custom-call | tf_op jit(solution)/shard_map/spread_blocks/pallas_call | solution.py:188
  14.1 8.2 %all-to-all-start = ((f32[16,192,640]{2,1,0:T(8,128)}), f32[16,192,640]{2,1,0:T(8,128)}, u32[]{:S(2)}, u32[]{:S(2)}) async-start(f32[16,192,640]{2,1,0:T(8,128)} %spread_blocks.1), calls=%async_computation | async-start | bytes 15728640 | tf_op jit(solution)/shard_map/all_to_all | solution.py:49
  22.7 1.3 collective-permute-start.6
  25.2 2.3 collective-permute-done.6
  27.5 43.8 %collective-permute-done.2 = f32[2,2,64,192]{3,2,1,0:T(8,128)S(1)} collective-permute-done((f32[2,2,64,192]{3,2,1,0:T(8,128)S(1)}, f32[2,2,64,192]{3,2,1,0:T(8,128)S(1)}, u32[]{:S(2)}, u32[]{:S(2)}) %collective-permute-start.2) | collective-permute-done | bytes 196640 | tf_op jit(solution)/shard_map/ppermute | solution.py:471
  71.5 0.9 collective-permute-start.3
  72.6 1.3 collective-permute-done.3
  74.7 1.1 bitcast_multiply_fusion.rot
  75.8 117.7 %all-to-all-done.x = f32[16,192,640]{2,1,0:T(8,128)} async-done(((f32[16,192,640]{2,1,0:T(8,128)}), f32[16,192,640]{2,1,0:T(8,128)}, u32[]{:S(2)}, u32[]{:S(2)}) %all-to-all-start) | async-done | bytes 7864352 | tf_op jit(solution)/shard_map/all_to_all | solution.py:49
  193.5 1.2 copy-done
  194.8 13.3 %project.1 = (f32[16,64,640]{2,1,0:T(8,128)S(1)}, f32[16,64,640]{2,1,0:T(8,128)}, f32[1,64,128]{2,1,0:T(8,128)S(1)}, f32[1,64,128]{2,1,0:T(8,128)S(1)}) custom-call(f32[16,192,640]{2,1,0:T(8,128)} %all-to-all-done.x, f32[16,64,192]{2,1,0:T(8,128)S(1)} %copy-done), custom_call_target="tpu_custom_call" | custom-call | tf_op jit(solution)/shard_map/project/pallas_call | solution.py:317
  208.1 3.5 collective-permute-start.4
  211.6 1.9 collective-permute-start.5
  214.4 3.3 collective-permute-done.5.right
  217.8 10.9 %stiffness.1 = (f32[16,64,640]{2,1,0:T(8,128)S(1)}, f32[2,1024]{1,0:T(2,128)S(1)}) custom-call(f32[16,64,640]{2,1,0:T(8,128)S(1)} %get-tuple-element.20.x, f32[1,64,128]{2,1,0:T(8,128)S(1)} %collective-permute-done.4.left, f32[1,64,128]{2,1,0:T(8,128)S(1)} %collective-permute-done.5.right, f32[18,640]{1,0:T(8,128)S(1)} %concatenate.8.band, f32[16]{0:T(128)S(1)} %fusion.6.lam), custom_call_target="tpu_custom_call" | custom-call | tf_op jit(solution)/shard_map/stiffness/pallas_call | solution.py:395
  228.7 1.5 copy-done.1
  230.2 3.4 collective-permute-done.7
  233.6 2.5 collective-permute-done.8
  236.1 5.7 %all-to-all-start.1 = ((f32[16,64,640]{2,1,0:T(8,128)}), f32[16,64,640]{2,1,0:T(8,128)}, u32[]{:S(2)}, u32[]{:S(2)}) async-start(f32[16,64,640]{2,1,0:T(8,128)} %get-tuple-element.24), calls=%async_computation.1 | async-start | bytes 5242880 | tf_op jit(solution)/shard_map/all_to_all | solution.py:49
  242.1 11.8 %collective-permute-done.9 = f32[2,1024]{1,0:T(2,128)S(1)} collective-permute-done((f32[2,1024]{1,0:T(2,128)S(1)}, f32[2,1024]{1,0:T(2,128)S(1)}, u32[]{:S(2)}, u32[]{:S(2)}) %collective-permute-start.9) | collective-permute-done | bytes 8224 | tf_op jit(solution)/shard_map/ppermute | solution.py:525
  253.9 0.8 collective-permute-start.10
  254.7 0.8 collective-permute-done.10
  255.9 2.5 collective-permute-done.11
  258.4 1.7 copy-done.2
  260.2 4.2 %residual_back.1 = (f32[16,64,640]{2,1,0:T(8,128)}, f32[1,1024]{1,0:T(1,128)S(1)}) custom-call(f32[16,64,640]{2,1,0:T(8,128)S(1)} %get-tuple-element.20.x, f32[16,64,640]{2,1,0:T(8,128)S(1)} %copy-done.2, f32[2,1024]{1,0:T(2,128)S(1)} %add.87.total), custom_call_target="tpu_custom_call" | custom-call | tf_op jit(solution)/shard_map/residual_back/pallas_call | solution.py:448
  264.3 36.3 %all-to-all-done.1.refs_0_ = f32[16,64,640]{2,1,0:T(8,128)} async-done(((f32[16,64,640]{2,1,0:T(8,128)}), f32[16,64,640]{2,1,0:T(8,128)}, u32[]{:S(2)}, u32[]{:S(2)}) %all-to-all-start.1) | async-done | bytes 2621472 | tf_op jit(solution)/shard_map/all_to_all | solution.py:49
  300.6 4.9 %all-to-all-start.2 = ((f32[16,64,640]{2,1,0:T(8,128)}), f32[16,64,640]{2,1,0:T(8,128)S(1)}, u32[]{:S(2)}, u32[]{:S(2)}) async-start(f32[16,64,640]{2,1,0:T(8,128)} %get-tuple-element.27), calls=%async_computation.2 | async-start | bytes 5242880 | tf_op jit(solution)/shard_map/all_to_all | solution.py:49
  306.1 58.1 %all-to-all-done.2.refs_1_ = f32[16,64,640]{2,1,0:T(8,128)S(1)} async-done(((f32[16,64,640]{2,1,0:T(8,128)}), f32[16,64,640]{2,1,0:T(8,128)S(1)}, u32[]{:S(2)}, u32[]{:S(2)}) %all-to-all-start.2) | async-done | bytes 2621472 | tf_op jit(solution)/shard_map/all_to_all | solution.py:49
  364.1 3.8 %collect_blocks.1 = (f32[1,64,10240]{2,1,0:T(8,128)}, f32[1,64,10240]{2,1,0:T(8,128)}) custom-call(f32[16,64,640]{2,1,0:T(8,128)} %all-to-all-done.1.refs_0_, f32[16,64,640]{2,1,0:T(8,128)S(1)} %all-to-all-done.2.refs_1_), custom_call_target="tpu_custom_call" | custom-call | tf_op jit(solution)/shard_map/collect_blocks/pallas_call | solution.py:213
  (48 shorter events, 4.8 us)
Async XLA Ops:
  0.6 5.3 %collective-permute-start = (f32[64,192]{1,0:T(8,128)}, f32[64,192]{1,0:T(8,128)S(1)}, u32[]{:S(2)}, u32[]{:S(2)}) collective-permute-start(f32[64,192]{1,0:T(8,128)} %bitcast.25), channel_id=1, source_target_pairs={{0,16},{2,18},{4,20},{6,22},{8,24},{10,26},{12,28},{14,30},{16,0},... | collective-permute-start | bytes 147464 | tf_op jit(solution)/shard_map/ppermute | solution.py:471
  6.8 7.2 %collective-permute-start.1 = (f32[2,64,192]{2,1,0:T(8,128)S(1)}, f32[2,64,192]{2,1,0:T(8,128)S(1)}, u32[]{:S(2)}, u32[]{:S(2)}) collective-permute-start(f32[2,64,192]{2,1,0:T(8,128)S(1)} %pad_maximum_fusion.2), channel_id=1, source_target_pairs={{0,8},{2,10},{4,12},{6,14},{8,0},{10,2},{12,4},{14,6},{16,24},{18,... | collective-permute-start | bytes 294920 | tf_op jit(solution)/shard_map/ppermute | solution.py:471
  14.1 8.3 %copy-start.3 = (f32[10240]{0:T(1024)S(1)}, f32[10240]{0:T(1024)}, u32[]{:S(2)}) copy-start(f32[10240]{0:T(1024)} %param.14) | copy-start | bytes 122884
  14.1 8.3 %copy-start.4 = (f32[10240]{0:T(1024)S(1)}, f32[10240]{0:T(1024)}, u32[]{:S(2)}) copy-start(f32[10240]{0:T(1024)} %param.15) | copy-start | bytes 122884
  14.1 8.3 %copy-start.5 = (s32[10240]{0:T(1024)S(1)}, s32[10240]{0:T(1024)}, u32[]{:S(2)}) copy-start(s32[10240]{0:T(1024)} %param.16) | copy-start | bytes 122884
  14.1 179.4 %all-to-all-start = ((f32[16,192,640]{2,1,0:T(8,128)}), f32[16,192,640]{2,1,0:T(8,128)}, u32[]{:S(2)}, u32[]{:S(2)}) async-start(f32[16,192,640]{2,1,0:T(8,128)} %spread_blocks.1), calls=%async_computation | async-start | bytes 15728640 | tf_op jit(solution)/shard_map/all_to_all | solution.py:49
  22.7 4.7 %collective-permute-start.6 = (f32[8,8]{1,0:T(8,128)S(1)}, f32[8,8]{1,0:T(8,128)S(1)}, u32[]{:S(2)}, u32[]{:S(2)}) collective-permute-start(f32[8,8]{1,0:T(8,128)S(1)} %slice.40), channel_id=1, source_target_pairs={{0,1},{2,3},{4,5},{6,7},{8,9},{10,11},{12,13},{14,15},{16,17},{18,... | collective-permute-start | bytes 776 | tf_op jit(solution)/shard_map/ppermute | solution.py:72
  24.0 47.4 %collective-permute-start.2 = (f32[2,2,64,192]{3,2,1,0:T(8,128)S(1)}, f32[2,2,64,192]{3,2,1,0:T(8,128)S(1)}, u32[]{:S(2)}, u32[]{:S(2)}) collective-permute-start(f32[2,2,64,192]{3,2,1,0:T(8,128)S(1)} %pad_maximum_fusion.1), channel_id=1, source_target_pairs={{0,4},{2,6},{4,0},{6,2},{8,12},{10,14},{12,8},{14,10},{16,20},{18,... | collective-permute-start | bytes 589832 | tf_op jit(solution)/shard_map/ppermute | solution.py:471
  71.5 2.5 collective-permute-start.3
  74.0 0.7 copy-start.6
  193.5 1.2 copy-start
  208.1 6.3 %collective-permute-start.4 = (f32[1,64,128]{2,1,0:T(8,128)S(1)}, f32[1,64,128]{2,1,0:T(8,128)S(1)}, u32[]{:S(2)}, u32[]{:S(2)}) collective-permute-start(f32[1,64,128]{2,1,0:T(8,128)S(1)} %get-tuple-element.21), channel_id=1, source_target_pairs={{0,2},{2,4},{4,6},{6,8},{8,10},{10,12},{12,14},{14,16},{16,18},{18... | collective-permute-start | bytes 98312 | tf_op jit(solution)/shard_map/ppermute | solution.py:58
  211.6 6.1 %collective-permute-start.5 = (f32[1,64,128]{2,1,0:T(8,128)S(1)}, f32[1,64,128]{2,1,0:T(8,128)S(1)}, u32[]{:S(2)}, u32[]{:S(2)}) collective-permute-start(f32[1,64,128]{2,1,0:T(8,128)S(1)} %get-tuple-element.22), channel_id=1, source_target_pairs={{2,0},{4,2},{6,4},{8,6},{10,8},{12,10},{14,12},{16,14},{18,16},{20... | collective-permute-start | bytes 98312 | tf_op jit(solution)/shard_map/ppermute | solution.py:58
  228.7 1.5 copy-start.1
  230.2 3.4 collective-permute-start.7
  233.6 2.5 collective-permute-start.8
  236.1 64.5 %all-to-all-start.1 = ((f32[16,64,640]{2,1,0:T(8,128)}), f32[16,64,640]{2,1,0:T(8,128)}, u32[]{:S(2)}, u32[]{:S(2)}) async-start(f32[16,64,640]{2,1,0:T(8,128)} %get-tuple-element.24), calls=%async_computation.1 | async-start | bytes 5242880 | tf_op jit(solution)/shard_map/all_to_all | solution.py:49
  241.8 12.1 %collective-permute-start.9 = (f32[2,1024]{1,0:T(2,128)S(1)}, f32[2,1024]{1,0:T(2,128)S(1)}, u32[]{:S(2)}, u32[]{:S(2)}) collective-permute-start(f32[2,1024]{1,0:T(2,128)S(1)} %add.84), channel_id=1, source_target_pairs={{0,4},{2,6},{4,0},{6,2},{8,12},{10,14},{12,8},{14,10},{16,20},{18,... | collective-permute-start | bytes 24584 | tf_op jit(solution)/shard_map/ppermute | solution.py:525
  253.9 1.6 collective-permute-start.10
  255.5 2.9 collective-permute-start.11
  258.4 1.7 copy-start.2
  300.6 63.5 %all-to-all-start.2 = ((f32[16,64,640]{2,1,0:T(8,128)}), f32[16,64,640]{2,1,0:T(8,128)S(1)}, u32[]{:S(2)}, u32[]{:S(2)}) async-start(f32[16,64,640]{2,1,0:T(8,128)} %get-tuple-element.27), calls=%async_computation.2 | async-start | bytes 5242880 | tf_op jit(solution)/shard_map/all_to_all | solution.py:49

commit v6 on v5

--- a/solution.py
+++ b/solution.py
@@ -473,10 +473,11 @@
     return jnp.stack([jnp.where(upper, other, held), jnp.where(upper, held, other)])
 
 
-def in_order(held, bits):
-    order = tuple(range(bits))[::-1] + tuple(range(bits, held.ndim))
-    held = held.transpose(order)
-    return held.reshape((-1,) + held.shape[bits:])
+def in_order(held, steps):
+    bits = [step for step, _ in steps][::-1]
+    order = tuple(sorted(range(len(bits)), key=lambda d: -bits[d]))
+    held = held.transpose(order + tuple(range(len(bits), held.ndim)))
+    return held.reshape((-1,) + held.shape[len(bits) :])
 
 
 def tiled_device(
@@ -494,16 +495,14 @@
     dofs = current_block.shape[2] // count
     rows = current_block.shape[1]
     steps = list(halvings("span"))
-    far, near = steps[: len(steps) // 2], steps[len(steps) // 2 :]
-    rotation = ritz_rotation[0].T
-    for step, pairs in far:
-        rotation = exchange_step(rotation, step, pairs)
+    rotation = exchange_step(ritz_rotation[0].T, *steps[0])
     pieces = spread_blocks((current_block, search_block, previous_block), count)
     pieces, rotation = lax.optimization_barrier((pieces, rotation))
     stacked = exchange(pieces)
-    for step, pairs in near:
+    order = steps[2:] + steps[1:2]
+    for step, pairs in order:
         rotation = exchange_step(rotation, step, pairs)
-    rotation = in_order(rotation, len(steps))
+    rotation = in_order(rotation, [steps[0]] + order)
     scales = jnp.array(slot_scales(count), jnp.float32)[:, None, None]
     weights, ground, link = coefficients(
         ground_spring, wire_tension, dropper_stiff, dropper_offset, span_link, count, dofs
@@ -516,15 +515,13 @@
     links = 2.0 * (1.0 - fourier_rows(count)[1])
     projected, spans, head, tail = project(stacked, rotation * scales)
     before, after = to_next(tail, 1), to_next(head, -1)
+    spans, before, after = lax.optimization_barrier((spans, before, after))
+    block_pieces = exchange(spans)
     stiff, sums = stiffness(projected, before, after, bands, links)
-    for _, pairs in far:
-        sums = sums + lax.ppermute(sums, "span", pairs)
-    spans, sums = lax.optimization_barrier((spans, sums))
-    block_pieces = exchange(spans)
-    for _, pairs in near:
-        sums = sums + lax.ppermute(sums, "span", pairs)
     for _, pairs in halvings("elem"):
         sums = sums + lax.ppermute(sums, "elem", pairs)
+    for _, pairs in steps[::-1]:
+        sums = sums + lax.ppermute(sums, "span", pairs)
     spans, ritz = residual_back(projected, stiff, sums)
     next_block, next_residual = collect_blocks([block_pieces, exchange(spans)])
     ritz = lax.dynamic_slice_in_dim(ritz, lax.axis_index("span") * rows, rows, 1)

time: 369 us -> 350 us (0.949)
  waiting for transfers between devices: 287 us -> 269 us
    all_to_all x3, waiting for transfers between devices: 212 us -> 88.4 us  [exchange(): lax.all_to_all(pieces, 'span', split_axis=0, concat_axis=0, tiled=True)]
    ppermute x4, waiting for transfers between devices: 48.1 us -> 138 us  [exchange_step(): other = lax.ppermute(held, 'span', pairs)]
    ppermute x4, waiting for transfers between devices: 18.5 us -> 32.9 us  [tiled_device(): sums = sums + lax.ppermute(sums, 'span', pairs)]
  transfers between devices with their start and end apart: 15 -> 15, of which waited for: 13 -> 12; matrix products, arithmetic and copies ran while one was open for 1% -> 1% of each run, Pallas kernels for 3% -> 6%
where the time goes in v6:
time: 350 us; the launch traced here: 347 us
  waiting for transfers between devices  269 us (77%)
  Pallas kernels  39 us (11%)
  starting transfers between devices  31.5 us (9%)
  local copies, waits for them, and re-layouts  5.3 us (2%)
    ppermute x4, waiting for transfers between devices, exchange_step(): other = lax.ppermute(held, 'span', pairs)  138 us
    all_to_all x3, waiting for transfers between devices, exchange(): lax.all_to_all(pieces, 'span', split_axis=0, concat_axis=0, tiled=True)  88.4 us
    ppermute x4, waiting for transfers between devices, tiled_device(): sums = sums + lax.ppermute(sums, 'span', pairs)  32.9 us
    all_to_all x3, starting transfers between devices, exchange(): lax.all_to_all(pieces, 'span', split_axis=0, concat_axis=0, tiled=True)  17.8 us
    pallas_call x1, Pallas kernels, project(): pl.pallas_call(kernel, grid=(tiles,), in_specs=[pl.BlockSpec((count, wide...  13.3 us
    pallas_call x1, Pallas kernels, stiffness(): pl.pallas_call(kernel, in_specs=[vmem, vmem, vmem, vmem, pl.BlockSpec(mem...  10.5 us
    pallas_call x1, Pallas kernels, spread_blocks(): pl.pallas_call(kernel, in_specs=[whole] * kinds, out_specs=whole, out_sha...  7.15 us
  transfers between devices with their start and end apart: 15, of which 12 were waited for; matrix products, arithmetic and copies ran while one was open for 1% of the time, Pallas kernels for 6%

profile of v6, /device:TPU:15, one launch (start us, length us, event | category | flops | bytes accessed | tf_op | source)
XLA Modules:
  0.0 347.3 jit_solution(10179755984986396655)
XLA Ops:
  0.6 2.4 collective-permute-start
  3.0 7.2 %spread_blocks.1 = f32[16,192,640]{2,1,0:T(8,128)} custom-call(f32[1,64,10240]{2,1,0:T(8,128)} %refs_0_.1, f32[1,64,10240]{2,1,0:T(8,128)} %refs_1_.1, f32[1,64,10240]{2,1,0:T(8,128)} %refs_2_.1), custom_call_target="tpu_custom_call" | custom-call | tf_op jit(solution)/shard_map/spread_blocks/pallas_call | solution.py:188
  10.2 5.5 %all-to-all-start = ((f32[16,192,640]{2,1,0:T(8,128)}), f32[16,192,640]{2,1,0:T(8,128)}, u32[]{:S(2)}, u32[]{:S(2)}) async-start(f32[16,192,640]{2,1,0:T(8,128)} %spread_blocks.1), calls=%async_computation | async-start | bytes 15728640 | tf_op jit(solution)/shard_map/all_to_all | solution.py:49
  16.0 45.8 %collective-permute-done.1 = f32[2,64,192]{2,1,0:T(8,128)S(1)} collective-permute-done((f32[2,64,192]{2,1,0:T(8,128)S(1)}, f32[2,64,192]{2,1,0:T(8,128)S(1)}, u32[]{:S(2)}, u32[]{:S(2)}) %collective-permute-start.1) | collective-permute-done | bytes 98336 | tf_op jit(solution)/shard_map/ppermute | solution.py:471
  61.9 1.0 collective-permute-start.2
  62.9 1.2 collective-permute-done.2
  64.5 91.2 %collective-permute-done.3 = f32[2,2,2,64,192]{4,3,2,1,0:T(8,128)S(1)} collective-permute-done((f32[2,2,2,64,192]{4,3,2,1,0:T(8,128)S(1)}, f32[2,2,2,64,192]{4,3,2,1,0:T(8,128)S(1)}, u32[]{:S(2)}, u32[]{:S(2)}) %collective-permute-start.3) | collective-permute-done | bytes 393248 | tf_op jit(solution)/shard_map/ppermute | solution.py:471
  156.1 0.5 copy-done.6
  156.7 30.2 %all-to-all-done.x = f32[16,192,640]{2,1,0:T(8,128)} async-done(((f32[16,192,640]{2,1,0:T(8,128)}), f32[16,192,640]{2,1,0:T(8,128)}, u32[]{:S(2)}, u32[]{:S(2)}) %all-to-all-start) | async-done | bytes 7864352 | tf_op jit(solution)/shard_map/all_to_all | solution.py:49
  186.9 13.3 %project.1 = (f32[16,64,640]{2,1,0:T(8,128)S(1)}, f32[16,64,640]{2,1,0:T(8,128)}, f32[1,64,128]{2,1,0:T(8,128)S(1)}, f32[1,64,128]{2,1,0:T(8,128)S(1)}) custom-call(f32[16,192,640]{2,1,0:T(8,128)} %all-to-all-done.x, f32[16,64,192]{2,1,0:T(8,128)S(1)} %bitcast_multiply_fusion.rot), custom_call_target="tpu_custom_call" | custom-call | tf_op jit(solution)/shard_map/project/pallas_call | solution.py:317
  200.3 1.5 copy-done
  201.7 3.5 %collective-permute-start.4 = (f32[1,64,128]{2,1,0:T(8,128)S(1)}, f32[1,64,128]{2,1,0:T(8,128)S(1)}, u32[]{:S(2)}, u32[]{:S(2)}) collective-permute-start(f32[1,64,128]{2,1,0:T(8,128)S(1)} %get-tuple-element.21), channel_id=1, source_target_pairs={{0,2},{2,4},{4,6},{6,8},{8,10},{10,12},{12,14},{14,16},{16,18},{18... | collective-permute-start | bytes 98312 | tf_op jit(solution)/shard_map/ppermute | solution.py:58
  205.3 1.9 collective-permute-start.5
  207.2 4.2 %collective-permute-done.5.right = f32[1,64,128]{2,1,0:T(8,128)S(1)} collective-permute-done((f32[1,64,128]{2,1,0:T(8,128)S(1)}, f32[1,64,128]{2,1,0:T(8,128)S(1)}, u32[]{:S(2)}, u32[]{:S(2)}) %collective-permute-start.5) | collective-permute-done | bytes 32800 | tf_op jit(solution)/shard_map/ppermute | solution.py:58
  211.4 4.1 %all-to-all-start.1 = ((f32[16,64,640]{2,1,0:T(8,128)}), f32[16,64,640]{2,1,0:T(8,128)S(1)}, u32[]{:S(2)}, u32[]{:S(2)}) async-start(f32[16,64,640]{2,1,0:T(8,128)} %get-tuple-element.23), calls=%async_computation.1 | async-start | bytes 5242880 | tf_op jit(solution)/shard_map/all_to_all | solution.py:49
  215.8 1.3 collective-permute-start.6
  217.2 0.8 dynamic_slice.14
  218.0 2.6 collective-permute-done.6
  220.8 0.8 add_add_fusion
  221.7 1.7 copy-done.1
  223.4 10.5 %stiffness.1 = (f32[16,64,640]{2,1,0:T(8,128)S(1)}, f32[2,1024]{1,0:T(2,128)S(1)}) custom-call(f32[16,64,640]{2,1,0:T(8,128)S(1)} %copy-done.1, f32[1,64,128]{2,1,0:T(8,128)S(1)} %collective-permute-done.4.left, f32[1,64,128]{2,1,0:T(8,128)S(1)} %collective-permute-done.5.right, f32[18,640]{1,0:T(8,128)S(1)} %concatenate.8.band, f32[16]{0:T(128)S(1)} %fusion.6.lam), custom_call_target="tpu_custom_call" | custom-call | tf_op jit(solution)/shard_map/stiffness/pallas_call | solution.py:395
  233.9 2.5 collective-permute-done.7
  236.5 2.3 collective-permute-start.8
  238.8 0.8 collective-permute-done.8
  239.9 3.4 collective-permute-done.9
  243.3 16.8 %collective-permute-done.10 = f32[2,1024]{1,0:T(2,128)S(1)} collective-permute-done((f32[2,1024]{1,0:T(2,128)S(1)}, f32[2,1024]{1,0:T(2,128)S(1)}, u32[]{:S(2)}, u32[]{:S(2)}) %collective-permute-start.10) | collective-permute-done | bytes 8224 | tf_op jit(solution)/shard_map/ppermute | solution.py:524
  260.4 11.9 %collective-permute-done.11 = f32[2,1024]{1,0:T(2,128)S(1)} collective-permute-done((f32[2,1024]{1,0:T(2,128)S(1)}, f32[2,1024]{1,0:T(2,128)S(1)}, u32[]{:S(2)}, u32[]{:S(2)}) %collective-permute-start.11) | collective-permute-done | bytes 8224 | tf_op jit(solution)/shard_map/ppermute | solution.py:524
  272.3 4.2 %residual_back.1 = (f32[16,64,640]{2,1,0:T(8,128)}, f32[1,1024]{1,0:T(1,128)S(1)}) custom-call(f32[16,64,640]{2,1,0:T(8,128)S(1)} %copy-done.1, f32[16,64,640]{2,1,0:T(8,128)S(1)} %get-tuple-element.27.kx, f32[2,1024]{1,0:T(2,128)S(1)} %add.87.total), custom_call_target="tpu_custom_call" | custom-call | tf_op jit(solution)/shard_map/residual_back/pallas_call | solution.py:448
  276.5 8.2 %all-to-all-start.2 = ((f32[16,64,640]{2,1,0:T(8,128)}), f32[16,64,640]{2,1,0:T(8,128)}, u32[]{:S(2)}, u32[]{:S(2)}) async-start(f32[16,64,640]{2,1,0:T(8,128)} %get-tuple-element.29), calls=%async_computation.2 | async-start | bytes 5242880 | tf_op jit(solution)/shard_map/all_to_all | solution.py:49
  284.7 0.6 constant_dynamic-slice_fusion
  285.3 58.2 %all-to-all-done.2.refs_1_ = f32[16,64,640]{2,1,0:T(8,128)} async-done(((f32[16,64,640]{2,1,0:T(8,128)}), f32[16,64,640]{2,1,0:T(8,128)}, u32[]{:S(2)}, u32[]{:S(2)}) %all-to-all-start.2) | async-done | bytes 2621472 | tf_op jit(solution)/shard_map/all_to_all | solution.py:49
  343.5 3.8 %collect_blocks.1 = (f32[1,64,10240]{2,1,0:T(8,128)}, f32[1,64,10240]{2,1,0:T(8,128)}) custom-call(f32[16,64,640]{2,1,0:T(8,128)S(1)} %all-to-all-done.1.refs_0_, f32[16,64,640]{2,1,0:T(8,128)} %all-to-all-done.2.refs_1_), custom_call_target="tpu_custom_call" | custom-call | tf_op jit(solution)/shard_map/collect_blocks/pallas_call | solution.py:213
  (48 shorter events, 2.5 us)
Async XLA Ops:
  0.6 9.5 %collective-permute-start = (f32[64,192]{1,0:T(8,128)}, f32[64,192]{1,0:T(8,128)S(1)}, u32[]{:S(2)}, u32[]{:S(2)}) collective-permute-start(f32[64,192]{1,0:T(8,128)} %bitcast.25), channel_id=1, source_target_pairs={{0,16},{2,18},{4,20},{6,22},{8,24},{10,26},{12,28},{14,30},{16,0},... | collective-permute-start | bytes 147464 | tf_op jit(solution)/shard_map/ppermute | solution.py:471
  3.0 7.2 %copy-start.2 = (f32[1,192,64]{1,2,0:T(8,128)S(1)}, f32[1,192,64]{1,2,0:T(8,128)}, u32[]{:S(2)}) copy-start(f32[1,192,64]{1,2,0:T(8,128)} %param.18) | copy-start | bytes 147460
  10.2 176.7 %all-to-all-start = ((f32[16,192,640]{2,1,0:T(8,128)}), f32[16,192,640]{2,1,0:T(8,128)}, u32[]{:S(2)}, u32[]{:S(2)}) async-start(f32[16,192,640]{2,1,0:T(8,128)} %spread_blocks.1), calls=%async_computation | async-start | bytes 15728640 | tf_op jit(solution)/shard_map/all_to_all | solution.py:49
  15.8 46.1 %collective-permute-start.1 = (f32[2,64,192]{2,1,0:T(8,128)S(1)}, f32[2,64,192]{2,1,0:T(8,128)S(1)}, u32[]{:S(2)}, u32[]{:S(2)}) collective-permute-start(f32[2,64,192]{2,1,0:T(8,128)S(1)} %pad_maximum_fusion.2), channel_id=1, source_target_pairs={{0,4},{2,6},{4,0},{6,2},{8,12},{10,14},{12,8},{14,10},{16,20},{18,... | collective-permute-start | bytes 294920 | tf_op jit(solution)/shard_map/ppermute | solution.py:471
  61.9 2.2 collective-permute-start.2
  64.2 91.6 %collective-permute-start.3 = (f32[2,2,2,64,192]{4,3,2,1,0:T(8,128)S(1)}, f32[2,2,2,64,192]{4,3,2,1,0:T(8,128)S(1)}, u32[]{:S(2)}, u32[]{:S(2)}) collective-permute-start(f32[2,2,2,64,192]{4,3,2,1,0:T(8,128)S(1)} %pad_maximum_fusion), channel_id=1, source_target_pairs={{0,8},{2,10},{4,12},{6,14},{8,0},{10,2},{12,4},{14,6},{16,24},{18,... | collective-permute-start | bytes 1179656 | tf_op jit(solution)/shard_map/ppermute | solution.py:471
  155.9 0.7 copy-start.6
  200.3 1.5 copy-start
  201.7 5.4 %collective-permute-start.4 = (f32[1,64,128]{2,1,0:T(8,128)S(1)}, f32[1,64,128]{2,1,0:T(8,128)S(1)}, u32[]{:S(2)}, u32[]{:S(2)}) collective-permute-start(f32[1,64,128]{2,1,0:T(8,128)S(1)} %get-tuple-element.21), channel_id=1, source_target_pairs={{0,2},{2,4},{4,6},{6,8},{8,10},{10,12},{12,14},{14,16},{16,18},{18... | collective-permute-start | bytes 98312 | tf_op jit(solution)/shard_map/ppermute | solution.py:58
  205.3 6.1 %collective-permute-start.5 = (f32[1,64,128]{2,1,0:T(8,128)S(1)}, f32[1,64,128]{2,1,0:T(8,128)S(1)}, u32[]{:S(2)}, u32[]{:S(2)}) collective-permute-start(f32[1,64,128]{2,1,0:T(8,128)S(1)} %get-tuple-element.22), channel_id=1, source_target_pairs={{2,0},{4,2},{6,4},{8,6},{10,8},{12,10},{14,12},{16,14},{18,16},{20... | collective-permute-start | bytes 98312 | tf_op jit(solution)/shard_map/ppermute | solution.py:58
  211.4 4.2 %copy-start.3 = (f32[10240]{0:T(1024)S(1)}, f32[10240]{0:T(1024)}, u32[]{:S(2)}) copy-start(f32[10240]{0:T(1024)} %param.14) | copy-start | bytes 122884
  211.4 4.2 %copy-start.4 = (f32[10240]{0:T(1024)S(1)}, f32[10240]{0:T(1024)}, u32[]{:S(2)}) copy-start(f32[10240]{0:T(1024)} %param.15) | copy-start | bytes 122884
  211.4 4.2 %copy-start.5 = (s32[10240]{0:T(1024)S(1)}, s32[10240]{0:T(1024)}, u32[]{:S(2)}) copy-start(s32[10240]{0:T(1024)} %param.16) | copy-start | bytes 122884
  211.4 65.1 %all-to-all-start.1 = ((f32[16,64,640]{2,1,0:T(8,128)}), f32[16,64,640]{2,1,0:T(8,128)S(1)}, u32[]{:S(2)}, u32[]{:S(2)}) async-start(f32[16,64,640]{2,1,0:T(8,128)} %get-tuple-element.23), calls=%async_computation.1 | async-start | bytes 5242880 | tf_op jit(solution)/shard_map/all_to_all | solution.py:49
  215.8 4.7 %collective-permute-start.6 = (f32[8,8]{1,0:T(8,128)S(1)}, f32[8,8]{1,0:T(8,128)S(1)}, u32[]{:S(2)}, u32[]{:S(2)}) collective-permute-start(f32[8,8]{1,0:T(8,128)S(1)} %slice.40), channel_id=1, source_target_pairs={{0,1},{2,3},{4,5},{6,7},{8,9},{10,11},{12,13},{14,15},{16,17},{18,... | collective-permute-start | bytes 776 | tf_op jit(solution)/shard_map/ppermute | solution.py:72
  221.7 1.7 copy-start.1
  233.9 2.5 collective-permute-start.7
  236.5 3.1 collective-permute-start.8
  239.6 3.7 %collective-permute-start.9 = (f32[2,1024]{1,0:T(2,128)S(1)}, f32[2,1024]{1,0:T(2,128)S(1)}, u32[]{:S(2)}, u32[]{:S(2)}) collective-permute-start(f32[2,1024]{1,0:T(2,128)S(1)} %add.84), channel_id=1, source_target_pairs={{0,4},{2,6},{4,0},{6,2},{8,12},{10,14},{12,8},{14,10},{16,20},{18,... | collective-permute-start | bytes 24584 | tf_op jit(solution)/shard_map/ppermute | solution.py:524
  243.3 16.8 %collective-permute-start.10 = (f32[2,1024]{1,0:T(2,128)S(1)}, f32[2,1024]{1,0:T(2,128)S(1)}, u32[]{:S(2)}, u32[]{:S(2)}) collective-permute-start(f32[2,1024]{1,0:T(2,128)S(1)} %add.85), channel_id=1, source_target_pairs={{0,8},{2,10},{4,12},{6,14},{8,0},{10,2},{12,4},{14,6},{16,24},{18,... | collective-permute-start | bytes 24584 | tf_op jit(solution)/shard_map/ppermute | solution.py:524
  260.1 12.2 %collective-permute-start.11 = (f32[2,1024]{1,0:T(2,128)S(1)}, f32[2,1024]{1,0:T(2,128)S(1)}, u32[]{:S(2)}, u32[]{:S(2)}) collective-permute-start(f32[2,1024]{1,0:T(2,128)S(1)} %add.86), channel_id=1, source_target_pairs={{0,16},{2,18},{4,20},{6,22},{8,24},{10,26},{12,28},{14,30},{16,0},... | collective-permute-start | bytes 24584 | tf_op jit(solution)/shard_map/ppermute | solution.py:524
  276.5 67.0 %all-to-all-start.2 = ((f32[16,64,640]{2,1,0:T(8,128)}), f32[16,64,640]{2,1,0:T(8,128)}, u32[]{:S(2)}, u32[]{:S(2)}) async-start(f32[16,64,640]{2,1,0:T(8,128)} %get-tuple-element.29), calls=%async_computation.2 | async-start | bytes 5242880 | tf_op jit(solution)/shard_map/all_to_all | solution.py:49

commit v7 on v6

--- a/solution.py
+++ b/solution.py
@@ -56,6 +56,15 @@
     if step < 0:
         pairs = [(b, a) for a, b in pairs]
     return lax.ppermute(cells, ("span", "elem"), pairs)
+
+
+def exchange_half(pieces):
+    count = lax.axis_size("span")
+    half = count // 2
+    groups = [list(range(half)), list(range(half, count))]
+    return lax.all_to_all(
+        pieces, "span", split_axis=0, concat_axis=0, tiled=True, axis_index_groups=groups
+    )
 
 
 def coefficients(ground, tension, stiff, offset, link, count, dofs):
@@ -90,13 +99,21 @@
     return value * factor
 
 
+def plus(a, b):
+    return a if b is None else a + b
+
+
+def minus(a, b):
+    return a if b is None else a - b
+
+
 def cosine_sums(a):
     n = len(a) - 1
     if n == 1:
-        return [a[0] + a[1], a[0] - a[1]]
+        return [plus(a[0], a[1]), minus(a[0], a[1])]
     half = n // 2
-    even = cosine_sums([a[s] + a[n - s] for s in range(half)] + [a[half]])
-    diff = [a[s] - a[n - s] for s in range(half)]
+    even = cosine_sums([plus(a[s], a[n - s]) for s in range(half)] + [a[half]])
+    diff = [minus(a[s], a[n - s]) for s in range(half)]
     out = [None] * (n + 1)
     out[0::2] = even
     for j in range(1, n, 2):
@@ -128,11 +145,12 @@
 
 
 def to_slots(x):
-    n = len(x)
-    half = n // 2
-    plus = [x[0]] + [x[s] + x[n - s] for s in range(1, half)] + [x[half]]
-    minus = [x[s] - x[n - s] for s in range(1, half)]
-    return cosine_sums(plus) + sine_sums(minus)
+    return cosine_sums(list(x) + [None]) + sine_sums(x[1:])
+
+
+def half_signs(count):
+    half = count // 2
+    return [-1.0 if (j if j <= half else j - half) % 2 else 1.0 for j in range(count)]
 
 
 def to_spans(y):
@@ -152,52 +170,53 @@
     return pltpu.CompilerParams(vmem_limit_bytes=VMEM_LIMIT, **kw)
 
 
-def spread_blocks(blocks, count):
-    _, rows, dof_dev = blocks[0].shape
-    dofs = dof_dev // count
+def spread_blocks(blocks, bases, dofs, many, cuts):
+    rows = blocks[0].shape[1]
     kinds = len(blocks)
-    cuts = 2 if rows % (2 * ROWS) == 0 else 1
-    strip = rows // cuts
-
-    def kernel(*refs):
-        out, held, come, go = refs[kinds:]
+
+    def kernel(base, *refs):
+        outs = refs[kinds : kinds + len(cuts)]
+        held = refs[kinds + len(cuts) : kinds + 2 * len(cuts)]
+        come, go = refs[-2:]
         arrivals = []
-        for c in range(cuts):
-            for k in range(kinds):
-                at = slice(c * strip, (c + 1) * strip)
-                copy = pltpu.make_async_copy(
-                    refs[k].at[0, at, :], held.at[k, at, :], come.at[c * kinds + k]
-                )
-                copy.start()
-                arrivals.append((c, k, copy))
+        for c, (which, first, width) in enumerate(cuts):
+            for q in range(many):
+                group = []
+                for k in range(kinds):
+                    start = pl.multiple_of(base[which] + (q * dofs + first), LANES)
+                    copy = pltpu.make_async_copy(
+                        refs[k].at[0, :, pl.ds(start, width)],
+                        held[c].at[q, k * rows : (k + 1) * rows, :],
+                        come.at[(c * many + q) * kinds + k],
+                    )
+                    copy.start()
+                    group.append(copy)
+                arrivals.append((c, q, group))
         leaving = []
-        for c, k, copy in arrivals:
-            copy.wait()
-            for i in range(count):
-                piece = pltpu.make_async_copy(
-                    held.at[k, c * strip : (c + 1) * strip, i * dofs : (i + 1) * dofs],
-                    out.at[i, k * rows + c * strip : k * rows + (c + 1) * strip, :],
-                    go.at[(c * kinds + k) * count + i],
-                )
-                piece.start()
-                leaving.append(piece)
+        for c, q, group in arrivals:
+            for copy in group:
+                copy.wait()
+            piece = pltpu.make_async_copy(held[c].at[q], outs[c].at[q], go.at[c * many + q])
+            piece.start()
+            leaving.append(piece)
         for piece in leaving:
             piece.wait()
 
     whole = pl.BlockSpec(memory_space=pltpu.HBM)
+    shapes = [(many, kinds * rows, width) for _, _, width in cuts]
     return pl.pallas_call(
         kernel,
-        in_specs=[whole] * kinds,
-        out_specs=whole,
-        out_shape=pltpu.HBM((count, kinds * rows, dofs), jnp.float32),
-        scratch_shapes=[
-            pltpu.VMEM((kinds, rows, dof_dev), jnp.float32),
-            pltpu.SemaphoreType.DMA((cuts * kinds,)),
-            pltpu.SemaphoreType.DMA((cuts * kinds * count,)),
+        in_specs=[pl.BlockSpec(memory_space=pltpu.SMEM)] + [whole] * kinds,
+        out_specs=[whole] * len(cuts),
+        out_shape=[pltpu.HBM(shape, jnp.float32) for shape in shapes],
+        scratch_shapes=[pltpu.VMEM(shape, jnp.float32) for shape in shapes]
+        + [
+            pltpu.SemaphoreType.DMA((len(cuts) * many * kinds,)),
+            pltpu.SemaphoreType.DMA((len(cuts) * many,)),
         ],
         compiler_params=pltpu.CompilerParams(vmem_limit_bytes=60 * 1024 * 1024),
         name="spread_blocks",
-    )(*blocks)
+    )(bases, *blocks)
 
 
 def collect_blocks(pieces):
@@ -234,19 +253,12 @@
 
 
 def project(stacked, rotation):
-    count, wide, dofs = stacked.shape
-    rows = rotation.shape[1]
-    tiles = dofs // LANES
-    scales = slot_scales(count)
-    groups = -(-count * REACH // LANES)
-    per = LANES // REACH
-
+    spans, wide, dofs = stacked.shape
+    count, rows = rotation.shape[:2]
     strip = 2 * ROWS
 
-    def kernel(x, rot, proj, back, head, tail, split_rot, *split_slots):
-        tile = pl.program_id(0)
-
-        @pl.when(tile == 0)
+    def kernel(x, rot, proj, split_rot, *split_slots):
+        @pl.when(pl.program_id(0) == 0)
         def _():
             def one(j, carry):
                 for i, part in enumerate(bf16_parts(rot[j])):
@@ -260,7 +272,7 @@
             halves = []
             for h in range(2):
                 own = pl.ds(pl.multiple_of(r * strip + h * ROWS, ROWS), ROWS)
-                halves.append(to_slots([x[s, own, :] for s in range(count)]))
+                halves.append(to_slots([x[s, own, :] for s in range(spans)]))
             for j in range(count):
                 value = jnp.concatenate([half[j] for half in halves], 0)
                 for part, ref in zip(bf16_parts(value), split_slots):
@@ -282,14 +294,57 @@
                     total = term if total is None else total + term
             proj[j] = total
 
-        def inverse(r, carry):
-            at = pl.ds(pl.multiple_of(r * ROWS, ROWS), ROWS)
-            out = to_spans([proj[j, at, :] * scales[j] for j in range(count)])
-            for s in range(count):
-                back[s, at, :] = out[s]
-            return carry
-
-        lax.fori_loop(0, rows // ROWS, inverse, 0)
+    return pl.pallas_call(
+        kernel,
+        grid=(dofs // LANES,),
+        in_specs=[
+            pl.BlockSpec((spans, wide, LANES), lambda t: (0, 0, t)),
+            pl.BlockSpec((count, rows, wide), lambda t: (0, 0, 0)),
+        ],
+        out_specs=pl.BlockSpec((count, rows, LANES), lambda t: (0, 0, t)),
+        out_shape=pltpu.HBM((count, rows, dofs), jnp.float32),
+        scratch_shapes=[pltpu.VMEM((count, PARTS * rows, wide), jnp.bfloat16)]
+        + [pltpu.VMEM((count, wide, LANES), jnp.bfloat16)] * PARTS,
+        compiler_params=params(),
+        name="project",
+    )(stacked, rotation)
+
+
+def combine(own, others):
+    count, rows, dofs = own.shape
+    tiles = dofs // LANES
+    scales = slot_scales(count)
+    groups = -(-count * REACH // LANES)
+    per = LANES // REACH
+    sizes = [other.shape[2] // LANES for other in others]
+    firsts = [sum(sizes[:c]) for c in range(len(sizes))]
+
+    def kernel(*refs):
+        x, parts = refs[0], refs[1 : 1 + len(others)]
+        proj, back, head, tail = refs[1 + len(others) :]
+        tile = pl.program_id(0)
+
+        def strip_of(part):
+            def strip(r, carry):
+                at = pl.ds(pl.multiple_of(r * ROWS, ROWS), ROWS)
+                terms = []
+                for j in range(count):
+                    value = x[j, at, :] + part[j, at, :]
+                    proj[j, at, :] = value
+                    terms.append(value * scales[j])
+                out = to_spans(terms)
+                for s in range(count):
+                    back[s, at, :] = out[s]
+                return carry
+
+            return strip
+
+        for first, size, part in zip(firsts, sizes, parts):
+
+            @pl.when((tile >= first) & (tile < first + size))
+            def _(part=part):
+                lax.fori_loop(0, rows // ROWS, strip_of(part), 0)
+
         lane = lax.broadcasted_iota(jnp.int32, (rows, LANES), 1)
 
         def pack(ref, start):
@@ -310,24 +365,28 @@
         def _():
             pack(tail, LANES - REACH)
 
-    cell = pl.BlockSpec((count, rows, LANES), lambda t: (0, 0, t))
+    def cell(first, size):
+        return pl.BlockSpec(
+            (count, rows, LANES), lambda t: (0, 0, jnp.clip(t - first, 0, size - 1))
+        )
+
+    plain = pl.BlockSpec((count, rows, LANES), lambda t: (0, 0, t))
     edge = pl.BlockSpec((groups, rows, LANES), lambda t: (0, 0, 0))
-    field = pltpu.HBM((count, rows, dofs), jnp.float32)
     edges = jax.ShapeDtypeStruct((groups, rows, LANES), jnp.float32)
     return pl.pallas_call(
         kernel,
         grid=(tiles,),
-        in_specs=[
-            pl.BlockSpec((count, wide, LANES), lambda t: (0, 0, t)),
-            pl.BlockSpec((count, rows, wide), lambda t: (0, 0, 0)),
+        in_specs=[plain] + [cell(f, z) for f, z in zip(firsts, sizes)],
+        out_specs=[plain, plain, edge, edge],
+        out_shape=[
+            jax.ShapeDtypeStruct((count, rows, dofs), jnp.float32),
+            pltpu.HBM((count, rows, dofs), jnp.float32),
+            edges,
+            edges,
         ],
-        out_specs=[cell, cell, edge, edge],
-        out_shape=[jax.ShapeDtypeStruct(field.shape, jnp.float32), field, edges, edges],
-        scratch_shapes=[pltpu.VMEM((count, PARTS * rows, wide), jnp.bfloat16)]
-        + [pltpu.VMEM((count, wide, LANES), jnp.bfloat16)] * PARTS,
         compiler_params=params(),
-        name="project",
-    )(stacked, rotation)
+        name="combine",
+    )(own, *others)
 
 
 def stiffness(projected, before, after, bands, links):
@@ -495,15 +554,40 @@
     dofs = current_block.shape[2] // count
     rows = current_block.shape[1]
     steps = list(halvings("span"))
-    rotation = exchange_step(ritz_rotation[0].T, *steps[0])
-    pieces = spread_blocks((current_block, search_block, previous_block), count)
+    half = count // 2
+    me = lax.axis_index("span")
+    upper = me >= half
+    blocks = (current_block, search_block, previous_block)
+    bases = jnp.stack([jnp.where(upper, 0, half * dofs), jnp.where(upper, half * dofs, 0)])
+    tiles = dofs // LANES
+    first = tiles * 2 // 5 * LANES
+    chunks = [(0, 0, first), (0, first, dofs - first)] if first else [(0, 0, dofs)]
+    rotation = ritz_rotation[0].T
+    for step, pairs in steps[:2]:
+        rotation = exchange_step(rotation, step, pairs)
+    (pieces,) = spread_blocks(blocks, bases, dofs, half, chunks[:1])
     pieces, rotation = lax.optimization_barrier((pieces, rotation))
-    stacked = exchange(pieces)
-    order = steps[2:] + steps[1:2]
-    for step, pairs in order:
+    arrived = [exchange_half(pieces)]
+    for step, pairs in steps[2:]:
         rotation = exchange_step(rotation, step, pairs)
-    rotation = in_order(rotation, [steps[0]] + order)
-    scales = jnp.array(slot_scales(count), jnp.float32)[:, None, None]
+    rotation = in_order(rotation, steps)
+    signs = [scale * sign for scale, sign in zip(slot_scales(count), half_signs(count))]
+    scales = jnp.where(
+        upper, jnp.array(signs, jnp.float32), jnp.array(slot_scales(count), jnp.float32)
+    )
+    rotation = rotation * scales[:, None, None]
+    rest = spread_blocks(blocks, bases, dofs, half, chunks[1:] + [(1, 0, dofs)])
+    swap = [(i, (i + half) % count) for i in range(count)]
+    others = []
+    for pieces in rest:
+        part = project(arrived[-1], rotation)
+        if others:
+            part, others[-1] = lax.optimization_barrier((part, others[-1]))
+        others.append(lax.ppermute(part, "span", swap))
+        pieces, _ = lax.optimization_barrier((pieces, arrived[-1]))
+        arrived.append(exchange_half(pieces))
+    own = project(arrived[-1], rotation)
+    projected, spans, head, tail = combine(own, others)
     weights, ground, link = coefficients(
         ground_spring, wire_tension, dropper_stiff, dropper_offset, span_link, count, dofs
     )
@@ -513,7 +597,6 @@
     diagonal = ground + jnp.sum(up, 0) + jnp.sum(down, 0)
     bands = jnp.concatenate([up, down, diagonal[None], link[None]])
     links = 2.0 * (1.0 - fourier_rows(count)[1])
-    projected, spans, head, tail = project(stacked, rotation * scales)
     before, after = to_next(tail, 1), to_next(head, -1)
     spans, before, after = lax.optimization_barrier((spans, before, after))
     block_pieces = exchange(spans)
@@ -574,7 +657,7 @@
 def by_shape(*args):
     count, dof_dev = lax.axis_size("span"), args[0].shape[2]
     halves = count & (count - 1) == 0 and lax.axis_size("elem") in (1, 2, 4, 8, 16)
-    if halves and count > 1 and dof_dev % (count * LANES) == 0:
+    if halves and count > 2 and dof_dev % (count * LANES) == 0:
         return tiled_device(*args)
     return on_device(*args)
 

time: 350 us -> 414 us (1.18)
  blocking collectives: 0 us -> 32.5 us
  starting transfers between devices: 31.5 us -> 49.1 us
  Pallas kernels: 39 us -> 54.1 us
  waiting for transfers between devices: 269 us -> 259 us
  local copies, waits for them, and re-layouts: 5.3 us -> 9.93 us
    ppermute x0 -> x2, waiting for transfers between devices: none -> 93.2 us  [tiled_device(): others.append(lax.ppermute(part, 'span', swap))]
    ppermute x4, waiting for transfers between devices: 138 us -> 53.8 us  [exchange_step(): other = lax.ppermute(held, 'span', pairs)]
    all_to_all x0 -> x1, blocking collectives: none -> 32.5 us  [exchange_half(): lax.all_to_all(pieces, 'span', split_axis=0, concat_axis=0, tiled=True, a...]
    all_to_all x3 -> x2, waiting for transfers between devices: 88.4 us -> 58.2 us  [exchange(): lax.all_to_all(pieces, 'span', split_axis=0, concat_axis=0, tiled=True)]
    pallas_call x2 -> x6, Pallas kernels: 20.5 us -> 35.5 us  [the longest x3 22.2 us: project(): pl.pallas_call(kernel, grid=(dofs // LANES,), in_specs=[pl.BlockSpec((spa...]
    all_to_all x0 -> x2, starting transfers between devices: none -> 13.3 us  [exchange_half(): lax.all_to_all(pieces, 'span', split_axis=0, concat_axis=0, tiled=True, a...]
    all_to_all x0 -> x2, waiting for transfers between devices: none -> 11.7 us  [exchange_half(): lax.all_to_all(pieces, 'span', split_axis=0, concat_axis=0, tiled=True, a...]
    ppermute x0 -> x2, starting transfers between devices: none -> 5.25 us  [tiled_device(): others.append(lax.ppermute(part, 'span', swap))]
  transfers between devices with their start and end apart: 15 -> 18, of which waited for: 12 -> 15; matrix products, arithmetic and copies ran while one was open for 1% -> 1% of each run, Pallas kernels for 6% -> 11%
where the time goes in v7:
time: 414 us; the launch traced here: 410 us
  waiting for transfers between devices  259 us (63%)
  Pallas kernels  54.1 us (13%)
  starting transfers between devices  49.1 us (12%)
  blocking collectives  32.5 us (8%)
  local copies, waits for them, and re-layouts  9.93 us (2%)
    ppermute x2, waiting for transfers between devices, tiled_device(): others.append(lax.ppermute(part, 'span', swap))  93.2 us
    all_to_all x2, waiting for transfers between devices, exchange(): lax.all_to_all(pieces, 'span', split_axis=0, concat_axis=0, tiled=True)  58.2 us
    ppermute x4, waiting for transfers between devices, exchange_step(): other = lax.ppermute(held, 'span', pairs)  53.8 us
    all_to_all x1, blocking collectives, exchange_half(): lax.all_to_all(pieces, 'span', split_axis=0, concat_axis=0, tiled=True, a...  32.5 us
    ppermute x4, waiting for transfers between devices, tiled_device(): sums = sums + lax.ppermute(sums, 'span', pairs)  31.9 us
    pallas_call x3, Pallas kernels, project(): pl.pallas_call(kernel, grid=(dofs // LANES,), in_specs=[pl.BlockSpec((spa...  22.2 us
    all_to_all x2, starting transfers between devices, exchange(): lax.all_to_all(pieces, 'span', split_axis=0, concat_axis=0, tiled=True)  16.4 us
    all_to_all x2, starting transfers between devices, exchange_half(): lax.all_to_all(pieces, 'span', split_axis=0, concat_axis=0, tiled=True, a...  13.3 us
  transfers between devices with their start and end apart: 18, of which 15 were waited for; matrix products, arithmetic and copies ran while one was open for 1% of the time, Pallas kernels for 11%

profile of v7, /device:TPU:15, one launch (start us, length us, event | category | flops | bytes accessed | tf_op | source)
XLA Modules:
  0.0 409.7 jit_solution(12749192704980090844)
XLA Ops:
  0.6 2.4 collective-permute-start
  3.0 2.9 collective-permute-done
  7.5 3.0 spread_blocks.3
  10.7 6.8 %all-to-all-start = ((f32[8,192,256]{2,1,0:T(8,128)}), f32[8,192,256]{2,1,0:T(8,128)S(1)}, u32[]{:S(2)}, u32[]{:S(2)}) async-start(f32[8,192,256]{2,1,0:T(8,128)} %spread_blocks.3), calls=%async_computation | async-start | bytes 3145728 | tf_op jit(solution)/shard_map/all_to_all | solution.py:65
  17.6 6.4 %spread_blocks.2 = (f32[8,192,384]{2,1,0:T(8,128)}, f32[8,192,640]{2,1,0:T(8,128)}) custom-call(s32[2]{0:T(128)} %pad_add_fusion.base, f32[1,64,10240]{2,1,0:T(8,128)} %refs_0_.3, f32[1,64,10240]{2,1,0:T(8,128)} %refs_1_.3, f32[1,64,10240]{2,1,0:T(8,128)} %refs_2_.3), custom_call_target="tpu_custom_call" | custom-call | tf_op jit(solution)/shard_map/spread_blocks/pallas_call | solution.py:207
  24.0 11.7 %all-to-all-done.x = f32[8,192,256]{2,1,0:T(8,128)S(1)} async-done(((f32[8,192,256]{2,1,0:T(8,128)}), f32[8,192,256]{2,1,0:T(8,128)S(1)}, u32[]{:S(2)}, u32[]{:S(2)}) %all-to-all-start) | async-done | bytes 1572896 | tf_op jit(solution)/shard_map/all_to_all | solution.py:65
  36.8 32.5 %all_to_all.25.x = f32[8,192,384]{2,1,0:T(8,128)S(1)} all-to-all(f32[8,192,384]{2,1,0:T(8,128)} %get-tuple-element.27), channel_id=1, replica_groups={{0,2,4,6,8,10,12,14},{16,18,20,22,24,26,28,30},{1,3,5,7,9,11,13,15},{17..., dimensions={0} | all-to-all | bytes 4718592 | tf_op jit(solution)/shard_map/all_to_all | solution.py:65
  69.3 6.4 %all-to-all-start.2 = ((f32[8,192,640]{2,1,0:T(8,128)}), f32[8,192,640]{2,1,0:T(8,128)}, u32[]{:S(2)}, u32[]{:S(2)}) async-start(f32[8,192,640]{2,1,0:T(8,128)} %get-tuple-element.28), calls=%async_computation.2 | async-start | bytes 7864320 | tf_op jit(solution)/shard_map/all_to_all | solution.py:65
  76.0 48.9 %collective-permute-done.2 = f32[2,2,64,192]{3,2,1,0:T(8,128)S(1)} collective-permute-done((f32[2,2,64,192]{3,2,1,0:T(8,128)S(1)}, f32[2,2,64,192]{3,2,1,0:T(8,128)S(1)}, u32[]{:S(2)}, u32[]{:S(2)}) %collective-permute-start.2) | collective-permute-done | bytes 196640 | tf_op jit(solution)/shard_map/ppermute | solution.py:530
  129.9 4.7 %project.5 = f32[16,64,256]{2,1,0:T(8,128)} custom-call(f32[8,192,256]{2,1,0:T(8,128)S(1)} %copy-done.4, f32[16,64,192]{2,1,0:T(8,128)S(1)} %bitcast_multiply_fusion.rot), custom_call_target="tpu_custom_call" | custom-call | tf_op jit(solution)/shard_map/project/pallas_call | solution.py:297
  134.6 2.3 collective-permute-start.4
  136.8 6.5 %project.4 = f32[16,64,384]{2,1,0:T(8,128)} custom-call(f32[8,192,384]{2,1,0:T(8,128)S(1)} %all_to_all.25.x, f32[16,64,192]{2,1,0:T(8,128)S(1)} %bitcast_multiply_fusion.rot), custom_call_target="tpu_custom_call" | custom-call | tf_op jit(solution)/shard_map/project/pallas_call | solution.py:297
  143.3 39.0 %collective-permute-done.4.refs_1_ = f32[16,64,256]{2,1,0:T(8,128)S(1)} collective-permute-done((f32[16,64,256]{2,1,0:T(8,128)}, f32[16,64,256]{2,1,0:T(8,128)S(1)}, u32[]{:S(2)}, u32[]{:S(2)}) %collective-permute-start.4) | collective-permute-done | bytes 1048608 | tf_op jit(solution)/shard_map/ppermute | solution.py:586
  183.3 3.0 collective-permute-start.5
  186.3 11.0 %project.3.refs_0_ = f32[16,64,640]{2,1,0:T(8,128)} custom-call(f32[8,192,640]{2,1,0:T(8,128)} %all-to-all-done.2.x, f32[16,64,192]{2,1,0:T(8,128)S(1)} %bitcast_multiply_fusion.rot), custom_call_target="tpu_custom_call" | custom-call | tf_op jit(solution)/shard_map/project/pallas_call | solution.py:297
  197.3 54.2 %collective-permute-done.5.refs_2_ = f32[16,64,384]{2,1,0:T(8,128)S(1)} collective-permute-done((f32[16,64,384]{2,1,0:T(8,128)}, f32[16,64,384]{2,1,0:T(8,128)S(1)}, u32[]{:S(2)}, u32[]{:S(2)}) %collective-permute-start.5) | collective-permute-done | bytes 1572896 | tf_op jit(solution)/shard_map/ppermute | solution.py:586
  253.2 4.0 combine.1
  258.7 4.8 %collective-permute-start.6 = (f32[1,64,128]{2,1,0:T(8,128)S(1)}, f32[1,64,128]{2,1,0:T(8,128)S(1)}, u32[]{:S(2)}, u32[]{:S(2)}) collective-permute-start(f32[1,64,128]{2,1,0:T(8,128)S(1)} %get-tuple-element.33), channel_id=1, source_target_pairs={{0,2},{2,4},{4,6},{6,8},{8,10},{10,12},{12,14},{14,16},{16,18},{18... | collective-permute-start | bytes 98312 | tf_op jit(solution)/shard_map/ppermute | solution.py:58
  263.5 1.9 collective-permute-start.7
  265.5 4.2 %collective-permute-done.7.right = f32[1,64,128]{2,1,0:T(8,128)S(1)} collective-permute-done((f32[1,64,128]{2,1,0:T(8,128)S(1)}, f32[1,64,128]{2,1,0:T(8,128)S(1)}, u32[]{:S(2)}, u32[]{:S(2)}) %collective-permute-start.7) | collective-permute-done | bytes 32800 | tf_op jit(solution)/shard_map/ppermute | solution.py:58
  269.7 8.2 %all-to-all-start.3 = ((f32[16,64,640]{2,1,0:T(8,128)}), f32[16,64,640]{2,1,0:T(8,128)S(1)}, u32[]{:S(2)}, u32[]{:S(2)}) async-start(f32[16,64,640]{2,1,0:T(8,128)} %get-tuple-element.35), calls=%async_computation.3 | async-start | bytes 5242880 | tf_op jit(solution)/shard_map/all_to_all | solution.py:49
  280.4 3.8 collective-permute-done.8
  287.0 10.5 %stiffness.1 = (f32[16,64,640]{2,1,0:T(8,128)S(1)}, f32[2,1024]{1,0:T(2,128)S(1)}) custom-call(f32[16,64,640]{2,1,0:T(8,128)S(1)} %copy-done.1, f32[1,64,128]{2,1,0:T(8,128)S(1)} %collective-permute-done.6.left, f32[1,64,128]{2,1,0:T(8,128)S(1)} %collective-permute-done.7.right, f32[18,640]{1,0:T(8,128)S(1)} %concatenate.8.band, f32[16]{0:T(128)S(1)} %fusion.6.lam), custom_call_target="tpu_custom_call" | custom-call | tf_op jit(solution)/shard_map/stiffness/pallas_call | solution.py:454
  297.6 2.5 collective-permute-done.9
  300.1 2.1 collective-permute-start.10
  303.3 3.4 collective-permute-done.11
  306.7 15.8 %collective-permute-done.12 = f32[2,1024]{1,0:T(2,128)S(1)} collective-permute-done((f32[2,1024]{1,0:T(2,128)S(1)}, f32[2,1024]{1,0:T(2,128)S(1)}, u32[]{:S(2)}, u32[]{:S(2)}) %collective-permute-start.12) | collective-permute-done | bytes 8224 | tf_op jit(solution)/shard_map/ppermute | solution.py:607
  322.9 11.9 %collective-permute-done.13 = f32[2,1024]{1,0:T(2,128)S(1)} collective-permute-done((f32[2,1024]{1,0:T(2,128)S(1)}, f32[2,1024]{1,0:T(2,128)S(1)}, u32[]{:S(2)}, u32[]{:S(2)}) %collective-permute-start.13) | collective-permute-done | bytes 8224 | tf_op jit(solution)/shard_map/ppermute | solution.py:607
  334.8 4.2 %residual_back.1 = (f32[16,64,640]{2,1,0:T(8,128)}, f32[1,1024]{1,0:T(1,128)S(1)}) custom-call(f32[16,64,640]{2,1,0:T(8,128)S(1)} %copy-done.1, f32[16,64,640]{2,1,0:T(8,128)S(1)} %get-tuple-element.39.kx, f32[2,1024]{1,0:T(2,128)S(1)} %add.87.total), custom_call_target="tpu_custom_call" | custom-call | tf_op jit(solution)/shard_map/residual_back/pallas_call | solution.py:507
  338.9 8.2 %all-to-all-start.4 = ((f32[16,64,640]{2,1,0:T(8,128)}), f32[16,64,640]{2,1,0:T(8,128)}, u32[]{:S(2)}, u32[]{:S(2)}) async-start(f32[16,64,640]{2,1,0:T(8,128)} %get-tuple-element.41), calls=%async_computation.4 | async-start | bytes 5242880 | tf_op jit(solution)/shard_map/all_to_all | solution.py:49
  347.7 58.2 %all-to-all-done.4.refs_1_ = f32[16,64,640]{2,1,0:T(8,128)} async-done(((f32[16,64,640]{2,1,0:T(8,128)}), f32[16,64,640]{2,1,0:T(8,128)}, u32[]{:S(2)}, u32[]{:S(2)}) %all-to-all-start.4) | async-done | bytes 2621472 | tf_op jit(solution)/shard_map/all_to_all | solution.py:49
  405.9 3.8 collect_blocks.1
  (71 shorter events, 19.7 us)
Async XLA Ops:
  0.6 5.3 %collective-permute-start = (f32[64,192]{1,0:T(8,128)}, f32[64,192]{1,0:T(8,128)S(1)}, u32[]{:S(2)}, u32[]{:S(2)}) collective-permute-start(f32[64,192]{1,0:T(8,128)} %bitcast.27), channel_id=1, source_target_pairs={{0,16},{2,18},{4,20},{6,22},{8,24},{10,26},{12,28},{14,30},{16,0},... | collective-permute-start | bytes 147464 | tf_op jit(solution)/shard_map/ppermute | solution.py:530
  6.8 3.9 collective-permute-start.1
  10.7 24.9 %all-to-all-start = ((f32[8,192,256]{2,1,0:T(8,128)}), f32[8,192,256]{2,1,0:T(8,128)S(1)}, u32[]{:S(2)}, u32[]{:S(2)}) async-start(f32[8,192,256]{2,1,0:T(8,128)} %spread_blocks.3), calls=%async_computation | async-start | bytes 3145728 | tf_op jit(solution)/shard_map/all_to_all | solution.py:65
  35.7 1.1 copy-start.3
  69.3 57.2 %copy-start.10 = (f32[16]{0:T(128)S(1)}, f32[16]{0:T(128)}, u32[]{:S(2)}) copy-start(f32[16]{0:T(128)} %constant.51.clone) | copy-start | bytes 196
  69.3 57.2 %copy-start.11 = (f32[16]{0:T(128)S(1)}, f32[16]{0:T(128)}, u32[]{:S(2)}) copy-start(f32[16]{0:T(128)} %constant.52.clone) | copy-start | bytes 196
  69.3 117.0 %all-to-all-start.2 = ((f32[8,192,640]{2,1,0:T(8,128)}), f32[8,192,640]{2,1,0:T(8,128)}, u32[]{:S(2)}, u32[]{:S(2)}) async-start(f32[8,192,640]{2,1,0:T(8,128)} %get-tuple-element.28), calls=%async_computation.2 | async-start | bytes 7864320 | tf_op jit(solution)/shard_map/all_to_all | solution.py:65
  75.7 49.2 %collective-permute-start.2 = (f32[2,2,64,192]{3,2,1,0:T(8,128)S(1)}, f32[2,2,64,192]{3,2,1,0:T(8,128)S(1)}, u32[]{:S(2)}, u32[]{:S(2)}) collective-permute-start(f32[2,2,64,192]{3,2,1,0:T(8,128)S(1)} %pad_maximum_fusion.1), channel_id=1, source_target_pairs={{0,4},{2,6},{4,0},{6,2},{8,12},{10,14},{12,8},{14,10},{16,20},{18,... | collective-permute-start | bytes 589832 | tf_op jit(solution)/shard_map/ppermute | solution.py:530
  125.8 2.4 collective-permute-start.3
  128.5 1.4 copy-start.4
  134.6 47.7 %collective-permute-start.4 = (f32[16,64,256]{2,1,0:T(8,128)}, f32[16,64,256]{2,1,0:T(8,128)S(1)}, u32[]{:S(2)}, u32[]{:S(2)}) collective-permute-start(f32[16,64,256]{2,1,0:T(8,128)} %project.5), channel_id=1, source_target_pairs={{0,16},{2,18},{4,20},{6,22},{8,24},{10,26},{12,28},{14,30},{16,0},... | collective-permute-start | bytes 3145736 | tf_op jit(solution)/shard_map/ppermute | solution.py:586
  182.3 1.0 copy-start.5
  183.3 68.2 %collective-permute-start.5 = (f32[16,64,384]{2,1,0:T(8,128)}, f32[16,64,384]{2,1,0:T(8,128)S(1)}, u32[]{:S(2)}, u32[]{:S(2)}) collective-permute-start(f32[16,64,384]{2,1,0:T(8,128)} %project.4), channel_id=1, source_target_pairs={{0,16},{2,18},{4,20},{6,22},{8,24},{10,26},{12,28},{14,30},{16,0},... | collective-permute-start | bytes 4718600 | tf_op jit(solution)/shard_map/ppermute | solution.py:586
  186.3 65.2 %copy-start.6 = (f32[16,64,256]{2,1,0:T(8,128)S(1)}, f32[16,64,256]{2,1,0:T(8,128)}, u32[]{:S(2)}) copy-start(f32[16,64,256]{2,1,0:T(8,128)} %copy-done.5) | copy-start | bytes 3145732
  251.5 1.7 copy-start.2
  257.2 1.5 copy-start
  258.7 6.8 %collective-permute-start.6 = (f32[1,64,128]{2,1,0:T(8,128)S(1)}, f32[1,64,128]{2,1,0:T(8,128)S(1)}, u32[]{:S(2)}, u32[]{:S(2)}) collective-permute-start(f32[1,64,128]{2,1,0:T(8,128)S(1)} %get-tuple-element.33), channel_id=1, source_target_pairs={{0,2},{2,4},{4,6},{6,8},{8,10},{10,12},{12,14},{14,16},{16,18},{18... | collective-permute-start | bytes 98312 | tf_op jit(solution)/shard_map/ppermute | solution.py:58
  263.5 6.1 %collective-permute-start.7 = (f32[1,64,128]{2,1,0:T(8,128)S(1)}, f32[1,64,128]{2,1,0:T(8,128)S(1)}, u32[]{:S(2)}, u32[]{:S(2)}) collective-permute-start(f32[1,64,128]{2,1,0:T(8,128)S(1)} %get-tuple-element.34), channel_id=1, source_target_pairs={{2,0},{4,2},{6,4},{8,6},{10,8},{12,10},{14,12},{16,14},{18,16},{20... | collective-permute-start | bytes 98312 | tf_op jit(solution)/shard_map/ppermute | solution.py:58
  269.7 8.3 %copy-start.7 = (f32[10240]{0:T(1024)S(1)}, f32[10240]{0:T(1024)}, u32[]{:S(2)}) copy-start(f32[10240]{0:T(1024)} %param.15) | copy-start | bytes 122884
  269.7 8.3 %copy-start.8 = (f32[10240]{0:T(1024)S(1)}, f32[10240]{0:T(1024)}, u32[]{:S(2)}) copy-start(f32[10240]{0:T(1024)} %param.16) | copy-start | bytes 122884
  269.7 8.3 %copy-start.9 = (s32[10240]{0:T(1024)S(1)}, s32[10240]{0:T(1024)}, u32[]{:S(2)}) copy-start(s32[10240]{0:T(1024)} %param.17) | copy-start | bytes 122884
  269.7 69.3 %all-to-all-start.3 = ((f32[16,64,640]{2,1,0:T(8,128)}), f32[16,64,640]{2,1,0:T(8,128)S(1)}, u32[]{:S(2)}, u32[]{:S(2)}) async-start(f32[16,64,640]{2,1,0:T(8,128)} %get-tuple-element.35), calls=%async_computation.3 | async-start | bytes 5242880 | tf_op jit(solution)/shard_map/all_to_all | solution.py:49
  278.2 5.9 %collective-permute-start.8 = (f32[8,8]{1,0:T(8,128)S(1)}, f32[8,8]{1,0:T(8,128)S(1)}, u32[]{:S(2)}, u32[]{:S(2)}) collective-permute-start(f32[8,8]{1,0:T(8,128)S(1)} %slice.40), channel_id=1, source_target_pairs={{0,1},{2,3},{4,5},{6,7},{8,9},{10,11},{12,13},{14,15},{16,17},{18,... | collective-permute-start | bytes 776 | tf_op jit(solution)/shard_map/ppermute | solution.py:81
  285.3 1.7 copy-start.1
  297.6 2.5 collective-permute-start.9
  300.1 2.9 collective-permute-start.10
  303.0 3.7 collective-permute-start.11
  306.7 15.8 %collective-permute-start.12 = (f32[2,1024]{1,0:T(2,128)S(1)}, f32[2,1024]{1,0:T(2,128)S(1)}, u32[]{:S(2)}, u32[]{:S(2)}) collective-permute-start(f32[2,1024]{1,0:T(2,128)S(1)} %add.85), channel_id=1, source_target_pairs={{0,8},{2,10},{4,12},{6,14},{8,0},{10,2},{12,4},{14,6},{16,24},{18,... | collective-permute-start | bytes 24584 | tf_op jit(solution)/shard_map/ppermute | solution.py:607
  322.5 12.3 %collective-permute-start.13 = (f32[2,1024]{1,0:T(2,128)S(1)}, f32[2,1024]{1,0:T(2,128)S(1)}, u32[]{:S(2)}, u32[]{:S(2)}) collective-permute-start(f32[2,1024]{1,0:T(2,128)S(1)} %add.86), channel_id=1, source_target_pairs={{0,16},{2,18},{4,20},{6,22},{8,24},{10,26},{12,28},{14,30},{16,0},... | collective-permute-start | bytes 24584 | tf_op jit(solution)/shard_map/ppermute | solution.py:607
  338.9 67.0 %all-to-all-start.4 = ((f32[16,64,640]{2,1,0:T(8,128)}), f32[16,64,640]{2,1,0:T(8,128)}, u32[]{:S(2)}, u32[]{:S(2)}) async-start(f32[16,64,640]{2,1,0:T(8,128)} %get-tuple-element.41), calls=%async_computation.4 | async-start | bytes 5242880 | tf_op jit(solution)/shard_map/all_to_all | solution.py:49

commit v8 on v7

--- a/solution.py
+++ b/solution.py
@@ -583,8 +583,10 @@
         part = project(arrived[-1], rotation)
         if others:
             part, others[-1] = lax.optimization_barrier((part, others[-1]))
+            pieces, arrived[-1] = lax.optimization_barrier((pieces, arrived[-1]))
+        else:
+            pieces, part = lax.optimization_barrier((pieces, part))
         others.append(lax.ppermute(part, "span", swap))
-        pieces, _ = lax.optimization_barrier((pieces, arrived[-1]))
         arrived.append(exchange_half(pieces))
     own = project(arrived[-1], rotation)
     projected, spans, head, tail = combine(own, others)

time: 414 us -> 387 us (0.935)
  waiting for transfers between devices: 259 us -> 243 us
  starting transfers between devices: 49.1 us -> 43.4 us
    ppermute x4, waiting for transfers between devices: 53.8 us -> 26.6 us  [exchange_step(): other = lax.ppermute(held, 'span', pairs)]
    ppermute x2, waiting for transfers between devices: 93.2 us -> 116 us  [tiled_device(): others.append(lax.ppermute(part, 'span', swap))]
    all_to_all x2, waiting for transfers between devices: 11.7 us -> 0.01 us  [exchange_half(): lax.all_to_all(pieces, 'span', split_axis=0, concat_axis=0, tiled=True, a...]
    unnamed x24 -> x22, local copies, waits for them, and re-layouts: 8.33 us -> 6.05 us
  transfers between devices with their start and end apart: 18 -> 18, of which waited for: 15 -> 13; matrix products, arithmetic and copies ran while one was open for 1% -> 1% of each run, Pallas kernels for 11% -> 11%
where the time goes in v8:
time: 387 us; the launch traced here: 383 us
  waiting for transfers between devices  243 us (63%)
  Pallas kernels  54.2 us (14%)
  starting transfers between devices  43.4 us (11%)
  blocking collectives  30.7 us (8%)
  local copies, waits for them, and re-layouts  7.65 us (2%)
    ppermute x2, waiting for transfers between devices, tiled_device(): others.append(lax.ppermute(part, 'span', swap))  116 us
    all_to_all x2, waiting for transfers between devices, exchange(): lax.all_to_all(pieces, 'span', split_axis=0, concat_axis=0, tiled=True)  58.2 us
    ppermute x4, waiting for transfers between devices, tiled_device(): sums = sums + lax.ppermute(sums, 'span', pairs)  31.9 us
    all_to_all x1, blocking collectives, exchange_half(): lax.all_to_all(pieces, 'span', split_axis=0, concat_axis=0, tiled=True, a...  30.7 us
    ppermute x4, waiting for transfers between devices, exchange_step(): other = lax.ppermute(held, 'span', pairs)  26.6 us
    pallas_call x3, Pallas kernels, project(): pl.pallas_call(kernel, grid=(dofs // LANES,), in_specs=[pl.BlockSpec((spa...  22.2 us
    all_to_all x2, starting transfers between devices, exchange(): lax.all_to_all(pieces, 'span', split_axis=0, concat_axis=0, tiled=True)  16.1 us
    all_to_all x2, starting transfers between devices, exchange_half(): lax.all_to_all(pieces, 'span', split_axis=0, concat_axis=0, tiled=True, a...  13.1 us
  transfers between devices with their start and end apart: 18, of which 13 were waited for; matrix products, arithmetic and copies ran while one was open for 1% of the time, Pallas kernels for 11%

profile of v8, /device:TPU:15, one launch (start us, length us, event | category | flops | bytes accessed | tf_op | source)
XLA Modules:
  0.0 383.0 jit_solution(14060800774152891653)
XLA Ops:
  0.6 2.4 collective-permute-start
  3.0 2.9 collective-permute-done
  7.6 3.0 spread_blocks.3
  10.7 6.8 %all-to-all-start = ((f32[8,192,256]{2,1,0:T(8,128)}), f32[8,192,256]{2,1,0:T(8,128)S(1)}, u32[]{:S(2)}, u32[]{:S(2)}) async-start(f32[8,192,256]{2,1,0:T(8,128)} %spread_blocks.3), calls=%async_computation | async-start | bytes 3145728 | tf_op jit(solution)/shard_map/all_to_all | solution.py:65
  17.8 23.6 %collective-permute-done.2 = f32[2,2,64,192]{3,2,1,0:T(8,128)S(1)} collective-permute-done((f32[2,2,64,192]{3,2,1,0:T(8,128)S(1)}, f32[2,2,64,192]{3,2,1,0:T(8,128)S(1)}, u32[]{:S(2)}, u32[]{:S(2)}) %collective-permute-start.2) | collective-permute-done | bytes 196640 | tf_op jit(solution)/shard_map/ppermute | solution.py:530
  42.4 6.4 %spread_blocks.2 = (f32[8,192,384]{2,1,0:T(8,128)}, f32[8,192,640]{2,1,0:T(8,128)}) custom-call(s32[2]{0:T(128)} %pad_add_fusion.base, f32[1,64,10240]{2,1,0:T(8,128)} %refs_0_.3, f32[1,64,10240]{2,1,0:T(8,128)} %refs_1_.3, f32[1,64,10240]{2,1,0:T(8,128)} %refs_2_.3), custom_call_target="tpu_custom_call" | custom-call | tf_op jit(solution)/shard_map/spread_blocks/pallas_call | solution.py:207
  49.2 4.7 %project.3 = f32[16,64,256]{2,1,0:T(8,128)} custom-call(f32[8,192,256]{2,1,0:T(8,128)S(1)} %all-to-all-done.x, f32[16,64,192]{2,1,0:T(8,128)S(1)} %bitcast_multiply_fusion.rot), custom_call_target="tpu_custom_call" | custom-call | tf_op jit(solution)/shard_map/project/pallas_call | solution.py:297
  54.0 30.7 %all_to_all.25.x = f32[8,192,384]{2,1,0:T(8,128)S(1)} all-to-all(f32[8,192,384]{2,1,0:T(8,128)S(1)} %copy-done.5), channel_id=1, replica_groups={{0,2,4,6,8,10,12,14},{16,18,20,22,24,26,28,30},{1,3,5,7,9,11,13,15},{17..., dimensions={0} | all-to-all | bytes 4718592 | tf_op jit(solution)/shard_map/all_to_all | solution.py:65
  84.7 6.3 %all-to-all-start.2 = ((f32[8,192,640]{2,1,0:T(8,128)}), f32[8,192,640]{2,1,0:T(8,128)}, u32[]{:S(2)}, u32[]{:S(2)}) async-start(f32[8,192,640]{2,1,0:T(8,128)} %get-tuple-element.30), calls=%async_computation.2 | async-start | bytes 7864320 | tf_op jit(solution)/shard_map/all_to_all | solution.py:65
  91.0 2.3 collective-permute-start.4
  93.3 6.5 %project.5 = f32[16,64,384]{2,1,0:T(8,128)} custom-call(f32[8,192,384]{2,1,0:T(8,128)S(1)} %all_to_all.25.x, f32[16,64,192]{2,1,0:T(8,128)S(1)} %bitcast_multiply_fusion.rot), custom_call_target="tpu_custom_call" | custom-call | tf_op jit(solution)/shard_map/project/pallas_call | solution.py:297
  99.8 59.1 %collective-permute-done.4.refs_1_ = f32[16,64,256]{2,1,0:T(8,128)S(1)} collective-permute-done((f32[16,64,256]{2,1,0:T(8,128)}, f32[16,64,256]{2,1,0:T(8,128)S(1)}, u32[]{:S(2)}, u32[]{:S(2)}) %collective-permute-start.4) | collective-permute-done | bytes 1048608 | tf_op jit(solution)/shard_map/ppermute | solution.py:589
  159.9 11.0 %project.4.refs_0_ = f32[16,64,640]{2,1,0:T(8,128)} custom-call(f32[8,192,640]{2,1,0:T(8,128)} %all-to-all-done.2.x, f32[16,64,192]{2,1,0:T(8,128)S(1)} %bitcast_multiply_fusion.rot), custom_call_target="tpu_custom_call" | custom-call | tf_op jit(solution)/shard_map/project/pallas_call | solution.py:297
  170.9 57.0 %collective-permute-done.5.refs_2_ = f32[16,64,384]{2,1,0:T(8,128)S(1)} collective-permute-done((f32[16,64,384]{2,1,0:T(8,128)}, f32[16,64,384]{2,1,0:T(8,128)S(1)}, u32[]{:S(2)}, u32[]{:S(2)}) %collective-permute-start.5) | collective-permute-done | bytes 1572896 | tf_op jit(solution)/shard_map/ppermute | solution.py:589
  228.0 1.7 copy-done.2
  229.7 4.0 %combine.1 = (f32[16,64,640]{2,1,0:T(8,128)S(1)}, f32[16,64,640]{2,1,0:T(8,128)}, f32[1,64,128]{2,1,0:T(8,128)S(1)}, f32[1,64,128]{2,1,0:T(8,128)S(1)}) custom-call(f32[16,64,640]{2,1,0:T(8,128)S(1)} %copy-done.2, f32[16,64,256]{2,1,0:T(8,128)S(1)} %copy-done.4, f32[16,64,384]{2,1,0:T(8,128)S(1)} %collective-permute-done.5.refs_2_), custom_call_target="tpu_custom_call" | custom-call | tf_op jit(solution)/shard_map/combine/pallas_call | solution.py:376
  235.2 1.9 collective-permute-start.6
  237.1 2.5 collective-permute-start.7
  239.6 3.6 collective-permute-done.7.right
  243.2 7.9 %all-to-all-start.3 = ((f32[16,64,640]{2,1,0:T(8,128)}), f32[16,64,640]{2,1,0:T(8,128)S(1)}, u32[]{:S(2)}, u32[]{:S(2)}) async-start(f32[16,64,640]{2,1,0:T(8,128)} %get-tuple-element.37), calls=%async_computation.3 | async-start | bytes 5242880 | tf_op jit(solution)/shard_map/all_to_all | solution.py:49
  253.6 3.8 collective-permute-done.8
  258.6 1.7 copy-done.1
  260.3 10.6 %stiffness.1 = (f32[16,64,640]{2,1,0:T(8,128)S(1)}, f32[2,1024]{1,0:T(2,128)S(1)}) custom-call(f32[16,64,640]{2,1,0:T(8,128)S(1)} %copy-done.1, f32[1,64,128]{2,1,0:T(8,128)S(1)} %collective-permute-done.6.left, f32[1,64,128]{2,1,0:T(8,128)S(1)} %collective-permute-done.7.right, f32[18,640]{1,0:T(8,128)S(1)} %concatenate.8.band, f32[16]{0:T(128)S(1)} %fusion.6.lam), custom_call_target="tpu_custom_call" | custom-call | tf_op jit(solution)/shard_map/stiffness/pallas_call | solution.py:454
  270.9 2.5 collective-permute-done.9
  273.4 2.1 collective-permute-start.10
  276.6 3.4 collective-permute-done.11
  280.0 15.7 %collective-permute-done.12 = f32[2,1024]{1,0:T(2,128)S(1)} collective-permute-done((f32[2,1024]{1,0:T(2,128)S(1)}, f32[2,1024]{1,0:T(2,128)S(1)}, u32[]{:S(2)}, u32[]{:S(2)}) %collective-permute-start.12) | collective-permute-done | bytes 8224 | tf_op jit(solution)/shard_map/ppermute | solution.py:609
  296.1 11.9 %collective-permute-done.13 = f32[2,1024]{1,0:T(2,128)S(1)} collective-permute-done((f32[2,1024]{1,0:T(2,128)S(1)}, f32[2,1024]{1,0:T(2,128)S(1)}, u32[]{:S(2)}, u32[]{:S(2)}) %collective-permute-start.13) | collective-permute-done | bytes 8224 | tf_op jit(solution)/shard_map/ppermute | solution.py:609
  308.0 4.2 %residual_back.1 = (f32[16,64,640]{2,1,0:T(8,128)}, f32[1,1024]{1,0:T(1,128)S(1)}) custom-call(f32[16,64,640]{2,1,0:T(8,128)S(1)} %copy-done.1, f32[16,64,640]{2,1,0:T(8,128)S(1)} %get-tuple-element.41.kx, f32[2,1024]{1,0:T(2,128)S(1)} %add.87.total), custom_call_target="tpu_custom_call" | custom-call | tf_op jit(solution)/shard_map/residual_back/pallas_call | solution.py:507
  312.2 8.2 %all-to-all-start.4 = ((f32[16,64,640]{2,1,0:T(8,128)}), f32[16,64,640]{2,1,0:T(8,128)}, u32[]{:S(2)}, u32[]{:S(2)}) async-start(f32[16,64,640]{2,1,0:T(8,128)} %get-tuple-element.43), calls=%async_computation.4 | async-start | bytes 5242880 | tf_op jit(solution)/shard_map/all_to_all | solution.py:49
  321.0 58.2 %all-to-all-done.4.refs_1_ = f32[16,64,640]{2,1,0:T(8,128)} async-done(((f32[16,64,640]{2,1,0:T(8,128)}), f32[16,64,640]{2,1,0:T(8,128)}, u32[]{:S(2)}, u32[]{:S(2)}) %all-to-all-start.4) | async-done | bytes 2621472 | tf_op jit(solution)/shard_map/all_to_all | solution.py:49
  379.1 3.8 %collect_blocks.1 = (f32[1,64,10240]{2,1,0:T(8,128)}, f32[1,64,10240]{2,1,0:T(8,128)}) custom-call(f32[16,64,640]{2,1,0:T(8,128)S(1)} %all-to-all-done.3.refs_0_, f32[16,64,640]{2,1,0:T(8,128)} %all-to-all-done.4.refs_1_), custom_call_target="tpu_custom_call" | custom-call | tf_op jit(solution)/shard_map/collect_blocks/pallas_call | solution.py:232
  (69 shorter events, 11.4 us)
Async XLA Ops:
  0.6 5.3 %collective-permute-start = (f32[64,192]{1,0:T(8,128)}, f32[64,192]{1,0:T(8,128)S(1)}, u32[]{:S(2)}, u32[]{:S(2)}) collective-permute-start(f32[64,192]{1,0:T(8,128)} %bitcast.27), channel_id=1, source_target_pairs={{0,16},{2,18},{4,20},{6,22},{8,24},{10,26},{12,28},{14,30},{16,0},... | collective-permute-start | bytes 147464 | tf_op jit(solution)/shard_map/ppermute | solution.py:530
  6.8 3.9 %collective-permute-start.1 = (f32[2,64,192]{2,1,0:T(8,128)S(1)}, f32[2,64,192]{2,1,0:T(8,128)S(1)}, u32[]{:S(2)}, u32[]{:S(2)}) collective-permute-start(f32[2,64,192]{2,1,0:T(8,128)S(1)} %pad_maximum_fusion.2), channel_id=1, source_target_pairs={{0,8},{2,10},{4,12},{6,14},{8,0},{10,2},{12,4},{14,6},{16,24},{18,... | collective-permute-start | bytes 294920 | tf_op jit(solution)/shard_map/ppermute | solution.py:530
  10.7 38.5 %all-to-all-start = ((f32[8,192,256]{2,1,0:T(8,128)}), f32[8,192,256]{2,1,0:T(8,128)S(1)}, u32[]{:S(2)}, u32[]{:S(2)}) async-start(f32[8,192,256]{2,1,0:T(8,128)} %spread_blocks.3), calls=%async_computation | async-start | bytes 3145728 | tf_op jit(solution)/shard_map/all_to_all | solution.py:65
  17.6 23.9 %collective-permute-start.2 = (f32[2,2,64,192]{3,2,1,0:T(8,128)S(1)}, f32[2,2,64,192]{3,2,1,0:T(8,128)S(1)}, u32[]{:S(2)}, u32[]{:S(2)}) collective-permute-start(f32[2,2,64,192]{3,2,1,0:T(8,128)S(1)} %pad_maximum_fusion.1), channel_id=1, source_target_pairs={{0,4},{2,6},{4,0},{6,2},{8,12},{10,14},{12,8},{14,10},{16,20},{18,... | collective-permute-start | bytes 589832 | tf_op jit(solution)/shard_map/ppermute | solution.py:530
  41.6 7.1 %copy-start.9 = (f32[16]{0:T(128)S(1)}, f32[16]{0:T(128)}, u32[]{:S(2)}) copy-start(f32[16]{0:T(128)} %constant.51.clone) | copy-start | bytes 196
  41.6 7.1 %copy-start.10 = (f32[16]{0:T(128)S(1)}, f32[16]{0:T(128)}, u32[]{:S(2)}) copy-start(f32[16]{0:T(128)} %constant.52.clone) | copy-start | bytes 196
  41.6 7.2 %collective-permute-start.3 = (f32[2,2,2,64,192]{4,3,2,1,0:T(8,128)S(1)}, f32[2,2,2,64,192]{4,3,2,1,0:T(8,128)S(1)}, u32[]{:S(2)}, u32[]{:S(2)}) collective-permute-start(f32[2,2,2,64,192]{4,3,2,1,0:T(8,128)S(1)} %pad_maximum_fusion), channel_id=1, source_target_pairs={{0,2},{2,0},{4,6},{6,4},{8,10},{10,8},{12,14},{14,12},{16,18},{18,... | collective-permute-start | bytes 1179656 | tf_op jit(solution)/shard_map/ppermute | solution.py:530
  49.2 4.7 %copy-start.5 = (f32[8,192,384]{2,1,0:T(8,128)S(1)}, f32[8,192,384]{2,1,0:T(8,128)}, u32[]{:S(2)}) copy-start(f32[8,192,384]{2,1,0:T(8,128)} %get-tuple-element.29) | copy-start | bytes 7077892
  84.7 75.2 %all-to-all-start.2 = ((f32[8,192,640]{2,1,0:T(8,128)}), f32[8,192,640]{2,1,0:T(8,128)}, u32[]{:S(2)}, u32[]{:S(2)}) async-start(f32[8,192,640]{2,1,0:T(8,128)} %get-tuple-element.30), calls=%async_computation.2 | async-start | bytes 7864320 | tf_op jit(solution)/shard_map/all_to_all | solution.py:65
  91.0 67.8 %collective-permute-start.4 = (f32[16,64,256]{2,1,0:T(8,128)}, f32[16,64,256]{2,1,0:T(8,128)S(1)}, u32[]{:S(2)}, u32[]{:S(2)}) collective-permute-start(f32[16,64,256]{2,1,0:T(8,128)} %project.3), channel_id=1, source_target_pairs={{0,16},{2,18},{4,20},{6,22},{8,24},{10,26},{12,28},{14,30},{16,0},... | collective-permute-start | bytes 3145736 | tf_op jit(solution)/shard_map/ppermute | solution.py:589
  158.9 1.1 copy-start.3
  159.9 68.1 %collective-permute-start.5 = (f32[16,64,384]{2,1,0:T(8,128)}, f32[16,64,384]{2,1,0:T(8,128)S(1)}, u32[]{:S(2)}, u32[]{:S(2)}) collective-permute-start(f32[16,64,384]{2,1,0:T(8,128)} %project.5), channel_id=1, source_target_pairs={{0,16},{2,18},{4,20},{6,22},{8,24},{10,26},{12,28},{14,30},{16,0},... | collective-permute-start | bytes 4718600 | tf_op jit(solution)/shard_map/ppermute | solution.py:589
  159.9 68.0 %copy-start.4 = (f32[16,64,256]{2,1,0:T(8,128)S(1)}, f32[16,64,256]{2,1,0:T(8,128)}, u32[]{:S(2)}) copy-start(f32[16,64,256]{2,1,0:T(8,128)} %copy-done.3) | copy-start | bytes 3145732
  228.0 1.7 copy-start.2
  233.7 1.5 copy-start
  235.2 4.4 %collective-permute-start.6 = (f32[1,64,128]{2,1,0:T(8,128)S(1)}, f32[1,64,128]{2,1,0:T(8,128)S(1)}, u32[]{:S(2)}, u32[]{:S(2)}) collective-permute-start(f32[1,64,128]{2,1,0:T(8,128)S(1)} %get-tuple-element.35), channel_id=1, source_target_pairs={{0,2},{2,4},{4,6},{6,8},{8,10},{10,12},{12,14},{14,16},{16,18},{18... | collective-permute-start | bytes 98312 | tf_op jit(solution)/shard_map/ppermute | solution.py:58
  237.1 6.1 %collective-permute-start.7 = (f32[1,64,128]{2,1,0:T(8,128)S(1)}, f32[1,64,128]{2,1,0:T(8,128)S(1)}, u32[]{:S(2)}, u32[]{:S(2)}) collective-permute-start(f32[1,64,128]{2,1,0:T(8,128)S(1)} %get-tuple-element.36), channel_id=1, source_target_pairs={{2,0},{4,2},{6,4},{8,6},{10,8},{12,10},{14,12},{16,14},{18,16},{20... | collective-permute-start | bytes 98312 | tf_op jit(solution)/shard_map/ppermute | solution.py:58
  243.2 8.0 %copy-start.6 = (f32[10240]{0:T(1024)S(1)}, f32[10240]{0:T(1024)}, u32[]{:S(2)}) copy-start(f32[10240]{0:T(1024)} %param.15) | copy-start | bytes 122884
  243.2 8.0 %copy-start.7 = (f32[10240]{0:T(1024)S(1)}, f32[10240]{0:T(1024)}, u32[]{:S(2)}) copy-start(f32[10240]{0:T(1024)} %param.16) | copy-start | bytes 122884
  243.2 8.0 %copy-start.8 = (s32[10240]{0:T(1024)S(1)}, s32[10240]{0:T(1024)}, u32[]{:S(2)}) copy-start(s32[10240]{0:T(1024)} %param.17) | copy-start | bytes 122884
  243.2 69.0 %all-to-all-start.3 = ((f32[16,64,640]{2,1,0:T(8,128)}), f32[16,64,640]{2,1,0:T(8,128)S(1)}, u32[]{:S(2)}, u32[]{:S(2)}) async-start(f32[16,64,640]{2,1,0:T(8,128)} %get-tuple-element.37), calls=%async_computation.3 | async-start | bytes 5242880 | tf_op jit(solution)/shard_map/all_to_all | solution.py:49
  251.5 5.9 %collective-permute-start.8 = (f32[8,8]{1,0:T(8,128)S(1)}, f32[8,8]{1,0:T(8,128)S(1)}, u32[]{:S(2)}, u32[]{:S(2)}) collective-permute-start(f32[8,8]{1,0:T(8,128)S(1)} %slice.40), channel_id=1, source_target_pairs={{0,1},{2,3},{4,5},{6,7},{8,9},{10,11},{12,13},{14,15},{16,17},{18,... | collective-permute-start | bytes 776 | tf_op jit(solution)/shard_map/ppermute | solution.py:81
  258.6 1.7 copy-start.1
  270.9 2.5 collective-permute-start.9
  273.4 2.9 collective-permute-start.10
  276.3 3.7 collective-permute-start.11
  280.0 15.7 %collective-permute-start.12 = (f32[2,1024]{1,0:T(2,128)S(1)}, f32[2,1024]{1,0:T(2,128)S(1)}, u32[]{:S(2)}, u32[]{:S(2)}) collective-permute-start(f32[2,1024]{1,0:T(2,128)S(1)} %add.85), channel_id=1, source_target_pairs={{0,8},{2,10},{4,12},{6,14},{8,0},{10,2},{12,4},{14,6},{16,24},{18,... | collective-permute-start | bytes 24584 | tf_op jit(solution)/shard_map/ppermute | solution.py:609
  295.8 12.3 %collective-permute-start.13 = (f32[2,1024]{1,0:T(2,128)S(1)}, f32[2,1024]{1,0:T(2,128)S(1)}, u32[]{:S(2)}, u32[]{:S(2)}) collective-permute-start(f32[2,1024]{1,0:T(2,128)S(1)} %add.86), channel_id=1, source_target_pairs={{0,16},{2,18},{4,20},{6,22},{8,24},{10,26},{12,28},{14,30},{16,0},... | collective-permute-start | bytes 24584 | tf_op jit(solution)/shard_map/ppermute | solution.py:609
  312.2 67.0 %all-to-all-start.4 = ((f32[16,64,640]{2,1,0:T(8,128)}), f32[16,64,640]{2,1,0:T(8,128)}, u32[]{:S(2)}, u32[]{:S(2)}) async-start(f32[16,64,640]{2,1,0:T(8,128)} %get-tuple-element.43), calls=%async_computation.4 | async-start | bytes 5242880 | tf_op jit(solution)/shard_map/all_to_all | solution.py:49

commit v9 on v6

--- a/solution.py
+++ b/solution.py
@@ -10,7 +10,7 @@
 REACH = 8
 LANES = 128
 ROWS = 8
-VMEM_LIMIT = 20 * 1024 * 1024
+VMEM_LIMIT = 24 * 1024 * 1024
 HIGHEST = lax.Precision.HIGHEST
 
 
@@ -233,41 +233,51 @@
     return parts
 
 
-def project(stacked, rotation):
+def project(stacked, rotation, tiles, prior=None):
     count, wide, dofs = stacked.shape
     rows = rotation.shape[1]
-    tiles = dofs // LANES
+    width = len(tiles) * LANES
     scales = slot_scales(count)
     groups = -(-count * REACH // LANES)
     per = LANES // REACH
-
     strip = 2 * ROWS
 
-    def kernel(x, rot, proj, back, head, tail, split_rot, *split_slots):
-        tile = pl.program_id(0)
-
-        @pl.when(tile == 0)
-        def _():
-            def one(j, carry):
-                for i, part in enumerate(bf16_parts(rot[j])):
-                    split_rot[j, i * rows : (i + 1) * rows, :] = part
+    def kernel(x, rot, *refs):
+        refs = refs[2:] if prior is not None else refs
+        proj, back = refs[:2]
+        edges, scratch = (refs[2:4], refs[4:]) if prior is None else ((), refs[2:])
+        held, split_rot, mine, sent, come, go = scratch[:6]
+        split_slots = scratch[6:]
+        arrivals = []
+        for c, t in enumerate(tiles):
+            copy = pltpu.make_async_copy(
+                x.at[:, :, t * LANES : (t + 1) * LANES], held.at[c], come.at[c]
+            )
+            copy.start()
+            arrivals.append(copy)
+
+        def one(j, carry):
+            for i, part in enumerate(bf16_parts(rot[j])):
+                split_rot[j, i * rows : (i + 1) * rows, :] = part
+            return carry
+
+        lax.fori_loop(0, count, one, 0)
+        for c, copy in enumerate(arrivals):
+            copy.wait()
+
+            def transform(r, carry, c=c):
+                at = pl.ds(pl.multiple_of(r * strip, strip), strip)
+                halves = []
+                for h in range(2):
+                    own = pl.ds(pl.multiple_of(r * strip + h * ROWS, ROWS), ROWS)
+                    halves.append(to_slots([held[c, s, own, :] for s in range(count)]))
+                for j in range(count):
+                    value = jnp.concatenate([half[j] for half in halves], 0)
+                    for part, ref in zip(bf16_parts(value), split_slots):
+                        ref[j, at, c * LANES : (c + 1) * LANES] = part
                 return carry
 
-            lax.fori_loop(0, count, one, 0)
-
-        def transform(r, carry):
-            at = pl.ds(pl.multiple_of(r * strip, strip), strip)
-            halves = []
-            for h in range(2):
-                own = pl.ds(pl.multiple_of(r * strip + h * ROWS, ROWS), ROWS)
-                halves.append(to_slots([x[s, own, :] for s in range(count)]))
-            for j in range(count):
-                value = jnp.concatenate([half[j] for half in halves], 0)
-                for part, ref in zip(bf16_parts(value), split_slots):
-                    ref[j, at, :] = part
-            return carry
-
-        lax.fori_loop(0, wide // strip, transform, 0)
+            lax.fori_loop(0, wide // strip, transform, 0)
         for j in range(count):
             total = None
             for i in range(PARTS - 1, -1, -1):
@@ -280,54 +290,69 @@
                 for q in range(terms - 1, -1, -1):
                     term = stacked_terms[q * rows : (q + 1) * rows]
                     total = term if total is None else total + term
-            proj[j] = total
-
-        def inverse(r, carry):
-            at = pl.ds(pl.multiple_of(r * ROWS, ROWS), ROWS)
-            out = to_spans([proj[j, at, :] * scales[j] for j in range(count)])
-            for s in range(count):
-                back[s, at, :] = out[s]
-            return carry
-
-        lax.fori_loop(0, rows // ROWS, inverse, 0)
+            mine[j] = total
+        leaving = []
+
+        def leave(source, target, c, t, at):
+            copy = pltpu.make_async_copy(
+                source.at[:, :, c * LANES : (c + 1) * LANES],
+                target.at[:, :, t * LANES : (t + 1) * LANES],
+                go.at[at],
+            )
+            copy.start()
+            leaving.append(copy)
+
+        for c, t in enumerate(tiles):
+            leave(mine, proj, c, t, c)
+        for c, t in enumerate(tiles):
+            lanes = slice(c * LANES, (c + 1) * LANES)
+
+            def inverse(r, carry, lanes=lanes):
+                at = pl.ds(pl.multiple_of(r * ROWS, ROWS), ROWS)
+                out = to_spans([mine[j, at, lanes] * scales[j] for j in range(count)])
+                for s in range(count):
+                    sent[s, at, lanes] = out[s]
+                return carry
+
+            lax.fori_loop(0, rows // ROWS, inverse, 0)
+            leave(sent, back, c, t, len(tiles) + c)
         lane = lax.broadcasted_iota(jnp.int32, (rows, LANES), 1)
-
-        def pack(ref, start):
+        ends = ((0, 0), (len(tiles) - 1, LANES - REACH))
+        for ref, (c, start) in zip(edges, ends):
             for g in range(groups):
                 packed = jnp.zeros((rows, LANES), jnp.float32)
                 for k in range(min(per, count - g * per)):
                     turn = (k * REACH - start) % LANES
-                    value = proj[g * per + k]
+                    value = mine[g * per + k, :, c * LANES : (c + 1) * LANES]
                     value = pltpu.roll(value, turn, 1) if turn else value
                     packed = jnp.where(lane // REACH == k, value, packed)
                 ref[g] = packed
-
-        @pl.when(tile == 0)
-        def _():
-            pack(head, 0)
-
-        @pl.when(tile == tiles - 1)
-        def _():
-            pack(tail, LANES - REACH)
-
-    cell = pl.BlockSpec((count, rows, LANES), lambda t: (0, 0, t))
-    edge = pl.BlockSpec((groups, rows, LANES), lambda t: (0, 0, 0))
+        for copy in leaving:
+            copy.wait()
+
+    whole = pl.BlockSpec(memory_space=pltpu.HBM)
+    vmem = pl.BlockSpec(memory_space=pltpu.VMEM)
     field = pltpu.HBM((count, rows, dofs), jnp.float32)
-    edges = jax.ShapeDtypeStruct((groups, rows, LANES), jnp.float32)
+    edge = jax.ShapeDtypeStruct((groups, rows, LANES), jnp.float32)
+    first = prior is None
     return pl.pallas_call(
         kernel,
-        grid=(tiles,),
-        in_specs=[
-            pl.BlockSpec((count, wide, LANES), lambda t: (0, 0, t)),
-            pl.BlockSpec((count, rows, wide), lambda t: (0, 0, 0)),
-        ],
-        out_specs=[cell, cell, edge, edge],
-        out_shape=[jax.ShapeDtypeStruct(field.shape, jnp.float32), field, edges, edges],
-        scratch_shapes=[pltpu.VMEM((count, PARTS * rows, wide), jnp.bfloat16)]
-        + [pltpu.VMEM((count, wide, LANES), jnp.bfloat16)] * PARTS,
+        in_specs=[whole, vmem] + ([] if first else [whole, whole]),
+        out_specs=[whole, whole] + ([vmem, vmem] if first else []),
+        out_shape=[field, field] + ([edge, edge] if first else []),
+        input_output_aliases={} if first else {2: 0, 3: 1},
+        scratch_shapes=[
+            pltpu.VMEM((len(tiles), count, wide, LANES), jnp.float32),
+            pltpu.VMEM((count, PARTS * rows, wide), jnp.bfloat16),
+            pltpu.VMEM((count, rows, width), jnp.float32),
+            pltpu.VMEM((count, rows, width), jnp.float32),
+            pltpu.SemaphoreType.DMA((len(tiles),)),
+            pltpu.SemaphoreType.DMA((2 * len(tiles),)),
+        ]
+        + [pltpu.VMEM((count, wide, width), jnp.bfloat16)] * PARTS,
         compiler_params=params(),
         name="project",
-    )(stacked, rotation)
+    )(stacked, rotation, *(() if first else prior))
 
 
 def stiffness(projected, before, after, bands, links):
@@ -513,7 +538,12 @@
     diagonal = ground + jnp.sum(up, 0) + jnp.sum(down, 0)
     bands = jnp.concatenate([up, down, diagonal[None], link[None]])
     links = 2.0 * (1.0 - fourier_rows(count)[1])
-    projected, spans, head, tail = project(stacked, rotation * scales)
+    rotation = rotation * scales
+    tiles = list(range(dofs // LANES))
+    outer, inner = sorted({0, tiles[-1]}), tiles[1:-1]
+    projected, spans, head, tail = project(stacked, rotation, outer)
+    if inner:
+        projected, spans = project(stacked, rotation, inner, (projected, spans))
     before, after = to_next(tail, 1), to_next(head, -1)
     spans, before, after = lax.optimization_barrier((spans, before, after))
     block_pieces = exchange(spans)
@@ -523,7 +553,8 @@
     for _, pairs in steps[::-1]:
         sums = sums + lax.ppermute(sums, "span", pairs)
     spans, ritz = residual_back(projected, stiff, sums)
-    next_block, next_residual = collect_blocks([block_pieces, exchange(spans)])
+    (next_block,) = collect_blocks([block_pieces])
+    (next_residual,) = collect_blocks([exchange(spans)])
     ritz = lax.dynamic_slice_in_dim(ritz, lax.axis_index("span") * rows, rows, 1)
     return (next_block, next_residual, ritz)
 

time: 350 us -> 341 us (0.974)
  waiting for transfers between devices: 269 us -> 263 us
    ppermute x2, waiting for transfers between devices: 4.2 us -> 0.01 us  [to_next(): return lax.ppermute(cells, ('span', 'elem'), pairs)]
    pallas_call x1 -> x2, Pallas kernels: 13.3 us -> 13.4 us  [project(): pl.pallas_call(kernel, in_specs=[whole, vmem] + ([] if first else [whole,...]
  transfers between devices with their start and end apart: 15 -> 15, of which waited for: 12 -> 11; matrix products, arithmetic and copies ran while one was open for 1% -> 1% of each run, Pallas kernels for 6% -> 10%
where the time goes in v9:
time: 341 us
  waiting for transfers between devices  263 us (77%)
  Pallas kernels  39.7 us (12%)
  starting transfers between devices  33.3 us (10%)
    ppermute x4, waiting for transfers between devices, exchange_step(): other = lax.ppermute(held, 'span', pairs)  138 us
    all_to_all x3, waiting for transfers between devices, exchange(): lax.all_to_all(pieces, 'span', split_axis=0, concat_axis=0, tiled=True)  85.5 us
    ppermute x4, waiting for transfers between devices, tiled_device(): sums = sums + lax.ppermute(sums, 'span', pairs)  34.4 us
    all_to_all x3, starting transfers between devices, exchange(): lax.all_to_all(pieces, 'span', split_axis=0, concat_axis=0, tiled=True)  19.4 us
    pallas_call x2, Pallas kernels, project(): pl.pallas_call(kernel, in_specs=[whole, vmem] + ([] if first else [whole,...  13.4 us
    pallas_call x1, Pallas kernels, stiffness(): pl.pallas_call(kernel, in_specs=[vmem, vmem, vmem, vmem, pl.BlockSpec(mem...  10.5 us
    pallas_call x1, Pallas kernels, spread_blocks(): pl.pallas_call(kernel, in_specs=[whole] * kinds, out_specs=whole, out_sha...  7.14 us
  transfers between devices with their start and end apart: 15, of which 11 were waited for; matrix products, arithmetic and copies ran while one was open for 1% of the time, Pallas kernels for 10%

profile of v9, /device:TPU:15, one launch (start us, length us, event | category | flops | bytes accessed | tf_op | source)
XLA Modules:
  0.0 341.0 jit_solution(8818830591601990055)
XLA Ops:
  0.6 2.4 collective-permute-start
  3.0 7.1 %spread_blocks.1 = f32[16,192,640]{2,1,0:T(8,128)} custom-call(f32[1,64,10240]{2,1,0:T(8,128)} %refs_0_.1, f32[1,64,10240]{2,1,0:T(8,128)} %refs_1_.1, f32[1,64,10240]{2,1,0:T(8,128)} %refs_2_.1), custom_call_target="tpu_custom_call" | custom-call | tf_op jit(solution)/shard_map/spread_blocks/pallas_call | solution.py:188
  10.2 5.5 %all-to-all-start = ((f32[16,192,640]{2,1,0:T(8,128)}), f32[16,192,640]{2,1,0:T(8,128)}, u32[]{:S(2)}, u32[]{:S(2)}) async-start(f32[16,192,640]{2,1,0:T(8,128)} %spread_blocks.1), calls=%async_computation | async-start | bytes 15728640 | tf_op jit(solution)/shard_map/all_to_all | solution.py:49
  16.0 45.8 %collective-permute-done.1 = f32[2,64,192]{2,1,0:T(8,128)S(1)} collective-permute-done((f32[2,64,192]{2,1,0:T(8,128)S(1)}, f32[2,64,192]{2,1,0:T(8,128)S(1)}, u32[]{:S(2)}, u32[]{:S(2)}) %collective-permute-start.1) | collective-permute-done | bytes 98336 | tf_op jit(solution)/shard_map/ppermute | solution.py:496
  61.9 1.0 collective-permute-start.2
  62.9 1.2 collective-permute-done.2
  64.2 0.3 collective-permute-start.3
  64.5 91.2 %collective-permute-done.3 = f32[2,2,2,64,192]{4,3,2,1,0:T(8,128)S(1)} collective-permute-done((f32[2,2,2,64,192]{4,3,2,1,0:T(8,128)S(1)}, f32[2,2,2,64,192]{4,3,2,1,0:T(8,128)S(1)}, u32[]{:S(2)}, u32[]{:S(2)}) %collective-permute-start.3) | collective-permute-done | bytes 393248 | tf_op jit(solution)/shard_map/ppermute | solution.py:496
  156.1 0.5 copy-done.5
  156.7 30.2 %all-to-all-done.x = f32[16,192,640]{2,1,0:T(8,128)} async-done(((f32[16,192,640]{2,1,0:T(8,128)}), f32[16,192,640]{2,1,0:T(8,128)}, u32[]{:S(2)}, u32[]{:S(2)}) %all-to-all-start) | async-done | bytes 7864352 | tf_op jit(solution)/shard_map/all_to_all | solution.py:49
  186.9 5.6 %project.2 = (f32[16,64,640]{2,1,0:T(8,128)}, f32[16,64,640]{2,1,0:T(8,128)}, f32[1,64,128]{2,1,0:T(8,128)S(1)}, f32[1,64,128]{2,1,0:T(8,128)S(1)}) custom-call(f32[16,192,640]{2,1,0:T(8,128)} %all-to-all-done.x, f32[16,64,192]{2,1,0:T(8,128)S(1)} %bitcast_multiply_fusion.rot), custom_call_target="tpu_custom_call" | custom-call | tf_op jit(solution)/shard_map/project/pallas_call | solution.py:338
  192.5 3.5 %collective-permute-start.4 = (f32[1,64,128]{2,1,0:T(8,128)S(1)}, f32[1,64,128]{2,1,0:T(8,128)S(1)}, u32[]{:S(2)}, u32[]{:S(2)}) collective-permute-start(f32[1,64,128]{2,1,0:T(8,128)S(1)} %get-tuple-element.23), channel_id=1, source_target_pairs={{0,2},{2,4},{4,6},{6,8},{8,10},{10,12},{12,14},{14,16},{16,18},{18... | collective-permute-start | bytes 98312 | tf_op jit(solution)/shard_map/ppermute | solution.py:58
  196.0 1.9 collective-permute-start.5
  198.0 7.8 %project.3 = (f32[16,64,640]{2,1,0:T(8,128)}, f32[16,64,640]{2,1,0:T(8,128)}) custom-call(f32[16,192,640]{2,1,0:T(8,128)} %all-to-all-done.x, f32[16,64,192]{2,1,0:T(8,128)S(1)} %bitcast_multiply_fusion.rot, f32[16,64,640]{2,1,0:T(8,128)} %get-tuple-element.20.refs_0_, ...), custom_call_target="tpu_custom_call", output_to_operand_aliasing={{0}: (2, {}), {1}: (3, {})} | custom-call | tf_op jit(solution)/shard_map/project/pallas_call | solution.py:338
  205.8 6.3 %all-to-all-start.1 = ((f32[16,64,640]{2,1,0:T(8,128)}), f32[16,64,640]{2,1,0:T(8,128)}, u32[]{:S(2)}, u32[]{:S(2)}) async-start(f32[16,64,640]{2,1,0:T(8,128)} %get-tuple-element.25), calls=%async_computation.1 | async-start | bytes 5242880 | tf_op jit(solution)/shard_map/all_to_all | solution.py:49
  212.5 1.3 collective-permute-start.6
  213.9 0.8 dynamic_slice.14
  214.7 2.6 collective-permute-done.6
  217.6 0.8 add_add_fusion
  218.4 10.5 %stiffness.1 = (f32[16,64,640]{2,1,0:T(8,128)S(1)}, f32[2,1024]{1,0:T(2,128)S(1)}) custom-call(f32[16,64,640]{2,1,0:T(8,128)S(1)} %copy-done, f32[1,64,128]{2,1,0:T(8,128)S(1)} %collective-permute-done.4.left, f32[1,64,128]{2,1,0:T(8,128)S(1)} %collective-permute-done.5.right, f32[18,640]{1,0:T(8,128)S(1)} %concatenate.8.band, f32[16]{0:T(128)S(1)} %fusion.6.lam), custom_call_target="tpu_custom_call" | custom-call | tf_op jit(solution)/shard_map/stiffness/pallas_call | solution.py:420
  229.0 2.5 collective-permute-done.7
  231.5 2.3 collective-permute-start.8
  233.7 0.8 collective-permute-done.8
  234.8 2.6 collective-permute-done.9
  237.8 19.0 %collective-permute-done.10 = f32[2,1024]{1,0:T(2,128)S(1)} collective-permute-done((f32[2,1024]{1,0:T(2,128)S(1)}, f32[2,1024]{1,0:T(2,128)S(1)}, u32[]{:S(2)}, u32[]{:S(2)}) %collective-permute-start.10) | collective-permute-done | bytes 8224 | tf_op jit(solution)/shard_map/ppermute | solution.py:554
  257.1 11.9 %collective-permute-done.11 = f32[2,1024]{1,0:T(2,128)S(1)} collective-permute-done((f32[2,1024]{1,0:T(2,128)S(1)}, f32[2,1024]{1,0:T(2,128)S(1)}, u32[]{:S(2)}, u32[]{:S(2)}) %collective-permute-start.11) | collective-permute-done | bytes 8224 | tf_op jit(solution)/shard_map/ppermute | solution.py:554
  269.0 4.2 %residual_back.1 = (f32[16,64,640]{2,1,0:T(8,128)}, f32[1,1024]{1,0:T(1,128)S(1)}) custom-call(f32[16,64,640]{2,1,0:T(8,128)S(1)} %copy-done, f32[16,64,640]{2,1,0:T(8,128)S(1)} %get-tuple-element.29.kx, f32[2,1024]{1,0:T(2,128)S(1)} %add.87.total), custom_call_target="tpu_custom_call" | custom-call | tf_op jit(solution)/shard_map/residual_back/pallas_call | solution.py:473
  273.2 7.6 %all-to-all-start.2 = ((f32[16,64,640]{2,1,0:T(8,128)}), f32[16,64,640]{2,1,0:T(8,128)S(1)}, u32[]{:S(2)}, u32[]{:S(2)}) async-start(f32[16,64,640]{2,1,0:T(8,128)} %get-tuple-element.31), calls=%async_computation.2 | async-start | bytes 5242880 | tf_op jit(solution)/shard_map/all_to_all | solution.py:49
  280.7 0.6 constant_dynamic-slice_fusion
  281.3 2.9 collect_blocks.2
  284.2 55.2 %all-to-all-done.2.refs_0_ = f32[16,64,640]{2,1,0:T(8,128)S(1)} async-done(((f32[16,64,640]{2,1,0:T(8,128)}), f32[16,64,640]{2,1,0:T(8,128)S(1)}, u32[]{:S(2)}, u32[]{:S(2)}) %all-to-all-start.2) | async-done | bytes 2621472 | tf_op jit(solution)/shard_map/all_to_all | solution.py:49
  339.4 1.6 collect_blocks.3
  (48 shorter events, 2.5 us)
Async XLA Ops:
  0.6 9.5 %collective-permute-start = (f32[64,192]{1,0:T(8,128)}, f32[64,192]{1,0:T(8,128)S(1)}, u32[]{:S(2)}, u32[]{:S(2)}) collective-permute-start(f32[64,192]{1,0:T(8,128)} %bitcast.25), channel_id=1, source_target_pairs={{0,16},{2,18},{4,20},{6,22},{8,24},{10,26},{12,28},{14,30},{16,0},... | collective-permute-start | bytes 147464 | tf_op jit(solution)/shard_map/ppermute | solution.py:496
  3.0 7.2 %copy-start.1 = (f32[1,192,64]{1,2,0:T(8,128)S(1)}, f32[1,192,64]{1,2,0:T(8,128)}, u32[]{:S(2)}) copy-start(f32[1,192,64]{1,2,0:T(8,128)} %param.18) | copy-start | bytes 147460
  10.2 176.7 %all-to-all-start = ((f32[16,192,640]{2,1,0:T(8,128)}), f32[16,192,640]{2,1,0:T(8,128)}, u32[]{:S(2)}, u32[]{:S(2)}) async-start(f32[16,192,640]{2,1,0:T(8,128)} %spread_blocks.1), calls=%async_computation | async-start | bytes 15728640 | tf_op jit(solution)/shard_map/all_to_all | solution.py:49
  15.7 46.1 %collective-permute-start.1 = (f32[2,64,192]{2,1,0:T(8,128)S(1)}, f32[2,64,192]{2,1,0:T(8,128)S(1)}, u32[]{:S(2)}, u32[]{:S(2)}) collective-permute-start(f32[2,64,192]{2,1,0:T(8,128)S(1)} %pad_maximum_fusion.2), channel_id=1, source_target_pairs={{0,4},{2,6},{4,0},{6,2},{8,12},{10,14},{12,8},{14,10},{16,20},{18,... | collective-permute-start | bytes 294920 | tf_op jit(solution)/shard_map/ppermute | solution.py:496
  61.9 2.2 collective-permute-start.2
  64.2 91.6 %collective-permute-start.3 = (f32[2,2,2,64,192]{4,3,2,1,0:T(8,128)S(1)}, f32[2,2,2,64,192]{4,3,2,1,0:T(8,128)S(1)}, u32[]{:S(2)}, u32[]{:S(2)}) collective-permute-start(f32[2,2,2,64,192]{4,3,2,1,0:T(8,128)S(1)} %pad_maximum_fusion), channel_id=1, source_target_pairs={{0,8},{2,10},{4,12},{6,14},{8,0},{10,2},{12,4},{14,6},{16,24},{18,... | collective-permute-start | bytes 1179656 | tf_op jit(solution)/shard_map/ppermute | solution.py:496
  155.9 0.7 copy-start.5
  192.5 13.3 %collective-permute-start.4 = (f32[1,64,128]{2,1,0:T(8,128)S(1)}, f32[1,64,128]{2,1,0:T(8,128)S(1)}, u32[]{:S(2)}, u32[]{:S(2)}) collective-permute-start(f32[1,64,128]{2,1,0:T(8,128)S(1)} %get-tuple-element.23), channel_id=1, source_target_pairs={{0,2},{2,4},{4,6},{6,8},{8,10},{10,12},{12,14},{14,16},{16,18},{18... | collective-permute-start | bytes 98312 | tf_op jit(solution)/shard_map/ppermute | solution.py:58
  196.0 9.8 %collective-permute-start.5 = (f32[1,64,128]{2,1,0:T(8,128)S(1)}, f32[1,64,128]{2,1,0:T(8,128)S(1)}, u32[]{:S(2)}, u32[]{:S(2)}) collective-permute-start(f32[1,64,128]{2,1,0:T(8,128)S(1)} %get-tuple-element.24), channel_id=1, source_target_pairs={{2,0},{4,2},{6,4},{8,6},{10,8},{12,10},{14,12},{16,14},{18,16},{20... | collective-permute-start | bytes 98312 | tf_op jit(solution)/shard_map/ppermute | solution.py:58
  205.8 6.4 %copy-start.2 = (f32[10240]{0:T(1024)S(1)}, f32[10240]{0:T(1024)}, u32[]{:S(2)}) copy-start(f32[10240]{0:T(1024)} %param.14) | copy-start | bytes 122884
  205.8 6.4 %copy-start.3 = (f32[10240]{0:T(1024)S(1)}, f32[10240]{0:T(1024)}, u32[]{:S(2)}) copy-start(f32[10240]{0:T(1024)} %param.15) | copy-start | bytes 122884
  205.8 6.4 %copy-start.4 = (s32[10240]{0:T(1024)S(1)}, s32[10240]{0:T(1024)}, u32[]{:S(2)}) copy-start(s32[10240]{0:T(1024)} %param.16) | copy-start | bytes 122884
  205.8 12.6 %copy-start = (f32[16,64,640]{2,1,0:T(8,128)S(1)}, f32[16,64,640]{2,1,0:T(8,128)}, u32[]{:S(2)}) copy-start(f32[16,64,640]{2,1,0:T(8,128)} %get-tuple-element.26.x) | copy-start | bytes 7864324
  205.8 67.3 %all-to-all-start.1 = ((f32[16,64,640]{2,1,0:T(8,128)}), f32[16,64,640]{2,1,0:T(8,128)}, u32[]{:S(2)}, u32[]{:S(2)}) async-start(f32[16,64,640]{2,1,0:T(8,128)} %get-tuple-element.25), calls=%async_computation.1 | async-start | bytes 5242880 | tf_op jit(solution)/shard_map/all_to_all | solution.py:49
  212.5 4.7 %collective-permute-start.6 = (f32[8,8]{1,0:T(8,128)S(1)}, f32[8,8]{1,0:T(8,128)S(1)}, u32[]{:S(2)}, u32[]{:S(2)}) collective-permute-start(f32[8,8]{1,0:T(8,128)S(1)} %slice.40), channel_id=1, source_target_pairs={{0,1},{2,3},{4,5},{6,7},{8,9},{10,11},{12,13},{14,15},{16,17},{18,... | collective-permute-start | bytes 776 | tf_op jit(solution)/shard_map/ppermute | solution.py:72
  229.0 2.5 collective-permute-start.7
  231.5 3.1 collective-permute-start.8
  234.6 2.9 collective-permute-start.9
  237.5 19.4 %collective-permute-start.10 = (f32[2,1024]{1,0:T(2,128)S(1)}, f32[2,1024]{1,0:T(2,128)S(1)}, u32[]{:S(2)}, u32[]{:S(2)}) collective-permute-start(f32[2,1024]{1,0:T(2,128)S(1)} %add.85), channel_id=1, source_target_pairs={{0,8},{2,10},{4,12},{6,14},{8,0},{10,2},{12,4},{14,6},{16,24},{18,... | collective-permute-start | bytes 24584 | tf_op jit(solution)/shard_map/ppermute | solution.py:554
  256.9 12.2 %collective-permute-start.11 = (f32[2,1024]{1,0:T(2,128)S(1)}, f32[2,1024]{1,0:T(2,128)S(1)}, u32[]{:S(2)}, u32[]{:S(2)}) collective-permute-start(f32[2,1024]{1,0:T(2,128)S(1)} %add.86), channel_id=1, source_target_pairs={{0,16},{2,18},{4,20},{6,22},{8,24},{10,26},{12,28},{14,30},{16,0},... | collective-permute-start | bytes 24584 | tf_op jit(solution)/shard_map/ppermute | solution.py:554
  273.2 66.2 %all-to-all-start.2 = ((f32[16,64,640]{2,1,0:T(8,128)}), f32[16,64,640]{2,1,0:T(8,128)S(1)}, u32[]{:S(2)}, u32[]{:S(2)}) async-start(f32[16,64,640]{2,1,0:T(8,128)} %get-tuple-element.31), calls=%async_computation.2 | async-start | bytes 5242880 | tf_op jit(solution)/shard_map/all_to_all | solution.py:49

commit v10 on v9

--- a/solution.py
+++ b/solution.py
@@ -152,35 +152,36 @@
     return pltpu.CompilerParams(vmem_limit_bytes=VMEM_LIMIT, **kw)
 
 
-def spread_blocks(blocks, count):
+def spread_blocks(blocks, count, ranges):
     _, rows, dof_dev = blocks[0].shape
     dofs = dof_dev // count
     kinds = len(blocks)
-    cuts = 2 if rows % (2 * ROWS) == 0 else 1
-    strip = rows // cuts
+    shape = (count, kinds * rows, sum(width for _, width in ranges))
+    many = kinds * len(ranges)
 
     def kernel(*refs):
         out, held, come, go = refs[kinds:]
         arrivals = []
-        for c in range(cuts):
-            for k in range(kinds):
-                at = slice(c * strip, (c + 1) * strip)
-                copy = pltpu.make_async_copy(
-                    refs[k].at[0, at, :], held.at[k, at, :], come.at[c * kinds + k]
-                )
-                copy.start()
-                arrivals.append((c, k, copy))
+        for i in range(count):
+            group, to = [], 0
+            for first, width in ranges:
+                for k in range(kinds):
+                    copy = pltpu.make_async_copy(
+                        refs[k].at[0, :, i * dofs + first : i * dofs + first + width],
+                        held.at[i, k * rows : (k + 1) * rows, to : to + width],
+                        come.at[i * many + len(group)],
+                    )
+                    copy.start()
+                    group.append(copy)
+                to += width
+            arrivals.append(group)
         leaving = []
-        for c, k, copy in arrivals:
-            copy.wait()
-            for i in range(count):
-                piece = pltpu.make_async_copy(
-                    held.at[k, c * strip : (c + 1) * strip, i * dofs : (i + 1) * dofs],
-                    out.at[i, k * rows + c * strip : k * rows + (c + 1) * strip, :],
-                    go.at[(c * kinds + k) * count + i],
-                )
-                piece.start()
-                leaving.append(piece)
+        for i, group in enumerate(arrivals):
+            for copy in group:
+                copy.wait()
+            piece = pltpu.make_async_copy(held.at[i], out.at[i], go.at[i])
+            piece.start()
+            leaving.append(piece)
         for piece in leaving:
             piece.wait()
 
@@ -189,36 +190,42 @@
         kernel,
         in_specs=[whole] * kinds,
         out_specs=whole,
-        out_shape=pltpu.HBM((count, kinds * rows, dofs), jnp.float32),
+        out_shape=pltpu.HBM(shape, jnp.float32),
         scratch_shapes=[
-            pltpu.VMEM((kinds, rows, dof_dev), jnp.float32),
-            pltpu.SemaphoreType.DMA((cuts * kinds,)),
-            pltpu.SemaphoreType.DMA((cuts * kinds * count,)),
+            pltpu.VMEM(shape, jnp.float32),
+            pltpu.SemaphoreType.DMA((count * many,)),
+            pltpu.SemaphoreType.DMA((count,)),
         ],
         compiler_params=pltpu.CompilerParams(vmem_limit_bytes=60 * 1024 * 1024),
         name="spread_blocks",
     )(*blocks)
 
 
-def collect_blocks(pieces):
-    count, rows, dofs = pieces[0].shape
+def collect_blocks(early, late, middle):
+    count, rows, early_width = early.shape
+    dofs = early_width + LANES
     many = max(n for n in (1, 2, 4, 8) if count % n == 0)
-    kinds = len(pieces)
-
-    def kernel(*refs):
-        for piece, out in zip(refs[:kinds], refs[kinds:]):
-            for i in range(many):
-                out[0, :, i * dofs : (i + 1) * dofs] = piece[i]
+
+    def kernel(first, last, block, residual):
+        for i in range(many):
+            at = i * dofs
+            block[0, :, at : at + middle] = first[i, :, :middle]
+            block[0, :, at + middle : at + middle + LANES] = last[i, :, dofs:]
+            block[0, :, at + middle + LANES : at + dofs] = first[i, :, middle:]
+            residual[0, :, at : at + dofs] = last[i, :, :dofs]
 
     return pl.pallas_call(
         kernel,
         grid=(count // many,),
-        in_specs=[pl.BlockSpec((many, rows, dofs), lambda i: (i, 0, 0))] * kinds,
-        out_specs=[pl.BlockSpec((1, rows, many * dofs), lambda i: (0, 0, i))] * kinds,
-        out_shape=[pltpu.HBM((1, rows, count * dofs), jnp.float32)] * kinds,
+        in_specs=[
+            pl.BlockSpec((many, rows, early_width), lambda i: (i, 0, 0)),
+            pl.BlockSpec((many, rows, dofs + LANES), lambda i: (i, 0, 0)),
+        ],
+        out_specs=[pl.BlockSpec((1, rows, many * dofs), lambda i: (0, 0, i))] * 2,
+        out_shape=[pltpu.HBM((1, rows, count * dofs), jnp.float32)] * 2,
         compiler_params=params(),
         name="collect_blocks",
-    )(*pieces)
+    )(early, late)
 
 
 PARTS = 3
@@ -233,8 +240,8 @@
     return parts
 
 
-def project(stacked, rotation, tiles, prior=None):
-    count, wide, dofs = stacked.shape
+def project(stacked, rotation, dofs, tiles, prior=None):
+    count, wide, _ = stacked.shape
     rows = rotation.shape[1]
     width = len(tiles) * LANES
     scales = slot_scales(count)
@@ -243,15 +250,15 @@
     strip = 2 * ROWS
 
     def kernel(x, rot, *refs):
-        refs = refs[2:] if prior is not None else refs
+        refs = refs[1:] if prior is not None else refs
         proj, back = refs[:2]
         edges, scratch = (refs[2:4], refs[4:]) if prior is None else ((), refs[2:])
         held, split_rot, mine, sent, come, go = scratch[:6]
         split_slots = scratch[6:]
         arrivals = []
-        for c, t in enumerate(tiles):
+        for c in range(len(tiles)):
             copy = pltpu.make_async_copy(
-                x.at[:, :, t * LANES : (t + 1) * LANES], held.at[c], come.at[c]
+                x.at[:, :, c * LANES : (c + 1) * LANES], held.at[c], come.at[c]
             )
             copy.start()
             arrivals.append(copy)
@@ -304,7 +311,7 @@
 
         for c, t in enumerate(tiles):
             leave(mine, proj, c, t, c)
-        for c, t in enumerate(tiles):
+        for c in range(len(tiles)):
             lanes = slice(c * LANES, (c + 1) * LANES)
 
             def inverse(r, carry, lanes=lanes):
@@ -315,7 +322,7 @@
                 return carry
 
             lax.fori_loop(0, rows // ROWS, inverse, 0)
-            leave(sent, back, c, t, len(tiles) + c)
+            leave(sent, back, c, c, len(tiles) + c)
         lane = lax.broadcasted_iota(jnp.int32, (rows, LANES), 1)
         ends = ((0, 0), (len(tiles) - 1, LANES - REACH))
         for ref, (c, start) in zip(edges, ends):
@@ -334,13 +341,21 @@
     vmem = pl.BlockSpec(memory_space=pltpu.VMEM)
     field = pltpu.HBM((count, rows, dofs), jnp.float32)
     edge = jax.ShapeDtypeStruct((groups, rows, LANES), jnp.float32)
+    sending = pltpu.HBM((count, rows, width), jnp.float32)
     first = prior is None
+    passes = PARTS * (PARTS + 1) // 2
+    cost = pl.CostEstimate(
+        flops=2 * passes * count * wide * rows * width,
+        bytes_accessed=4 * count * (wide + 2 * rows) * width,
+        transcendentals=0,
+    )
     return pl.pallas_call(
         kernel,
-        in_specs=[whole, vmem] + ([] if first else [whole, whole]),
+        in_specs=[whole, vmem] + ([] if first else [whole]),
         out_specs=[whole, whole] + ([vmem, vmem] if first else []),
-        out_shape=[field, field] + ([edge, edge] if first else []),
-        input_output_aliases={} if first else {2: 0, 3: 1},
+        out_shape=[field, sending] + ([edge, edge] if first else []),
+        input_output_aliases={} if first else {2: 0},
+        cost_estimate=cost,
         scratch_shapes=[
             pltpu.VMEM((len(tiles), count, wide, LANES), jnp.float32),
             pltpu.VMEM((count, PARTS * rows, wide), jnp.bfloat16),
@@ -352,7 +367,7 @@
         + [pltpu.VMEM((count, wide, width), jnp.bfloat16)] * PARTS,
         compiler_params=params(),
         name="project",
-    )(stacked, rotation, *(() if first else prior))
+    )(stacked, rotation, *(() if first else (prior,)))
 
 
 def stiffness(projected, before, after, bands, links):
@@ -435,11 +450,13 @@
     )(projected, before, after, bands, links)
 
 
-def residual_back(projected, stiff, sums):
+def residual_back(projected, stiff, sums, late):
     count, rows, dofs = projected.shape
     scales = slot_scales(count)
 
-    def kernel(x, kx, total, back, ritz, wide):
+    tiles = dofs // LANES
+
+    def kernel(x, kx, total, extra, back, ritz, wide):
         @pl.when(pl.program_id(0) == 0)
         def _():
             value = total[0:1, :] / (total[1:2, :] + 1e-06)
@@ -467,22 +484,34 @@
                 back[s, at, :] = out[s]
             return carry
 
-        lax.fori_loop(0, rows // ROWS, strip, 0)
-
+        @pl.when(pl.program_id(0) < tiles)
+        def _():
+            lax.fori_loop(0, rows // ROWS, strip, 0)
+
+        @pl.when(pl.program_id(0) == tiles)
+        def _():
+            back[...] = extra[...]
+
+    inner = pl.BlockSpec((count, rows, LANES), lambda t: (0, 0, jnp.minimum(t, tiles - 1)))
     cell = pl.BlockSpec((count, rows, LANES), lambda t: (0, 0, t))
     return pl.pallas_call(
         kernel,
-        grid=(dofs // LANES,),
-        in_specs=[cell, cell, pl.BlockSpec((2, count * rows), lambda t: (0, 0))],
+        grid=(tiles + 1,),
+        in_specs=[
+            inner,
+            inner,
+            pl.BlockSpec((2, count * rows), lambda t: (0, 0)),
+            pl.BlockSpec((count, rows, LANES), lambda t: (0, 0, 0)),
+        ],
         out_specs=[cell, pl.BlockSpec((1, count * rows), lambda t: (0, 0))],
         out_shape=[
-            pltpu.HBM((count, rows, dofs), jnp.float32),
+            pltpu.HBM((count, rows, dofs + LANES), jnp.float32),
             jax.ShapeDtypeStruct((1, count * rows), jnp.float32),
         ],
         scratch_shapes=[pltpu.VMEM((count * rows, LANES), jnp.float32)],
         compiler_params=params(),
         name="residual_back",
-    )(projected, stiff, sums)
+    )(projected, stiff, sums, late)
 
 
 def halvings(axis):
@@ -520,8 +549,13 @@
     dofs = current_block.shape[2] // count
     rows = current_block.shape[1]
     steps = list(halvings("span"))
+    tiles = list(range(dofs // LANES))
+    middle = tiles[len(tiles) // 2]
+    early = [t for t in tiles if t != middle]
+    at = middle * LANES
+    blocks = (current_block, search_block, previous_block)
     rotation = exchange_step(ritz_rotation[0].T, *steps[0])
-    pieces = spread_blocks((current_block, search_block, previous_block), count)
+    pieces = spread_blocks(blocks, count, [(0, at), (at + LANES, dofs - at - LANES)])
     pieces, rotation = lax.optimization_barrier((pieces, rotation))
     stacked = exchange(pieces)
     order = steps[2:] + steps[1:2]
@@ -529,6 +563,10 @@
         rotation = exchange_step(rotation, step, pairs)
     rotation = in_order(rotation, [steps[0]] + order)
     scales = jnp.array(slot_scales(count), jnp.float32)[:, None, None]
+    rotation = rotation * scales
+    pieces = spread_blocks(blocks, count, [(at, LANES)])
+    pieces, rotation = lax.optimization_barrier((pieces, rotation))
+    stacked_late = exchange(pieces)
     weights, ground, link = coefficients(
         ground_spring, wire_tension, dropper_stiff, dropper_offset, span_link, count, dofs
     )
@@ -538,23 +576,18 @@
     diagonal = ground + jnp.sum(up, 0) + jnp.sum(down, 0)
     bands = jnp.concatenate([up, down, diagonal[None], link[None]])
     links = 2.0 * (1.0 - fourier_rows(count)[1])
-    rotation = rotation * scales
-    tiles = list(range(dofs // LANES))
-    outer, inner = sorted({0, tiles[-1]}), tiles[1:-1]
-    projected, spans, head, tail = project(stacked, rotation, outer)
-    if inner:
-        projected, spans = project(stacked, rotation, inner, (projected, spans))
+    projected, spans, head, tail = project(stacked, rotation, dofs, early)
     before, after = to_next(tail, 1), to_next(head, -1)
     spans, before, after = lax.optimization_barrier((spans, before, after))
-    block_pieces = exchange(spans)
+    early_pieces = exchange(spans)
+    projected, late = project(stacked_late, rotation, dofs, [middle], projected)
     stiff, sums = stiffness(projected, before, after, bands, links)
     for _, pairs in halvings("elem"):
         sums = sums + lax.ppermute(sums, "elem", pairs)
     for _, pairs in steps[::-1]:
         sums = sums + lax.ppermute(sums, "span", pairs)
-    spans, ritz = residual_back(projected, stiff, sums)
-    (next_block,) = collect_blocks([block_pieces])
-    (next_residual,) = collect_blocks([exchange(spans)])
+    spans, ritz = residual_back(projected, stiff, sums, late)
+    next_block, next_residual = collect_blocks(early_pieces, exchange(spans), at)
     ritz = lax.dynamic_slice_in_dim(ritz, lax.axis_index("span") * rows, rows, 1)
     return (next_block, next_residual, ritz)
 
@@ -605,7 +638,7 @@
 def by_shape(*args):
     count, dof_dev = lax.axis_size("span"), args[0].shape[2]
     halves = count & (count - 1) == 0 and lax.axis_size("elem") in (1, 2, 4, 8, 16)
-    if halves and count > 1 and dof_dev % (count * LANES) == 0:
+    if halves and count > 2 and dof_dev % (count * LANES) == 0 and dof_dev > 2 * count * LANES:
         return tiled_device(*args)
     return on_device(*args)
 

time: 341 us -> 334 us (0.979)
  waiting for transfers between devices: 263 us -> 242 us
  local copies, waits for them, and re-layouts: 2.09 us -> 10 us
  starting transfers between devices: 33.3 us -> 38.4 us
    ppermute x4, waiting for transfers between devices: 138 us -> 110 us  [exchange_step(): other = lax.ppermute(held, 'span', pairs)]
    ppermute x2, waiting for transfers between devices: 0.01 us -> 22.1 us  [to_next(): return lax.ppermute(cells, ('span', 'elem'), pairs)]
    ppermute x4, waiting for transfers between devices: 34.4 us -> 13.2 us  [tiled_device(): sums = sums + lax.ppermute(sums, 'span', pairs)]
    unnamed x12 -> x24, local copies, waits for them, and re-layouts: 0.49 us -> 8.43 us
    all_to_all x3 -> x4, waiting for transfers between devices: 85.5 us -> 91.1 us  [exchange(): lax.all_to_all(pieces, 'span', split_axis=0, concat_axis=0, tiled=True)]
    all_to_all x3 -> x4, starting transfers between devices: 19.4 us -> 22.8 us  [exchange(): lax.all_to_all(pieces, 'span', split_axis=0, concat_axis=0, tiled=True)]
    pallas_call x1 -> x2, Pallas kernels: 7.14 us -> 8.8 us  [spread_blocks(): pl.pallas_call(kernel, in_specs=[whole] * kinds, out_specs=whole, out_sha...]
  transfers between devices with their start and end apart: 15 -> 16, of which waited for: 11 -> 13; matrix products, arithmetic and copies ran while one was open for 1% -> 1% of each run, Pallas kernels for 10% -> 11%
where the time goes in v10:
time: 334 us; the launch traced here: 333 us
  waiting for transfers between devices  242 us (72%)
  Pallas kernels  38.7 us (12%)
  starting transfers between devices  38.4 us (11%)
  local copies, waits for them, and re-layouts  10 us (3%)
    ppermute x4, waiting for transfers between devices, exchange_step(): other = lax.ppermute(held, 'span', pairs)  110 us
    all_to_all x4, waiting for transfers between devices, exchange(): lax.all_to_all(pieces, 'span', split_axis=0, concat_axis=0, tiled=True)  91.1 us
    all_to_all x4, starting transfers between devices, exchange(): lax.all_to_all(pieces, 'span', split_axis=0, concat_axis=0, tiled=True)  22.8 us
    ppermute x2, waiting for transfers between devices, to_next(): return lax.ppermute(cells, ('span', 'elem'), pairs)  22.1 us
    ppermute x4, waiting for transfers between devices, tiled_device(): sums = sums + lax.ppermute(sums, 'span', pairs)  13.2 us
    pallas_call x2, Pallas kernels, project(): pl.pallas_call(kernel, in_specs=[whole, vmem] + ([] if first else [whole]...  12.1 us
    pallas_call x1, Pallas kernels, stiffness(): pl.pallas_call(kernel, in_specs=[vmem, vmem, vmem, vmem, pl.BlockSpec(mem...  10.6 us
    pallas_call x2, Pallas kernels, spread_blocks(): pl.pallas_call(kernel, in_specs=[whole] * kinds, out_specs=whole, out_sha...  8.8 us
  transfers between devices with their start and end apart: 16, of which 13 were waited for; matrix products, arithmetic and copies ran while one was open for 1% of the time, Pallas kernels for 11%

profile of v10, /device:TPU:15, one launch (start us, length us, event | category | flops | bytes accessed | tf_op | source)
XLA Modules:
  0.0 332.8 jit_solution(10394301688590945530)
XLA Ops:
  0.6 2.4 collective-permute-start
  3.0 6.2 %spread_blocks.2 = f32[16,192,512]{2,1,0:T(8,128)} custom-call(f32[1,64,10240]{2,1,0:T(8,128)} %refs_0_.3, f32[1,64,10240]{2,1,0:T(8,128)} %refs_1_.3, f32[1,64,10240]{2,1,0:T(8,128)} %refs_2_.3), custom_call_target="tpu_custom_call" | custom-call | tf_op jit(solution)/shard_map/spread_blocks/pallas_call | solution.py:189
  9.3 5.4 %all-to-all-start = ((f32[16,192,512]{2,1,0:T(8,128)}), f32[16,192,512]{2,1,0:T(8,128)}, u32[]{:S(2)}, u32[]{:S(2)}) async-start(f32[16,192,512]{2,1,0:T(8,128)} %spread_blocks.2), calls=%async_computation | async-start | bytes 12582912 | tf_op jit(solution)/shard_map/all_to_all | solution.py:49
  15.0 37.4 %collective-permute-done.1 = f32[2,64,192]{2,1,0:T(8,128)S(1)} collective-permute-done((f32[2,64,192]{2,1,0:T(8,128)S(1)}, f32[2,64,192]{2,1,0:T(8,128)S(1)}, u32[]{:S(2)}, u32[]{:S(2)}) %collective-permute-start.1) | collective-permute-done | bytes 98336 | tf_op jit(solution)/shard_map/ppermute | solution.py:525
  55.1 2.6 spread_blocks.3
  57.7 71.8 %collective-permute-done.3 = f32[2,2,2,64,192]{4,3,2,1,0:T(8,128)S(1)} collective-permute-done((f32[2,2,2,64,192]{4,3,2,1,0:T(8,128)S(1)}, f32[2,2,2,64,192]{4,3,2,1,0:T(8,128)S(1)}, u32[]{:S(2)}, u32[]{:S(2)}) %collective-permute-start.3) | collective-permute-done | bytes 393248 | tf_op jit(solution)/shard_map/ppermute | solution.py:525
  130.4 21.8 %all-to-all-done.x = f32[16,192,512]{2,1,0:T(8,128)} async-done(((f32[16,192,512]{2,1,0:T(8,128)}), f32[16,192,512]{2,1,0:T(8,128)}, u32[]{:S(2)}, u32[]{:S(2)}) %all-to-all-start) | async-done | bytes 6291488 | tf_op jit(solution)/shard_map/all_to_all | solution.py:49
  152.2 4.9 %all-to-all-start.2 = ((f32[16,192,128]{2,1,0:T(8,128)}), f32[16,192,128]{2,1,0:T(8,128)S(1)}, u32[]{:S(2)}, u32[]{:S(2)}) async-start(f32[16,192,128]{2,1,0:T(8,128)} %spread_blocks.3), calls=%async_computation.2 | async-start | bytes 3145728 | tf_op jit(solution)/shard_map/all_to_all | solution.py:49
  157.1 8.9 %project.2 = (f32[16,64,640]{2,1,0:T(8,128)}, f32[16,64,512]{2,1,0:T(8,128)}, f32[1,64,128]{2,1,0:T(8,128)S(1)}, f32[1,64,128]{2,1,0:T(8,128)S(1)}) custom-call(f32[16,192,512]{2,1,0:T(8,128)} %all-to-all-done.x, f32[16,64,192]{2,1,0:T(8,128)S(1)} %bitcast_multiply_fusion.rot), custom_call_target="tpu_custom_call" | custom-call | flops 1207959552 | bytes 10485760 | tf_op jit(solution)/shard_map/project/pallas_call | solution.py:352
  166.0 3.5 %collective-permute-start.4 = (f32[1,64,128]{2,1,0:T(8,128)S(1)}, f32[1,64,128]{2,1,0:T(8,128)S(1)}, u32[]{:S(2)}, u32[]{:S(2)}) collective-permute-start(f32[1,64,128]{2,1,0:T(8,128)S(1)} %get-tuple-element.26), channel_id=1, source_target_pairs={{0,2},{2,4},{4,6},{6,8},{8,10},{10,12},{12,14},{14,16},{16,18},{18... | collective-permute-start | bytes 98312 | tf_op jit(solution)/shard_map/ppermute | solution.py:58
  169.5 1.9 collective-permute-start.5
  171.4 20.3 %collective-permute-done.4.left = f32[1,64,128]{2,1,0:T(8,128)S(1)} collective-permute-done((f32[1,64,128]{2,1,0:T(8,128)S(1)}, f32[1,64,128]{2,1,0:T(8,128)S(1)}, u32[]{:S(2)}, u32[]{:S(2)}) %collective-permute-start.4) | collective-permute-done | bytes 32800 | tf_op jit(solution)/shard_map/ppermute | solution.py:58
  191.8 1.8 collective-permute-done.5.right
  194.7 5.0 %all-to-all-start.1 = ((f32[16,64,512]{2,1,0:T(8,128)}), f32[16,64,512]{2,1,0:T(8,128)S(1)}, u32[]{:S(2)}, u32[]{:S(2)}) async-start(f32[16,64,512]{2,1,0:T(8,128)} %get-tuple-element.28), calls=%async_computation.1 | async-start | bytes 4194304 | tf_op jit(solution)/shard_map/all_to_all | solution.py:49
  200.8 1.3 collective-permute-start.6
  202.9 2.5 collective-permute-done.6
  207.3 1.4 copy-done.4
  208.7 3.2 project.3
  211.9 1.7 copy-done
  213.7 10.6 %stiffness.1 = (f32[16,64,640]{2,1,0:T(8,128)S(1)}, f32[2,1024]{1,0:T(2,128)S(1)}) custom-call(f32[16,64,640]{2,1,0:T(8,128)S(1)} %copy-done, f32[1,64,128]{2,1,0:T(8,128)S(1)} %collective-permute-done.4.left, f32[1,64,128]{2,1,0:T(8,128)S(1)} %collective-permute-done.5.right, f32[18,640]{1,0:T(8,128)S(1)} %concatenate.8.band, f32[16]{0:T(128)S(1)} %fusion.6.lam), custom_call_target="tpu_custom_call" | custom-call | tf_op jit(solution)/shard_map/stiffness/pallas_call | solution.py:435
  224.3 2.8 collective-permute-done.7
  227.1 2.1 collective-permute-start.8
  230.3 2.5 collective-permute-done.9
  232.8 2.9 collective-permute-done.10
  235.8 2.6 collective-permute-start.11
  238.3 7.0 %collective-permute-done.11 = f32[2,1024]{1,0:T(2,128)S(1)} collective-permute-done((f32[2,1024]{1,0:T(2,128)S(1)}, f32[2,1024]{1,0:T(2,128)S(1)}, u32[]{:S(2)}, u32[]{:S(2)}) %collective-permute-start.11) | collective-permute-done | bytes 8224 | tf_op jit(solution)/shard_map/ppermute | solution.py:588
  245.3 4.6 %residual_back.1 = (f32[16,64,768]{2,1,0:T(8,128)}, f32[1,1024]{1,0:T(1,128)S(1)}) custom-call(f32[16,64,640]{2,1,0:T(8,128)S(1)} %copy-done, f32[16,64,640]{2,1,0:T(8,128)S(1)} %get-tuple-element.34.kx, f32[2,1024]{1,0:T(2,128)S(1)} %add.87.total, f32[16,64,128]{2,1,0:T(8,128)S(1)} %copy-done.5), custom_call_target="tpu_custom_call" | custom-call | tf_op jit(solution)/shard_map/residual_back/pallas_call | solution.py:497
  249.9 1.3 copy-done.1
  251.2 7.5 %all-to-all-start.3 = ((f32[16,64,768]{2,1,0:T(8,128)}), f32[16,64,768]{2,1,0:T(8,128)S(1)}, u32[]{:S(2)}, u32[]{:S(2)}) async-start(f32[16,64,768]{2,1,0:T(8,128)} %get-tuple-element.37), calls=%async_computation.3 | async-start | bytes 6291456 | tf_op jit(solution)/shard_map/all_to_all | solution.py:49
  259.3 69.3 %all-to-all-done.3.last = f32[16,64,768]{2,1,0:T(8,128)S(1)} async-done(((f32[16,64,768]{2,1,0:T(8,128)}), f32[16,64,768]{2,1,0:T(8,128)S(1)}, u32[]{:S(2)}, u32[]{:S(2)}) %all-to-all-start.3) | async-done | bytes 3145760 | tf_op jit(solution)/shard_map/all_to_all | solution.py:49
  328.6 1.6 copy-done.2
  330.2 2.5 collect_blocks.1
  (62 shorter events, 10.5 us)
Async XLA Ops:
  0.6 8.6 %collective-permute-start = (f32[64,192]{1,0:T(8,128)}, f32[64,192]{1,0:T(8,128)S(1)}, u32[]{:S(2)}, u32[]{:S(2)}) collective-permute-start(f32[64,192]{1,0:T(8,128)} %bitcast.25), channel_id=1, source_target_pairs={{0,16},{2,18},{4,20},{6,22},{8,24},{10,26},{12,28},{14,30},{16,0},... | collective-permute-start | bytes 147464 | tf_op jit(solution)/shard_map/ppermute | solution.py:525
  3.0 6.2 %copy-start.7 = (f32[1,192,64]{1,2,0:T(8,128)S(1)}, f32[1,192,64]{1,2,0:T(8,128)}, u32[]{:S(2)}) copy-start(f32[1,192,64]{1,2,0:T(8,128)} %param.18) | copy-start | bytes 147460
  9.3 142.9 %all-to-all-start = ((f32[16,192,512]{2,1,0:T(8,128)}), f32[16,192,512]{2,1,0:T(8,128)}, u32[]{:S(2)}, u32[]{:S(2)}) async-start(f32[16,192,512]{2,1,0:T(8,128)} %spread_blocks.2), calls=%async_computation | async-start | bytes 12582912 | tf_op jit(solution)/shard_map/all_to_all | solution.py:49
  14.7 37.7 %collective-permute-start.1 = (f32[2,64,192]{2,1,0:T(8,128)S(1)}, f32[2,64,192]{2,1,0:T(8,128)S(1)}, u32[]{:S(2)}, u32[]{:S(2)}) collective-permute-start(f32[2,64,192]{2,1,0:T(8,128)S(1)} %pad_maximum_fusion.2), channel_id=1, source_target_pairs={{0,4},{2,6},{4,0},{6,2},{8,12},{10,14},{12,8},{14,10},{16,20},{18,... | collective-permute-start | bytes 294920 | tf_op jit(solution)/shard_map/ppermute | solution.py:525
  52.5 2.2 collective-permute-start.2
  54.7 74.8 %collective-permute-start.3 = (f32[2,2,2,64,192]{4,3,2,1,0:T(8,128)S(1)}, f32[2,2,2,64,192]{4,3,2,1,0:T(8,128)S(1)}, u32[]{:S(2)}, u32[]{:S(2)}) collective-permute-start(f32[2,2,2,64,192]{4,3,2,1,0:T(8,128)S(1)} %pad_maximum_fusion), channel_id=1, source_target_pairs={{0,8},{2,10},{4,12},{6,14},{8,0},{10,2},{12,4},{14,6},{16,24},{18,... | collective-permute-start | bytes 1179656 | tf_op jit(solution)/shard_map/ppermute | solution.py:525
  129.6 0.7 copy-start.11
  152.2 41.4 %all-to-all-start.2 = ((f32[16,192,128]{2,1,0:T(8,128)}), f32[16,192,128]{2,1,0:T(8,128)S(1)}, u32[]{:S(2)}, u32[]{:S(2)}) async-start(f32[16,192,128]{2,1,0:T(8,128)} %spread_blocks.3), calls=%async_computation.2 | async-start | bytes 3145728 | tf_op jit(solution)/shard_map/all_to_all | solution.py:49
  166.0 33.8 %copy-start.8 = (f32[10240]{0:T(1024)S(1)}, f32[10240]{0:T(1024)}, u32[]{:S(2)}) copy-start(f32[10240]{0:T(1024)} %param.14) | copy-start | bytes 122884
  166.0 33.8 %copy-start.9 = (f32[10240]{0:T(1024)S(1)}, f32[10240]{0:T(1024)}, u32[]{:S(2)}) copy-start(f32[10240]{0:T(1024)} %param.15) | copy-start | bytes 122884
  166.0 33.7 %copy-start.10 = (s32[10240]{0:T(1024)S(1)}, s32[10240]{0:T(1024)}, u32[]{:S(2)}) copy-start(s32[10240]{0:T(1024)} %param.16) | copy-start | bytes 122884
  166.0 25.7 %collective-permute-start.4 = (f32[1,64,128]{2,1,0:T(8,128)S(1)}, f32[1,64,128]{2,1,0:T(8,128)S(1)}, u32[]{:S(2)}, u32[]{:S(2)}) collective-permute-start(f32[1,64,128]{2,1,0:T(8,128)S(1)} %get-tuple-element.26), channel_id=1, source_target_pairs={{0,2},{2,4},{4,6},{6,8},{8,10},{10,12},{12,14},{14,16},{16,18},{18... | collective-permute-start | bytes 98312 | tf_op jit(solution)/shard_map/ppermute | solution.py:58
  169.5 24.0 %collective-permute-start.5 = (f32[1,64,128]{2,1,0:T(8,128)S(1)}, f32[1,64,128]{2,1,0:T(8,128)S(1)}, u32[]{:S(2)}, u32[]{:S(2)}) collective-permute-start(f32[1,64,128]{2,1,0:T(8,128)S(1)} %get-tuple-element.27), channel_id=1, source_target_pairs={{2,0},{4,2},{6,4},{8,6},{10,8},{12,10},{14,12},{16,14},{18,16},{20... | collective-permute-start | bytes 98312 | tf_op jit(solution)/shard_map/ppermute | solution.py:58
  193.6 1.2 copy-start.3
  194.7 55.1 %all-to-all-start.1 = ((f32[16,64,512]{2,1,0:T(8,128)}), f32[16,64,512]{2,1,0:T(8,128)S(1)}, u32[]{:S(2)}, u32[]{:S(2)}) async-start(f32[16,64,512]{2,1,0:T(8,128)} %get-tuple-element.28), calls=%async_computation.1 | async-start | bytes 4194304 | tf_op jit(solution)/shard_map/all_to_all | solution.py:49
  200.0 0.7 copy-start.6
  200.8 4.6 %collective-permute-start.6 = (f32[8,8]{1,0:T(8,128)S(1)}, f32[8,8]{1,0:T(8,128)S(1)}, u32[]{:S(2)}, u32[]{:S(2)}) collective-permute-start(f32[8,8]{1,0:T(8,128)S(1)} %slice.40), channel_id=1, source_target_pairs={{0,1},{2,3},{4,5},{6,7},{8,9},{10,11},{12,13},{14,15},{16,17},{18,... | collective-permute-start | bytes 776 | tf_op jit(solution)/shard_map/ppermute | solution.py:72
  207.3 1.4 copy-start.4
  211.9 1.7 copy-start
  213.7 31.6 %copy-start.5 = (f32[16,64,128]{2,1,0:T(8,128)S(1)}, f32[16,64,128]{2,1,0:T(8,128)}, u32[]{:S(2)}) copy-start(f32[16,64,128]{2,1,0:T(8,128)} %get-tuple-element.36.extra) | copy-start | bytes 1572868
  224.3 2.8 collective-permute-start.7
  227.1 2.9 collective-permute-start.8
  230.0 2.8 collective-permute-start.9
  232.8 2.9 collective-permute-start.10
  235.8 9.5 %collective-permute-start.11 = (f32[2,1024]{1,0:T(2,128)S(1)}, f32[2,1024]{1,0:T(2,128)S(1)}, u32[]{:S(2)}, u32[]{:S(2)}) collective-permute-start(f32[2,1024]{1,0:T(2,128)S(1)} %add.86), channel_id=1, source_target_pairs={{0,16},{2,18},{4,20},{6,22},{8,24},{10,26},{12,28},{14,30},{16,0},... | collective-permute-start | bytes 24584 | tf_op jit(solution)/shard_map/ppermute | solution.py:588
  249.9 1.3 copy-start.1
  251.2 77.4 %all-to-all-start.3 = ((f32[16,64,768]{2,1,0:T(8,128)}), f32[16,64,768]{2,1,0:T(8,128)S(1)}, u32[]{:S(2)}, u32[]{:S(2)}) async-start(f32[16,64,768]{2,1,0:T(8,128)} %get-tuple-element.37), calls=%async_computation.3 | async-start | bytes 6291456 | tf_op jit(solution)/shard_map/all_to_all | solution.py:49
  328.6 1.6 copy-start.2

commit v11 on v10

--- a/solution.py
+++ b/solution.py
@@ -201,31 +201,62 @@
     )(*blocks)
 
 
-def collect_blocks(early, late, middle):
+def collect_early(early, middle):
     count, rows, early_width = early.shape
     dofs = early_width + LANES
     many = max(n for n in (1, 2, 4, 8) if count % n == 0)
 
-    def kernel(first, last, block, residual):
+    def kernel(first, block):
         for i in range(many):
             at = i * dofs
             block[0, :, at : at + middle] = first[i, :, :middle]
-            block[0, :, at + middle : at + middle + LANES] = last[i, :, dofs:]
             block[0, :, at + middle + LANES : at + dofs] = first[i, :, middle:]
-            residual[0, :, at : at + dofs] = last[i, :, :dofs]
 
     return pl.pallas_call(
         kernel,
         grid=(count // many,),
-        in_specs=[
-            pl.BlockSpec((many, rows, early_width), lambda i: (i, 0, 0)),
-            pl.BlockSpec((many, rows, dofs + LANES), lambda i: (i, 0, 0)),
-        ],
-        out_specs=[pl.BlockSpec((1, rows, many * dofs), lambda i: (0, 0, i))] * 2,
-        out_shape=[pltpu.HBM((1, rows, count * dofs), jnp.float32)] * 2,
+        in_specs=[pl.BlockSpec((many, rows, early_width), lambda i: (i, 0, 0))],
+        out_specs=pl.BlockSpec((1, rows, many * dofs), lambda i: (0, 0, i)),
+        out_shape=pltpu.HBM((1, rows, count * dofs), jnp.float32),
         compiler_params=params(),
-        name="collect_blocks",
-    )(early, late)
+        name="collect_early",
+    )(early)
+
+
+def collect_late(late, block, middle):
+    count, rows, width = late.shape
+    dofs = width - LANES
+    many = max(n for n in (1, 2, 4, 8) if count % n == 0)
+
+    def kernel(last, _, residual, whole, sem):
+        copies = []
+        for i in range(many):
+            at = (pl.program_id(0) * many + i) * dofs + middle
+            copy = pltpu.make_async_copy(
+                last.at[i, :, pl.ds(dofs, LANES)],
+                whole.at[0, :, pl.ds(pl.multiple_of(at, LANES), LANES)],
+                sem.at[i],
+            )
+            copy.start()
+            copies.append(copy)
+        for i in range(many):
+            residual[0, :, i * dofs : (i + 1) * dofs] = last[i, :, :dofs]
+        for copy in copies:
+            copy.wait()
+
+    place = pl.BlockSpec(memory_space=pltpu.HBM)
+    shape = pltpu.HBM((1, rows, count * dofs), jnp.float32)
+    return pl.pallas_call(
+        kernel,
+        grid=(count // many,),
+        in_specs=[pl.BlockSpec((many, rows, width), lambda i: (i, 0, 0)), place],
+        out_specs=[pl.BlockSpec((1, rows, many * dofs), lambda i: (0, 0, i)), place],
+        out_shape=[shape, shape],
+        input_output_aliases={1: 1},
+        scratch_shapes=[pltpu.SemaphoreType.DMA((many,))],
+        compiler_params=params(),
+        name="collect_late",
+    )(late, block)
 
 
 PARTS = 3
@@ -587,7 +618,8 @@
     for _, pairs in steps[::-1]:
         sums = sums + lax.ppermute(sums, "span", pairs)
     spans, ritz = residual_back(projected, stiff, sums, late)
-    next_block, next_residual = collect_blocks(early_pieces, exchange(spans), at)
+    next_block = collect_early(early_pieces, at)
+    next_residual, next_block = collect_late(exchange(spans), next_block, at)
     ritz = lax.dynamic_slice_in_dim(ritz, lax.axis_index("span") * rows, rows, 1)
     return (next_block, next_residual, ritz)
 

time: 334 us -> 332 us (level)
  no operation moved by 1% of the time
where the time goes in v11:
time: 332 us
  waiting for transfers between devices  239 us (72%)
  Pallas kernels  40.6 us (12%)
  starting transfers between devices  38.4 us (12%)
  local copies, waits for them, and re-layouts  10 us (3%)
    ppermute x4, waiting for transfers between devices, exchange_step(): other = lax.ppermute(held, 'span', pairs)  110 us
    all_to_all x4, waiting for transfers between devices, exchange(): lax.all_to_all(pieces, 'span', split_axis=0, concat_axis=0, tiled=True)  87.9 us
    all_to_all x4, starting transfers between devices, exchange(): lax.all_to_all(pieces, 'span', split_axis=0, concat_axis=0, tiled=True)  22.8 us
    ppermute x2, waiting for transfers between devices, to_next(): return lax.ppermute(cells, ('span', 'elem'), pairs)  22.1 us
    ppermute x4, waiting for transfers between devices, tiled_device(): sums = sums + lax.ppermute(sums, 'span', pairs)  13.2 us
    pallas_call x2, Pallas kernels, project(): pl.pallas_call(kernel, in_specs=[whole, vmem] + ([] if first else [whole]...  12.1 us
    pallas_call x1, Pallas kernels, stiffness(): pl.pallas_call(kernel, in_specs=[vmem, vmem, vmem, vmem, pl.BlockSpec(mem...  10.6 us
    pallas_call x2, Pallas kernels, spread_blocks(): pl.pallas_call(kernel, in_specs=[whole] * kinds, out_specs=whole, out_sha...  8.8 us
  transfers between devices with their start and end apart: 16, of which 13 were waited for; matrix products, arithmetic and copies ran while one was open for 1% of the time, Pallas kernels for 11%

profile of v11, /device:TPU:15, one launch (start us, length us, event | category | flops | bytes accessed | tf_op | source)
XLA Modules:
  0.0 331.6 jit_solution(3593596438593243203)
XLA Ops:
  0.6 2.4 collective-permute-start
  3.0 6.2 %spread_blocks.3 = f32[16,192,512]{2,1,0:T(8,128)} custom-call(f32[1,64,10240]{2,1,0:T(8,128)} %refs_0_.3, f32[1,64,10240]{2,1,0:T(8,128)} %refs_1_.3, f32[1,64,10240]{2,1,0:T(8,128)} %refs_2_.3), custom_call_target="tpu_custom_call" | custom-call | tf_op jit(solution)/shard_map/spread_blocks/pallas_call | solution.py:189
  9.3 5.4 %all-to-all-start.1 = ((f32[16,192,512]{2,1,0:T(8,128)}), f32[16,192,512]{2,1,0:T(8,128)}, u32[]{:S(2)}, u32[]{:S(2)}) async-start(f32[16,192,512]{2,1,0:T(8,128)} %spread_blocks.3), calls=%async_computation.1 | async-start | bytes 12582912 | tf_op jit(solution)/shard_map/all_to_all | solution.py:49
  15.0 37.4 %collective-permute-done.1 = f32[2,64,192]{2,1,0:T(8,128)S(1)} collective-permute-done((f32[2,64,192]{2,1,0:T(8,128)S(1)}, f32[2,64,192]{2,1,0:T(8,128)S(1)}, u32[]{:S(2)}, u32[]{:S(2)}) %collective-permute-start.1) | collective-permute-done | bytes 98336 | tf_op jit(solution)/shard_map/ppermute | solution.py:556
  55.1 2.6 spread_blocks.2
  57.7 71.8 %collective-permute-done.3 = f32[2,2,2,64,192]{4,3,2,1,0:T(8,128)S(1)} collective-permute-done((f32[2,2,2,64,192]{4,3,2,1,0:T(8,128)S(1)}, f32[2,2,2,64,192]{4,3,2,1,0:T(8,128)S(1)}, u32[]{:S(2)}, u32[]{:S(2)}) %collective-permute-start.3) | collective-permute-done | bytes 393248 | tf_op jit(solution)/shard_map/ppermute | solution.py:556
  130.4 21.8 %all-to-all-done.1.x = f32[16,192,512]{2,1,0:T(8,128)} async-done(((f32[16,192,512]{2,1,0:T(8,128)}), f32[16,192,512]{2,1,0:T(8,128)}, u32[]{:S(2)}, u32[]{:S(2)}) %all-to-all-start.1) | async-done | bytes 6291488 | tf_op jit(solution)/shard_map/all_to_all | solution.py:49
  152.2 4.9 %all-to-all-start = ((f32[16,192,128]{2,1,0:T(8,128)}), f32[16,192,128]{2,1,0:T(8,128)S(1)}, u32[]{:S(2)}, u32[]{:S(2)}) async-start(f32[16,192,128]{2,1,0:T(8,128)} %spread_blocks.2), calls=%async_computation | async-start | bytes 3145728 | tf_op jit(solution)/shard_map/all_to_all | solution.py:49
  157.1 8.9 %project.2 = (f32[16,64,640]{2,1,0:T(8,128)}, f32[16,64,512]{2,1,0:T(8,128)}, f32[1,64,128]{2,1,0:T(8,128)S(1)}, f32[1,64,128]{2,1,0:T(8,128)S(1)}) custom-call(f32[16,192,512]{2,1,0:T(8,128)} %all-to-all-done.1.x, f32[16,64,192]{2,1,0:T(8,128)S(1)} %bitcast_multiply_fusion.rot), custom_call_target="tpu_custom_call" | custom-call | flops 1207959552 | bytes 10485760 | tf_op jit(solution)/shard_map/project/pallas_call | solution.py:383
  166.0 3.5 %collective-permute-start.4 = (f32[1,64,128]{2,1,0:T(8,128)S(1)}, f32[1,64,128]{2,1,0:T(8,128)S(1)}, u32[]{:S(2)}, u32[]{:S(2)}) collective-permute-start(f32[1,64,128]{2,1,0:T(8,128)S(1)} %get-tuple-element.29), channel_id=1, source_target_pairs={{0,2},{2,4},{4,6},{6,8},{8,10},{10,12},{12,14},{14,16},{16,18},{18... | collective-permute-start | bytes 98312 | tf_op jit(solution)/shard_map/ppermute | solution.py:58
  169.5 1.9 collective-permute-start.5
  171.4 20.3 %collective-permute-done.4.left = f32[1,64,128]{2,1,0:T(8,128)S(1)} collective-permute-done((f32[1,64,128]{2,1,0:T(8,128)S(1)}, f32[1,64,128]{2,1,0:T(8,128)S(1)}, u32[]{:S(2)}, u32[]{:S(2)}) %collective-permute-start.4) | collective-permute-done | bytes 32800 | tf_op jit(solution)/shard_map/ppermute | solution.py:58
  191.8 1.8 collective-permute-done.5.right
  194.7 5.0 %all-to-all-start.3 = ((f32[16,64,512]{2,1,0:T(8,128)}), f32[16,64,512]{2,1,0:T(8,128)S(1)}, u32[]{:S(2)}, u32[]{:S(2)}) async-start(f32[16,64,512]{2,1,0:T(8,128)} %get-tuple-element.37), calls=%async_computation.3 | async-start | bytes 4194304 | tf_op jit(solution)/shard_map/all_to_all | solution.py:49
  202.9 2.5 collective-permute-done.6
  207.3 1.4 copy-done.4
  208.7 3.2 project.3
  211.9 1.7 copy-done
  213.7 10.6 %stiffness.1 = (f32[16,64,640]{2,1,0:T(8,128)S(1)}, f32[2,1024]{1,0:T(2,128)S(1)}) custom-call(f32[16,64,640]{2,1,0:T(8,128)S(1)} %copy-done, f32[1,64,128]{2,1,0:T(8,128)S(1)} %collective-permute-done.4.left, f32[1,64,128]{2,1,0:T(8,128)S(1)} %collective-permute-done.5.right, f32[18,640]{1,0:T(8,128)S(1)} %concatenate.8.band, f32[16]{0:T(128)S(1)} %fusion.6.lam), custom_call_target="tpu_custom_call" | custom-call | tf_op jit(solution)/shard_map/stiffness/pallas_call | solution.py:466
  224.3 2.8 collective-permute-done.7
  227.1 2.1 collective-permute-start.8
  230.3 2.5 collective-permute-done.9
  232.8 2.9 collective-permute-done.10
  235.8 2.6 collective-permute-start.11
  238.3 7.0 %collective-permute-done.11 = f32[2,1024]{1,0:T(2,128)S(1)} collective-permute-done((f32[2,1024]{1,0:T(2,128)S(1)}, f32[2,1024]{1,0:T(2,128)S(1)}, u32[]{:S(2)}, u32[]{:S(2)}) %collective-permute-start.11) | collective-permute-done | bytes 8224 | tf_op jit(solution)/shard_map/ppermute | solution.py:619
  245.3 4.6 %residual_back.1 = (f32[16,64,768]{2,1,0:T(8,128)}, f32[1,1024]{1,0:T(1,128)S(1)}) custom-call(f32[16,64,640]{2,1,0:T(8,128)S(1)} %copy-done, f32[16,64,640]{2,1,0:T(8,128)S(1)} %get-tuple-element.33.kx, f32[2,1024]{1,0:T(2,128)S(1)} %add.87.total, f32[16,64,128]{2,1,0:T(8,128)S(1)} %copy-done.5), custom_call_target="tpu_custom_call" | custom-call | tf_op jit(solution)/shard_map/residual_back/pallas_call | solution.py:528
  249.9 1.3 copy-done.1
  251.2 7.5 %all-to-all-start.2 = ((f32[16,64,768]{2,1,0:T(8,128)}), f32[16,64,768]{2,1,0:T(8,128)S(1)}, u32[]{:S(2)}, u32[]{:S(2)}) async-start(f32[16,64,768]{2,1,0:T(8,128)} %get-tuple-element.36), calls=%async_computation.2 | async-start | bytes 6291456 | tf_op jit(solution)/shard_map/all_to_all | solution.py:49
  259.3 1.6 copy-done.2
  260.9 1.6 collect_early.1._
  262.5 66.2 %all-to-all-done.2.last = f32[16,64,768]{2,1,0:T(8,128)S(1)} async-done(((f32[16,64,768]{2,1,0:T(8,128)}), f32[16,64,768]{2,1,0:T(8,128)S(1)}, u32[]{:S(2)}, u32[]{:S(2)}) %all-to-all-start.2) | async-done | bytes 3145760 | tf_op jit(solution)/shard_map/all_to_all | solution.py:49
  328.6 2.9 collect_late.1
  (63 shorter events, 11.8 us)
Async XLA Ops:
  0.6 8.6 %collective-permute-start = (f32[64,192]{1,0:T(8,128)}, f32[64,192]{1,0:T(8,128)S(1)}, u32[]{:S(2)}, u32[]{:S(2)}) collective-permute-start(f32[64,192]{1,0:T(8,128)} %bitcast.25), channel_id=1, source_target_pairs={{0,16},{2,18},{4,20},{6,22},{8,24},{10,26},{12,28},{14,30},{16,0},... | collective-permute-start | bytes 147464 | tf_op jit(solution)/shard_map/ppermute | solution.py:556
  3.0 6.2 %copy-start.7 = (f32[1,192,64]{1,2,0:T(8,128)S(1)}, f32[1,192,64]{1,2,0:T(8,128)}, u32[]{:S(2)}) copy-start(f32[1,192,64]{1,2,0:T(8,128)} %param.18) | copy-start | bytes 147460
  9.3 142.9 %all-to-all-start.1 = ((f32[16,192,512]{2,1,0:T(8,128)}), f32[16,192,512]{2,1,0:T(8,128)}, u32[]{:S(2)}, u32[]{:S(2)}) async-start(f32[16,192,512]{2,1,0:T(8,128)} %spread_blocks.3), calls=%async_computation.1 | async-start | bytes 12582912 | tf_op jit(solution)/shard_map/all_to_all | solution.py:49
  14.7 37.7 %collective-permute-start.1 = (f32[2,64,192]{2,1,0:T(8,128)S(1)}, f32[2,64,192]{2,1,0:T(8,128)S(1)}, u32[]{:S(2)}, u32[]{:S(2)}) collective-permute-start(f32[2,64,192]{2,1,0:T(8,128)S(1)} %pad_maximum_fusion.2), channel_id=1, source_target_pairs={{0,4},{2,6},{4,0},{6,2},{8,12},{10,14},{12,8},{14,10},{16,20},{18,... | collective-permute-start | bytes 294920 | tf_op jit(solution)/shard_map/ppermute | solution.py:556
  52.5 2.2 collective-permute-start.2
  54.7 74.8 %collective-permute-start.3 = (f32[2,2,2,64,192]{4,3,2,1,0:T(8,128)S(1)}, f32[2,2,2,64,192]{4,3,2,1,0:T(8,128)S(1)}, u32[]{:S(2)}, u32[]{:S(2)}) collective-permute-start(f32[2,2,2,64,192]{4,3,2,1,0:T(8,128)S(1)} %pad_maximum_fusion), channel_id=1, source_target_pairs={{0,8},{2,10},{4,12},{6,14},{8,0},{10,2},{12,4},{14,6},{16,24},{18,... | collective-permute-start | bytes 1179656 | tf_op jit(solution)/shard_map/ppermute | solution.py:556
  129.6 0.7 copy-start.11
  152.2 41.4 %all-to-all-start = ((f32[16,192,128]{2,1,0:T(8,128)}), f32[16,192,128]{2,1,0:T(8,128)S(1)}, u32[]{:S(2)}, u32[]{:S(2)}) async-start(f32[16,192,128]{2,1,0:T(8,128)} %spread_blocks.2), calls=%async_computation | async-start | bytes 3145728 | tf_op jit(solution)/shard_map/all_to_all | solution.py:49
  166.0 33.8 %copy-start.8 = (f32[10240]{0:T(1024)S(1)}, f32[10240]{0:T(1024)}, u32[]{:S(2)}) copy-start(f32[10240]{0:T(1024)} %param.14) | copy-start | bytes 122884
  166.0 33.8 %copy-start.9 = (f32[10240]{0:T(1024)S(1)}, f32[10240]{0:T(1024)}, u32[]{:S(2)}) copy-start(f32[10240]{0:T(1024)} %param.15) | copy-start | bytes 122884
  166.0 33.7 %copy-start.10 = (s32[10240]{0:T(1024)S(1)}, s32[10240]{0:T(1024)}, u32[]{:S(2)}) copy-start(s32[10240]{0:T(1024)} %param.16) | copy-start | bytes 122884
  166.0 25.7 %collective-permute-start.4 = (f32[1,64,128]{2,1,0:T(8,128)S(1)}, f32[1,64,128]{2,1,0:T(8,128)S(1)}, u32[]{:S(2)}, u32[]{:S(2)}) collective-permute-start(f32[1,64,128]{2,1,0:T(8,128)S(1)} %get-tuple-element.29), channel_id=1, source_target_pairs={{0,2},{2,4},{4,6},{6,8},{8,10},{10,12},{12,14},{14,16},{16,18},{18... | collective-permute-start | bytes 98312 | tf_op jit(solution)/shard_map/ppermute | solution.py:58
  169.5 24.0 %collective-permute-start.5 = (f32[1,64,128]{2,1,0:T(8,128)S(1)}, f32[1,64,128]{2,1,0:T(8,128)S(1)}, u32[]{:S(2)}, u32[]{:S(2)}) collective-permute-start(f32[1,64,128]{2,1,0:T(8,128)S(1)} %get-tuple-element.30), channel_id=1, source_target_pairs={{2,0},{4,2},{6,4},{8,6},{10,8},{12,10},{14,12},{16,14},{18,16},{20... | collective-permute-start | bytes 98312 | tf_op jit(solution)/shard_map/ppermute | solution.py:58
  193.6 1.2 copy-start.3
  194.7 55.1 %all-to-all-start.3 = ((f32[16,64,512]{2,1,0:T(8,128)}), f32[16,64,512]{2,1,0:T(8,128)S(1)}, u32[]{:S(2)}, u32[]{:S(2)}) async-start(f32[16,64,512]{2,1,0:T(8,128)} %get-tuple-element.37), calls=%async_computation.3 | async-start | bytes 4194304 | tf_op jit(solution)/shard_map/all_to_all | solution.py:49
  200.0 0.7 copy-start.6
  200.8 4.6 %collective-permute-start.6 = (f32[8,8]{1,0:T(8,128)S(1)}, f32[8,8]{1,0:T(8,128)S(1)}, u32[]{:S(2)}, u32[]{:S(2)}) collective-permute-start(f32[8,8]{1,0:T(8,128)S(1)} %slice.40), channel_id=1, source_target_pairs={{0,1},{2,3},{4,5},{6,7},{8,9},{10,11},{12,13},{14,15},{16,17},{18,... | collective-permute-start | bytes 776 | tf_op jit(solution)/shard_map/ppermute | solution.py:72
  207.3 1.4 copy-start.4
  211.9 1.7 copy-start
  213.7 31.6 %copy-start.5 = (f32[16,64,128]{2,1,0:T(8,128)S(1)}, f32[16,64,128]{2,1,0:T(8,128)}, u32[]{:S(2)}) copy-start(f32[16,64,128]{2,1,0:T(8,128)} %get-tuple-element.35.extra) | copy-start | bytes 1572868
  224.3 2.8 collective-permute-start.7
  227.1 2.9 collective-permute-start.8
  230.0 2.8 collective-permute-start.9
  232.8 2.9 collective-permute-start.10
  235.8 9.5 %collective-permute-start.11 = (f32[2,1024]{1,0:T(2,128)S(1)}, f32[2,1024]{1,0:T(2,128)S(1)}, u32[]{:S(2)}, u32[]{:S(2)}) collective-permute-start(f32[2,1024]{1,0:T(2,128)S(1)} %add.86), channel_id=1, source_target_pairs={{0,16},{2,18},{4,20},{6,22},{8,24},{10,26},{12,28},{14,30},{16,0},... | collective-permute-start | bytes 24584 | tf_op jit(solution)/shard_map/ppermute | solution.py:619
  249.9 1.3 copy-start.1
  251.2 77.4 %all-to-all-start.2 = ((f32[16,64,768]{2,1,0:T(8,128)}), f32[16,64,768]{2,1,0:T(8,128)S(1)}, u32[]{:S(2)}, u32[]{:S(2)}) async-start(f32[16,64,768]{2,1,0:T(8,128)} %get-tuple-element.36), calls=%async_computation.2 | async-start | bytes 6291456 | tf_op jit(solution)/shard_map/all_to_all | solution.py:49
  259.3 1.6 copy-start.2

commit v12 on v11

--- a/solution.py
+++ b/solution.py
@@ -558,6 +558,34 @@
     return jnp.stack([jnp.where(upper, other, held), jnp.where(upper, held, other)])
 
 
+def exchange_bits(held, steps):
+    bits = len(steps)
+    tail = held.shape[1:]
+    held = held.reshape((2,) * bits + tail)
+
+    def halves(held, step, d):
+        upper = (lax.axis_index("span") & step) != 0
+        low, high = (lax.index_in_dim(held, side, d, keepdims=False) for side in (0, 1))
+        return jnp.where(upper, high, low), jnp.where(upper, low, high)
+
+    def join(mine, other, step, pairs, d):
+        upper = (lax.axis_index("span") & step) != 0
+        got = lax.ppermute(other, "span", pairs)
+        return jnp.stack([jnp.where(upper, got, mine), jnp.where(upper, mine, got)], d)
+
+    near = steps[::-1]
+    for k, (step, pairs) in enumerate(near[:-1]):
+        d = bits - 1 - k
+        held = join(*halves(held, step, d), step, pairs, d)
+    step, pairs = near[-1]
+    mine, other = halves(held, step, 0)
+
+    def finish(mine, other):
+        return join(mine, other, step, pairs, 0).reshape((-1,) + tail)
+
+    return mine, other, finish
+
+
 def in_order(held, steps):
     bits = [step for step, _ in steps][::-1]
     order = tuple(sorted(range(len(bits)), key=lambda d: -bits[d]))
@@ -596,8 +624,9 @@
     scales = jnp.array(slot_scales(count), jnp.float32)[:, None, None]
     rotation = rotation * scales
     pieces = spread_blocks(blocks, count, [(at, LANES)])
-    pieces, rotation = lax.optimization_barrier((pieces, rotation))
-    stacked_late = exchange(pieces)
+    mine, other, finish = exchange_bits(pieces, steps)
+    rotation, mine, other = lax.optimization_barrier((rotation, mine, other))
+    stacked_late = finish(mine, other)
     weights, ground, link = coefficients(
         ground_spring, wire_tension, dropper_stiff, dropper_offset, span_link, count, dofs
     )
@@ -609,7 +638,9 @@
     links = 2.0 * (1.0 - fourier_rows(count)[1])
     projected, spans, head, tail = project(stacked, rotation, dofs, early)
     before, after = to_next(tail, 1), to_next(head, -1)
-    spans, before, after = lax.optimization_barrier((spans, before, after))
+    spans, before, after, stacked_late = lax.optimization_barrier(
+        (spans, before, after, stacked_late)
+    )
     early_pieces = exchange(spans)
     projected, late = project(stacked_late, rotation, dofs, [middle], projected)
     stiff, sums = stiffness(projected, before, after, bands, links)

time: 332 us -> 347 us (1.045); the launches traced: 332 us -> 343 us
  starting transfers between devices: 38.4 us -> 55.2 us
  waiting for transfers between devices: 239 us -> 229 us
  other arithmetic: 2.58 us -> 7.67 us
    ppermute x0 -> x4, waiting for transfers between devices: none -> 65.4 us  [join(): got = lax.ppermute(other, 'span', pairs)]
    ppermute x4, waiting for transfers between devices: 110 us -> 74.8 us  [exchange_step(): other = lax.ppermute(held, 'span', pairs)]
    all_to_all x4 -> x3, waiting for transfers between devices: 87.9 us -> 66.2 us  [exchange(): lax.all_to_all(pieces, 'span', split_axis=0, concat_axis=0, tiled=True)]
    ppermute x2, waiting for transfers between devices: 22.1 us -> 2.91 us  [to_next(): return lax.ppermute(cells, ('span', 'elem'), pairs)]
    ppermute x0 -> x4, starting transfers between devices: none -> 17.7 us  [join(): got = lax.ppermute(other, 'span', pairs)]
    unnamed x24 -> x14, local copies, waits for them, and re-layouts: 8.43 us -> 6.61 us
    all_to_all x4 -> x3, starting transfers between devices: 22.8 us -> 21.2 us  [exchange(): lax.all_to_all(pieces, 'span', split_axis=0, concat_axis=0, tiled=True)]
  transfers between devices with their start and end apart: 16 -> 19, of which waited for: 13 -> 15; matrix products, arithmetic and copies ran while one was open for 1% -> 3% of each run, Pallas kernels for 11% -> 8%
where the time goes in v12:
time: 347 us; the launch traced here: 343 us
  waiting for transfers between devices  229 us (66%)
  starting transfers between devices  55.2 us (16%)
  Pallas kernels  40.5 us (12%)
  local copies, waits for them, and re-layouts  9.69 us (3%)
  other arithmetic  7.67 us (2%)
    ppermute x4, waiting for transfers between devices, exchange_step(): other = lax.ppermute(held, 'span', pairs)  74.8 us
    all_to_all x3, waiting for transfers between devices, exchange(): lax.all_to_all(pieces, 'span', split_axis=0, concat_axis=0, tiled=True)  66.2 us
    ppermute x4, waiting for transfers between devices, join(): got = lax.ppermute(other, 'span', pairs)  65.4 us
    all_to_all x3, starting transfers between devices, exchange(): lax.all_to_all(pieces, 'span', split_axis=0, concat_axis=0, tiled=True)  21.2 us
    ppermute x4, starting transfers between devices, join(): got = lax.ppermute(other, 'span', pairs)  17.7 us
    ppermute x4, waiting for transfers between devices, tiled_device(): sums = sums + lax.ppermute(sums, 'span', pairs)  12.9 us
    pallas_call x2, Pallas kernels, project(): pl.pallas_call(kernel, in_specs=[whole, vmem] + ([] if first else [whole]...  12.2 us
    pallas_call x1, Pallas kernels, stiffness(): pl.pallas_call(kernel, in_specs=[vmem, vmem, vmem, vmem, pl.BlockSpec(mem...  10.5 us
  transfers between devices with their start and end apart: 19, of which 15 were waited for; matrix products, arithmetic and copies ran while one was open for 3% of the time, Pallas kernels for 8%

profile of v12, /device:TPU:15, one launch (start us, length us, event | category | flops | bytes accessed | tf_op | source)
XLA Modules:
  0.0 342.9 jit_solution(8562177489940569714)
XLA Ops:
  0.6 2.4 collective-permute-start
  3.0 6.2 %spread_blocks.2 = f32[16,192,512]{2,1,0:T(8,128)} custom-call(f32[1,64,10240]{2,1,0:T(8,128)} %refs_0_.3, f32[1,64,10240]{2,1,0:T(8,128)} %refs_1_.3, f32[1,64,10240]{2,1,0:T(8,128)} %refs_2_.3), custom_call_target="tpu_custom_call" | custom-call | tf_op jit(solution)/shard_map/spread_blocks/pallas_call | solution.py:189
  9.3 5.4 %all-to-all-start = ((f32[16,192,512]{2,1,0:T(8,128)}), f32[16,192,512]{2,1,0:T(8,128)}, u32[]{:S(2)}, u32[]{:S(2)}) async-start(f32[16,192,512]{2,1,0:T(8,128)} %spread_blocks.2), calls=%async_computation | async-start | bytes 12582912 | tf_op jit(solution)/shard_map/all_to_all | solution.py:49
  14.7 2.6 spread_blocks.3
  19.6 1.8 collective-permute-done.4
  23.1 29.3 %collective-permute-done.1 = f32[2,64,192]{2,1,0:T(8,128)S(1)} collective-permute-done((f32[2,64,192]{2,1,0:T(8,128)S(1)}, f32[2,64,192]{2,1,0:T(8,128)S(1)}, u32[]{:S(2)}, u32[]{:S(2)}) %collective-permute-start.1) | collective-permute-done | bytes 98336 | tf_op jit(solution)/shard_map/ppermute | solution.py:556
  57.5 12.0 %collective-permute-done.5 = f32[2,2,2,192,128]{4,3,2,0,1:T(8,128)S(1)} collective-permute-done((f32[2,2,2,192,128]{4,3,2,0,1:T(8,128)S(1)}, f32[2,2,2,192,128]{4,3,2,0,1:T(8,128)S(1)}, u32[]{:S(2)}, u32[]{:S(2)}) %collective-permute-start.5) | collective-permute-done | bytes 786464 | tf_op jit(solution)/shard_map/ppermute | solution.py:573
  69.7 15.9 %collective-permute-start.6 = (f32[2,2,2,192,128]{4,3,2,1,0:T(8,128)S(1)}, f32[2,2,2,192,128]{4,3,2,1,0:T(8,128)S(1)}, u32[]{:S(2)}, u32[]{:S(2)}) collective-permute-start(f32[2,2,2,192,128]{4,3,2,1,0:T(8,128)S(1)} %select_bitcast_fusion.4), channel_id=1, source_target_pairs={{0,8},{2,10},{4,12},{6,14},{8,0},{10,2},{12,4},{14,6},{16,24},{18,... | collective-permute-start | bytes 2359304 | tf_op jit(solution)/shard_map/ppermute | solution.py:573
  85.6 44.0 %collective-permute-done.3 = f32[2,2,2,64,192]{4,3,2,1,0:T(8,128)S(1)} collective-permute-done((f32[2,2,2,64,192]{4,3,2,1,0:T(8,128)S(1)}, f32[2,2,2,64,192]{4,3,2,1,0:T(8,128)S(1)}, u32[]{:S(2)}, u32[]{:S(2)}) %collective-permute-start.3) | collective-permute-done | bytes 393248 | tf_op jit(solution)/shard_map/ppermute | solution.py:556
  130.6 16.0 %collective-permute-done.6 = f32[2,2,2,192,128]{4,3,2,1,0:T(8,128)S(1)} collective-permute-done((f32[2,2,2,192,128]{4,3,2,1,0:T(8,128)S(1)}, f32[2,2,2,192,128]{4,3,2,1,0:T(8,128)S(1)}, u32[]{:S(2)}, u32[]{:S(2)}) %collective-permute-start.6) | collective-permute-done | bytes 786464 | tf_op jit(solution)/shard_map/ppermute | solution.py:573
  147.9 35.7 %collective-permute-done.9 = f32[2,2,2,192,128]{4,3,2,1,0:T(8,128)S(1)} collective-permute-done((f32[2,2,2,192,128]{4,3,2,1,0:T(8,128)S(1)}, f32[2,2,2,192,128]{4,3,2,1,0:T(8,128)S(1)}, u32[]{:S(2)}, u32[]{:S(2)}) %collective-permute-start.9) | collective-permute-done | bytes 786464 | tf_op jit(solution)/shard_map/ppermute | solution.py:573
  183.7 8.9 %project.2 = (f32[16,64,640]{2,1,0:T(8,128)}, f32[16,64,512]{2,1,0:T(8,128)}, f32[1,64,128]{2,1,0:T(8,128)S(1)}, f32[1,64,128]{2,1,0:T(8,128)S(1)}) custom-call(f32[16,192,512]{2,1,0:T(8,128)} %all-to-all-done.x, f32[16,64,192]{2,1,0:T(8,128)S(1)} %bitcast_multiply_fusion.rot), custom_call_target="tpu_custom_call" | custom-call | flops 1207959552 | bytes 10485760 | tf_op jit(solution)/shard_map/project/pallas_call | solution.py:383
  192.7 4.0 %collective-permute-start.7 = (f32[1,64,128]{2,1,0:T(8,128)S(1)}, f32[1,64,128]{2,1,0:T(8,128)S(1)}, u32[]{:S(2)}, u32[]{:S(2)}) collective-permute-start(f32[1,64,128]{2,1,0:T(8,128)S(1)} %get-tuple-element.28), channel_id=1, source_target_pairs={{0,2},{2,4},{4,6},{6,8},{8,10},{10,12},{12,14},{14,16},{16,18},{18... | collective-permute-start | bytes 98312 | tf_op jit(solution)/shard_map/ppermute | solution.py:58
  196.7 1.9 collective-permute-start.8
  199.9 2.9 collective-permute-done.8.right
  202.8 8.2 %all-to-all-start.2 = ((f32[16,64,512]{2,1,0:T(8,128)}), f32[16,64,512]{2,1,0:T(8,128)S(1)}, u32[]{:S(2)}, u32[]{:S(2)}) async-start(f32[16,64,512]{2,1,0:T(8,128)} %get-tuple-element.41), calls=%async_computation.2 | async-start | bytes 4194304 | tf_op jit(solution)/shard_map/all_to_all | solution.py:49
  214.3 3.8 %collective-permute-done.10 = f32[8,8]{1,0:T(8,128)S(1)} collective-permute-done((f32[8,8]{1,0:T(8,128)S(1)}, f32[8,8]{1,0:T(8,128)S(1)}, u32[]{:S(2)}, u32[]{:S(2)}) %collective-permute-start.10) | collective-permute-done | bytes 288 | tf_op jit(solution)/shard_map/ppermute | solution.py:72
  220.6 3.2 project.3
  223.9 1.7 copy-done
  225.6 10.5 %stiffness.1 = (f32[16,64,640]{2,1,0:T(8,128)S(1)}, f32[2,1024]{1,0:T(2,128)S(1)}) custom-call(f32[16,64,640]{2,1,0:T(8,128)S(1)} %copy-done, f32[1,64,128]{2,1,0:T(8,128)S(1)} %collective-permute-done.7.left, f32[1,64,128]{2,1,0:T(8,128)S(1)} %collective-permute-done.8.right, f32[18,640]{1,0:T(8,128)S(1)} %concatenate.8.band, f32[16]{0:T(128)S(1)} %fusion.15.lam), custom_call_target="tpu_custom_call" | custom-call | tf_op jit(solution)/shard_map/stiffness/pallas_call | solution.py:466
  236.1 2.8 collective-permute-done.11
  239.0 1.8 collective-permute-start.12
  241.9 2.6 collective-permute-done.13
  244.5 2.8 collective-permute-done.14
  247.3 2.6 collective-permute-start.15
  249.9 6.7 %collective-permute-done.15 = f32[2,1024]{1,0:T(2,128)S(1)} collective-permute-done((f32[2,1024]{1,0:T(2,128)S(1)}, f32[2,1024]{1,0:T(2,128)S(1)}, u32[]{:S(2)}, u32[]{:S(2)}) %collective-permute-start.15) | collective-permute-done | bytes 8224 | tf_op jit(solution)/shard_map/ppermute | solution.py:650
  256.6 4.6 %residual_back.1 = (f32[16,64,768]{2,1,0:T(8,128)}, f32[1,1024]{1,0:T(1,128)S(1)}) custom-call(f32[16,64,640]{2,1,0:T(8,128)S(1)} %copy-done, f32[16,64,640]{2,1,0:T(8,128)S(1)} %get-tuple-element.37.kx, f32[2,1024]{1,0:T(2,128)S(1)} %add.87.total, f32[16,64,128]{2,1,0:T(8,128)S(1)} %copy-done.4), custom_call_target="tpu_custom_call" | custom-call | tf_op jit(solution)/shard_map/residual_back/pallas_call | solution.py:528
  262.5 7.5 %all-to-all-start.1 = ((f32[16,64,768]{2,1,0:T(8,128)}), f32[16,64,768]{2,1,0:T(8,128)S(1)}, u32[]{:S(2)}, u32[]{:S(2)}) async-start(f32[16,64,768]{2,1,0:T(8,128)} %get-tuple-element.40), calls=%async_computation.1 | async-start | bytes 6291456 | tf_op jit(solution)/shard_map/all_to_all | solution.py:49
  270.7 1.6 copy-done.2
  272.2 1.6 collect_early.1._
  273.8 66.2 %all-to-all-done.1.last = f32[16,64,768]{2,1,0:T(8,128)S(1)} async-done(((f32[16,64,768]{2,1,0:T(8,128)}), f32[16,64,768]{2,1,0:T(8,128)S(1)}, u32[]{:S(2)}, u32[]{:S(2)}) %all-to-all-start.1) | async-done | bytes 3145760 | tf_op jit(solution)/shard_map/all_to_all | solution.py:49
  340.0 2.9 collect_late.1
  (69 shorter events, 21.7 us)
Async XLA Ops:
  0.6 8.6 %collective-permute-start = (f32[64,192]{1,0:T(8,128)}, f32[64,192]{1,0:T(8,128)S(1)}, u32[]{:S(2)}, u32[]{:S(2)}) collective-permute-start(f32[64,192]{1,0:T(8,128)} %bitcast.82), channel_id=1, source_target_pairs={{0,16},{2,18},{4,20},{6,22},{8,24},{10,26},{12,28},{14,30},{16,0},... | collective-permute-start | bytes 147464 | tf_op jit(solution)/shard_map/ppermute | solution.py:556
  3.0 6.2 %copy-start.5 = (f32[1,192,64]{1,2,0:T(8,128)S(1)}, f32[1,192,64]{1,2,0:T(8,128)}, u32[]{:S(2)}) copy-start(f32[1,192,64]{1,2,0:T(8,128)} %param.18) | copy-start | bytes 147460
  9.3 174.4 %all-to-all-start = ((f32[16,192,512]{2,1,0:T(8,128)}), f32[16,192,512]{2,1,0:T(8,128)}, u32[]{:S(2)}, u32[]{:S(2)}) async-start(f32[16,192,512]{2,1,0:T(8,128)} %spread_blocks.2), calls=%async_computation | async-start | bytes 12582912 | tf_op jit(solution)/shard_map/all_to_all | solution.py:49
  18.9 2.5 collective-permute-start.4
  19.3 33.1 %collective-permute-start.1 = (f32[2,64,192]{2,1,0:T(8,128)S(1)}, f32[2,64,192]{2,1,0:T(8,128)S(1)}, u32[]{:S(2)}, u32[]{:S(2)}) collective-permute-start(f32[2,64,192]{2,1,0:T(8,128)S(1)} %pad_maximum_fusion.6), channel_id=1, source_target_pairs={{0,4},{2,6},{4,0},{6,2},{8,12},{10,14},{12,8},{14,10},{16,20},{18,... | collective-permute-start | bytes 294920 | tf_op jit(solution)/shard_map/ppermute | solution.py:556
  22.7 46.7 %collective-permute-start.5 = (f32[2,2,2,192,128]{4,3,2,0,1:T(8,128)S(1)}, f32[2,2,2,192,128]{4,3,2,0,1:T(8,128)S(1)}, u32[]{:S(2)}, u32[]{:S(2)}) collective-permute-start(f32[2,2,2,192,128]{4,3,2,0,1:T(8,128)S(1)} %select_bitcast_fusion.5), channel_id=1, source_target_pairs={{0,4},{2,6},{4,0},{6,2},{8,12},{10,14},{12,8},{14,10},{16,20},{18,... | collective-permute-start | bytes 2359304 | tf_op jit(solution)/shard_map/ppermute | solution.py:573
  53.1 2.9 collective-permute-start.2
  57.1 72.5 %collective-permute-start.3 = (f32[2,2,2,64,192]{4,3,2,1,0:T(8,128)S(1)}, f32[2,2,2,64,192]{4,3,2,1,0:T(8,128)S(1)}, u32[]{:S(2)}, u32[]{:S(2)}) collective-permute-start(f32[2,2,2,64,192]{4,3,2,1,0:T(8,128)S(1)} %pad_maximum_fusion.4), channel_id=1, source_target_pairs={{0,8},{2,10},{4,12},{6,14},{8,0},{10,2},{12,4},{14,6},{16,24},{18,... | collective-permute-start | bytes 1179656 | tf_op jit(solution)/shard_map/ppermute | solution.py:556
  69.7 76.9 %collective-permute-start.6 = (f32[2,2,2,192,128]{4,3,2,1,0:T(8,128)S(1)}, f32[2,2,2,192,128]{4,3,2,1,0:T(8,128)S(1)}, u32[]{:S(2)}, u32[]{:S(2)}) collective-permute-start(f32[2,2,2,192,128]{4,3,2,1,0:T(8,128)S(1)} %select_bitcast_fusion.4), channel_id=1, source_target_pairs={{0,8},{2,10},{4,12},{6,14},{8,0},{10,2},{12,4},{14,6},{16,24},{18,... | collective-permute-start | bytes 2359304 | tf_op jit(solution)/shard_map/ppermute | solution.py:573
  129.8 0.7 copy-start.6
  146.9 36.7 %collective-permute-start.9 = (f32[2,2,2,192,128]{4,3,2,1,0:T(8,128)S(1)}, f32[2,2,2,192,128]{4,3,2,1,0:T(8,128)S(1)}, u32[]{:S(2)}, u32[]{:S(2)}) collective-permute-start(f32[2,2,2,192,128]{4,3,2,1,0:T(8,128)S(1)} %get-tuple-element.30), channel_id=1, source_target_pairs={{0,16},{2,18},{4,20},{6,22},{8,24},{10,26},{12,28},{14,30},{16,0},... | collective-permute-start | bytes 2359304 | tf_op jit(solution)/shard_map/ppermute | solution.py:573
  192.7 7.2 %collective-permute-start.7 = (f32[1,64,128]{2,1,0:T(8,128)S(1)}, f32[1,64,128]{2,1,0:T(8,128)S(1)}, u32[]{:S(2)}, u32[]{:S(2)}) collective-permute-start(f32[1,64,128]{2,1,0:T(8,128)S(1)} %get-tuple-element.28), channel_id=1, source_target_pairs={{0,2},{2,4},{4,6},{6,8},{8,10},{10,12},{12,14},{14,16},{16,18},{18... | collective-permute-start | bytes 98312 | tf_op jit(solution)/shard_map/ppermute | solution.py:58
  196.7 6.1 %collective-permute-start.8 = (f32[1,64,128]{2,1,0:T(8,128)S(1)}, f32[1,64,128]{2,1,0:T(8,128)S(1)}, u32[]{:S(2)}, u32[]{:S(2)}) collective-permute-start(f32[1,64,128]{2,1,0:T(8,128)S(1)} %get-tuple-element.29), channel_id=1, source_target_pairs={{2,0},{4,2},{6,4},{8,6},{10,8},{12,10},{14,12},{16,14},{18,16},{20... | collective-permute-start | bytes 98312 | tf_op jit(solution)/shard_map/ppermute | solution.py:58
  202.8 58.4 %all-to-all-start.2 = ((f32[16,64,512]{2,1,0:T(8,128)}), f32[16,64,512]{2,1,0:T(8,128)S(1)}, u32[]{:S(2)}, u32[]{:S(2)}) async-start(f32[16,64,512]{2,1,0:T(8,128)} %get-tuple-element.41), calls=%async_computation.2 | async-start | bytes 4194304 | tf_op jit(solution)/shard_map/all_to_all | solution.py:49
  212.2 5.9 %collective-permute-start.10 = (f32[8,8]{1,0:T(8,128)S(1)}, f32[8,8]{1,0:T(8,128)S(1)}, u32[]{:S(2)}, u32[]{:S(2)}) collective-permute-start(f32[8,8]{1,0:T(8,128)S(1)} %slice.80), channel_id=1, source_target_pairs={{0,1},{2,3},{4,5},{6,7},{8,9},{10,11},{12,13},{14,15},{16,17},{18,... | collective-permute-start | bytes 776 | tf_op jit(solution)/shard_map/ppermute | solution.py:72
  219.2 1.4 copy-start.3
  223.9 1.7 copy-start
  225.6 31.0 %copy-start.4 = (f32[16,64,128]{2,1,0:T(8,128)S(1)}, f32[16,64,128]{2,1,0:T(8,128)}, u32[]{:S(2)}) copy-start(f32[16,64,128]{2,1,0:T(8,128)} %get-tuple-element.39.extra) | copy-start | bytes 1572868
  236.1 2.8 collective-permute-start.11
  239.0 2.6 collective-permute-start.12
  241.6 2.9 collective-permute-start.13
  244.5 2.8 collective-permute-start.14
  247.3 9.3 %collective-permute-start.15 = (f32[2,1024]{1,0:T(2,128)S(1)}, f32[2,1024]{1,0:T(2,128)S(1)}, u32[]{:S(2)}, u32[]{:S(2)}) collective-permute-start(f32[2,1024]{1,0:T(2,128)S(1)} %add.86), channel_id=1, source_target_pairs={{0,16},{2,18},{4,20},{6,22},{8,24},{10,26},{12,28},{14,30},{16,0},... | collective-permute-start | bytes 24584 | tf_op jit(solution)/shard_map/ppermute | solution.py:650
  261.2 1.3 copy-start.1
  262.5 77.4 %all-to-all-start.1 = ((f32[16,64,768]{2,1,0:T(8,128)}), f32[16,64,768]{2,1,0:T(8,128)S(1)}, u32[]{:S(2)}, u32[]{:S(2)}) async-start(f32[16,64,768]{2,1,0:T(8,128)} %get-tuple-element.40), calls=%async_computation.1 | async-start | bytes 6291456 | tf_op jit(solution)/shard_map/all_to_all | solution.py:49
  270.7 1.6 copy-start.2

commit v13 on v12

--- a/solution.py
+++ b/solution.py
@@ -638,9 +638,7 @@
     links = 2.0 * (1.0 - fourier_rows(count)[1])
     projected, spans, head, tail = project(stacked, rotation, dofs, early)
     before, after = to_next(tail, 1), to_next(head, -1)
-    spans, before, after, stacked_late = lax.optimization_barrier(
-        (spans, before, after, stacked_late)
-    )
+    spans, before, after = lax.optimization_barrier((spans, before, after))
     early_pieces = exchange(spans)
     projected, late = project(stacked_late, rotation, dofs, [middle], projected)
     stiff, sums = stiffness(projected, before, after, bands, links)

time: 347 us -> 377 us (1.086)
  waiting for transfers between devices: 229 us -> 258 us
    ppermute x4, waiting for transfers between devices: 65.4 us -> 101 us  [join(): got = lax.ppermute(other, 'span', pairs)]
    ppermute x4, waiting for transfers between devices: 12.9 us -> 6.08 us  [tiled_device(): sums = sums + lax.ppermute(sums, 'span', pairs)]
    all_to_all x3, waiting for transfers between devices: 66.2 us -> 70.4 us  [exchange(): lax.all_to_all(pieces, 'span', split_axis=0, concat_axis=0, tiled=True)]
  transfers between devices with their start and end apart: 19 -> 19, of which waited for: 15 -> 16; matrix products, arithmetic and copies ran while one was open for 3% -> 3% of each run, Pallas kernels for 8% -> 8%
where the time goes in v13:
time: 377 us; the launch traced here: 375 us
  waiting for transfers between devices  258 us (68%)
  starting transfers between devices  56.9 us (15%)
  Pallas kernels  40.6 us (11%)
  local copies, waits for them, and re-layouts  9.02 us (2%)
  other arithmetic  8.95 us (2%)
    ppermute x4, waiting for transfers between devices, join(): got = lax.ppermute(other, 'span', pairs)  101 us
    ppermute x4, waiting for transfers between devices, exchange_step(): other = lax.ppermute(held, 'span', pairs)  74.8 us
    all_to_all x3, waiting for transfers between devices, exchange(): lax.all_to_all(pieces, 'span', split_axis=0, concat_axis=0, tiled=True)  70.4 us
    ppermute x4, starting transfers between devices, join(): got = lax.ppermute(other, 'span', pairs)  18.8 us
    all_to_all x3, starting transfers between devices, exchange(): lax.all_to_all(pieces, 'span', split_axis=0, concat_axis=0, tiled=True)  18.3 us
    pallas_call x2, Pallas kernels, project(): pl.pallas_call(kernel, in_specs=[whole, vmem] + ([] if first else [whole]...  12.2 us
    pallas_call x1, Pallas kernels, stiffness(): pl.pallas_call(kernel, in_specs=[vmem, vmem, vmem, vmem, pl.BlockSpec(mem...  10.6 us
    pallas_call x2, Pallas kernels, spread_blocks(): pl.pallas_call(kernel, in_specs=[whole] * kinds, out_specs=whole, out_sha...  8.77 us
  transfers between devices with their start and end apart: 19, of which 16 were waited for; matrix products, arithmetic and copies ran while one was open for 3% of the time, Pallas kernels for 8%

profile of v13, /device:TPU:15, one launch (start us, length us, event | category | flops | bytes accessed | tf_op | source)
XLA Modules:
  0.0 374.6 jit_solution(4734227752813512421)
XLA Ops:
  0.6 2.4 collective-permute-start
  3.0 6.2 %spread_blocks.2 = f32[16,192,512]{2,1,0:T(8,128)} custom-call(f32[1,64,10240]{2,1,0:T(8,128)} %refs_0_.3, f32[1,64,10240]{2,1,0:T(8,128)} %refs_1_.3, f32[1,64,10240]{2,1,0:T(8,128)} %refs_2_.3), custom_call_target="tpu_custom_call" | custom-call | tf_op jit(solution)/shard_map/spread_blocks/pallas_call | solution.py:189
  9.3 5.4 %all-to-all-start = ((f32[16,192,512]{2,1,0:T(8,128)}), f32[16,192,512]{2,1,0:T(8,128)}, u32[]{:S(2)}, u32[]{:S(2)}) async-start(f32[16,192,512]{2,1,0:T(8,128)} %spread_blocks.2), calls=%async_computation | async-start | bytes 12582912 | tf_op jit(solution)/shard_map/all_to_all | solution.py:49
  14.7 2.6 spread_blocks.3
  19.6 1.8 collective-permute-done.4
  23.1 29.3 %collective-permute-done.1 = f32[2,64,192]{2,1,0:T(8,128)S(1)} collective-permute-done((f32[2,64,192]{2,1,0:T(8,128)S(1)}, f32[2,64,192]{2,1,0:T(8,128)S(1)}, u32[]{:S(2)}, u32[]{:S(2)}) %collective-permute-start.1) | collective-permute-done | bytes 98336 | tf_op jit(solution)/shard_map/ppermute | solution.py:556
  57.4 12.0 %collective-permute-done.5 = f32[2,2,2,192,128]{4,3,2,0,1:T(8,128)S(1)} collective-permute-done((f32[2,2,2,192,128]{4,3,2,0,1:T(8,128)S(1)}, f32[2,2,2,192,128]{4,3,2,0,1:T(8,128)S(1)}, u32[]{:S(2)}, u32[]{:S(2)}) %collective-permute-start.5) | collective-permute-done | bytes 786464 | tf_op jit(solution)/shard_map/ppermute | solution.py:573
  69.7 15.9 %collective-permute-start.6 = (f32[2,2,2,192,128]{4,3,2,1,0:T(8,128)S(1)}, f32[2,2,2,192,128]{4,3,2,1,0:T(8,128)S(1)}, u32[]{:S(2)}, u32[]{:S(2)}) collective-permute-start(f32[2,2,2,192,128]{4,3,2,1,0:T(8,128)S(1)} %select_bitcast_fusion.4), channel_id=1, source_target_pairs={{0,8},{2,10},{4,12},{6,14},{8,0},{10,2},{12,4},{14,6},{16,24},{18,... | collective-permute-start | bytes 2359304 | tf_op jit(solution)/shard_map/ppermute | solution.py:573
  85.6 44.0 %collective-permute-done.3 = f32[2,2,2,64,192]{4,3,2,1,0:T(8,128)S(1)} collective-permute-done((f32[2,2,2,64,192]{4,3,2,1,0:T(8,128)S(1)}, f32[2,2,2,64,192]{4,3,2,1,0:T(8,128)S(1)}, u32[]{:S(2)}, u32[]{:S(2)}) %collective-permute-start.3) | collective-permute-done | bytes 393248 | tf_op jit(solution)/shard_map/ppermute | solution.py:556
  130.6 16.0 %collective-permute-done.6 = f32[2,2,2,192,128]{4,3,2,1,0:T(8,128)S(1)} collective-permute-done((f32[2,2,2,192,128]{4,3,2,1,0:T(8,128)S(1)}, f32[2,2,2,192,128]{4,3,2,1,0:T(8,128)S(1)}, u32[]{:S(2)}, u32[]{:S(2)}) %collective-permute-start.6) | collective-permute-done | bytes 786464 | tf_op jit(solution)/shard_map/ppermute | solution.py:573
  148.0 4.2 %all-to-all-done.x = f32[16,192,512]{2,1,0:T(8,128)} async-done(((f32[16,192,512]{2,1,0:T(8,128)}), f32[16,192,512]{2,1,0:T(8,128)}, u32[]{:S(2)}, u32[]{:S(2)}) %all-to-all-start) | async-done | bytes 6291488 | tf_op jit(solution)/shard_map/all_to_all | solution.py:49
  152.2 8.9 %project.2 = (f32[16,64,640]{2,1,0:T(8,128)}, f32[16,64,512]{2,1,0:T(8,128)}, f32[1,64,128]{2,1,0:T(8,128)S(1)}, f32[1,64,128]{2,1,0:T(8,128)S(1)}) custom-call(f32[16,192,512]{2,1,0:T(8,128)} %all-to-all-done.x, f32[16,64,192]{2,1,0:T(8,128)S(1)} %bitcast_multiply_fusion.rot), custom_call_target="tpu_custom_call" | custom-call | flops 1207959552 | bytes 10485760 | tf_op jit(solution)/shard_map/project/pallas_call | solution.py:383
  161.2 3.5 collective-permute-start.8
  164.7 1.9 collective-permute-start.9
  166.7 4.2 %collective-permute-done.9.right = f32[1,64,128]{2,1,0:T(8,128)S(1)} collective-permute-done((f32[1,64,128]{2,1,0:T(8,128)S(1)}, f32[1,64,128]{2,1,0:T(8,128)S(1)}, u32[]{:S(2)}, u32[]{:S(2)}) %collective-permute-start.9) | collective-permute-done | bytes 32800 | tf_op jit(solution)/shard_map/ppermute | solution.py:58
  170.8 4.1 %all-to-all-start.2 = ((f32[16,64,512]{2,1,0:T(8,128)}), f32[16,64,512]{2,1,0:T(8,128)S(1)}, u32[]{:S(2)}, u32[]{:S(2)}) async-start(f32[16,64,512]{2,1,0:T(8,128)} %get-tuple-element.39), calls=%async_computation.2 | async-start | bytes 4194304 | tf_op jit(solution)/shard_map/all_to_all | solution.py:49
  178.1 2.1 collective-permute-start.7
  182.6 71.4 %collective-permute-done.7 = f32[2,2,2,192,128]{4,3,2,1,0:T(8,128)} collective-permute-done((f32[2,2,2,192,128]{4,3,2,1,0:T(8,128)}, f32[2,2,2,192,128]{4,3,2,1,0:T(8,128)}, u32[]{:S(2)}, u32[]{:S(2)}) %collective-permute-start.7) | collective-permute-done | bytes 786464 | tf_op jit(solution)/shard_map/ppermute | solution.py:573
  255.6 3.2 project.3
  258.9 1.7 copy-done
  260.6 10.6 %stiffness.1 = (f32[16,64,640]{2,1,0:T(8,128)S(1)}, f32[2,1024]{1,0:T(2,128)S(1)}) custom-call(f32[16,64,640]{2,1,0:T(8,128)S(1)} %copy-done, f32[1,64,128]{2,1,0:T(8,128)S(1)} %collective-permute-done.8.left, f32[1,64,128]{2,1,0:T(8,128)S(1)} %collective-permute-done.9.right, f32[18,640]{1,0:T(8,128)S(1)} %concatenate.8.band, f32[16]{0:T(128)S(1)} %fusion.15.lam), custom_call_target="tpu_custom_call" | custom-call | tf_op jit(solution)/shard_map/stiffness/pallas_call | solution.py:466
  271.2 2.1 collective-permute-start.11
  274.4 1.7 collective-permute-start.12
  277.3 2.2 collective-permute-done.13
  279.5 3.2 collective-permute-start.14
  285.1 2.0 collective-permute-done.15
  287.1 4.6 %residual_back.1 = (f32[16,64,768]{2,1,0:T(8,128)}, f32[1,1024]{1,0:T(1,128)S(1)}) custom-call(f32[16,64,640]{2,1,0:T(8,128)S(1)} %copy-done, f32[16,64,640]{2,1,0:T(8,128)S(1)} %get-tuple-element.35.kx, f32[2,1024]{1,0:T(2,128)S(1)} %add.87.total, f32[16,64,128]{2,1,0:T(8,128)S(1)} %copy-done.3), custom_call_target="tpu_custom_call" | custom-call | tf_op jit(solution)/shard_map/residual_back/pallas_call | solution.py:528
  293.0 8.7 %all-to-all-start.1 = ((f32[16,64,768]{2,1,0:T(8,128)}), f32[16,64,768]{2,1,0:T(8,128)S(1)}, u32[]{:S(2)}, u32[]{:S(2)}) async-start(f32[16,64,768]{2,1,0:T(8,128)} %get-tuple-element.38), calls=%async_computation.1 | async-start | bytes 6291456 | tf_op jit(solution)/shard_map/all_to_all | solution.py:49
  302.3 1.6 copy-done.2
  303.9 1.6 collect_early.1._
  305.5 66.2 %all-to-all-done.1.last = f32[16,64,768]{2,1,0:T(8,128)S(1)} async-done(((f32[16,64,768]{2,1,0:T(8,128)}), f32[16,64,768]{2,1,0:T(8,128)S(1)}, u32[]{:S(2)}, u32[]{:S(2)}) %all-to-all-start.1) | async-done | bytes 3145760 | tf_op jit(solution)/shard_map/all_to_all | solution.py:49
  371.6 2.9 collect_late.1
  (75 shorter events, 25.3 us)
Async XLA Ops:
  0.6 8.6 %collective-permute-start = (f32[64,192]{1,0:T(8,128)}, f32[64,192]{1,0:T(8,128)S(1)}, u32[]{:S(2)}, u32[]{:S(2)}) collective-permute-start(f32[64,192]{1,0:T(8,128)} %bitcast.82), channel_id=1, source_target_pairs={{0,16},{2,18},{4,20},{6,22},{8,24},{10,26},{12,28},{14,30},{16,0},... | collective-permute-start | bytes 147464 | tf_op jit(solution)/shard_map/ppermute | solution.py:556
  3.0 6.2 %copy-start.5 = (f32[1,192,64]{1,2,0:T(8,128)S(1)}, f32[1,192,64]{1,2,0:T(8,128)}, u32[]{:S(2)}) copy-start(f32[1,192,64]{1,2,0:T(8,128)} %param.18) | copy-start | bytes 147460
  9.3 142.9 %all-to-all-start = ((f32[16,192,512]{2,1,0:T(8,128)}), f32[16,192,512]{2,1,0:T(8,128)}, u32[]{:S(2)}, u32[]{:S(2)}) async-start(f32[16,192,512]{2,1,0:T(8,128)} %spread_blocks.2), calls=%async_computation | async-start | bytes 12582912 | tf_op jit(solution)/shard_map/all_to_all | solution.py:49
  18.9 2.5 collective-permute-start.4
  19.3 33.1 %collective-permute-start.1 = (f32[2,64,192]{2,1,0:T(8,128)S(1)}, f32[2,64,192]{2,1,0:T(8,128)S(1)}, u32[]{:S(2)}, u32[]{:S(2)}) collective-permute-start(f32[2,64,192]{2,1,0:T(8,128)S(1)} %pad_maximum_fusion.6), channel_id=1, source_target_pairs={{0,4},{2,6},{4,0},{6,2},{8,12},{10,14},{12,8},{14,10},{16,20},{18,... | collective-permute-start | bytes 294920 | tf_op jit(solution)/shard_map/ppermute | solution.py:556
  22.7 46.7 %collective-permute-start.5 = (f32[2,2,2,192,128]{4,3,2,0,1:T(8,128)S(1)}, f32[2,2,2,192,128]{4,3,2,0,1:T(8,128)S(1)}, u32[]{:S(2)}, u32[]{:S(2)}) collective-permute-start(f32[2,2,2,192,128]{4,3,2,0,1:T(8,128)S(1)} %select_bitcast_fusion.5), channel_id=1, source_target_pairs={{0,4},{2,6},{4,0},{6,2},{8,12},{10,14},{12,8},{14,10},{16,20},{18,... | collective-permute-start | bytes 2359304 | tf_op jit(solution)/shard_map/ppermute | solution.py:573
  53.1 2.9 collective-permute-start.2
  57.1 72.5 %collective-permute-start.3 = (f32[2,2,2,64,192]{4,3,2,1,0:T(8,128)S(1)}, f32[2,2,2,64,192]{4,3,2,1,0:T(8,128)S(1)}, u32[]{:S(2)}, u32[]{:S(2)}) collective-permute-start(f32[2,2,2,64,192]{4,3,2,1,0:T(8,128)S(1)} %pad_maximum_fusion.4), channel_id=1, source_target_pairs={{0,8},{2,10},{4,12},{6,14},{8,0},{10,2},{12,4},{14,6},{16,24},{18,... | collective-permute-start | bytes 1179656 | tf_op jit(solution)/shard_map/ppermute | solution.py:556
  69.7 76.9 %collective-permute-start.6 = (f32[2,2,2,192,128]{4,3,2,1,0:T(8,128)S(1)}, f32[2,2,2,192,128]{4,3,2,1,0:T(8,128)S(1)}, u32[]{:S(2)}, u32[]{:S(2)}) collective-permute-start(f32[2,2,2,192,128]{4,3,2,1,0:T(8,128)S(1)} %select_bitcast_fusion.4), channel_id=1, source_target_pairs={{0,8},{2,10},{4,12},{6,14},{8,0},{10,2},{12,4},{14,6},{16,24},{18,... | collective-permute-start | bytes 2359304 | tf_op jit(solution)/shard_map/ppermute | solution.py:573
  129.8 0.7 copy-start.9
  161.2 5.5 %collective-permute-start.8 = (f32[1,64,128]{2,1,0:T(8,128)S(1)}, f32[1,64,128]{2,1,0:T(8,128)S(1)}, u32[]{:S(2)}, u32[]{:S(2)}) collective-permute-start(f32[1,64,128]{2,1,0:T(8,128)S(1)} %get-tuple-element.31), channel_id=1, source_target_pairs={{0,2},{2,4},{4,6},{6,8},{8,10},{10,12},{12,14},{14,16},{16,18},{18... | collective-permute-start | bytes 98312 | tf_op jit(solution)/shard_map/ppermute | solution.py:58
  164.7 6.1 %collective-permute-start.9 = (f32[1,64,128]{2,1,0:T(8,128)S(1)}, f32[1,64,128]{2,1,0:T(8,128)S(1)}, u32[]{:S(2)}, u32[]{:S(2)}) collective-permute-start(f32[1,64,128]{2,1,0:T(8,128)S(1)} %get-tuple-element.32), channel_id=1, source_target_pairs={{2,0},{4,2},{6,4},{8,6},{10,8},{12,10},{14,12},{16,14},{18,16},{20... | collective-permute-start | bytes 98312 | tf_op jit(solution)/shard_map/ppermute | solution.py:58
  170.8 4.1 %copy-start.6 = (f32[10240]{0:T(1024)S(1)}, f32[10240]{0:T(1024)}, u32[]{:S(2)}) copy-start(f32[10240]{0:T(1024)} %param.14) | copy-start | bytes 122884
  170.8 4.1 %copy-start.7 = (f32[10240]{0:T(1024)S(1)}, f32[10240]{0:T(1024)}, u32[]{:S(2)}) copy-start(f32[10240]{0:T(1024)} %param.15) | copy-start | bytes 122884
  170.8 4.1 %copy-start.8 = (s32[10240]{0:T(1024)S(1)}, s32[10240]{0:T(1024)}, u32[]{:S(2)}) copy-start(s32[10240]{0:T(1024)} %param.16) | copy-start | bytes 122884
  170.8 120.9 %all-to-all-start.2 = ((f32[16,64,512]{2,1,0:T(8,128)}), f32[16,64,512]{2,1,0:T(8,128)S(1)}, u32[]{:S(2)}, u32[]{:S(2)}) async-start(f32[16,64,512]{2,1,0:T(8,128)} %get-tuple-element.39), calls=%async_computation.2 | async-start | bytes 4194304 | tf_op jit(solution)/shard_map/all_to_all | solution.py:49
  175.2 0.7 copy-start.4
  176.0 4.7 %collective-permute-start.10 = (f32[8,8]{1,0:T(8,128)S(1)}, f32[8,8]{1,0:T(8,128)S(1)}, u32[]{:S(2)}, u32[]{:S(2)}) collective-permute-start(f32[8,8]{1,0:T(8,128)S(1)} %slice.80), channel_id=1, source_target_pairs={{0,1},{2,3},{4,5},{6,7},{8,9},{10,11},{12,13},{14,15},{16,17},{18,... | collective-permute-start | bytes 776 | tf_op jit(solution)/shard_map/ppermute | solution.py:72
  178.1 75.9 %collective-permute-start.7 = (f32[2,2,2,192,128]{4,3,2,1,0:T(8,128)}, f32[2,2,2,192,128]{4,3,2,1,0:T(8,128)}, u32[]{:S(2)}, u32[]{:S(2)}) collective-permute-start(f32[2,2,2,192,128]{4,3,2,1,0:T(8,128)} %get-tuple-element.24), channel_id=1, source_target_pairs={{0,16},{2,18},{4,20},{6,22},{8,24},{10,26},{12,28},{14,30},{16,0},... | collective-permute-start | bytes 2359304 | tf_op jit(solution)/shard_map/ppermute | solution.py:573
  258.8 1.7 copy-start
  260.6 26.5 %copy-start.3 = (f32[16,64,128]{2,1,0:T(8,128)S(1)}, f32[16,64,128]{2,1,0:T(8,128)}, u32[]{:S(2)}) copy-start(f32[16,64,128]{2,1,0:T(8,128)} %get-tuple-element.37.extra) | copy-start | bytes 1572868
  271.2 3.2 collective-permute-start.11
  274.4 2.6 collective-permute-start.12
  276.9 2.5 collective-permute-start.13
  279.5 4.3 %collective-permute-start.14 = (f32[2,1024]{1,0:T(2,128)S(1)}, f32[2,1024]{1,0:T(2,128)S(1)}, u32[]{:S(2)}, u32[]{:S(2)}) collective-permute-start(f32[2,1024]{1,0:T(2,128)S(1)} %add.85), channel_id=1, source_target_pairs={{0,8},{2,10},{4,12},{6,14},{8,0},{10,2},{12,4},{14,6},{16,24},{18,... | collective-permute-start | bytes 24584 | tf_op jit(solution)/shard_map/ppermute | solution.py:648
  283.7 3.4 collective-permute-start.15
  291.7 1.3 copy-start.1
  293.0 78.6 %all-to-all-start.1 = ((f32[16,64,768]{2,1,0:T(8,128)}), f32[16,64,768]{2,1,0:T(8,128)S(1)}, u32[]{:S(2)}, u32[]{:S(2)}) async-start(f32[16,64,768]{2,1,0:T(8,128)} %get-tuple-element.38), calls=%async_computation.1 | async-start | bytes 6291456 | tf_op jit(solution)/shard_map/all_to_all | solution.py:49
  302.3 1.6 copy-start.2

commit v14 on v11

--- a/solution.py
+++ b/solution.py
@@ -11,6 +11,7 @@
 LANES = 128
 ROWS = 8
 VMEM_LIMIT = 24 * 1024 * 1024
+VMEM_MOST = 61_500_000
 HIGHEST = lax.Precision.HIGHEST
 
 
@@ -148,8 +149,8 @@
     return out
 
 
-def params(**kw):
-    return pltpu.CompilerParams(vmem_limit_bytes=VMEM_LIMIT, **kw)
+def params(limit=VMEM_LIMIT):
+    return pltpu.CompilerParams(vmem_limit_bytes=limit)
 
 
 def spread_blocks(blocks, count, ranges):
@@ -196,7 +197,7 @@
             pltpu.SemaphoreType.DMA((count * many,)),
             pltpu.SemaphoreType.DMA((count,)),
         ],
-        compiler_params=pltpu.CompilerParams(vmem_limit_bytes=60 * 1024 * 1024),
+        compiler_params=params(VMEM_MOST),
         name="spread_blocks",
     )(*blocks)
 
@@ -218,7 +219,7 @@
         in_specs=[pl.BlockSpec((many, rows, early_width), lambda i: (i, 0, 0))],
         out_specs=pl.BlockSpec((1, rows, many * dofs), lambda i: (0, 0, i)),
         out_shape=pltpu.HBM((1, rows, count * dofs), jnp.float32),
-        compiler_params=params(),
+        compiler_params=params(VMEM_MOST),
         name="collect_early",
     )(early)
 
@@ -396,7 +397,7 @@
             pltpu.SemaphoreType.DMA((2 * len(tiles),)),
         ]
         + [pltpu.VMEM((count, wide, width), jnp.bfloat16)] * PARTS,
-        compiler_params=params(),
+        compiler_params=params(VMEM_MOST),
         name="project",
     )(stacked, rotation, *(() if first else (prior,)))
 
@@ -484,62 +485,58 @@
 def residual_back(projected, stiff, sums, late):
     count, rows, dofs = projected.shape
     scales = slot_scales(count)
-
     tiles = dofs // LANES
 
-    def kernel(x, kx, total, extra, back, ritz, wide):
-        @pl.when(pl.program_id(0) == 0)
-        def _():
-            value = total[0:1, :] / (total[1:2, :] + 1e-06)
-            ritz[...] = value
-            row = lax.broadcasted_iota(jnp.int32, (ROWS, count * rows), 0)
-            first = jnp.where(row == 0, value, 0.0)
-            ones = jnp.ones((ROWS, LANES), jnp.float32)
-            spread_out = lax.dot_general(
-                first,
-                ones,
-                (((0,), (0,)), ((), ())),
-                precision=HIGHEST,
-                preferred_element_type=jnp.float32,
-            )
-            wide[...] = spread_out
-
-        def strip(r, carry):
-            at = pl.ds(pl.multiple_of(r * ROWS, ROWS), ROWS)
-            terms = []
-            for j in range(count):
-                to = pl.ds(pl.multiple_of(j * rows + r * ROWS, ROWS), ROWS)
-                terms.append((kx[j, at, :] - wide[to, :] * x[j, at, :]) * scales[j])
-            out = to_spans(terms)
-            for s in range(count):
-                back[s, at, :] = out[s]
-            return carry
-
-        @pl.when(pl.program_id(0) < tiles)
-        def _():
+    def kernel(x, kx, total, extra, back, ritz, wide, sent, go):
+        leaving = [pltpu.make_async_copy(extra, back.at[:, :, dofs : dofs + LANES], go.at[tiles])]
+        leaving[0].start()
+        value = total[0:1, :] / (total[1:2, :] + 1e-06)
+        ritz[...] = value
+        row = lax.broadcasted_iota(jnp.int32, (2 * ROWS, count * rows), 0)
+        stack = jnp.zeros((2 * ROWS, count * rows), jnp.float32)
+        for i, part in enumerate(bf16_parts(value)):
+            stack = jnp.where(row == i, part.astype(jnp.float32), stack)
+        wide[...] = lax.dot_general(
+            stack.astype(jnp.bfloat16),
+            jnp.ones((2 * ROWS, LANES), jnp.bfloat16),
+            (((0,), (0,)), ((), ())),
+            preferred_element_type=jnp.float32,
+        )
+        for t in range(tiles):
+            lanes = slice(t * LANES, (t + 1) * LANES)
+
+            def strip(r, carry, lanes=lanes):
+                at = pl.ds(pl.multiple_of(r * ROWS, ROWS), ROWS)
+                terms = []
+                for j in range(count):
+                    to = pl.ds(pl.multiple_of(j * rows + r * ROWS, ROWS), ROWS)
+                    terms.append((kx[j, at, lanes] - wide[to, :] * x[j, at, lanes]) * scales[j])
+                out = to_spans(terms)
+                for s in range(count):
+                    sent[s, at, lanes] = out[s]
+                return carry
+
             lax.fori_loop(0, rows // ROWS, strip, 0)
-
-        @pl.when(pl.program_id(0) == tiles)
-        def _():
-            back[...] = extra[...]
-
-    inner = pl.BlockSpec((count, rows, LANES), lambda t: (0, 0, jnp.minimum(t, tiles - 1)))
-    cell = pl.BlockSpec((count, rows, LANES), lambda t: (0, 0, t))
+            copy = pltpu.make_async_copy(sent.at[:, :, lanes], back.at[:, :, lanes], go.at[t])
+            copy.start()
+            leaving.append(copy)
+        for copy in leaving:
+            copy.wait()
+
+    vmem = pl.BlockSpec(memory_space=pltpu.VMEM)
     return pl.pallas_call(
         kernel,
-        grid=(tiles + 1,),
-        in_specs=[
-            inner,
-            inner,
-            pl.BlockSpec((2, count * rows), lambda t: (0, 0)),
-            pl.BlockSpec((count, rows, LANES), lambda t: (0, 0, 0)),
-        ],
-        out_specs=[cell, pl.BlockSpec((1, count * rows), lambda t: (0, 0))],
+        in_specs=[vmem] * 4,
+        out_specs=[pl.BlockSpec(memory_space=pltpu.HBM), vmem],
         out_shape=[
             pltpu.HBM((count, rows, dofs + LANES), jnp.float32),
             jax.ShapeDtypeStruct((1, count * rows), jnp.float32),
         ],
-        scratch_shapes=[pltpu.VMEM((count * rows, LANES), jnp.float32)],
+        scratch_shapes=[
+            pltpu.VMEM((count * rows, LANES), jnp.float32),
+            pltpu.VMEM((count, rows, dofs), jnp.float32),
+            pltpu.SemaphoreType.DMA((tiles + 1,)),
+        ],
         compiler_params=params(),
         name="residual_back",
     )(projected, stiff, sums, late)

time: 332 us -> 330 us (level)
  local copies, waits for them, and re-layouts: 10 us -> 6.32 us
    pallas_call x2, Pallas kernels: 12.1 us -> 16.2 us  [project(): pl.pallas_call(kernel, in_specs=[whole, vmem] + ([] if first else [whole]...]
    unnamed x24 -> x18, local copies, waits for them, and re-layouts: 8.43 us -> 4.71 us
  transfers between devices with their start and end apart: 16 -> 16, of which waited for: 13 -> 13; matrix products, arithmetic and copies ran while one was open for 1% -> 1% of each run, Pallas kernels for 11% -> 12%
where the time goes in v14:
time: 330 us
  waiting for transfers between devices  238 us (72%)
  Pallas kernels  43.8 us (13%)
  starting transfers between devices  37.5 us (11%)
  local copies, waits for them, and re-layouts  6.32 us (2%)
    ppermute x4, waiting for transfers between devices, exchange_step(): other = lax.ppermute(held, 'span', pairs)  110 us
    all_to_all x4, waiting for transfers between devices, exchange(): lax.all_to_all(pieces, 'span', split_axis=0, concat_axis=0, tiled=True)  87.3 us
    all_to_all x4, starting transfers between devices, exchange(): lax.all_to_all(pieces, 'span', split_axis=0, concat_axis=0, tiled=True)  22.8 us
    ppermute x2, waiting for transfers between devices, to_next(): return lax.ppermute(cells, ('span', 'elem'), pairs)  20.3 us
    pallas_call x2, Pallas kernels, project(): pl.pallas_call(kernel, in_specs=[whole, vmem] + ([] if first else [whole]...  16.2 us
    ppermute x4, waiting for transfers between devices, tiled_device(): sums = sums + lax.ppermute(sums, 'span', pairs)  14.9 us
    pallas_call x1, Pallas kernels, stiffness(): pl.pallas_call(kernel, in_specs=[vmem, vmem, vmem, vmem, pl.BlockSpec(mem...  10.5 us
    pallas_call x2, Pallas kernels, spread_blocks(): pl.pallas_call(kernel, in_specs=[whole] * kinds, out_specs=whole, out_sha...  8.79 us
  transfers between devices with their start and end apart: 16, of which 13 were waited for; matrix products, arithmetic and copies ran while one was open for 1% of the time, Pallas kernels for 12%

profile of v14, /device:TPU:15, one launch (start us, length us, event | category | flops | bytes accessed | tf_op | source)
XLA Modules:
  0.0 329.5 jit_solution(2313522068129712600)
XLA Ops:
  0.6 2.4 collective-permute-start
  3.0 6.2 %spread_blocks.3 = f32[16,192,512]{2,1,0:T(8,128)} custom-call(f32[1,64,10240]{2,1,0:T(8,128)} %refs_0_.3, f32[1,64,10240]{2,1,0:T(8,128)} %refs_1_.3, f32[1,64,10240]{2,1,0:T(8,128)} %refs_2_.3), custom_call_target="tpu_custom_call" | custom-call | tf_op jit(solution)/shard_map/spread_blocks/pallas_call | solution.py:190
  9.3 5.4 %all-to-all-start.1 = ((f32[16,192,512]{2,1,0:T(8,128)}), f32[16,192,512]{2,1,0:T(8,128)}, u32[]{:S(2)}, u32[]{:S(2)}) async-start(f32[16,192,512]{2,1,0:T(8,128)} %spread_blocks.3), calls=%async_computation.1 | async-start | bytes 12582912 | tf_op jit(solution)/shard_map/all_to_all | solution.py:50
  15.0 37.4 %collective-permute-done.1 = f32[2,64,192]{2,1,0:T(8,128)S(1)} collective-permute-done((f32[2,64,192]{2,1,0:T(8,128)S(1)}, f32[2,64,192]{2,1,0:T(8,128)S(1)}, u32[]{:S(2)}, u32[]{:S(2)}) %collective-permute-start.1) | collective-permute-done | bytes 98336 | tf_op jit(solution)/shard_map/ppermute | solution.py:553
  55.0 2.6 spread_blocks.2
  57.6 71.8 %collective-permute-done.3 = f32[2,2,2,64,192]{4,3,2,1,0:T(8,128)S(1)} collective-permute-done((f32[2,2,2,64,192]{4,3,2,1,0:T(8,128)S(1)}, f32[2,2,2,64,192]{4,3,2,1,0:T(8,128)S(1)}, u32[]{:S(2)}, u32[]{:S(2)}) %collective-permute-start.3) | collective-permute-done | bytes 393248 | tf_op jit(solution)/shard_map/ppermute | solution.py:553
  131.4 20.8 %all-to-all-done.1.x = f32[16,192,512]{2,1,0:T(8,128)} async-done(((f32[16,192,512]{2,1,0:T(8,128)}), f32[16,192,512]{2,1,0:T(8,128)}, u32[]{:S(2)}, u32[]{:S(2)}) %all-to-all-start.1) | async-done | bytes 6291488 | tf_op jit(solution)/shard_map/all_to_all | solution.py:50
  152.2 4.9 %all-to-all-start = ((f32[16,192,128]{2,1,0:T(8,128)}), f32[16,192,128]{2,1,0:T(8,128)S(1)}, u32[]{:S(2)}, u32[]{:S(2)}) async-start(f32[16,192,128]{2,1,0:T(8,128)} %spread_blocks.2), calls=%async_computation | async-start | bytes 3145728 | tf_op jit(solution)/shard_map/all_to_all | solution.py:50
  157.0 10.8 %project.2 = (f32[16,64,640]{2,1,0:T(8,128)}, f32[16,64,512]{2,1,0:T(8,128)}, f32[1,64,128]{2,1,0:T(8,128)}, f32[1,64,128]{2,1,0:T(8,128)}) custom-call(f32[16,192,512]{2,1,0:T(8,128)} %all-to-all-done.1.x, f32[16,64,192]{2,1,0:T(8,128)} %bitcast_multiply_fusion.rot), custom_call_target="tpu_custom_call" | custom-call | flops 1207959552 | bytes 10485760 | tf_op jit(solution)/shard_map/project/pallas_call | solution.py:384
  167.9 3.5 %collective-permute-start.4 = (f32[1,64,128]{2,1,0:T(8,128)}, f32[1,64,128]{2,1,0:T(8,128)S(1)}, u32[]{:S(2)}, u32[]{:S(2)}) collective-permute-start(f32[1,64,128]{2,1,0:T(8,128)} %get-tuple-element.29), channel_id=1, source_target_pairs={{0,2},{2,4},{4,6},{6,8},{8,10},{10,12},{12,14},{14,16},{16,18},{18... | collective-permute-start | bytes 98312 | tf_op jit(solution)/shard_map/ppermute | solution.py:59
  171.3 1.9 collective-permute-start.5
  173.3 18.6 %collective-permute-done.4.left = f32[1,64,128]{2,1,0:T(8,128)S(1)} collective-permute-done((f32[1,64,128]{2,1,0:T(8,128)}, f32[1,64,128]{2,1,0:T(8,128)S(1)}, u32[]{:S(2)}, u32[]{:S(2)}) %collective-permute-start.4) | collective-permute-done | bytes 32800 | tf_op jit(solution)/shard_map/ppermute | solution.py:59
  191.8 1.7 collective-permute-done.5.right
  193.5 1.2 copy-done.3
  194.7 5.0 %all-to-all-start.3 = ((f32[16,64,512]{2,1,0:T(8,128)}), f32[16,64,512]{2,1,0:T(8,128)S(1)}, u32[]{:S(2)}, u32[]{:S(2)}) async-start(f32[16,64,512]{2,1,0:T(8,128)} %get-tuple-element.37), calls=%async_computation.3 | async-start | bytes 4194304 | tf_op jit(solution)/shard_map/all_to_all | solution.py:50
  200.0 1.3 collective-permute-start.6
  202.1 2.5 collective-permute-done.6
  205.8 5.5 %project.3 = (f32[16,64,640]{2,1,0:T(8,128)}, f32[16,64,128]{2,1,0:T(8,128)}) custom-call(f32[16,192,128]{2,1,0:T(8,128)} %copy-done.3, f32[16,64,192]{2,1,0:T(8,128)} %bitcast_multiply_fusion.rot, f32[16,64,640]{2,1,0:T(8,128)} %get-tuple-element.26.refs_0_), custom_call_target="tpu_custom_call", output_to_operand_aliasing={{0}: (2, {})} | custom-call | flops 301989888 | bytes 2621440 | tf_op jit(solution)/shard_map/project/pallas_call | solution.py:384
  211.3 1.7 copy-done
  213.0 10.5 %stiffness.1 = (f32[16,64,640]{2,1,0:T(8,128)S(1)}, f32[2,1024]{1,0:T(2,128)S(1)}) custom-call(f32[16,64,640]{2,1,0:T(8,128)S(1)} %copy-done, f32[1,64,128]{2,1,0:T(8,128)S(1)} %collective-permute-done.4.left, f32[1,64,128]{2,1,0:T(8,128)S(1)} %collective-permute-done.5.right, f32[18,640]{1,0:T(8,128)S(1)} %concatenate.8.band, f32[16]{0:T(128)S(1)} %fusion.6.lam), custom_call_target="tpu_custom_call" | custom-call | tf_op jit(solution)/shard_map/stiffness/pallas_call | solution.py:467
  223.5 2.8 collective-permute-done.7
  226.3 2.1 collective-permute-start.8
  229.6 2.5 collective-permute-done.9
  232.1 3.2 collective-permute-done.10
  235.3 1.6 collective-permute-start.11
  236.9 8.3 %collective-permute-done.11 = f32[2,1024]{1,0:T(2,128)S(1)} collective-permute-done((f32[2,1024]{1,0:T(2,128)S(1)}, f32[2,1024]{1,0:T(2,128)S(1)}, u32[]{:S(2)}, u32[]{:S(2)}) %collective-permute-start.11) | collective-permute-done | bytes 8224 | tf_op jit(solution)/shard_map/ppermute | solution.py:616
  245.3 2.6 residual_back.1
  247.9 1.3 copy-done.2
  249.2 7.5 %all-to-all-start.2 = ((f32[16,64,768]{2,1,0:T(8,128)}), f32[16,64,768]{2,1,0:T(8,128)S(1)}, u32[]{:S(2)}, u32[]{:S(2)}) async-start(f32[16,64,768]{2,1,0:T(8,128)} %get-tuple-element.36), calls=%async_computation.2 | async-start | bytes 6291456 | tf_op jit(solution)/shard_map/all_to_all | solution.py:50
  257.3 2.8 collect_early.1._
  260.1 66.5 %all-to-all-done.2.last = f32[16,64,768]{2,1,0:T(8,128)S(1)} async-done(((f32[16,64,768]{2,1,0:T(8,128)}), f32[16,64,768]{2,1,0:T(8,128)S(1)}, u32[]{:S(2)}, u32[]{:S(2)}) %all-to-all-start.2) | async-done | bytes 3145760 | tf_op jit(solution)/shard_map/all_to_all | solution.py:50
  326.6 2.9 collect_late.1
  (57 shorter events, 8.8 us)
Async XLA Ops:
  0.6 8.6 %collective-permute-start = (f32[64,192]{1,0:T(8,128)}, f32[64,192]{1,0:T(8,128)S(1)}, u32[]{:S(2)}, u32[]{:S(2)}) collective-permute-start(f32[64,192]{1,0:T(8,128)} %bitcast.25), channel_id=1, source_target_pairs={{0,16},{2,18},{4,20},{6,22},{8,24},{10,26},{12,28},{14,30},{16,0},... | collective-permute-start | bytes 147464 | tf_op jit(solution)/shard_map/ppermute | solution.py:553
  3.0 6.2 %copy-start.4 = (f32[1,192,64]{1,2,0:T(8,128)S(1)}, f32[1,192,64]{1,2,0:T(8,128)}, u32[]{:S(2)}) copy-start(f32[1,192,64]{1,2,0:T(8,128)} %param.18) | copy-start | bytes 147460
  9.3 142.9 %all-to-all-start.1 = ((f32[16,192,512]{2,1,0:T(8,128)}), f32[16,192,512]{2,1,0:T(8,128)}, u32[]{:S(2)}, u32[]{:S(2)}) async-start(f32[16,192,512]{2,1,0:T(8,128)} %spread_blocks.3), calls=%async_computation.1 | async-start | bytes 12582912 | tf_op jit(solution)/shard_map/all_to_all | solution.py:50
  14.7 37.7 %collective-permute-start.1 = (f32[2,64,192]{2,1,0:T(8,128)S(1)}, f32[2,64,192]{2,1,0:T(8,128)S(1)}, u32[]{:S(2)}, u32[]{:S(2)}) collective-permute-start(f32[2,64,192]{2,1,0:T(8,128)S(1)} %pad_maximum_fusion.2), channel_id=1, source_target_pairs={{0,4},{2,6},{4,0},{6,2},{8,12},{10,14},{12,8},{14,10},{16,20},{18,... | collective-permute-start | bytes 294920 | tf_op jit(solution)/shard_map/ppermute | solution.py:553
  52.4 2.2 collective-permute-start.2
  54.7 74.8 %collective-permute-start.3 = (f32[2,2,2,64,192]{4,3,2,1,0:T(8,128)S(1)}, f32[2,2,2,64,192]{4,3,2,1,0:T(8,128)S(1)}, u32[]{:S(2)}, u32[]{:S(2)}) collective-permute-start(f32[2,2,2,64,192]{4,3,2,1,0:T(8,128)S(1)} %pad_maximum_fusion), channel_id=1, source_target_pairs={{0,8},{2,10},{4,12},{6,14},{8,0},{10,2},{12,4},{14,6},{16,24},{18,... | collective-permute-start | bytes 1179656 | tf_op jit(solution)/shard_map/ppermute | solution.py:553
  129.6 0.7 copy-start.8
  152.2 41.4 %all-to-all-start = ((f32[16,192,128]{2,1,0:T(8,128)}), f32[16,192,128]{2,1,0:T(8,128)S(1)}, u32[]{:S(2)}, u32[]{:S(2)}) async-start(f32[16,192,128]{2,1,0:T(8,128)} %spread_blocks.2), calls=%async_computation | async-start | bytes 3145728 | tf_op jit(solution)/shard_map/all_to_all | solution.py:50
  167.8 31.9 %copy-start.5 = (f32[10240]{0:T(1024)S(1)}, f32[10240]{0:T(1024)}, u32[]{:S(2)}) copy-start(f32[10240]{0:T(1024)} %param.14) | copy-start | bytes 122884
  167.8 31.9 %copy-start.6 = (f32[10240]{0:T(1024)S(1)}, f32[10240]{0:T(1024)}, u32[]{:S(2)}) copy-start(f32[10240]{0:T(1024)} %param.15) | copy-start | bytes 122884
  167.9 31.9 %copy-start.7 = (s32[10240]{0:T(1024)S(1)}, s32[10240]{0:T(1024)}, u32[]{:S(2)}) copy-start(s32[10240]{0:T(1024)} %param.16) | copy-start | bytes 122884
  167.9 24.0 %collective-permute-start.4 = (f32[1,64,128]{2,1,0:T(8,128)}, f32[1,64,128]{2,1,0:T(8,128)S(1)}, u32[]{:S(2)}, u32[]{:S(2)}) collective-permute-start(f32[1,64,128]{2,1,0:T(8,128)} %get-tuple-element.29), channel_id=1, source_target_pairs={{0,2},{2,4},{4,6},{6,8},{8,10},{10,12},{12,14},{14,16},{16,18},{18... | collective-permute-start | bytes 98312 | tf_op jit(solution)/shard_map/ppermute | solution.py:59
  171.3 22.2 %collective-permute-start.5 = (f32[1,64,128]{2,1,0:T(8,128)}, f32[1,64,128]{2,1,0:T(8,128)S(1)}, u32[]{:S(2)}, u32[]{:S(2)}) collective-permute-start(f32[1,64,128]{2,1,0:T(8,128)} %get-tuple-element.30), channel_id=1, source_target_pairs={{2,0},{4,2},{6,4},{8,6},{10,8},{12,10},{14,12},{16,14},{18,16},{20... | collective-permute-start | bytes 98312 | tf_op jit(solution)/shard_map/ppermute | solution.py:59
  193.5 1.2 copy-start.3
  194.7 53.1 %all-to-all-start.3 = ((f32[16,64,512]{2,1,0:T(8,128)}), f32[16,64,512]{2,1,0:T(8,128)S(1)}, u32[]{:S(2)}, u32[]{:S(2)}) async-start(f32[16,64,512]{2,1,0:T(8,128)} %get-tuple-element.37), calls=%async_computation.3 | async-start | bytes 4194304 | tf_op jit(solution)/shard_map/all_to_all | solution.py:50
  200.0 4.6 %collective-permute-start.6 = (f32[8,8]{1,0:T(8,128)S(1)}, f32[8,8]{1,0:T(8,128)S(1)}, u32[]{:S(2)}, u32[]{:S(2)}) collective-permute-start(f32[8,8]{1,0:T(8,128)S(1)} %slice.40), channel_id=1, source_target_pairs={{0,1},{2,3},{4,5},{6,7},{8,9},{10,11},{12,13},{14,15},{16,17},{18,... | collective-permute-start | bytes 776 | tf_op jit(solution)/shard_map/ppermute | solution.py:73
  211.3 1.7 copy-start
  213.0 32.2 %copy-start.1 = (f32[16,64,128]{2,1,0:T(8,128)S(1)}, f32[16,64,128]{2,1,0:T(8,128)}, u32[]{:S(2)}) copy-start(f32[16,64,128]{2,1,0:T(8,128)} %get-tuple-element.35.extra) | copy-start | bytes 1572868
  223.5 2.8 collective-permute-start.7
  226.3 2.9 collective-permute-start.8
  229.3 2.8 collective-permute-start.9
  232.1 3.3 collective-permute-start.10
  235.3 9.9 %collective-permute-start.11 = (f32[2,1024]{1,0:T(2,128)S(1)}, f32[2,1024]{1,0:T(2,128)S(1)}, u32[]{:S(2)}, u32[]{:S(2)}) collective-permute-start(f32[2,1024]{1,0:T(2,128)S(1)} %add.86), channel_id=1, source_target_pairs={{0,16},{2,18},{4,20},{6,22},{8,24},{10,26},{12,28},{14,30},{16,0},... | collective-permute-start | bytes 24584 | tf_op jit(solution)/shard_map/ppermute | solution.py:616
  247.9 1.3 copy-start.2
  249.2 77.4 %all-to-all-start.2 = ((f32[16,64,768]{2,1,0:T(8,128)}), f32[16,64,768]{2,1,0:T(8,128)S(1)}, u32[]{:S(2)}, u32[]{:S(2)}) async-start(f32[16,64,768]{2,1,0:T(8,128)} %get-tuple-element.36), calls=%async_computation.2 | async-start | bytes 6291456 | tf_op jit(solution)/shard_map/all_to_all | solution.py:50

commit v15 on v14

--- a/solution.py
+++ b/solution.py
@@ -592,9 +592,6 @@
     rotation = in_order(rotation, [steps[0]] + order)
     scales = jnp.array(slot_scales(count), jnp.float32)[:, None, None]
     rotation = rotation * scales
-    pieces = spread_blocks(blocks, count, [(at, LANES)])
-    pieces, rotation = lax.optimization_barrier((pieces, rotation))
-    stacked_late = exchange(pieces)
     weights, ground, link = coefficients(
         ground_spring, wire_tension, dropper_stiff, dropper_offset, span_link, count, dofs
     )
@@ -604,6 +601,9 @@
     diagonal = ground + jnp.sum(up, 0) + jnp.sum(down, 0)
     bands = jnp.concatenate([up, down, diagonal[None], link[None]])
     links = 2.0 * (1.0 - fourier_rows(count)[1])
+    pieces = spread_blocks(blocks, count, [(at, LANES)])
+    pieces, rotation, bands = lax.optimization_barrier((pieces, rotation, bands))
+    stacked_late = exchange(pieces)
     projected, spans, head, tail = project(stacked, rotation, dofs, early)
     before, after = to_next(tail, 1), to_next(head, -1)
     spans, before, after = lax.optimization_barrier((spans, before, after))

time: 330 us -> 331 us (level)
    ppermute x4, waiting for transfers between devices: 14.9 us -> 21.1 us  [tiled_device(): sums = sums + lax.ppermute(sums, 'span', pairs)]
    ppermute x4, waiting for transfers between devices: 110 us -> 107 us  [exchange_step(): other = lax.ppermute(held, 'span', pairs)]
  transfers between devices with their start and end apart: 16 -> 16, of which waited for: 13 -> 12; matrix products, arithmetic and copies ran while one was open for 1% -> 1% of each run, Pallas kernels for 12% -> 12%
where the time goes in v15:
time: 331 us; the launch traced here: 330 us
  waiting for transfers between devices  239 us (72%)
  Pallas kernels  43.9 us (13%)
  starting transfers between devices  37.2 us (11%)
  local copies, waits for them, and re-layouts  6.31 us (2%)
    ppermute x4, waiting for transfers between devices, exchange_step(): other = lax.ppermute(held, 'span', pairs)  107 us
    all_to_all x4, waiting for transfers between devices, exchange(): lax.all_to_all(pieces, 'span', split_axis=0, concat_axis=0, tiled=True)  87.3 us
    all_to_all x4, starting transfers between devices, exchange(): lax.all_to_all(pieces, 'span', split_axis=0, concat_axis=0, tiled=True)  22.9 us
    ppermute x4, waiting for transfers between devices, tiled_device(): sums = sums + lax.ppermute(sums, 'span', pairs)  21.1 us
    ppermute x2, waiting for transfers between devices, to_next(): return lax.ppermute(cells, ('span', 'elem'), pairs)  20.4 us
    pallas_call x2, Pallas kernels, project(): pl.pallas_call(kernel, in_specs=[whole, vmem] + ([] if first else [whole]...  16.3 us
    pallas_call x1, Pallas kernels, stiffness(): pl.pallas_call(kernel, in_specs=[vmem, vmem, vmem, vmem, pl.BlockSpec(mem...  10.6 us
    pallas_call x2, Pallas kernels, spread_blocks(): pl.pallas_call(kernel, in_specs=[whole] * kinds, out_specs=whole, out_sha...  8.8 us
  transfers between devices with their start and end apart: 16, of which 12 were waited for; matrix products, arithmetic and copies ran while one was open for 1% of the time, Pallas kernels for 12%

profile of v15, /device:TPU:15, one launch (start us, length us, event | category | flops | bytes accessed | tf_op | source)
XLA Modules:
  0.0 329.7 jit_solution(15298829025929360884)
XLA Ops:
  0.6 2.4 collective-permute-start
  3.0 6.2 %spread_blocks.3 = f32[16,192,512]{2,1,0:T(8,128)} custom-call(f32[1,64,10240]{2,1,0:T(8,128)} %refs_0_.3, f32[1,64,10240]{2,1,0:T(8,128)} %refs_1_.3, f32[1,64,10240]{2,1,0:T(8,128)} %refs_2_.3), custom_call_target="tpu_custom_call" | custom-call | tf_op jit(solution)/shard_map/spread_blocks/pallas_call | solution.py:190
  9.3 5.6 %all-to-all-start.1 = ((f32[16,192,512]{2,1,0:T(8,128)}), f32[16,192,512]{2,1,0:T(8,128)}, u32[]{:S(2)}, u32[]{:S(2)}) async-start(f32[16,192,512]{2,1,0:T(8,128)} %spread_blocks.3), calls=%async_computation.1 | async-start | bytes 12582912 | tf_op jit(solution)/shard_map/all_to_all | solution.py:50
  15.2 1.3 collective-permute-start.4
  16.5 2.6 spread_blocks.2
  20.3 32.3 %collective-permute-done.1 = f32[2,64,192]{2,1,0:T(8,128)S(1)} collective-permute-done((f32[2,64,192]{2,1,0:T(8,128)S(1)}, f32[2,64,192]{2,1,0:T(8,128)S(1)}, u32[]{:S(2)}, u32[]{:S(2)}) %collective-permute-start.1) | collective-permute-done | bytes 98336 | tf_op jit(solution)/shard_map/ppermute | solution.py:553
  56.2 73.5 %collective-permute-done.3 = f32[2,2,2,64,192]{4,3,2,1,0:T(8,128)S(1)} collective-permute-done((f32[2,2,2,64,192]{4,3,2,1,0:T(8,128)S(1)}, f32[2,2,2,64,192]{4,3,2,1,0:T(8,128)S(1)}, u32[]{:S(2)}, u32[]{:S(2)}) %collective-permute-start.3) | collective-permute-done | bytes 393248 | tf_op jit(solution)/shard_map/ppermute | solution.py:553
  130.4 1.1 bitcast_multiply_fusion.rot
  131.5 20.8 %all-to-all-done.1.x = f32[16,192,512]{2,1,0:T(8,128)} async-done(((f32[16,192,512]{2,1,0:T(8,128)}), f32[16,192,512]{2,1,0:T(8,128)}, u32[]{:S(2)}, u32[]{:S(2)}) %all-to-all-start.1) | async-done | bytes 6291488 | tf_op jit(solution)/shard_map/all_to_all | solution.py:50
  152.3 4.9 %all-to-all-start = ((f32[16,192,128]{2,1,0:T(8,128)}), f32[16,192,128]{2,1,0:T(8,128)S(1)}, u32[]{:S(2)}, u32[]{:S(2)}) async-start(f32[16,192,128]{2,1,0:T(8,128)} %spread_blocks.2), calls=%async_computation | async-start | bytes 3145728 | tf_op jit(solution)/shard_map/all_to_all | solution.py:50
  157.2 10.8 %project.2 = (f32[16,64,640]{2,1,0:T(8,128)}, f32[16,64,512]{2,1,0:T(8,128)}, f32[1,64,128]{2,1,0:T(8,128)}, f32[1,64,128]{2,1,0:T(8,128)}) custom-call(f32[16,192,512]{2,1,0:T(8,128)} %all-to-all-done.1.x, f32[16,64,192]{2,1,0:T(8,128)} %bitcast_multiply_fusion.rot), custom_call_target="tpu_custom_call" | custom-call | flops 1207959552 | bytes 10485760 | tf_op jit(solution)/shard_map/project/pallas_call | solution.py:384
  168.0 3.4 %collective-permute-start.5 = (f32[1,64,128]{2,1,0:T(8,128)}, f32[1,64,128]{2,1,0:T(8,128)S(1)}, u32[]{:S(2)}, u32[]{:S(2)}) collective-permute-start(f32[1,64,128]{2,1,0:T(8,128)} %get-tuple-element.30), channel_id=1, source_target_pairs={{0,2},{2,4},{4,6},{6,8},{8,10},{10,12},{12,14},{14,16},{16,18},{18... | collective-permute-start | bytes 98312 | tf_op jit(solution)/shard_map/ppermute | solution.py:59
  171.4 1.9 collective-permute-start.6
  173.3 18.7 %collective-permute-done.5.left = f32[1,64,128]{2,1,0:T(8,128)S(1)} collective-permute-done((f32[1,64,128]{2,1,0:T(8,128)}, f32[1,64,128]{2,1,0:T(8,128)S(1)}, u32[]{:S(2)}, u32[]{:S(2)}) %collective-permute-start.5) | collective-permute-done | bytes 32800 | tf_op jit(solution)/shard_map/ppermute | solution.py:59
  192.0 1.7 collective-permute-done.6.right
  193.7 1.2 copy-done.3
  194.9 5.0 %all-to-all-start.3 = ((f32[16,64,512]{2,1,0:T(8,128)}), f32[16,64,512]{2,1,0:T(8,128)S(1)}, u32[]{:S(2)}, u32[]{:S(2)}) async-start(f32[16,64,512]{2,1,0:T(8,128)} %get-tuple-element.39), calls=%async_computation.3 | async-start | bytes 4194304 | tf_op jit(solution)/shard_map/all_to_all | solution.py:50
  199.9 5.5 %project.3 = (f32[16,64,640]{2,1,0:T(8,128)}, f32[16,64,128]{2,1,0:T(8,128)}) custom-call(f32[16,192,128]{2,1,0:T(8,128)} %copy-done.3, f32[16,64,192]{2,1,0:T(8,128)} %bitcast_multiply_fusion.rot, f32[16,64,640]{2,1,0:T(8,128)} %get-tuple-element.27.refs_0_), custom_call_target="tpu_custom_call", output_to_operand_aliasing={{0}: (2, {})} | custom-call | flops 301989888 | bytes 2621440 | tf_op jit(solution)/shard_map/project/pallas_call | solution.py:384
  205.4 1.7 copy-done
  207.1 10.6 %stiffness.1 = (f32[16,64,640]{2,1,0:T(8,128)S(1)}, f32[2,1024]{1,0:T(2,128)S(1)}) custom-call(f32[16,64,640]{2,1,0:T(8,128)S(1)} %copy-done, f32[1,64,128]{2,1,0:T(8,128)S(1)} %collective-permute-done.5.left, f32[1,64,128]{2,1,0:T(8,128)S(1)} %collective-permute-done.6.right, f32[18,640]{1,0:T(8,128)S(1)} %concatenate.8.band, f32[16]{0:T(128)S(1)} %fusion.6.lam), custom_call_target="tpu_custom_call" | custom-call | tf_op jit(solution)/shard_map/stiffness/pallas_call | solution.py:467
  217.7 2.8 collective-permute-done.7
  220.5 1.2 collective-permute-start.8
  222.8 2.2 collective-permute-done.9
  225.1 1.5 collective-permute-start.10
  226.5 9.0 %collective-permute-done.10 = f32[2,1024]{1,0:T(2,128)S(1)} collective-permute-done((f32[2,1024]{1,0:T(2,128)S(1)}, f32[2,1024]{1,0:T(2,128)S(1)}, u32[]{:S(2)}, u32[]{:S(2)}) %collective-permute-start.10) | collective-permute-done | bytes 8224 | tf_op jit(solution)/shard_map/ppermute | solution.py:616
  236.3 9.1 %collective-permute-done.11 = f32[2,1024]{1,0:T(2,128)S(1)} collective-permute-done((f32[2,1024]{1,0:T(2,128)S(1)}, f32[2,1024]{1,0:T(2,128)S(1)}, u32[]{:S(2)}, u32[]{:S(2)}) %collective-permute-start.11) | collective-permute-done | bytes 8224 | tf_op jit(solution)/shard_map/ppermute | solution.py:616
  245.4 2.6 residual_back.1
  248.0 1.3 copy-done.2
  249.3 7.5 %all-to-all-start.2 = ((f32[16,64,768]{2,1,0:T(8,128)}), f32[16,64,768]{2,1,0:T(8,128)S(1)}, u32[]{:S(2)}, u32[]{:S(2)}) async-start(f32[16,64,768]{2,1,0:T(8,128)} %get-tuple-element.38), calls=%async_computation.2 | async-start | bytes 6291456 | tf_op jit(solution)/shard_map/all_to_all | solution.py:50
  257.5 2.8 collect_early.1._
  260.2 66.5 %all-to-all-done.2.last = f32[16,64,768]{2,1,0:T(8,128)S(1)} async-done(((f32[16,64,768]{2,1,0:T(8,128)}), f32[16,64,768]{2,1,0:T(8,128)S(1)}, u32[]{:S(2)}, u32[]{:S(2)}) %all-to-all-start.2) | async-done | bytes 3145760 | tf_op jit(solution)/shard_map/all_to_all | solution.py:50
  326.8 2.9 collect_late.1
  (57 shorter events, 8.4 us)
Async XLA Ops:
  0.6 8.6 %collective-permute-start = (f32[64,192]{1,0:T(8,128)}, f32[64,192]{1,0:T(8,128)S(1)}, u32[]{:S(2)}, u32[]{:S(2)}) collective-permute-start(f32[64,192]{1,0:T(8,128)} %bitcast.25), channel_id=1, source_target_pairs={{0,16},{2,18},{4,20},{6,22},{8,24},{10,26},{12,28},{14,30},{16,0},... | collective-permute-start | bytes 147464 | tf_op jit(solution)/shard_map/ppermute | solution.py:553
  3.0 6.2 %copy-start.4 = (f32[1,192,64]{1,2,0:T(8,128)S(1)}, f32[1,192,64]{1,2,0:T(8,128)}, u32[]{:S(2)}) copy-start(f32[1,192,64]{1,2,0:T(8,128)} %param.18) | copy-start | bytes 147460
  9.3 5.6 %copy-start.5 = (f32[10240]{0:T(1024)S(1)}, f32[10240]{0:T(1024)}, u32[]{:S(2)}) copy-start(f32[10240]{0:T(1024)} %param.14) | copy-start | bytes 122884
  9.3 5.6 %copy-start.6 = (f32[10240]{0:T(1024)S(1)}, f32[10240]{0:T(1024)}, u32[]{:S(2)}) copy-start(f32[10240]{0:T(1024)} %param.15) | copy-start | bytes 122884
  9.3 5.6 %copy-start.7 = (s32[10240]{0:T(1024)S(1)}, s32[10240]{0:T(1024)}, u32[]{:S(2)}) copy-start(s32[10240]{0:T(1024)} %param.16) | copy-start | bytes 122884
  9.3 143.0 %all-to-all-start.1 = ((f32[16,192,512]{2,1,0:T(8,128)}), f32[16,192,512]{2,1,0:T(8,128)}, u32[]{:S(2)}, u32[]{:S(2)}) async-start(f32[16,192,512]{2,1,0:T(8,128)} %spread_blocks.3), calls=%async_computation.1 | async-start | bytes 12582912 | tf_op jit(solution)/shard_map/all_to_all | solution.py:50
  15.2 5.0 %collective-permute-start.4 = (f32[8,8]{1,0:T(8,128)S(1)}, f32[8,8]{1,0:T(8,128)S(1)}, u32[]{:S(2)}, u32[]{:S(2)}) collective-permute-start(f32[8,8]{1,0:T(8,128)S(1)} %slice.40), channel_id=1, source_target_pairs={{0,1},{2,3},{4,5},{6,7},{8,9},{10,11},{12,13},{14,15},{16,17},{18,... | collective-permute-start | bytes 776 | tf_op jit(solution)/shard_map/ppermute | solution.py:73
  19.9 32.6 %collective-permute-start.1 = (f32[2,64,192]{2,1,0:T(8,128)S(1)}, f32[2,64,192]{2,1,0:T(8,128)S(1)}, u32[]{:S(2)}, u32[]{:S(2)}) collective-permute-start(f32[2,64,192]{2,1,0:T(8,128)S(1)} %pad_maximum_fusion.2), channel_id=1, source_target_pairs={{0,4},{2,6},{4,0},{6,2},{8,12},{10,14},{12,8},{14,10},{16,20},{18,... | collective-permute-start | bytes 294920 | tf_op jit(solution)/shard_map/ppermute | solution.py:553
  52.6 2.2 collective-permute-start.2
  54.9 74.8 %collective-permute-start.3 = (f32[2,2,2,64,192]{4,3,2,1,0:T(8,128)S(1)}, f32[2,2,2,64,192]{4,3,2,1,0:T(8,128)S(1)}, u32[]{:S(2)}, u32[]{:S(2)}) collective-permute-start(f32[2,2,2,64,192]{4,3,2,1,0:T(8,128)S(1)} %pad_maximum_fusion), channel_id=1, source_target_pairs={{0,8},{2,10},{4,12},{6,14},{8,0},{10,2},{12,4},{14,6},{16,24},{18,... | collective-permute-start | bytes 1179656 | tf_op jit(solution)/shard_map/ppermute | solution.py:553
  129.7 0.7 copy-start.8
  152.3 41.4 %all-to-all-start = ((f32[16,192,128]{2,1,0:T(8,128)}), f32[16,192,128]{2,1,0:T(8,128)S(1)}, u32[]{:S(2)}, u32[]{:S(2)}) async-start(f32[16,192,128]{2,1,0:T(8,128)} %spread_blocks.2), calls=%async_computation | async-start | bytes 3145728 | tf_op jit(solution)/shard_map/all_to_all | solution.py:50
  168.0 24.0 %collective-permute-start.5 = (f32[1,64,128]{2,1,0:T(8,128)}, f32[1,64,128]{2,1,0:T(8,128)S(1)}, u32[]{:S(2)}, u32[]{:S(2)}) collective-permute-start(f32[1,64,128]{2,1,0:T(8,128)} %get-tuple-element.30), channel_id=1, source_target_pairs={{0,2},{2,4},{4,6},{6,8},{8,10},{10,12},{12,14},{14,16},{16,18},{18... | collective-permute-start | bytes 98312 | tf_op jit(solution)/shard_map/ppermute | solution.py:59
  171.4 22.3 %collective-permute-start.6 = (f32[1,64,128]{2,1,0:T(8,128)}, f32[1,64,128]{2,1,0:T(8,128)S(1)}, u32[]{:S(2)}, u32[]{:S(2)}) collective-permute-start(f32[1,64,128]{2,1,0:T(8,128)} %get-tuple-element.31), channel_id=1, source_target_pairs={{2,0},{4,2},{6,4},{8,6},{10,8},{12,10},{14,12},{16,14},{18,16},{20... | collective-permute-start | bytes 98312 | tf_op jit(solution)/shard_map/ppermute | solution.py:59
  193.7 1.2 copy-start.3
  194.9 53.1 %all-to-all-start.3 = ((f32[16,64,512]{2,1,0:T(8,128)}), f32[16,64,512]{2,1,0:T(8,128)S(1)}, u32[]{:S(2)}, u32[]{:S(2)}) async-start(f32[16,64,512]{2,1,0:T(8,128)} %get-tuple-element.39), calls=%async_computation.3 | async-start | bytes 4194304 | tf_op jit(solution)/shard_map/all_to_all | solution.py:50
  205.4 1.7 copy-start
  207.1 38.3 %copy-start.1 = (f32[16,64,128]{2,1,0:T(8,128)S(1)}, f32[16,64,128]{2,1,0:T(8,128)}, u32[]{:S(2)}) copy-start(f32[16,64,128]{2,1,0:T(8,128)} %get-tuple-element.37.extra) | copy-start | bytes 1572868
  217.7 2.8 collective-permute-start.7
  220.5 2.0 collective-permute-start.8
  222.6 2.5 collective-permute-start.9
  225.1 10.5 %collective-permute-start.10 = (f32[2,1024]{1,0:T(2,128)S(1)}, f32[2,1024]{1,0:T(2,128)S(1)}, u32[]{:S(2)}, u32[]{:S(2)}) collective-permute-start(f32[2,1024]{1,0:T(2,128)S(1)} %add.85), channel_id=1, source_target_pairs={{0,8},{2,10},{4,12},{6,14},{8,0},{10,2},{12,4},{14,6},{16,24},{18,... | collective-permute-start | bytes 24584 | tf_op jit(solution)/shard_map/ppermute | solution.py:616
  235.6 9.9 %collective-permute-start.11 = (f32[2,1024]{1,0:T(2,128)S(1)}, f32[2,1024]{1,0:T(2,128)S(1)}, u32[]{:S(2)}, u32[]{:S(2)}) collective-permute-start(f32[2,1024]{1,0:T(2,128)S(1)} %add.86), channel_id=1, source_target_pairs={{0,16},{2,18},{4,20},{6,22},{8,24},{10,26},{12,28},{14,30},{16,0},... | collective-permute-start | bytes 24584 | tf_op jit(solution)/shard_map/ppermute | solution.py:616
  248.0 1.3 copy-start.2
  249.3 77.4 %all-to-all-start.2 = ((f32[16,64,768]{2,1,0:T(8,128)}), f32[16,64,768]{2,1,0:T(8,128)S(1)}, u32[]{:S(2)}, u32[]{:S(2)}) async-start(f32[16,64,768]{2,1,0:T(8,128)} %get-tuple-element.38), calls=%async_computation.2 | async-start | bytes 6291456 | tf_op jit(solution)/shard_map/all_to_all | solution.py:50

commit v16 on v15

--- a/solution.py
+++ b/solution.py
@@ -227,21 +227,25 @@
 def collect_late(late, block, middle):
     count, rows, width = late.shape
     dofs = width - LANES
-    many = max(n for n in (1, 2, 4, 8) if count % n == 0)
 
     def kernel(last, _, residual, whole, sem):
         copies = []
-        for i in range(many):
-            at = (pl.program_id(0) * many + i) * dofs + middle
-            copy = pltpu.make_async_copy(
-                last.at[i, :, pl.ds(dofs, LANES)],
-                whole.at[0, :, pl.ds(pl.multiple_of(at, LANES), LANES)],
-                sem.at[i],
+        for i in range(count):
+            at = i * dofs + middle
+            copies.append(
+                pltpu.make_async_copy(
+                    last.at[i, :, :dofs],
+                    residual.at[0, :, i * dofs : (i + 1) * dofs],
+                    sem.at[2 * i],
+                )
             )
+            copies.append(
+                pltpu.make_async_copy(
+                    last.at[i, :, dofs:width], whole.at[0, :, at : at + LANES], sem.at[2 * i + 1]
+                )
+            )
+        for copy in copies:
             copy.start()
-            copies.append(copy)
-        for i in range(many):
-            residual[0, :, i * dofs : (i + 1) * dofs] = last[i, :, :dofs]
         for copy in copies:
             copy.wait()
 
@@ -249,12 +253,11 @@
     shape = pltpu.HBM((1, rows, count * dofs), jnp.float32)
     return pl.pallas_call(
         kernel,
-        grid=(count // many,),
-        in_specs=[pl.BlockSpec((many, rows, width), lambda i: (i, 0, 0)), place],
-        out_specs=[pl.BlockSpec((1, rows, many * dofs), lambda i: (0, 0, i)), place],
+        in_specs=[pl.BlockSpec(memory_space=pltpu.VMEM), place],
+        out_specs=[place, place],
         out_shape=[shape, shape],
         input_output_aliases={1: 1},
-        scratch_shapes=[pltpu.SemaphoreType.DMA((many,))],
+        scratch_shapes=[pltpu.SemaphoreType.DMA((2 * count,))],
         compiler_params=params(),
         name="collect_late",
     )(late, block)
@@ -397,7 +400,7 @@
             pltpu.SemaphoreType.DMA((2 * len(tiles),)),
         ]
         + [pltpu.VMEM((count, wide, width), jnp.bfloat16)] * PARTS,
-        compiler_params=params(VMEM_MOST),
+        compiler_params=params(65_400_000),
         name="project",
     )(stacked, rotation, *(() if first else (prior,)))
 
@@ -537,7 +540,7 @@
             pltpu.VMEM((count, rows, dofs), jnp.float32),
             pltpu.SemaphoreType.DMA((tiles + 1,)),
         ],
-        compiler_params=params(),
+        compiler_params=params(60_500_000),
         name="residual_back",
     )(projected, stiff, sums, late)
 

time: 331 us -> 331 us (level)
  transfers between devices with their start and end apart: 16 -> 16, of which waited for: 12 -> 12; matrix products, arithmetic and copies ran while one was open for 1% -> 2% of each run, Pallas kernels for 12% -> 13%
where the time goes in v16:
time: 331 us; the launch traced here: 330 us
  waiting for transfers between devices  237 us (72%)
  Pallas kernels  46.4 us (14%)
  starting transfers between devices  36 us (11%)
  local copies, waits for them, and re-layouts  5.96 us (2%)
  other arithmetic  3.4 us (1%)
    ppermute x4, waiting for transfers between devices, exchange_step(): other = lax.ppermute(held, 'span', pairs)  107 us
    all_to_all x4, waiting for transfers between devices, exchange(): lax.all_to_all(pieces, 'span', split_axis=0, concat_axis=0, tiled=True)  86.7 us
    all_to_all x4, starting transfers between devices, exchange(): lax.all_to_all(pieces, 'span', split_axis=0, concat_axis=0, tiled=True)  23.1 us
    ppermute x4, waiting for transfers between devices, tiled_device(): sums = sums + lax.ppermute(sums, 'span', pairs)  20.6 us
    ppermute x2, waiting for transfers between devices, to_next(): return lax.ppermute(cells, ('span', 'elem'), pairs)  20.4 us
    pallas_call x2, Pallas kernels, project(): pl.pallas_call(kernel, in_specs=[whole, vmem] + ([] if first else [whole]...  16.3 us
    pallas_call x1, Pallas kernels, stiffness(): pl.pallas_call(kernel, in_specs=[vmem, vmem, vmem, vmem, pl.BlockSpec(mem...  10.9 us
    pallas_call x2, Pallas kernels, spread_blocks(): pl.pallas_call(kernel, in_specs=[whole] * kinds, out_specs=whole, out_sha...  8.77 us
  transfers between devices with their start and end apart: 16, of which 12 were waited for; matrix products, arithmetic and copies ran while one was open for 2% of the time, Pallas kernels for 13%

profile of v16, /device:TPU:15, one launch (start us, length us, event | category | flops | bytes accessed | tf_op | source)
XLA Modules:
  0.0 330.1 jit_solution(10868631696266793162)
XLA Ops:
  0.6 2.4 collective-permute-start
  3.0 6.2 %spread_blocks.3 = f32[16,192,512]{2,1,0:T(8,128)} custom-call(f32[1,64,10240]{2,1,0:T(8,128)} %refs_0_.3, f32[1,64,10240]{2,1,0:T(8,128)} %refs_1_.3, f32[1,64,10240]{2,1,0:T(8,128)} %refs_2_.3), custom_call_target="tpu_custom_call" | custom-call | tf_op jit(solution)/shard_map/spread_blocks/pallas_call | solution.py:190
  9.3 5.6 %all-to-all-start.1 = ((f32[16,192,512]{2,1,0:T(8,128)}), f32[16,192,512]{2,1,0:T(8,128)}, u32[]{:S(2)}, u32[]{:S(2)}) async-start(f32[16,192,512]{2,1,0:T(8,128)} %spread_blocks.3), calls=%async_computation.1 | async-start | bytes 12582912 | tf_op jit(solution)/shard_map/all_to_all | solution.py:50
  15.2 1.3 collective-permute-start.4
  16.5 2.6 spread_blocks.2
  20.2 32.3 %collective-permute-done.1 = f32[2,64,192]{2,1,0:T(8,128)S(1)} collective-permute-done((f32[2,64,192]{2,1,0:T(8,128)S(1)}, f32[2,64,192]{2,1,0:T(8,128)S(1)}, u32[]{:S(2)}, u32[]{:S(2)}) %collective-permute-start.1) | collective-permute-done | bytes 98336 | tf_op jit(solution)/shard_map/ppermute | solution.py:556
  53.7 1.1 collective-permute-done.2
  56.2 73.5 %collective-permute-done.3 = f32[2,2,2,64,192]{4,3,2,1,0:T(8,128)S(1)} collective-permute-done((f32[2,2,2,64,192]{4,3,2,1,0:T(8,128)S(1)}, f32[2,2,2,64,192]{4,3,2,1,0:T(8,128)S(1)}, u32[]{:S(2)}, u32[]{:S(2)}) %collective-permute-start.3) | collective-permute-done | bytes 393248 | tf_op jit(solution)/shard_map/ppermute | solution.py:556
  130.5 1.1 bitcast_multiply_fusion.rot
  131.6 20.8 %all-to-all-done.1.x = f32[16,192,512]{2,1,0:T(8,128)} async-done(((f32[16,192,512]{2,1,0:T(8,128)}), f32[16,192,512]{2,1,0:T(8,128)}, u32[]{:S(2)}, u32[]{:S(2)}) %all-to-all-start.1) | async-done | bytes 6291488 | tf_op jit(solution)/shard_map/all_to_all | solution.py:50
  152.4 4.9 %all-to-all-start = ((f32[16,192,128]{2,1,0:T(8,128)}), f32[16,192,128]{2,1,0:T(8,128)}, u32[]{:S(2)}, u32[]{:S(2)}) async-start(f32[16,192,128]{2,1,0:T(8,128)} %spread_blocks.2), calls=%async_computation | async-start | bytes 3145728 | tf_op jit(solution)/shard_map/all_to_all | solution.py:50
  157.2 10.8 %project.2 = (f32[16,64,640]{2,1,0:T(8,128)}, f32[16,64,512]{2,1,0:T(8,128)}, f32[1,64,128]{2,1,0:T(8,128)}, f32[1,64,128]{2,1,0:T(8,128)}) custom-call(f32[16,192,512]{2,1,0:T(8,128)} %all-to-all-done.1.x, f32[16,64,192]{2,1,0:T(8,128)} %bitcast_multiply_fusion.rot), custom_call_target="tpu_custom_call" | custom-call | flops 1207959552 | bytes 10485760 | tf_op jit(solution)/shard_map/project/pallas_call | solution.py:387
  168.1 3.3 %collective-permute-start.5 = (f32[1,64,128]{2,1,0:T(8,128)}, f32[1,64,128]{2,1,0:T(8,128)S(1)}, u32[]{:S(2)}, u32[]{:S(2)}) collective-permute-start(f32[1,64,128]{2,1,0:T(8,128)} %get-tuple-element.30), channel_id=1, source_target_pairs={{0,2},{2,4},{4,6},{6,8},{8,10},{10,12},{12,14},{14,16},{16,18},{18... | collective-permute-start | bytes 98312 | tf_op jit(solution)/shard_map/ppermute | solution.py:59
  171.4 1.9 collective-permute-start.6
  173.4 18.7 %collective-permute-done.5.left = f32[1,64,128]{2,1,0:T(8,128)S(1)} collective-permute-done((f32[1,64,128]{2,1,0:T(8,128)}, f32[1,64,128]{2,1,0:T(8,128)S(1)}, u32[]{:S(2)}, u32[]{:S(2)}) %collective-permute-start.5) | collective-permute-done | bytes 32800 | tf_op jit(solution)/shard_map/ppermute | solution.py:59
  192.0 1.7 collective-permute-done.6.right
  193.7 5.1 %all-to-all-start.3 = ((f32[16,64,512]{2,1,0:T(8,128)}), f32[16,64,512]{2,1,0:T(8,128)}, u32[]{:S(2)}, u32[]{:S(2)}) async-start(f32[16,64,512]{2,1,0:T(8,128)} %get-tuple-element.39), calls=%async_computation.3 | async-start | bytes 4194304 | tf_op jit(solution)/shard_map/all_to_all | solution.py:50
  198.8 5.5 %project.3 = (f32[16,64,640]{2,1,0:T(8,128)}, f32[16,64,128]{2,1,0:T(8,128)}) custom-call(f32[16,192,128]{2,1,0:T(8,128)} %all-to-all-done.x, f32[16,64,192]{2,1,0:T(8,128)} %bitcast_multiply_fusion.rot, f32[16,64,640]{2,1,0:T(8,128)} %get-tuple-element.27.refs_0_), custom_call_target="tpu_custom_call", output_to_operand_aliasing={{0}: (2, {})} | custom-call | flops 301989888 | bytes 2621440 | tf_op jit(solution)/shard_map/project/pallas_call | solution.py:387
  204.3 1.7 copy-done
  206.1 10.9 %stiffness.1 = (f32[16,64,640]{2,1,0:T(8,128)S(1)}, f32[2,1024]{1,0:T(2,128)S(1)}) custom-call(f32[16,64,640]{2,1,0:T(8,128)S(1)} %copy-done, f32[1,64,128]{2,1,0:T(8,128)S(1)} %collective-permute-done.5.left, f32[1,64,128]{2,1,0:T(8,128)S(1)} %collective-permute-done.6.right, f32[18,640]{1,0:T(8,128)S(1)} %concatenate.8.band, f32[16]{0:T(128)S(1)} %fusion.6.lam), custom_call_target="tpu_custom_call" | custom-call | tf_op jit(solution)/shard_map/stiffness/pallas_call | solution.py:470
  217.0 1.5 copy-done.1
  218.5 2.9 collective-permute-done.7
  221.4 1.1 collective-permute-start.8
  223.6 2.6 collective-permute-done.9
  226.5 8.0 %collective-permute-done.10 = f32[2,1024]{1,0:T(2,128)S(1)} collective-permute-done((f32[2,1024]{1,0:T(2,128)S(1)}, f32[2,1024]{1,0:T(2,128)S(1)}, u32[]{:S(2)}, u32[]{:S(2)}) %collective-permute-start.10) | collective-permute-done | bytes 8224 | tf_op jit(solution)/shard_map/ppermute | solution.py:619
  235.3 9.1 %collective-permute-done.11 = f32[2,1024]{1,0:T(2,128)S(1)} collective-permute-done((f32[2,1024]{1,0:T(2,128)S(1)}, f32[2,1024]{1,0:T(2,128)S(1)}, u32[]{:S(2)}, u32[]{:S(2)}) %collective-permute-start.11) | collective-permute-done | bytes 8224 | tf_op jit(solution)/shard_map/ppermute | solution.py:619
  245.0 5.8 %residual_back.1 = (f32[16,64,768]{2,1,0:T(8,128)}, f32[1,1024]{1,0:T(1,128)}) custom-call(f32[16,64,640]{2,1,0:T(8,128)} %get-tuple-element.28.x, f32[16,64,640]{2,1,0:T(8,128)} %copy-done.1, f32[2,1024]{1,0:T(2,128)} %add.87.total, f32[16,64,128]{2,1,0:T(8,128)} %get-tuple-element.37.extra), custom_call_target="tpu_custom_call" | custom-call | tf_op jit(solution)/shard_map/residual_back/pallas_call | solution.py:530
  250.7 7.6 %all-to-all-start.2 = ((f32[16,64,768]{2,1,0:T(8,128)}), f32[16,64,768]{2,1,0:T(8,128)S(1)}, u32[]{:S(2)}, u32[]{:S(2)}) async-start(f32[16,64,768]{2,1,0:T(8,128)} %get-tuple-element.38), calls=%async_computation.2 | async-start | bytes 6291456 | tf_op jit(solution)/shard_map/all_to_all | solution.py:50
  258.3 1.2 constant_dynamic-slice_fusion
  259.5 2.8 collect_early.1._
  262.3 65.9 %all-to-all-done.2.last = f32[16,64,768]{2,1,0:T(8,128)S(1)} async-done(((f32[16,64,768]{2,1,0:T(8,128)}), f32[16,64,768]{2,1,0:T(8,128)S(1)}, u32[]{:S(2)}, u32[]{:S(2)}) %all-to-all-start.2) | async-done | bytes 3145760 | tf_op jit(solution)/shard_map/all_to_all | solution.py:50
  328.2 1.9 collect_late.1
  (53 shorter events, 7.5 us)
Async XLA Ops:
  0.6 8.6 %collective-permute-start = (f32[64,192]{1,0:T(8,128)}, f32[64,192]{1,0:T(8,128)S(1)}, u32[]{:S(2)}, u32[]{:S(2)}) collective-permute-start(f32[64,192]{1,0:T(8,128)} %bitcast.25), channel_id=1, source_target_pairs={{0,16},{2,18},{4,20},{6,22},{8,24},{10,26},{12,28},{14,30},{16,0},... | collective-permute-start | bytes 147464 | tf_op jit(solution)/shard_map/ppermute | solution.py:556
  3.0 6.2 %copy-start.2 = (f32[1,192,64]{1,2,0:T(8,128)S(1)}, f32[1,192,64]{1,2,0:T(8,128)}, u32[]{:S(2)}) copy-start(f32[1,192,64]{1,2,0:T(8,128)} %param.18) | copy-start | bytes 147460
  9.3 5.7 %copy-start.3 = (f32[10240]{0:T(1024)S(1)}, f32[10240]{0:T(1024)}, u32[]{:S(2)}) copy-start(f32[10240]{0:T(1024)} %param.14) | copy-start | bytes 122884
  9.3 5.7 %copy-start.4 = (f32[10240]{0:T(1024)S(1)}, f32[10240]{0:T(1024)}, u32[]{:S(2)}) copy-start(f32[10240]{0:T(1024)} %param.15) | copy-start | bytes 122884
  9.3 5.7 %copy-start.5 = (s32[10240]{0:T(1024)S(1)}, s32[10240]{0:T(1024)}, u32[]{:S(2)}) copy-start(s32[10240]{0:T(1024)} %param.16) | copy-start | bytes 122884
  9.3 143.0 %all-to-all-start.1 = ((f32[16,192,512]{2,1,0:T(8,128)}), f32[16,192,512]{2,1,0:T(8,128)}, u32[]{:S(2)}, u32[]{:S(2)}) async-start(f32[16,192,512]{2,1,0:T(8,128)} %spread_blocks.3), calls=%async_computation.1 | async-start | bytes 12582912 | tf_op jit(solution)/shard_map/all_to_all | solution.py:50
  15.2 4.9 %collective-permute-start.4 = (f32[8,8]{1,0:T(8,128)S(1)}, f32[8,8]{1,0:T(8,128)S(1)}, u32[]{:S(2)}, u32[]{:S(2)}) collective-permute-start(f32[8,8]{1,0:T(8,128)S(1)} %slice.40), channel_id=1, source_target_pairs={{0,1},{2,3},{4,5},{6,7},{8,9},{10,11},{12,13},{14,15},{16,17},{18,... | collective-permute-start | bytes 776 | tf_op jit(solution)/shard_map/ppermute | solution.py:73
  19.9 32.7 %collective-permute-start.1 = (f32[2,64,192]{2,1,0:T(8,128)S(1)}, f32[2,64,192]{2,1,0:T(8,128)S(1)}, u32[]{:S(2)}, u32[]{:S(2)}) collective-permute-start(f32[2,64,192]{2,1,0:T(8,128)S(1)} %pad_maximum_fusion.2), channel_id=1, source_target_pairs={{0,4},{2,6},{4,0},{6,2},{8,12},{10,14},{12,8},{14,10},{16,20},{18,... | collective-permute-start | bytes 294920 | tf_op jit(solution)/shard_map/ppermute | solution.py:556
  52.6 2.2 collective-permute-start.2
  54.9 74.8 %collective-permute-start.3 = (f32[2,2,2,64,192]{4,3,2,1,0:T(8,128)S(1)}, f32[2,2,2,64,192]{4,3,2,1,0:T(8,128)S(1)}, u32[]{:S(2)}, u32[]{:S(2)}) collective-permute-start(f32[2,2,2,64,192]{4,3,2,1,0:T(8,128)S(1)} %pad_maximum_fusion), channel_id=1, source_target_pairs={{0,8},{2,10},{4,12},{6,14},{8,0},{10,2},{12,4},{14,6},{16,24},{18,... | collective-permute-start | bytes 1179656 | tf_op jit(solution)/shard_map/ppermute | solution.py:556
  129.8 0.7 copy-start.6
  152.4 41.4 %all-to-all-start = ((f32[16,192,128]{2,1,0:T(8,128)}), f32[16,192,128]{2,1,0:T(8,128)}, u32[]{:S(2)}, u32[]{:S(2)}) async-start(f32[16,192,128]{2,1,0:T(8,128)} %spread_blocks.2), calls=%async_computation | async-start | bytes 3145728 | tf_op jit(solution)/shard_map/all_to_all | solution.py:50
  168.1 24.0 %collective-permute-start.5 = (f32[1,64,128]{2,1,0:T(8,128)}, f32[1,64,128]{2,1,0:T(8,128)S(1)}, u32[]{:S(2)}, u32[]{:S(2)}) collective-permute-start(f32[1,64,128]{2,1,0:T(8,128)} %get-tuple-element.30), channel_id=1, source_target_pairs={{0,2},{2,4},{4,6},{6,8},{8,10},{10,12},{12,14},{14,16},{16,18},{18... | collective-permute-start | bytes 98312 | tf_op jit(solution)/shard_map/ppermute | solution.py:59
  171.4 22.3 %collective-permute-start.6 = (f32[1,64,128]{2,1,0:T(8,128)}, f32[1,64,128]{2,1,0:T(8,128)S(1)}, u32[]{:S(2)}, u32[]{:S(2)}) collective-permute-start(f32[1,64,128]{2,1,0:T(8,128)} %get-tuple-element.31), channel_id=1, source_target_pairs={{2,0},{4,2},{6,4},{8,6},{10,8},{12,10},{14,12},{16,14},{18,16},{20... | collective-permute-start | bytes 98312 | tf_op jit(solution)/shard_map/ppermute | solution.py:59
  193.7 57.0 %all-to-all-start.3 = ((f32[16,64,512]{2,1,0:T(8,128)}), f32[16,64,512]{2,1,0:T(8,128)}, u32[]{:S(2)}, u32[]{:S(2)}) async-start(f32[16,64,512]{2,1,0:T(8,128)} %get-tuple-element.39), calls=%async_computation.3 | async-start | bytes 4194304 | tf_op jit(solution)/shard_map/all_to_all | solution.py:50
  204.3 1.7 copy-start
  217.0 1.5 copy-start.1
  218.5 2.9 collective-permute-start.7
  221.4 1.9 collective-permute-start.8
  223.3 2.9 collective-permute-start.9
  226.2 8.3 %collective-permute-start.10 = (f32[2,1024]{1,0:T(2,128)S(1)}, f32[2,1024]{1,0:T(2,128)S(1)}, u32[]{:S(2)}, u32[]{:S(2)}) collective-permute-start(f32[2,1024]{1,0:T(2,128)S(1)} %add.85), channel_id=1, source_target_pairs={{0,8},{2,10},{4,12},{6,14},{8,0},{10,2},{12,4},{14,6},{16,24},{18,... | collective-permute-start | bytes 24584 | tf_op jit(solution)/shard_map/ppermute | solution.py:619
  234.6 9.8 %collective-permute-start.11 = (f32[2,1024]{1,0:T(2,128)S(1)}, f32[2,1024]{1,0:T(2,128)S(1)}, u32[]{:S(2)}, u32[]{:S(2)}) collective-permute-start(f32[2,1024]{1,0:T(2,128)S(1)} %add.86), channel_id=1, source_target_pairs={{0,16},{2,18},{4,20},{6,22},{8,24},{10,26},{12,28},{14,30},{16,0},... | collective-permute-start | bytes 24584 | tf_op jit(solution)/shard_map/ppermute | solution.py:619
  250.7 77.4 %all-to-all-start.2 = ((f32[16,64,768]{2,1,0:T(8,128)}), f32[16,64,768]{2,1,0:T(8,128)S(1)}, u32[]{:S(2)}, u32[]{:S(2)}) async-start(f32[16,64,768]{2,1,0:T(8,128)} %get-tuple-element.38), calls=%async_computation.2 | async-start | bytes 6291456 | tf_op jit(solution)/shard_map/all_to_all | solution.py:50

commit v17 on v16

--- a/solution.py
+++ b/solution.py
@@ -540,7 +540,7 @@
             pltpu.VMEM((count, rows, dofs), jnp.float32),
             pltpu.SemaphoreType.DMA((tiles + 1,)),
         ],
-        compiler_params=params(60_500_000),
+        compiler_params=params(57_400_000),
         name="residual_back",
     )(projected, stiff, sums, late)
 

time: 331 us -> 331 us (level)
  no operation moved by 1% of the time
where the time goes in v17:
time: 331 us; the launch traced here: 330 us
  waiting for transfers between devices  237 us (72%)
  Pallas kernels  46.4 us (14%)
  starting transfers between devices  36 us (11%)
  local copies, waits for them, and re-layouts  5.96 us (2%)
  other arithmetic  3.4 us (1%)
    ppermute x4, waiting for transfers between devices, exchange_step(): other = lax.ppermute(held, 'span', pairs)  107 us
    all_to_all x4, waiting for transfers between devices, exchange(): lax.all_to_all(pieces, 'span', split_axis=0, concat_axis=0, tiled=True)  86.7 us
    all_to_all x4, starting transfers between devices, exchange(): lax.all_to_all(pieces, 'span', split_axis=0, concat_axis=0, tiled=True)  23.1 us
    ppermute x4, waiting for transfers between devices, tiled_device(): sums = sums + lax.ppermute(sums, 'span', pairs)  20.6 us
    ppermute x2, waiting for transfers between devices, to_next(): return lax.ppermute(cells, ('span', 'elem'), pairs)  20.4 us
    pallas_call x2, Pallas kernels, project(): pl.pallas_call(kernel, in_specs=[whole, vmem] + ([] if first else [whole]...  16.3 us
    pallas_call x1, Pallas kernels, stiffness(): pl.pallas_call(kernel, in_specs=[vmem, vmem, vmem, vmem, pl.BlockSpec(mem...  10.9 us
    pallas_call x2, Pallas kernels, spread_blocks(): pl.pallas_call(kernel, in_specs=[whole] * kinds, out_specs=whole, out_sha...  8.77 us
  transfers between devices with their start and end apart: 16, of which 12 were waited for; matrix products, arithmetic and copies ran while one was open for 2% of the time, Pallas kernels for 13%

profile of v17, /device:TPU:15, one launch (start us, length us, event | category | flops | bytes accessed | tf_op | source)
XLA Modules:
  0.0 330.1 jit_solution(10868631696266793162)
XLA Ops:
  0.6 2.4 collective-permute-start
  3.0 6.2 %spread_blocks.3 = f32[16,192,512]{2,1,0:T(8,128)} custom-call(f32[1,64,10240]{2,1,0:T(8,128)} %refs_0_.3, f32[1,64,10240]{2,1,0:T(8,128)} %refs_1_.3, f32[1,64,10240]{2,1,0:T(8,128)} %refs_2_.3), custom_call_target="tpu_custom_call" | custom-call | tf_op jit(solution)/shard_map/spread_blocks/pallas_call | solution.py:190
  9.3 5.6 %all-to-all-start.1 = ((f32[16,192,512]{2,1,0:T(8,128)}), f32[16,192,512]{2,1,0:T(8,128)}, u32[]{:S(2)}, u32[]{:S(2)}) async-start(f32[16,192,512]{2,1,0:T(8,128)} %spread_blocks.3), calls=%async_computation.1 | async-start | bytes 12582912 | tf_op jit(solution)/shard_map/all_to_all | solution.py:50
  15.2 1.3 collective-permute-start.4
  16.5 2.6 spread_blocks.2
  20.2 32.3 %collective-permute-done.1 = f32[2,64,192]{2,1,0:T(8,128)S(1)} collective-permute-done((f32[2,64,192]{2,1,0:T(8,128)S(1)}, f32[2,64,192]{2,1,0:T(8,128)S(1)}, u32[]{:S(2)}, u32[]{:S(2)}) %collective-permute-start.1) | collective-permute-done | bytes 98336 | tf_op jit(solution)/shard_map/ppermute | solution.py:556
  53.7 1.1 collective-permute-done.2
  56.2 73.5 %collective-permute-done.3 = f32[2,2,2,64,192]{4,3,2,1,0:T(8,128)S(1)} collective-permute-done((f32[2,2,2,64,192]{4,3,2,1,0:T(8,128)S(1)}, f32[2,2,2,64,192]{4,3,2,1,0:T(8,128)S(1)}, u32[]{:S(2)}, u32[]{:S(2)}) %collective-permute-start.3) | collective-permute-done | bytes 393248 | tf_op jit(solution)/shard_map/ppermute | solution.py:556
  130.5 1.1 bitcast_multiply_fusion.rot
  131.6 20.8 %all-to-all-done.1.x = f32[16,192,512]{2,1,0:T(8,128)} async-done(((f32[16,192,512]{2,1,0:T(8,128)}), f32[16,192,512]{2,1,0:T(8,128)}, u32[]{:S(2)}, u32[]{:S(2)}) %all-to-all-start.1) | async-done | bytes 6291488 | tf_op jit(solution)/shard_map/all_to_all | solution.py:50
  152.4 4.9 %all-to-all-start = ((f32[16,192,128]{2,1,0:T(8,128)}), f32[16,192,128]{2,1,0:T(8,128)}, u32[]{:S(2)}, u32[]{:S(2)}) async-start(f32[16,192,128]{2,1,0:T(8,128)} %spread_blocks.2), calls=%async_computation | async-start | bytes 3145728 | tf_op jit(solution)/shard_map/all_to_all | solution.py:50
  157.2 10.8 %project.2 = (f32[16,64,640]{2,1,0:T(8,128)}, f32[16,64,512]{2,1,0:T(8,128)}, f32[1,64,128]{2,1,0:T(8,128)}, f32[1,64,128]{2,1,0:T(8,128)}) custom-call(f32[16,192,512]{2,1,0:T(8,128)} %all-to-all-done.1.x, f32[16,64,192]{2,1,0:T(8,128)} %bitcast_multiply_fusion.rot), custom_call_target="tpu_custom_call" | custom-call | flops 1207959552 | bytes 10485760 | tf_op jit(solution)/shard_map/project/pallas_call | solution.py:387
  168.1 3.3 %collective-permute-start.5 = (f32[1,64,128]{2,1,0:T(8,128)}, f32[1,64,128]{2,1,0:T(8,128)S(1)}, u32[]{:S(2)}, u32[]{:S(2)}) collective-permute-start(f32[1,64,128]{2,1,0:T(8,128)} %get-tuple-element.30), channel_id=1, source_target_pairs={{0,2},{2,4},{4,6},{6,8},{8,10},{10,12},{12,14},{14,16},{16,18},{18... | collective-permute-start | bytes 98312 | tf_op jit(solution)/shard_map/ppermute | solution.py:59
  171.4 1.9 collective-permute-start.6
  173.4 18.7 %collective-permute-done.5.left = f32[1,64,128]{2,1,0:T(8,128)S(1)} collective-permute-done((f32[1,64,128]{2,1,0:T(8,128)}, f32[1,64,128]{2,1,0:T(8,128)S(1)}, u32[]{:S(2)}, u32[]{:S(2)}) %collective-permute-start.5) | collective-permute-done | bytes 32800 | tf_op jit(solution)/shard_map/ppermute | solution.py:59
  192.0 1.7 collective-permute-done.6.right
  193.7 5.1 %all-to-all-start.3 = ((f32[16,64,512]{2,1,0:T(8,128)}), f32[16,64,512]{2,1,0:T(8,128)}, u32[]{:S(2)}, u32[]{:S(2)}) async-start(f32[16,64,512]{2,1,0:T(8,128)} %get-tuple-element.39), calls=%async_computation.3 | async-start | bytes 4194304 | tf_op jit(solution)/shard_map/all_to_all | solution.py:50
  198.8 5.5 %project.3 = (f32[16,64,640]{2,1,0:T(8,128)}, f32[16,64,128]{2,1,0:T(8,128)}) custom-call(f32[16,192,128]{2,1,0:T(8,128)} %all-to-all-done.x, f32[16,64,192]{2,1,0:T(8,128)} %bitcast_multiply_fusion.rot, f32[16,64,640]{2,1,0:T(8,128)} %get-tuple-element.27.refs_0_), custom_call_target="tpu_custom_call", output_to_operand_aliasing={{0}: (2, {})} | custom-call | flops 301989888 | bytes 2621440 | tf_op jit(solution)/shard_map/project/pallas_call | solution.py:387
  204.3 1.7 copy-done
  206.1 10.9 %stiffness.1 = (f32[16,64,640]{2,1,0:T(8,128)S(1)}, f32[2,1024]{1,0:T(2,128)S(1)}) custom-call(f32[16,64,640]{2,1,0:T(8,128)S(1)} %copy-done, f32[1,64,128]{2,1,0:T(8,128)S(1)} %collective-permute-done.5.left, f32[1,64,128]{2,1,0:T(8,128)S(1)} %collective-permute-done.6.right, f32[18,640]{1,0:T(8,128)S(1)} %concatenate.8.band, f32[16]{0:T(128)S(1)} %fusion.6.lam), custom_call_target="tpu_custom_call" | custom-call | tf_op jit(solution)/shard_map/stiffness/pallas_call | solution.py:470
  217.0 1.5 copy-done.1
  218.5 2.9 collective-permute-done.7
  221.4 1.1 collective-permute-start.8
  223.6 2.6 collective-permute-done.9
  226.5 8.0 %collective-permute-done.10 = f32[2,1024]{1,0:T(2,128)S(1)} collective-permute-done((f32[2,1024]{1,0:T(2,128)S(1)}, f32[2,1024]{1,0:T(2,128)S(1)}, u32[]{:S(2)}, u32[]{:S(2)}) %collective-permute-start.10) | collective-permute-done | bytes 8224 | tf_op jit(solution)/shard_map/ppermute | solution.py:619
  235.3 9.1 %collective-permute-done.11 = f32[2,1024]{1,0:T(2,128)S(1)} collective-permute-done((f32[2,1024]{1,0:T(2,128)S(1)}, f32[2,1024]{1,0:T(2,128)S(1)}, u32[]{:S(2)}, u32[]{:S(2)}) %collective-permute-start.11) | collective-permute-done | bytes 8224 | tf_op jit(solution)/shard_map/ppermute | solution.py:619
  245.0 5.8 %residual_back.1 = (f32[16,64,768]{2,1,0:T(8,128)}, f32[1,1024]{1,0:T(1,128)}) custom-call(f32[16,64,640]{2,1,0:T(8,128)} %get-tuple-element.28.x, f32[16,64,640]{2,1,0:T(8,128)} %copy-done.1, f32[2,1024]{1,0:T(2,128)} %add.87.total, f32[16,64,128]{2,1,0:T(8,128)} %get-tuple-element.37.extra), custom_call_target="tpu_custom_call" | custom-call | tf_op jit(solution)/shard_map/residual_back/pallas_call | solution.py:530
  250.7 7.6 %all-to-all-start.2 = ((f32[16,64,768]{2,1,0:T(8,128)}), f32[16,64,768]{2,1,0:T(8,128)S(1)}, u32[]{:S(2)}, u32[]{:S(2)}) async-start(f32[16,64,768]{2,1,0:T(8,128)} %get-tuple-element.38), calls=%async_computation.2 | async-start | bytes 6291456 | tf_op jit(solution)/shard_map/all_to_all | solution.py:50
  258.3 1.2 constant_dynamic-slice_fusion
  259.5 2.8 collect_early.1._
  262.3 65.9 %all-to-all-done.2.last = f32[16,64,768]{2,1,0:T(8,128)S(1)} async-done(((f32[16,64,768]{2,1,0:T(8,128)}), f32[16,64,768]{2,1,0:T(8,128)S(1)}, u32[]{:S(2)}, u32[]{:S(2)}) %all-to-all-start.2) | async-done | bytes 3145760 | tf_op jit(solution)/shard_map/all_to_all | solution.py:50
  328.2 1.9 collect_late.1
  (53 shorter events, 7.5 us)
Async XLA Ops:
  0.6 8.6 %collective-permute-start = (f32[64,192]{1,0:T(8,128)}, f32[64,192]{1,0:T(8,128)S(1)}, u32[]{:S(2)}, u32[]{:S(2)}) collective-permute-start(f32[64,192]{1,0:T(8,128)} %bitcast.25), channel_id=1, source_target_pairs={{0,16},{2,18},{4,20},{6,22},{8,24},{10,26},{12,28},{14,30},{16,0},... | collective-permute-start | bytes 147464 | tf_op jit(solution)/shard_map/ppermute | solution.py:556
  3.0 6.2 %copy-start.2 = (f32[1,192,64]{1,2,0:T(8,128)S(1)}, f32[1,192,64]{1,2,0:T(8,128)}, u32[]{:S(2)}) copy-start(f32[1,192,64]{1,2,0:T(8,128)} %param.18) | copy-start | bytes 147460
  9.3 5.7 %copy-start.3 = (f32[10240]{0:T(1024)S(1)}, f32[10240]{0:T(1024)}, u32[]{:S(2)}) copy-start(f32[10240]{0:T(1024)} %param.14) | copy-start | bytes 122884
  9.3 5.7 %copy-start.4 = (f32[10240]{0:T(1024)S(1)}, f32[10240]{0:T(1024)}, u32[]{:S(2)}) copy-start(f32[10240]{0:T(1024)} %param.15) | copy-start | bytes 122884
  9.3 5.7 %copy-start.5 = (s32[10240]{0:T(1024)S(1)}, s32[10240]{0:T(1024)}, u32[]{:S(2)}) copy-start(s32[10240]{0:T(1024)} %param.16) | copy-start | bytes 122884
  9.3 143.0 %all-to-all-start.1 = ((f32[16,192,512]{2,1,0:T(8,128)}), f32[16,192,512]{2,1,0:T(8,128)}, u32[]{:S(2)}, u32[]{:S(2)}) async-start(f32[16,192,512]{2,1,0:T(8,128)} %spread_blocks.3), calls=%async_computation.1 | async-start | bytes 12582912 | tf_op jit(solution)/shard_map/all_to_all | solution.py:50
  15.2 4.9 %collective-permute-start.4 = (f32[8,8]{1,0:T(8,128)S(1)}, f32[8,8]{1,0:T(8,128)S(1)}, u32[]{:S(2)}, u32[]{:S(2)}) collective-permute-start(f32[8,8]{1,0:T(8,128)S(1)} %slice.40), channel_id=1, source_target_pairs={{0,1},{2,3},{4,5},{6,7},{8,9},{10,11},{12,13},{14,15},{16,17},{18,... | collective-permute-start | bytes 776 | tf_op jit(solution)/shard_map/ppermute | solution.py:73
  19.9 32.7 %collective-permute-start.1 = (f32[2,64,192]{2,1,0:T(8,128)S(1)}, f32[2,64,192]{2,1,0:T(8,128)S(1)}, u32[]{:S(2)}, u32[]{:S(2)}) collective-permute-start(f32[2,64,192]{2,1,0:T(8,128)S(1)} %pad_maximum_fusion.2), channel_id=1, source_target_pairs={{0,4},{2,6},{4,0},{6,2},{8,12},{10,14},{12,8},{14,10},{16,20},{18,... | collective-permute-start | bytes 294920 | tf_op jit(solution)/shard_map/ppermute | solution.py:556
  52.6 2.2 collective-permute-start.2
  54.9 74.8 %collective-permute-start.3 = (f32[2,2,2,64,192]{4,3,2,1,0:T(8,128)S(1)}, f32[2,2,2,64,192]{4,3,2,1,0:T(8,128)S(1)}, u32[]{:S(2)}, u32[]{:S(2)}) collective-permute-start(f32[2,2,2,64,192]{4,3,2,1,0:T(8,128)S(1)} %pad_maximum_fusion), channel_id=1, source_target_pairs={{0,8},{2,10},{4,12},{6,14},{8,0},{10,2},{12,4},{14,6},{16,24},{18,... | collective-permute-start | bytes 1179656 | tf_op jit(solution)/shard_map/ppermute | solution.py:556
  129.8 0.7 copy-start.6
  152.4 41.4 %all-to-all-start = ((f32[16,192,128]{2,1,0:T(8,128)}), f32[16,192,128]{2,1,0:T(8,128)}, u32[]{:S(2)}, u32[]{:S(2)}) async-start(f32[16,192,128]{2,1,0:T(8,128)} %spread_blocks.2), calls=%async_computation | async-start | bytes 3145728 | tf_op jit(solution)/shard_map/all_to_all | solution.py:50
  168.1 24.0 %collective-permute-start.5 = (f32[1,64,128]{2,1,0:T(8,128)}, f32[1,64,128]{2,1,0:T(8,128)S(1)}, u32[]{:S(2)}, u32[]{:S(2)}) collective-permute-start(f32[1,64,128]{2,1,0:T(8,128)} %get-tuple-element.30), channel_id=1, source_target_pairs={{0,2},{2,4},{4,6},{6,8},{8,10},{10,12},{12,14},{14,16},{16,18},{18... | collective-permute-start | bytes 98312 | tf_op jit(solution)/shard_map/ppermute | solution.py:59
  171.4 22.3 %collective-permute-start.6 = (f32[1,64,128]{2,1,0:T(8,128)}, f32[1,64,128]{2,1,0:T(8,128)S(1)}, u32[]{:S(2)}, u32[]{:S(2)}) collective-permute-start(f32[1,64,128]{2,1,0:T(8,128)} %get-tuple-element.31), channel_id=1, source_target_pairs={{2,0},{4,2},{6,4},{8,6},{10,8},{12,10},{14,12},{16,14},{18,16},{20... | collective-permute-start | bytes 98312 | tf_op jit(solution)/shard_map/ppermute | solution.py:59
  193.7 57.0 %all-to-all-start.3 = ((f32[16,64,512]{2,1,0:T(8,128)}), f32[16,64,512]{2,1,0:T(8,128)}, u32[]{:S(2)}, u32[]{:S(2)}) async-start(f32[16,64,512]{2,1,0:T(8,128)} %get-tuple-element.39), calls=%async_computation.3 | async-start | bytes 4194304 | tf_op jit(solution)/shard_map/all_to_all | solution.py:50
  204.3 1.7 copy-start
  217.0 1.5 copy-start.1
  218.5 2.9 collective-permute-start.7
  221.4 1.9 collective-permute-start.8
  223.3 2.9 collective-permute-start.9
  226.2 8.3 %collective-permute-start.10 = (f32[2,1024]{1,0:T(2,128)S(1)}, f32[2,1024]{1,0:T(2,128)S(1)}, u32[]{:S(2)}, u32[]{:S(2)}) collective-permute-start(f32[2,1024]{1,0:T(2,128)S(1)} %add.85), channel_id=1, source_target_pairs={{0,8},{2,10},{4,12},{6,14},{8,0},{10,2},{12,4},{14,6},{16,24},{18,... | collective-permute-start | bytes 24584 | tf_op jit(solution)/shard_map/ppermute | solution.py:619
  234.6 9.8 %collective-permute-start.11 = (f32[2,1024]{1,0:T(2,128)S(1)}, f32[2,1024]{1,0:T(2,128)S(1)}, u32[]{:S(2)}, u32[]{:S(2)}) collective-permute-start(f32[2,1024]{1,0:T(2,128)S(1)} %add.86), channel_id=1, source_target_pairs={{0,16},{2,18},{4,20},{6,22},{8,24},{10,26},{12,28},{14,30},{16,0},... | collective-permute-start | bytes 24584 | tf_op jit(solution)/shard_map/ppermute | solution.py:619
  250.7 77.4 %all-to-all-start.2 = ((f32[16,64,768]{2,1,0:T(8,128)}), f32[16,64,768]{2,1,0:T(8,128)S(1)}, u32[]{:S(2)}, u32[]{:S(2)}) async-start(f32[16,64,768]{2,1,0:T(8,128)} %get-tuple-element.38), calls=%async_computation.2 | async-start | bytes 6291456 | tf_op jit(solution)/shard_map/all_to_all | solution.py:50

commit v18 on v17

--- a/solution.py
+++ b/solution.py
@@ -540,7 +540,7 @@
             pltpu.VMEM((count, rows, dofs), jnp.float32),
             pltpu.SemaphoreType.DMA((tiles + 1,)),
         ],
-        compiler_params=params(57_400_000),
+        compiler_params=params(),
         name="residual_back",
     )(projected, stiff, sums, late)
 

time: 331 us -> 327 us (0.988)
  Pallas kernels: 46.4 us -> 42.9 us
  transfers between devices with their start and end apart: 16 -> 16, of which waited for: 12 -> 12; matrix products, arithmetic and copies ran while one was open for 2% -> 1% of each run, Pallas kernels for 13% -> 13%
where the time goes in v18:
time: 327 us; the launch traced here: 326 us
  waiting for transfers between devices  239 us (73%)
  Pallas kernels  42.9 us (13%)
  starting transfers between devices  37.3 us (11%)
  local copies, waits for them, and re-layouts  3.82 us (1%)
    ppermute x4, waiting for transfers between devices, exchange_step(): other = lax.ppermute(held, 'span', pairs)  107 us
    all_to_all x4, waiting for transfers between devices, exchange(): lax.all_to_all(pieces, 'span', split_axis=0, concat_axis=0, tiled=True)  87.3 us
    all_to_all x4, starting transfers between devices, exchange(): lax.all_to_all(pieces, 'span', split_axis=0, concat_axis=0, tiled=True)  23.1 us
    ppermute x4, waiting for transfers between devices, tiled_device(): sums = sums + lax.ppermute(sums, 'span', pairs)  21.1 us
    ppermute x2, waiting for transfers between devices, to_next(): return lax.ppermute(cells, ('span', 'elem'), pairs)  20.4 us
    pallas_call x2, Pallas kernels, project(): pl.pallas_call(kernel, in_specs=[whole, vmem] + ([] if first else [whole]...  16.3 us
    pallas_call x1, Pallas kernels, stiffness(): pl.pallas_call(kernel, in_specs=[vmem, vmem, vmem, vmem, pl.BlockSpec(mem...  10.6 us
    pallas_call x2, Pallas kernels, spread_blocks(): pl.pallas_call(kernel, in_specs=[whole] * kinds, out_specs=whole, out_sha...  8.8 us
  transfers between devices with their start and end apart: 16, of which 12 were waited for; matrix products, arithmetic and copies ran while one was open for 1% of the time, Pallas kernels for 13%

profile of v18, /device:TPU:15, one launch (start us, length us, event | category | flops | bytes accessed | tf_op | source)
XLA Modules:
  0.0 326.3 jit_solution(17534939803576538066)
XLA Ops:
  0.6 2.4 collective-permute-start
  3.0 6.2 %spread_blocks.3 = f32[16,192,512]{2,1,0:T(8,128)} custom-call(f32[1,64,10240]{2,1,0:T(8,128)} %refs_0_.3, f32[1,64,10240]{2,1,0:T(8,128)} %refs_1_.3, f32[1,64,10240]{2,1,0:T(8,128)} %refs_2_.3), custom_call_target="tpu_custom_call" | custom-call | tf_op jit(solution)/shard_map/spread_blocks/pallas_call | solution.py:190
  9.3 5.6 %all-to-all-start.1 = ((f32[16,192,512]{2,1,0:T(8,128)}), f32[16,192,512]{2,1,0:T(8,128)}, u32[]{:S(2)}, u32[]{:S(2)}) async-start(f32[16,192,512]{2,1,0:T(8,128)} %spread_blocks.3), calls=%async_computation.1 | async-start | bytes 12582912 | tf_op jit(solution)/shard_map/all_to_all | solution.py:50
  15.2 1.3 collective-permute-start.4
  16.5 2.6 spread_blocks.2
  20.3 32.3 %collective-permute-done.1 = f32[2,64,192]{2,1,0:T(8,128)S(1)} collective-permute-done((f32[2,64,192]{2,1,0:T(8,128)S(1)}, f32[2,64,192]{2,1,0:T(8,128)S(1)}, u32[]{:S(2)}, u32[]{:S(2)}) %collective-permute-start.1) | collective-permute-done | bytes 98336 | tf_op jit(solution)/shard_map/ppermute | solution.py:556
  52.6 1.0 collective-permute-start.2
  53.7 1.1 collective-permute-done.2
  56.2 73.5 %collective-permute-done.3 = f32[2,2,2,64,192]{4,3,2,1,0:T(8,128)S(1)} collective-permute-done((f32[2,2,2,64,192]{4,3,2,1,0:T(8,128)S(1)}, f32[2,2,2,64,192]{4,3,2,1,0:T(8,128)S(1)}, u32[]{:S(2)}, u32[]{:S(2)}) %collective-permute-start.3) | collective-permute-done | bytes 393248 | tf_op jit(solution)/shard_map/ppermute | solution.py:556
  130.5 1.1 bitcast_multiply_fusion.rot
  131.6 20.8 %all-to-all-done.1.x = f32[16,192,512]{2,1,0:T(8,128)} async-done(((f32[16,192,512]{2,1,0:T(8,128)}), f32[16,192,512]{2,1,0:T(8,128)}, u32[]{:S(2)}, u32[]{:S(2)}) %all-to-all-start.1) | async-done | bytes 6291488 | tf_op jit(solution)/shard_map/all_to_all | solution.py:50
  152.4 4.9 %all-to-all-start = ((f32[16,192,128]{2,1,0:T(8,128)}), f32[16,192,128]{2,1,0:T(8,128)}, u32[]{:S(2)}, u32[]{:S(2)}) async-start(f32[16,192,128]{2,1,0:T(8,128)} %spread_blocks.2), calls=%async_computation | async-start | bytes 3145728 | tf_op jit(solution)/shard_map/all_to_all | solution.py:50
  157.2 10.8 %project.2 = (f32[16,64,640]{2,1,0:T(8,128)}, f32[16,64,512]{2,1,0:T(8,128)}, f32[1,64,128]{2,1,0:T(8,128)}, f32[1,64,128]{2,1,0:T(8,128)}) custom-call(f32[16,192,512]{2,1,0:T(8,128)} %all-to-all-done.1.x, f32[16,64,192]{2,1,0:T(8,128)} %bitcast_multiply_fusion.rot), custom_call_target="tpu_custom_call" | custom-call | flops 1207959552 | bytes 10485760 | tf_op jit(solution)/shard_map/project/pallas_call | solution.py:387
  168.0 3.3 %collective-permute-start.5 = (f32[1,64,128]{2,1,0:T(8,128)}, f32[1,64,128]{2,1,0:T(8,128)S(1)}, u32[]{:S(2)}, u32[]{:S(2)}) collective-permute-start(f32[1,64,128]{2,1,0:T(8,128)} %get-tuple-element.30), channel_id=1, source_target_pairs={{0,2},{2,4},{4,6},{6,8},{8,10},{10,12},{12,14},{14,16},{16,18},{18... | collective-permute-start | bytes 98312 | tf_op jit(solution)/shard_map/ppermute | solution.py:59
  171.4 1.9 collective-permute-start.6
  173.3 18.7 %collective-permute-done.5.left = f32[1,64,128]{2,1,0:T(8,128)S(1)} collective-permute-done((f32[1,64,128]{2,1,0:T(8,128)}, f32[1,64,128]{2,1,0:T(8,128)S(1)}, u32[]{:S(2)}, u32[]{:S(2)}) %collective-permute-start.5) | collective-permute-done | bytes 32800 | tf_op jit(solution)/shard_map/ppermute | solution.py:59
  192.0 1.7 collective-permute-done.6.right
  193.7 5.1 %all-to-all-start.3 = ((f32[16,64,512]{2,1,0:T(8,128)}), f32[16,64,512]{2,1,0:T(8,128)}, u32[]{:S(2)}, u32[]{:S(2)}) async-start(f32[16,64,512]{2,1,0:T(8,128)} %get-tuple-element.39), calls=%async_computation.3 | async-start | bytes 4194304 | tf_op jit(solution)/shard_map/all_to_all | solution.py:50
  198.8 5.5 %project.3 = (f32[16,64,640]{2,1,0:T(8,128)}, f32[16,64,128]{2,1,0:T(8,128)}) custom-call(f32[16,192,128]{2,1,0:T(8,128)} %all-to-all-done.x, f32[16,64,192]{2,1,0:T(8,128)} %bitcast_multiply_fusion.rot, f32[16,64,640]{2,1,0:T(8,128)} %get-tuple-element.27.refs_0_), custom_call_target="tpu_custom_call", output_to_operand_aliasing={{0}: (2, {})} | custom-call | flops 301989888 | bytes 2621440 | tf_op jit(solution)/shard_map/project/pallas_call | solution.py:387
  204.3 1.7 copy-done
  206.1 10.6 %stiffness.1 = (f32[16,64,640]{2,1,0:T(8,128)S(1)}, f32[2,1024]{1,0:T(2,128)S(1)}) custom-call(f32[16,64,640]{2,1,0:T(8,128)S(1)} %copy-done, f32[1,64,128]{2,1,0:T(8,128)S(1)} %collective-permute-done.5.left, f32[1,64,128]{2,1,0:T(8,128)S(1)} %collective-permute-done.6.right, f32[18,640]{1,0:T(8,128)S(1)} %concatenate.8.band, f32[16]{0:T(128)S(1)} %fusion.6.lam), custom_call_target="tpu_custom_call" | custom-call | tf_op jit(solution)/shard_map/stiffness/pallas_call | solution.py:470
  216.7 2.9 collective-permute-done.7
  219.6 1.1 collective-permute-start.8
  221.8 2.2 collective-permute-done.9
  224.0 1.6 collective-permute-start.10
  225.6 9.0 %collective-permute-done.10 = f32[2,1024]{1,0:T(2,128)S(1)} collective-permute-done((f32[2,1024]{1,0:T(2,128)S(1)}, f32[2,1024]{1,0:T(2,128)S(1)}, u32[]{:S(2)}, u32[]{:S(2)}) %collective-permute-start.10) | collective-permute-done | bytes 8224 | tf_op jit(solution)/shard_map/ppermute | solution.py:619
  235.3 9.1 %collective-permute-done.11 = f32[2,1024]{1,0:T(2,128)S(1)} collective-permute-done((f32[2,1024]{1,0:T(2,128)S(1)}, f32[2,1024]{1,0:T(2,128)S(1)}, u32[]{:S(2)}, u32[]{:S(2)}) %collective-permute-start.11) | collective-permute-done | bytes 8224 | tf_op jit(solution)/shard_map/ppermute | solution.py:619
  244.4 2.6 residual_back.1
  247.0 7.6 %all-to-all-start.2 = ((f32[16,64,768]{2,1,0:T(8,128)}), f32[16,64,768]{2,1,0:T(8,128)S(1)}, u32[]{:S(2)}, u32[]{:S(2)}) async-start(f32[16,64,768]{2,1,0:T(8,128)} %get-tuple-element.38), calls=%async_computation.2 | async-start | bytes 6291456 | tf_op jit(solution)/shard_map/all_to_all | solution.py:50
  255.1 2.8 collect_early.1._
  257.9 66.5 %all-to-all-done.2.last = f32[16,64,768]{2,1,0:T(8,128)S(1)} async-done(((f32[16,64,768]{2,1,0:T(8,128)}), f32[16,64,768]{2,1,0:T(8,128)S(1)}, u32[]{:S(2)}, u32[]{:S(2)}) %all-to-all-start.2) | async-done | bytes 3145760 | tf_op jit(solution)/shard_map/all_to_all | solution.py:50
  324.4 1.9 collect_late.1
  (53 shorter events, 6.2 us)
Async XLA Ops:
  0.6 8.6 %collective-permute-start = (f32[64,192]{1,0:T(8,128)}, f32[64,192]{1,0:T(8,128)S(1)}, u32[]{:S(2)}, u32[]{:S(2)}) collective-permute-start(f32[64,192]{1,0:T(8,128)} %bitcast.25), channel_id=1, source_target_pairs={{0,16},{2,18},{4,20},{6,22},{8,24},{10,26},{12,28},{14,30},{16,0},... | collective-permute-start | bytes 147464 | tf_op jit(solution)/shard_map/ppermute | solution.py:556
  3.0 6.2 %copy-start.2 = (f32[1,192,64]{1,2,0:T(8,128)S(1)}, f32[1,192,64]{1,2,0:T(8,128)}, u32[]{:S(2)}) copy-start(f32[1,192,64]{1,2,0:T(8,128)} %param.18) | copy-start | bytes 147460
  9.3 5.7 %copy-start.3 = (f32[10240]{0:T(1024)S(1)}, f32[10240]{0:T(1024)}, u32[]{:S(2)}) copy-start(f32[10240]{0:T(1024)} %param.14) | copy-start | bytes 122884
  9.3 5.7 %copy-start.4 = (f32[10240]{0:T(1024)S(1)}, f32[10240]{0:T(1024)}, u32[]{:S(2)}) copy-start(f32[10240]{0:T(1024)} %param.15) | copy-start | bytes 122884
  9.3 5.7 %copy-start.5 = (s32[10240]{0:T(1024)S(1)}, s32[10240]{0:T(1024)}, u32[]{:S(2)}) copy-start(s32[10240]{0:T(1024)} %param.16) | copy-start | bytes 122884
  9.3 143.0 %all-to-all-start.1 = ((f32[16,192,512]{2,1,0:T(8,128)}), f32[16,192,512]{2,1,0:T(8,128)}, u32[]{:S(2)}, u32[]{:S(2)}) async-start(f32[16,192,512]{2,1,0:T(8,128)} %spread_blocks.3), calls=%async_computation.1 | async-start | bytes 12582912 | tf_op jit(solution)/shard_map/all_to_all | solution.py:50
  15.2 5.0 %collective-permute-start.4 = (f32[8,8]{1,0:T(8,128)S(1)}, f32[8,8]{1,0:T(8,128)S(1)}, u32[]{:S(2)}, u32[]{:S(2)}) collective-permute-start(f32[8,8]{1,0:T(8,128)S(1)} %slice.40), channel_id=1, source_target_pairs={{0,1},{2,3},{4,5},{6,7},{8,9},{10,11},{12,13},{14,15},{16,17},{18,... | collective-permute-start | bytes 776 | tf_op jit(solution)/shard_map/ppermute | solution.py:73
  19.9 32.6 %collective-permute-start.1 = (f32[2,64,192]{2,1,0:T(8,128)S(1)}, f32[2,64,192]{2,1,0:T(8,128)S(1)}, u32[]{:S(2)}, u32[]{:S(2)}) collective-permute-start(f32[2,64,192]{2,1,0:T(8,128)S(1)} %pad_maximum_fusion.2), channel_id=1, source_target_pairs={{0,4},{2,6},{4,0},{6,2},{8,12},{10,14},{12,8},{14,10},{16,20},{18,... | collective-permute-start | bytes 294920 | tf_op jit(solution)/shard_map/ppermute | solution.py:556
  52.6 2.2 collective-permute-start.2
  54.9 74.8 %collective-permute-start.3 = (f32[2,2,2,64,192]{4,3,2,1,0:T(8,128)S(1)}, f32[2,2,2,64,192]{4,3,2,1,0:T(8,128)S(1)}, u32[]{:S(2)}, u32[]{:S(2)}) collective-permute-start(f32[2,2,2,64,192]{4,3,2,1,0:T(8,128)S(1)} %pad_maximum_fusion), channel_id=1, source_target_pairs={{0,8},{2,10},{4,12},{6,14},{8,0},{10,2},{12,4},{14,6},{16,24},{18,... | collective-permute-start | bytes 1179656 | tf_op jit(solution)/shard_map/ppermute | solution.py:556
  129.8 0.7 copy-start.6
  152.4 41.4 %all-to-all-start = ((f32[16,192,128]{2,1,0:T(8,128)}), f32[16,192,128]{2,1,0:T(8,128)}, u32[]{:S(2)}, u32[]{:S(2)}) async-start(f32[16,192,128]{2,1,0:T(8,128)} %spread_blocks.2), calls=%async_computation | async-start | bytes 3145728 | tf_op jit(solution)/shard_map/all_to_all | solution.py:50
  168.0 24.0 %collective-permute-start.5 = (f32[1,64,128]{2,1,0:T(8,128)}, f32[1,64,128]{2,1,0:T(8,128)S(1)}, u32[]{:S(2)}, u32[]{:S(2)}) collective-permute-start(f32[1,64,128]{2,1,0:T(8,128)} %get-tuple-element.30), channel_id=1, source_target_pairs={{0,2},{2,4},{4,6},{6,8},{8,10},{10,12},{12,14},{14,16},{16,18},{18... | collective-permute-start | bytes 98312 | tf_op jit(solution)/shard_map/ppermute | solution.py:59
  171.4 22.3 %collective-permute-start.6 = (f32[1,64,128]{2,1,0:T(8,128)}, f32[1,64,128]{2,1,0:T(8,128)S(1)}, u32[]{:S(2)}, u32[]{:S(2)}) collective-permute-start(f32[1,64,128]{2,1,0:T(8,128)} %get-tuple-element.31), channel_id=1, source_target_pairs={{2,0},{4,2},{6,4},{8,6},{10,8},{12,10},{14,12},{16,14},{18,16},{20... | collective-permute-start | bytes 98312 | tf_op jit(solution)/shard_map/ppermute | solution.py:59
  193.7 53.2 %all-to-all-start.3 = ((f32[16,64,512]{2,1,0:T(8,128)}), f32[16,64,512]{2,1,0:T(8,128)}, u32[]{:S(2)}, u32[]{:S(2)}) async-start(f32[16,64,512]{2,1,0:T(8,128)} %get-tuple-element.39), calls=%async_computation.3 | async-start | bytes 4194304 | tf_op jit(solution)/shard_map/all_to_all | solution.py:50
  204.3 1.7 copy-start
  206.1 38.3 %copy-start.1 = (f32[16,64,128]{2,1,0:T(8,128)S(1)}, f32[16,64,128]{2,1,0:T(8,128)}, u32[]{:S(2)}) copy-start(f32[16,64,128]{2,1,0:T(8,128)} %get-tuple-element.37.extra) | copy-start | bytes 1572868
  216.7 2.9 collective-permute-start.7
  219.6 1.9 collective-permute-start.8
  221.5 2.5 collective-permute-start.9
  224.0 10.6 %collective-permute-start.10 = (f32[2,1024]{1,0:T(2,128)S(1)}, f32[2,1024]{1,0:T(2,128)S(1)}, u32[]{:S(2)}, u32[]{:S(2)}) collective-permute-start(f32[2,1024]{1,0:T(2,128)S(1)} %add.85), channel_id=1, source_target_pairs={{0,8},{2,10},{4,12},{6,14},{8,0},{10,2},{12,4},{14,6},{16,24},{18,... | collective-permute-start | bytes 24584 | tf_op jit(solution)/shard_map/ppermute | solution.py:619
  234.6 9.8 %collective-permute-start.11 = (f32[2,1024]{1,0:T(2,128)S(1)}, f32[2,1024]{1,0:T(2,128)S(1)}, u32[]{:S(2)}, u32[]{:S(2)}) collective-permute-start(f32[2,1024]{1,0:T(2,128)S(1)} %add.86), channel_id=1, source_target_pairs={{0,16},{2,18},{4,20},{6,22},{8,24},{10,26},{12,28},{14,30},{16,0},... | collective-permute-start | bytes 24584 | tf_op jit(solution)/shard_map/ppermute | solution.py:619
  247.0 77.4 %all-to-all-start.2 = ((f32[16,64,768]{2,1,0:T(8,128)}), f32[16,64,768]{2,1,0:T(8,128)S(1)}, u32[]{:S(2)}, u32[]{:S(2)}) async-start(f32[16,64,768]{2,1,0:T(8,128)} %get-tuple-element.38), calls=%async_computation.2 | async-start | bytes 6291456 | tf_op jit(solution)/shard_map/all_to_all | solution.py:50

commit v19 on v18

--- a/solution.py
+++ b/solution.py
@@ -615,8 +615,15 @@
     stiff, sums = stiffness(projected, before, after, bands, links)
     for _, pairs in halvings("elem"):
         sums = sums + lax.ppermute(sums, "elem", pairs)
-    for _, pairs in steps[::-1]:
+    for _, pairs in steps[:1:-1]:
         sums = sums + lax.ppermute(sums, "span", pairs)
+    (far, _), (near, _) = steps[:2]
+    sums = sums + add_up(
+        [
+            lax.ppermute(sums, "span", [(i, i ^ flip) for i in range(count)])
+            for flip in (far | near, far, near)
+        ]
+    )
     spans, ritz = residual_back(projected, stiff, sums, late)
     next_block = collect_early(early_pieces, at)
     next_residual, next_block = collect_late(exchange(spans), next_block, at)

time: 327 us -> 327 us (level)
    ppermute x0 -> x3, waiting for transfers between devices: none -> 19.6 us  [tiled_device(): lax.ppermute(sums, 'span', [(i, i ^ flip) for i in range(count)])]
    ppermute x4 -> x2, waiting for transfers between devices: 21.1 us -> 3.05 us  [tiled_device(): sums = sums + lax.ppermute(sums, 'span', pairs)]
  transfers between devices with their start and end apart: 16 -> 17, of which waited for: 12 -> 13; matrix products, arithmetic and copies ran while one was open for 1% -> 1% of each run, Pallas kernels for 13% -> 13%
where the time goes in v19:
time: 327 us
  waiting for transfers between devices  240 us (73%)
  Pallas kernels  42.9 us (13%)
  starting transfers between devices  36 us (11%)
  local copies, waits for them, and re-layouts  3.82 us (1%)
    ppermute x4, waiting for transfers between devices, exchange_step(): other = lax.ppermute(held, 'span', pairs)  107 us
    all_to_all x4, waiting for transfers between devices, exchange(): lax.all_to_all(pieces, 'span', split_axis=0, concat_axis=0, tiled=True)  87.3 us
    all_to_all x4, starting transfers between devices, exchange(): lax.all_to_all(pieces, 'span', split_axis=0, concat_axis=0, tiled=True)  21.2 us
    ppermute x2, waiting for transfers between devices, to_next(): return lax.ppermute(cells, ('span', 'elem'), pairs)  20.4 us
    ppermute x3, waiting for transfers between devices, tiled_device(): lax.ppermute(sums, 'span', [(i, i ^ flip) for i in range(count)])  19.6 us
    pallas_call x2, Pallas kernels, project(): pl.pallas_call(kernel, in_specs=[whole, vmem] + ([] if first else [whole]...  16.3 us
    pallas_call x1, Pallas kernels, stiffness(): pl.pallas_call(kernel, in_specs=[vmem, vmem, vmem, vmem, pl.BlockSpec(mem...  10.6 us
    pallas_call x2, Pallas kernels, spread_blocks(): pl.pallas_call(kernel, in_specs=[whole] * kinds, out_specs=whole, out_sha...  8.79 us
  transfers between devices with their start and end apart: 17, of which 13 were waited for; matrix products, arithmetic and copies ran while one was open for 1% of the time, Pallas kernels for 13%

profile of v19, /device:TPU:15, one launch (start us, length us, event | category | flops | bytes accessed | tf_op | source)
XLA Modules:
  0.0 326.6 jit_solution(7608520664085770116)
XLA Ops:
  0.6 2.4 collective-permute-start
  3.0 6.2 %spread_blocks.3 = f32[16,192,512]{2,1,0:T(8,128)} custom-call(f32[1,64,10240]{2,1,0:T(8,128)} %refs_0_.3, f32[1,64,10240]{2,1,0:T(8,128)} %refs_1_.3, f32[1,64,10240]{2,1,0:T(8,128)} %refs_2_.3), custom_call_target="tpu_custom_call" | custom-call | tf_op jit(solution)/shard_map/spread_blocks/pallas_call | solution.py:190
  9.3 5.6 %all-to-all-start.1 = ((f32[16,192,512]{2,1,0:T(8,128)}), f32[16,192,512]{2,1,0:T(8,128)}, u32[]{:S(2)}, u32[]{:S(2)}) async-start(f32[16,192,512]{2,1,0:T(8,128)} %spread_blocks.3), calls=%async_computation.1 | async-start | bytes 12582912 | tf_op jit(solution)/shard_map/all_to_all | solution.py:50
  15.2 1.3 collective-permute-start.4
  16.5 2.6 spread_blocks.2
  20.2 32.3 %collective-permute-done.1 = f32[2,64,192]{2,1,0:T(8,128)S(1)} collective-permute-done((f32[2,64,192]{2,1,0:T(8,128)S(1)}, f32[2,64,192]{2,1,0:T(8,128)S(1)}, u32[]{:S(2)}, u32[]{:S(2)}) %collective-permute-start.1) | collective-permute-done | bytes 98336 | tf_op jit(solution)/shard_map/ppermute | solution.py:556
  56.2 73.5 %collective-permute-done.3 = f32[2,2,2,64,192]{4,3,2,1,0:T(8,128)S(1)} collective-permute-done((f32[2,2,2,64,192]{4,3,2,1,0:T(8,128)S(1)}, f32[2,2,2,64,192]{4,3,2,1,0:T(8,128)S(1)}, u32[]{:S(2)}, u32[]{:S(2)}) %collective-permute-start.3) | collective-permute-done | bytes 393248 | tf_op jit(solution)/shard_map/ppermute | solution.py:556
  130.4 1.1 bitcast_multiply_fusion.rot
  131.6 20.8 %all-to-all-done.1.x = f32[16,192,512]{2,1,0:T(8,128)} async-done(((f32[16,192,512]{2,1,0:T(8,128)}), f32[16,192,512]{2,1,0:T(8,128)}, u32[]{:S(2)}, u32[]{:S(2)}) %all-to-all-start.1) | async-done | bytes 6291488 | tf_op jit(solution)/shard_map/all_to_all | solution.py:50
  152.3 4.9 %all-to-all-start = ((f32[16,192,128]{2,1,0:T(8,128)}), f32[16,192,128]{2,1,0:T(8,128)}, u32[]{:S(2)}, u32[]{:S(2)}) async-start(f32[16,192,128]{2,1,0:T(8,128)} %spread_blocks.2), calls=%async_computation | async-start | bytes 3145728 | tf_op jit(solution)/shard_map/all_to_all | solution.py:50
  157.2 10.8 %project.2 = (f32[16,64,640]{2,1,0:T(8,128)}, f32[16,64,512]{2,1,0:T(8,128)}, f32[1,64,128]{2,1,0:T(8,128)}, f32[1,64,128]{2,1,0:T(8,128)}) custom-call(f32[16,192,512]{2,1,0:T(8,128)} %all-to-all-done.1.x, f32[16,64,192]{2,1,0:T(8,128)} %bitcast_multiply_fusion.rot), custom_call_target="tpu_custom_call" | custom-call | flops 1207959552 | bytes 10485760 | tf_op jit(solution)/shard_map/project/pallas_call | solution.py:387
  168.0 3.4 %collective-permute-start.5 = (f32[1,64,128]{2,1,0:T(8,128)}, f32[1,64,128]{2,1,0:T(8,128)S(1)}, u32[]{:S(2)}, u32[]{:S(2)}) collective-permute-start(f32[1,64,128]{2,1,0:T(8,128)} %get-tuple-element.30), channel_id=1, source_target_pairs={{0,2},{2,4},{4,6},{6,8},{8,10},{10,12},{12,14},{14,16},{16,18},{18... | collective-permute-start | bytes 98312 | tf_op jit(solution)/shard_map/ppermute | solution.py:59
  171.4 1.9 collective-permute-start.6
  173.3 18.7 %collective-permute-done.5.left = f32[1,64,128]{2,1,0:T(8,128)S(1)} collective-permute-done((f32[1,64,128]{2,1,0:T(8,128)}, f32[1,64,128]{2,1,0:T(8,128)S(1)}, u32[]{:S(2)}, u32[]{:S(2)}) %collective-permute-start.5) | collective-permute-done | bytes 32800 | tf_op jit(solution)/shard_map/ppermute | solution.py:59
  192.0 1.7 collective-permute-done.6.right
  193.7 5.1 %all-to-all-start.3 = ((f32[16,64,512]{2,1,0:T(8,128)}), f32[16,64,512]{2,1,0:T(8,128)}, u32[]{:S(2)}, u32[]{:S(2)}) async-start(f32[16,64,512]{2,1,0:T(8,128)} %get-tuple-element.39), calls=%async_computation.3 | async-start | bytes 4194304 | tf_op jit(solution)/shard_map/all_to_all | solution.py:50
  198.8 5.5 %project.3 = (f32[16,64,640]{2,1,0:T(8,128)}, f32[16,64,128]{2,1,0:T(8,128)}) custom-call(f32[16,192,128]{2,1,0:T(8,128)} %all-to-all-done.x, f32[16,64,192]{2,1,0:T(8,128)} %bitcast_multiply_fusion.rot, f32[16,64,640]{2,1,0:T(8,128)} %get-tuple-element.27.refs_0_), custom_call_target="tpu_custom_call", output_to_operand_aliasing={{0}: (2, {})} | custom-call | flops 301989888 | bytes 2621440 | tf_op jit(solution)/shard_map/project/pallas_call | solution.py:387
  204.3 1.7 copy-done
  206.1 10.6 %stiffness.1 = (f32[16,64,640]{2,1,0:T(8,128)S(1)}, f32[2,1024]{1,0:T(2,128)S(1)}) custom-call(f32[16,64,640]{2,1,0:T(8,128)S(1)} %copy-done, f32[1,64,128]{2,1,0:T(8,128)S(1)} %collective-permute-done.5.left, f32[1,64,128]{2,1,0:T(8,128)S(1)} %collective-permute-done.6.right, f32[18,640]{1,0:T(8,128)S(1)} %concatenate.8.band, f32[16]{0:T(128)S(1)} %fusion.6.lam), custom_call_target="tpu_custom_call" | custom-call | tf_op jit(solution)/shard_map/stiffness/pallas_call | solution.py:470
  216.7 2.9 collective-permute-done.7
  219.6 1.1 collective-permute-start.8
  221.8 2.2 collective-permute-done.9
  224.0 1.6 collective-permute-start.12
  225.6 1.2 collective-permute-start.11
  226.9 7.7 %collective-permute-done.12 = f32[2,1024]{1,0:T(2,128)S(1)} collective-permute-done((f32[2,1024]{1,0:T(2,128)S(1)}, f32[2,1024]{1,0:T(2,128)S(1)}, u32[]{:S(2)}, u32[]{:S(2)}) %collective-permute-start.12) | collective-permute-done | bytes 8224 | tf_op jit(solution)/shard_map/ppermute | solution.py:623
  234.6 9.9 %collective-permute-done.11 = f32[2,1024]{1,0:T(2,128)S(1)} collective-permute-done((f32[2,1024]{1,0:T(2,128)S(1)}, f32[2,1024]{1,0:T(2,128)S(1)}, u32[]{:S(2)}, u32[]{:S(2)}) %collective-permute-start.11) | collective-permute-done | bytes 8224 | tf_op jit(solution)/shard_map/ppermute | solution.py:623
  244.5 1.9 collective-permute-done.10
  246.5 2.6 residual_back.1
  249.1 5.7 %all-to-all-start.2 = ((f32[16,64,768]{2,1,0:T(8,128)}), f32[16,64,768]{2,1,0:T(8,128)S(1)}, u32[]{:S(2)}, u32[]{:S(2)}) async-start(f32[16,64,768]{2,1,0:T(8,128)} %get-tuple-element.38), calls=%async_computation.2 | async-start | bytes 6291456 | tf_op jit(solution)/shard_map/all_to_all | solution.py:50
  255.4 2.8 collect_early.1._
  258.2 66.5 %all-to-all-done.2.last = f32[16,64,768]{2,1,0:T(8,128)S(1)} async-done(((f32[16,64,768]{2,1,0:T(8,128)}), f32[16,64,768]{2,1,0:T(8,128)S(1)}, u32[]{:S(2)}, u32[]{:S(2)}) %all-to-all-start.2) | async-done | bytes 3145760 | tf_op jit(solution)/shard_map/all_to_all | solution.py:50
  324.7 1.9 collect_late.1
  (54 shorter events, 7.7 us)
Async XLA Ops:
  0.6 8.6 %collective-permute-start = (f32[64,192]{1,0:T(8,128)}, f32[64,192]{1,0:T(8,128)S(1)}, u32[]{:S(2)}, u32[]{:S(2)}) collective-permute-start(f32[64,192]{1,0:T(8,128)} %bitcast.25), channel_id=1, source_target_pairs={{0,16},{2,18},{4,20},{6,22},{8,24},{10,26},{12,28},{14,30},{16,0},... | collective-permute-start | bytes 147464 | tf_op jit(solution)/shard_map/ppermute | solution.py:556
  3.0 6.2 %copy-start.2 = (f32[1,192,64]{1,2,0:T(8,128)S(1)}, f32[1,192,64]{1,2,0:T(8,128)}, u32[]{:S(2)}) copy-start(f32[1,192,64]{1,2,0:T(8,128)} %param.18) | copy-start | bytes 147460
  9.3 5.7 %copy-start.3 = (f32[10240]{0:T(1024)S(1)}, f32[10240]{0:T(1024)}, u32[]{:S(2)}) copy-start(f32[10240]{0:T(1024)} %param.14) | copy-start | bytes 122884
  9.3 5.6 %copy-start.4 = (f32[10240]{0:T(1024)S(1)}, f32[10240]{0:T(1024)}, u32[]{:S(2)}) copy-start(f32[10240]{0:T(1024)} %param.15) | copy-start | bytes 122884
  9.3 5.6 %copy-start.5 = (s32[10240]{0:T(1024)S(1)}, s32[10240]{0:T(1024)}, u32[]{:S(2)}) copy-start(s32[10240]{0:T(1024)} %param.16) | copy-start | bytes 122884
  9.3 143.0 %all-to-all-start.1 = ((f32[16,192,512]{2,1,0:T(8,128)}), f32[16,192,512]{2,1,0:T(8,128)}, u32[]{:S(2)}, u32[]{:S(2)}) async-start(f32[16,192,512]{2,1,0:T(8,128)} %spread_blocks.3), calls=%async_computation.1 | async-start | bytes 12582912 | tf_op jit(solution)/shard_map/all_to_all | solution.py:50
  15.2 5.0 %collective-permute-start.4 = (f32[8,8]{1,0:T(8,128)S(1)}, f32[8,8]{1,0:T(8,128)S(1)}, u32[]{:S(2)}, u32[]{:S(2)}) collective-permute-start(f32[8,8]{1,0:T(8,128)S(1)} %slice.40), channel_id=1, source_target_pairs={{0,1},{2,3},{4,5},{6,7},{8,9},{10,11},{12,13},{14,15},{16,17},{18,... | collective-permute-start | bytes 776 | tf_op jit(solution)/shard_map/ppermute | solution.py:73
  19.9 32.7 %collective-permute-start.1 = (f32[2,64,192]{2,1,0:T(8,128)S(1)}, f32[2,64,192]{2,1,0:T(8,128)S(1)}, u32[]{:S(2)}, u32[]{:S(2)}) collective-permute-start(f32[2,64,192]{2,1,0:T(8,128)S(1)} %pad_maximum_fusion.2), channel_id=1, source_target_pairs={{0,4},{2,6},{4,0},{6,2},{8,12},{10,14},{12,8},{14,10},{16,20},{18,... | collective-permute-start | bytes 294920 | tf_op jit(solution)/shard_map/ppermute | solution.py:556
  52.6 2.2 collective-permute-start.2
  54.9 74.8 %collective-permute-start.3 = (f32[2,2,2,64,192]{4,3,2,1,0:T(8,128)S(1)}, f32[2,2,2,64,192]{4,3,2,1,0:T(8,128)S(1)}, u32[]{:S(2)}, u32[]{:S(2)}) collective-permute-start(f32[2,2,2,64,192]{4,3,2,1,0:T(8,128)S(1)} %pad_maximum_fusion), channel_id=1, source_target_pairs={{0,8},{2,10},{4,12},{6,14},{8,0},{10,2},{12,4},{14,6},{16,24},{18,... | collective-permute-start | bytes 1179656 | tf_op jit(solution)/shard_map/ppermute | solution.py:556
  129.8 0.7 copy-start.6
  152.3 41.4 %all-to-all-start = ((f32[16,192,128]{2,1,0:T(8,128)}), f32[16,192,128]{2,1,0:T(8,128)}, u32[]{:S(2)}, u32[]{:S(2)}) async-start(f32[16,192,128]{2,1,0:T(8,128)} %spread_blocks.2), calls=%async_computation | async-start | bytes 3145728 | tf_op jit(solution)/shard_map/all_to_all | solution.py:50
  168.0 24.0 %collective-permute-start.5 = (f32[1,64,128]{2,1,0:T(8,128)}, f32[1,64,128]{2,1,0:T(8,128)S(1)}, u32[]{:S(2)}, u32[]{:S(2)}) collective-permute-start(f32[1,64,128]{2,1,0:T(8,128)} %get-tuple-element.30), channel_id=1, source_target_pairs={{0,2},{2,4},{4,6},{6,8},{8,10},{10,12},{12,14},{14,16},{16,18},{18... | collective-permute-start | bytes 98312 | tf_op jit(solution)/shard_map/ppermute | solution.py:59
  171.4 22.3 %collective-permute-start.6 = (f32[1,64,128]{2,1,0:T(8,128)}, f32[1,64,128]{2,1,0:T(8,128)S(1)}, u32[]{:S(2)}, u32[]{:S(2)}) collective-permute-start(f32[1,64,128]{2,1,0:T(8,128)} %get-tuple-element.31), channel_id=1, source_target_pairs={{2,0},{4,2},{6,4},{8,6},{10,8},{12,10},{14,12},{16,14},{18,16},{20... | collective-permute-start | bytes 98312 | tf_op jit(solution)/shard_map/ppermute | solution.py:59
  193.7 55.4 %all-to-all-start.3 = ((f32[16,64,512]{2,1,0:T(8,128)}), f32[16,64,512]{2,1,0:T(8,128)}, u32[]{:S(2)}, u32[]{:S(2)}) async-start(f32[16,64,512]{2,1,0:T(8,128)} %get-tuple-element.39), calls=%async_computation.3 | async-start | bytes 4194304 | tf_op jit(solution)/shard_map/all_to_all | solution.py:50
  204.3 1.7 copy-start
  206.1 40.4 %copy-start.1 = (f32[16,64,128]{2,1,0:T(8,128)S(1)}, f32[16,64,128]{2,1,0:T(8,128)}, u32[]{:S(2)}) copy-start(f32[16,64,128]{2,1,0:T(8,128)} %get-tuple-element.37.extra) | copy-start | bytes 1572868
  216.7 2.9 collective-permute-start.7
  219.6 1.9 collective-permute-start.8
  221.5 2.5 collective-permute-start.9
  224.0 10.5 %collective-permute-start.12 = (f32[2,1024]{1,0:T(2,128)S(1)}, f32[2,1024]{1,0:T(2,128)S(1)}, u32[]{:S(2)}, u32[]{:S(2)}) collective-permute-start(f32[2,1024]{1,0:T(2,128)S(1)} %add.88), channel_id=1, source_target_pairs={{0,8},{2,10},{4,12},{6,14},{8,0},{10,2},{12,4},{14,6},{16,24},{18,... | collective-permute-start | bytes 24584 | tf_op jit(solution)/shard_map/ppermute | solution.py:623
  225.6 18.9 %collective-permute-start.11 = (f32[2,1024]{1,0:T(2,128)S(1)}, f32[2,1024]{1,0:T(2,128)S(1)}, u32[]{:S(2)}, u32[]{:S(2)}) collective-permute-start(f32[2,1024]{1,0:T(2,128)S(1)} %add.88), channel_id=1, source_target_pairs={{0,16},{2,18},{4,20},{6,22},{8,24},{10,26},{12,28},{14,30},{16,0},... | collective-permute-start | bytes 24584 | tf_op jit(solution)/shard_map/ppermute | solution.py:623
  226.8 19.7 %collective-permute-start.10 = (f32[2,1024]{1,0:T(2,128)S(1)}, f32[2,1024]{1,0:T(2,128)S(1)}, u32[]{:S(2)}, u32[]{:S(2)}) collective-permute-start(f32[2,1024]{1,0:T(2,128)S(1)} %add.88), channel_id=1, source_target_pairs={{0,24},{2,26},{4,28},{6,30},{8,16},{10,18},{12,20},{14,22},{16,8},... | collective-permute-start | bytes 24584 | tf_op jit(solution)/shard_map/ppermute | solution.py:623
  249.1 75.6 %all-to-all-start.2 = ((f32[16,64,768]{2,1,0:T(8,128)}), f32[16,64,768]{2,1,0:T(8,128)S(1)}, u32[]{:S(2)}, u32[]{:S(2)}) async-start(f32[16,64,768]{2,1,0:T(8,128)} %get-tuple-element.38), calls=%async_computation.2 | async-start | bytes 6291456 | tf_op jit(solution)/shard_map/all_to_all | solution.py:50

commit v20 on v19

--- a/solution.py
+++ b/solution.py
@@ -162,8 +162,9 @@
 
     def kernel(*refs):
         out, held, come, go = refs[kinds:]
-        arrivals = []
-        for i in range(count):
+        ahead = min(4, count)
+
+        def fetch(i):
             group, to = [], 0
             for first, width in ranges:
                 for k in range(kinds):
@@ -175,10 +176,14 @@
                     copy.start()
                     group.append(copy)
                 to += width
-            arrivals.append(group)
+            return group
+
+        arrivals = [fetch(i) for i in range(ahead)]
         leaving = []
-        for i, group in enumerate(arrivals):
-            for copy in group:
+        for i in range(count):
+            if i + ahead < count:
+                arrivals.append(fetch(i + ahead))
+            for copy in arrivals[i]:
                 copy.wait()
             piece = pltpu.make_async_copy(held.at[i], out.at[i], go.at[i])
             piece.start()

time: 327 us -> 329 us (level)
  no operation moved by 1% of the time
where the time goes in v20:
time: 329 us; the launch traced here: 327 us
  waiting for transfers between devices  238 us (72%)
  Pallas kernels  45.6 us (14%)
  starting transfers between devices  36 us (11%)
  local copies, waits for them, and re-layouts  3.82 us (1%)
    ppermute x4, waiting for transfers between devices, exchange_step(): other = lax.ppermute(held, 'span', pairs)  105 us
    all_to_all x4, waiting for transfers between devices, exchange(): lax.all_to_all(pieces, 'span', split_axis=0, concat_axis=0, tiled=True)  87.3 us
    all_to_all x4, starting transfers between devices, exchange(): lax.all_to_all(pieces, 'span', split_axis=0, concat_axis=0, tiled=True)  21.2 us
    ppermute x2, waiting for transfers between devices, to_next(): return lax.ppermute(cells, ('span', 'elem'), pairs)  20.4 us
    ppermute x3, waiting for transfers between devices, tiled_device(): lax.ppermute(sums, 'span', [(i, i ^ flip) for i in range(count)])  19.6 us
    pallas_call x2, Pallas kernels, project(): pl.pallas_call(kernel, in_specs=[whole, vmem] + ([] if first else [whole]...  16.3 us
    pallas_call x2, Pallas kernels, spread_blocks(): pl.pallas_call(kernel, in_specs=[whole] * kinds, out_specs=whole, out_sha...  11.5 us
    pallas_call x1, Pallas kernels, stiffness(): pl.pallas_call(kernel, in_specs=[vmem, vmem, vmem, vmem, pl.BlockSpec(mem...  10.6 us
  transfers between devices with their start and end apart: 17, of which 13 were waited for; matrix products, arithmetic and copies ran while one was open for 1% of the time, Pallas kernels for 13%

profile of v20, /device:TPU:15, one launch (start us, length us, event | category | flops | bytes accessed | tf_op | source)
XLA Modules:
  0.0 327.2 jit_solution(17311108146868635356)
XLA Ops:
  0.6 2.4 collective-permute-start
  3.0 6.8 %spread_blocks.3 = f32[16,192,512]{2,1,0:T(8,128)} custom-call(f32[1,64,10240]{2,1,0:T(8,128)} %refs_0_.3, f32[1,64,10240]{2,1,0:T(8,128)} %refs_1_.3, f32[1,64,10240]{2,1,0:T(8,128)} %refs_2_.3), custom_call_target="tpu_custom_call" | custom-call | tf_op jit(solution)/shard_map/spread_blocks/pallas_call | solution.py:195
  9.9 5.6 %all-to-all-start.1 = ((f32[16,192,512]{2,1,0:T(8,128)}), f32[16,192,512]{2,1,0:T(8,128)}, u32[]{:S(2)}, u32[]{:S(2)}) async-start(f32[16,192,512]{2,1,0:T(8,128)} %spread_blocks.3), calls=%async_computation.1 | async-start | bytes 12582912 | tf_op jit(solution)/shard_map/all_to_all | solution.py:50
  15.8 1.3 collective-permute-start.4
  17.1 4.7 %spread_blocks.2 = f32[16,192,128]{2,1,0:T(8,128)} custom-call(f32[1,64,10240]{2,1,0:T(8,128)} %refs_0_.3, f32[1,64,10240]{2,1,0:T(8,128)} %refs_1_.3, f32[1,64,10240]{2,1,0:T(8,128)} %refs_2_.3), custom_call_target="tpu_custom_call" | custom-call | tf_op jit(solution)/shard_map/spread_blocks/pallas_call | solution.py:195
  22.9 30.2 %collective-permute-done.1 = f32[2,64,192]{2,1,0:T(8,128)S(1)} collective-permute-done((f32[2,64,192]{2,1,0:T(8,128)S(1)}, f32[2,64,192]{2,1,0:T(8,128)S(1)}, u32[]{:S(2)}, u32[]{:S(2)}) %collective-permute-start.1) | collective-permute-done | bytes 98336 | tf_op jit(solution)/shard_map/ppermute | solution.py:561
  56.8 73.5 %collective-permute-done.3 = f32[2,2,2,64,192]{4,3,2,1,0:T(8,128)S(1)} collective-permute-done((f32[2,2,2,64,192]{4,3,2,1,0:T(8,128)S(1)}, f32[2,2,2,64,192]{4,3,2,1,0:T(8,128)S(1)}, u32[]{:S(2)}, u32[]{:S(2)}) %collective-permute-start.3) | collective-permute-done | bytes 393248 | tf_op jit(solution)/shard_map/ppermute | solution.py:561
  131.1 1.1 bitcast_multiply_fusion.rot
  132.2 20.8 %all-to-all-done.1.x = f32[16,192,512]{2,1,0:T(8,128)} async-done(((f32[16,192,512]{2,1,0:T(8,128)}), f32[16,192,512]{2,1,0:T(8,128)}, u32[]{:S(2)}, u32[]{:S(2)}) %all-to-all-start.1) | async-done | bytes 6291488 | tf_op jit(solution)/shard_map/all_to_all | solution.py:50
  153.0 4.9 %all-to-all-start = ((f32[16,192,128]{2,1,0:T(8,128)}), f32[16,192,128]{2,1,0:T(8,128)}, u32[]{:S(2)}, u32[]{:S(2)}) async-start(f32[16,192,128]{2,1,0:T(8,128)} %spread_blocks.2), calls=%async_computation | async-start | bytes 3145728 | tf_op jit(solution)/shard_map/all_to_all | solution.py:50
  157.8 10.8 %project.2 = (f32[16,64,640]{2,1,0:T(8,128)}, f32[16,64,512]{2,1,0:T(8,128)}, f32[1,64,128]{2,1,0:T(8,128)}, f32[1,64,128]{2,1,0:T(8,128)}) custom-call(f32[16,192,512]{2,1,0:T(8,128)} %all-to-all-done.1.x, f32[16,64,192]{2,1,0:T(8,128)} %bitcast_multiply_fusion.rot), custom_call_target="tpu_custom_call" | custom-call | flops 1207959552 | bytes 10485760 | tf_op jit(solution)/shard_map/project/pallas_call | solution.py:392
  168.6 3.3 %collective-permute-start.5 = (f32[1,64,128]{2,1,0:T(8,128)}, f32[1,64,128]{2,1,0:T(8,128)S(1)}, u32[]{:S(2)}, u32[]{:S(2)}) collective-permute-start(f32[1,64,128]{2,1,0:T(8,128)} %get-tuple-element.30), channel_id=1, source_target_pairs={{0,2},{2,4},{4,6},{6,8},{8,10},{10,12},{12,14},{14,16},{16,18},{18... | collective-permute-start | bytes 98312 | tf_op jit(solution)/shard_map/ppermute | solution.py:59
  172.0 1.9 collective-permute-start.6
  173.9 18.7 %collective-permute-done.5.left = f32[1,64,128]{2,1,0:T(8,128)S(1)} collective-permute-done((f32[1,64,128]{2,1,0:T(8,128)}, f32[1,64,128]{2,1,0:T(8,128)S(1)}, u32[]{:S(2)}, u32[]{:S(2)}) %collective-permute-start.5) | collective-permute-done | bytes 32800 | tf_op jit(solution)/shard_map/ppermute | solution.py:59
  192.6 1.7 collective-permute-done.6.right
  194.3 5.1 %all-to-all-start.3 = ((f32[16,64,512]{2,1,0:T(8,128)}), f32[16,64,512]{2,1,0:T(8,128)}, u32[]{:S(2)}, u32[]{:S(2)}) async-start(f32[16,64,512]{2,1,0:T(8,128)} %get-tuple-element.39), calls=%async_computation.3 | async-start | bytes 4194304 | tf_op jit(solution)/shard_map/all_to_all | solution.py:50
  199.4 5.5 %project.3 = (f32[16,64,640]{2,1,0:T(8,128)}, f32[16,64,128]{2,1,0:T(8,128)}) custom-call(f32[16,192,128]{2,1,0:T(8,128)} %all-to-all-done.x, f32[16,64,192]{2,1,0:T(8,128)} %bitcast_multiply_fusion.rot, f32[16,64,640]{2,1,0:T(8,128)} %get-tuple-element.27.refs_0_), custom_call_target="tpu_custom_call", output_to_operand_aliasing={{0}: (2, {})} | custom-call | flops 301989888 | bytes 2621440 | tf_op jit(solution)/shard_map/project/pallas_call | solution.py:392
  204.9 1.7 copy-done
  206.7 10.6 %stiffness.1 = (f32[16,64,640]{2,1,0:T(8,128)S(1)}, f32[2,1024]{1,0:T(2,128)S(1)}) custom-call(f32[16,64,640]{2,1,0:T(8,128)S(1)} %copy-done, f32[1,64,128]{2,1,0:T(8,128)S(1)} %collective-permute-done.5.left, f32[1,64,128]{2,1,0:T(8,128)S(1)} %collective-permute-done.6.right, f32[18,640]{1,0:T(8,128)S(1)} %concatenate.8.band, f32[16]{0:T(128)S(1)} %fusion.6.lam), custom_call_target="tpu_custom_call" | custom-call | tf_op jit(solution)/shard_map/stiffness/pallas_call | solution.py:475
  217.3 2.9 collective-permute-done.7
  220.2 1.1 collective-permute-start.8
  222.4 2.2 collective-permute-done.9
  224.6 1.6 collective-permute-start.12
  226.2 1.2 collective-permute-start.11
  227.5 7.7 %collective-permute-done.12 = f32[2,1024]{1,0:T(2,128)S(1)} collective-permute-done((f32[2,1024]{1,0:T(2,128)S(1)}, f32[2,1024]{1,0:T(2,128)S(1)}, u32[]{:S(2)}, u32[]{:S(2)}) %collective-permute-start.12) | collective-permute-done | bytes 8224 | tf_op jit(solution)/shard_map/ppermute | solution.py:628
  235.2 9.9 %collective-permute-done.11 = f32[2,1024]{1,0:T(2,128)S(1)} collective-permute-done((f32[2,1024]{1,0:T(2,128)S(1)}, f32[2,1024]{1,0:T(2,128)S(1)}, u32[]{:S(2)}, u32[]{:S(2)}) %collective-permute-start.11) | collective-permute-done | bytes 8224 | tf_op jit(solution)/shard_map/ppermute | solution.py:628
  245.1 1.9 collective-permute-done.10
  247.1 2.6 residual_back.1
  249.7 5.7 %all-to-all-start.2 = ((f32[16,64,768]{2,1,0:T(8,128)}), f32[16,64,768]{2,1,0:T(8,128)S(1)}, u32[]{:S(2)}, u32[]{:S(2)}) async-start(f32[16,64,768]{2,1,0:T(8,128)} %get-tuple-element.38), calls=%async_computation.2 | async-start | bytes 6291456 | tf_op jit(solution)/shard_map/all_to_all | solution.py:50
  256.0 2.8 collect_early.1._
  258.8 66.5 %all-to-all-done.2.last = f32[16,64,768]{2,1,0:T(8,128)S(1)} async-done(((f32[16,64,768]{2,1,0:T(8,128)}), f32[16,64,768]{2,1,0:T(8,128)S(1)}, u32[]{:S(2)}, u32[]{:S(2)}) %all-to-all-start.2) | async-done | bytes 3145760 | tf_op jit(solution)/shard_map/all_to_all | solution.py:50
  325.3 1.9 collect_late.1
  (54 shorter events, 7.7 us)
Async XLA Ops:
  0.6 9.2 %collective-permute-start = (f32[64,192]{1,0:T(8,128)}, f32[64,192]{1,0:T(8,128)S(1)}, u32[]{:S(2)}, u32[]{:S(2)}) collective-permute-start(f32[64,192]{1,0:T(8,128)} %bitcast.25), channel_id=1, source_target_pairs={{0,16},{2,18},{4,20},{6,22},{8,24},{10,26},{12,28},{14,30},{16,0},... | collective-permute-start | bytes 147464 | tf_op jit(solution)/shard_map/ppermute | solution.py:561
  3.0 6.9 %copy-start.2 = (f32[1,192,64]{1,2,0:T(8,128)S(1)}, f32[1,192,64]{1,2,0:T(8,128)}, u32[]{:S(2)}) copy-start(f32[1,192,64]{1,2,0:T(8,128)} %param.18) | copy-start | bytes 147460
  9.9 5.7 %copy-start.3 = (f32[10240]{0:T(1024)S(1)}, f32[10240]{0:T(1024)}, u32[]{:S(2)}) copy-start(f32[10240]{0:T(1024)} %param.14) | copy-start | bytes 122884
  9.9 5.6 %copy-start.4 = (f32[10240]{0:T(1024)S(1)}, f32[10240]{0:T(1024)}, u32[]{:S(2)}) copy-start(f32[10240]{0:T(1024)} %param.15) | copy-start | bytes 122884
  9.9 5.6 %copy-start.5 = (s32[10240]{0:T(1024)S(1)}, s32[10240]{0:T(1024)}, u32[]{:S(2)}) copy-start(s32[10240]{0:T(1024)} %param.16) | copy-start | bytes 122884
  9.9 143.0 %all-to-all-start.1 = ((f32[16,192,512]{2,1,0:T(8,128)}), f32[16,192,512]{2,1,0:T(8,128)}, u32[]{:S(2)}, u32[]{:S(2)}) async-start(f32[16,192,512]{2,1,0:T(8,128)} %spread_blocks.3), calls=%async_computation.1 | async-start | bytes 12582912 | tf_op jit(solution)/shard_map/all_to_all | solution.py:50
  15.8 7.0 %collective-permute-start.4 = (f32[8,8]{1,0:T(8,128)S(1)}, f32[8,8]{1,0:T(8,128)S(1)}, u32[]{:S(2)}, u32[]{:S(2)}) collective-permute-start(f32[8,8]{1,0:T(8,128)S(1)} %slice.40), channel_id=1, source_target_pairs={{0,1},{2,3},{4,5},{6,7},{8,9},{10,11},{12,13},{14,15},{16,17},{18,... | collective-permute-start | bytes 776 | tf_op jit(solution)/shard_map/ppermute | solution.py:73
  22.6 30.6 %collective-permute-start.1 = (f32[2,64,192]{2,1,0:T(8,128)S(1)}, f32[2,64,192]{2,1,0:T(8,128)S(1)}, u32[]{:S(2)}, u32[]{:S(2)}) collective-permute-start(f32[2,64,192]{2,1,0:T(8,128)S(1)} %pad_maximum_fusion.2), channel_id=1, source_target_pairs={{0,4},{2,6},{4,0},{6,2},{8,12},{10,14},{12,8},{14,10},{16,20},{18,... | collective-permute-start | bytes 294920 | tf_op jit(solution)/shard_map/ppermute | solution.py:561
  53.2 2.2 collective-permute-start.2
  55.5 74.8 %collective-permute-start.3 = (f32[2,2,2,64,192]{4,3,2,1,0:T(8,128)S(1)}, f32[2,2,2,64,192]{4,3,2,1,0:T(8,128)S(1)}, u32[]{:S(2)}, u32[]{:S(2)}) collective-permute-start(f32[2,2,2,64,192]{4,3,2,1,0:T(8,128)S(1)} %pad_maximum_fusion), channel_id=1, source_target_pairs={{0,8},{2,10},{4,12},{6,14},{8,0},{10,2},{12,4},{14,6},{16,24},{18,... | collective-permute-start | bytes 1179656 | tf_op jit(solution)/shard_map/ppermute | solution.py:561
  130.4 0.7 copy-start.6
  153.0 41.4 %all-to-all-start = ((f32[16,192,128]{2,1,0:T(8,128)}), f32[16,192,128]{2,1,0:T(8,128)}, u32[]{:S(2)}, u32[]{:S(2)}) async-start(f32[16,192,128]{2,1,0:T(8,128)} %spread_blocks.2), calls=%async_computation | async-start | bytes 3145728 | tf_op jit(solution)/shard_map/all_to_all | solution.py:50
  168.6 24.0 %collective-permute-start.5 = (f32[1,64,128]{2,1,0:T(8,128)}, f32[1,64,128]{2,1,0:T(8,128)S(1)}, u32[]{:S(2)}, u32[]{:S(2)}) collective-permute-start(f32[1,64,128]{2,1,0:T(8,128)} %get-tuple-element.30), channel_id=1, source_target_pairs={{0,2},{2,4},{4,6},{6,8},{8,10},{10,12},{12,14},{14,16},{16,18},{18... | collective-permute-start | bytes 98312 | tf_op jit(solution)/shard_map/ppermute | solution.py:59
  172.0 22.3 %collective-permute-start.6 = (f32[1,64,128]{2,1,0:T(8,128)}, f32[1,64,128]{2,1,0:T(8,128)S(1)}, u32[]{:S(2)}, u32[]{:S(2)}) collective-permute-start(f32[1,64,128]{2,1,0:T(8,128)} %get-tuple-element.31), channel_id=1, source_target_pairs={{2,0},{4,2},{6,4},{8,6},{10,8},{12,10},{14,12},{16,14},{18,16},{20... | collective-permute-start | bytes 98312 | tf_op jit(solution)/shard_map/ppermute | solution.py:59
  194.3 55.4 %all-to-all-start.3 = ((f32[16,64,512]{2,1,0:T(8,128)}), f32[16,64,512]{2,1,0:T(8,128)}, u32[]{:S(2)}, u32[]{:S(2)}) async-start(f32[16,64,512]{2,1,0:T(8,128)} %get-tuple-element.39), calls=%async_computation.3 | async-start | bytes 4194304 | tf_op jit(solution)/shard_map/all_to_all | solution.py:50
  204.9 1.7 copy-start
  206.7 40.4 %copy-start.1 = (f32[16,64,128]{2,1,0:T(8,128)S(1)}, f32[16,64,128]{2,1,0:T(8,128)}, u32[]{:S(2)}) copy-start(f32[16,64,128]{2,1,0:T(8,128)} %get-tuple-element.37.extra) | copy-start | bytes 1572868
  217.3 2.9 collective-permute-start.7
  220.2 1.9 collective-permute-start.8
  222.1 2.5 collective-permute-start.9
  224.6 10.6 %collective-permute-start.12 = (f32[2,1024]{1,0:T(2,128)S(1)}, f32[2,1024]{1,0:T(2,128)S(1)}, u32[]{:S(2)}, u32[]{:S(2)}) collective-permute-start(f32[2,1024]{1,0:T(2,128)S(1)} %add.88), channel_id=1, source_target_pairs={{0,8},{2,10},{4,12},{6,14},{8,0},{10,2},{12,4},{14,6},{16,24},{18,... | collective-permute-start | bytes 24584 | tf_op jit(solution)/shard_map/ppermute | solution.py:628
  226.2 18.9 %collective-permute-start.11 = (f32[2,1024]{1,0:T(2,128)S(1)}, f32[2,1024]{1,0:T(2,128)S(1)}, u32[]{:S(2)}, u32[]{:S(2)}) collective-permute-start(f32[2,1024]{1,0:T(2,128)S(1)} %add.88), channel_id=1, source_target_pairs={{0,16},{2,18},{4,20},{6,22},{8,24},{10,26},{12,28},{14,30},{16,0},... | collective-permute-start | bytes 24584 | tf_op jit(solution)/shard_map/ppermute | solution.py:628
  227.4 19.7 %collective-permute-start.10 = (f32[2,1024]{1,0:T(2,128)S(1)}, f32[2,1024]{1,0:T(2,128)S(1)}, u32[]{:S(2)}, u32[]{:S(2)}) collective-permute-start(f32[2,1024]{1,0:T(2,128)S(1)} %add.88), channel_id=1, source_target_pairs={{0,24},{2,26},{4,28},{6,30},{8,16},{10,18},{12,20},{14,22},{16,8},... | collective-permute-start | bytes 24584 | tf_op jit(solution)/shard_map/ppermute | solution.py:628
  249.7 75.6 %all-to-all-start.2 = ((f32[16,64,768]{2,1,0:T(8,128)}), f32[16,64,768]{2,1,0:T(8,128)S(1)}, u32[]{:S(2)}, u32[]{:S(2)}) async-start(f32[16,64,768]{2,1,0:T(8,128)} %get-tuple-element.38), calls=%async_computation.2 | async-start | bytes 6291456 | tf_op jit(solution)/shard_map/all_to_all | solution.py:50
